TPU v7x, 128 devices: a whole 4x4x4 slice. The times are simulated.
128 devices in a mesh: ctx: 16 (over x, y), fsdp: 8 (over z, core).
Axes of the slice: x: 4, y: 4, z: 4, core: 2. Of those that a mesh axis runs over, the one named last changes fastest.
Arguments:
- tokens: bfloat16 [8, 32, 64, 2048], P('fsdp', 'ctx'), may hold values from -6 to 6
- norm_gain: float32 [2048], replicated, may hold values from 0.5 to 1.5
- w_in: bfloat16 [2048, 6704], P('fsdp'), may hold values from -0.125 to 0.125
- w_qkv: bfloat16 [2048, 1536], P('fsdp'), may hold values from -0.125 to 0.125
- conv_weight: float32 [4, 3584], replicated, may hold values from -3 to 3
- conv_bias: float32 [3584], replicated, may hold values from -3 to 3
- dt_bias: float32 [48], replicated, may hold values from -1 to 1
- a_log: float32 [48], replicated, may hold values from -7 to -3
- d_skip: float32 [48], replicated, may hold values from 0.5 to 1.5
- mamba_gain: float32 [3072], replicated, may hold values from 0.5 to 1.5
- w_mout: bfloat16 [3072, 2048], P('fsdp'), may hold values from -0.109375 to 0.109375
- w_aout: bfloat16 [1024, 2048], P('fsdp'), may hold values from -0.5 to 0.5
- mlp_gain: float32 [2048], replicated, may hold values from 0.5 to 1.5
- w_gate_up: bfloat16 [2048, 8192], P('fsdp'), may hold values from -0.125 to 0.125
- w_down: bfloat16 [4096, 2048], P('fsdp'), may hold values from -0.09375 to 0.09375
- cotangent: bfloat16 [8, 32, 64, 2048], P('fsdp', 'ctx'), may hold values from -6 to 6
Outputs:
- output: bfloat16 [8, 32, 64, 2048], P('fsdp', 'ctx')
- d_tokens: bfloat16 [8, 32, 64, 2048], P('fsdp', 'ctx')
- g_norm_gain: float32 [2048], replicated
- g_w_in: float32 [2048, 6704], P('fsdp')
- g_w_qkv: float32 [2048, 1536], P('fsdp')
- g_conv_weight: float32 [4, 3584], replicated
- g_conv_bias: float32 [3584], replicated
- g_dt_bias: float32 [48], replicated
- g_a_log: float32 [48], replicated
- g_d_skip: float32 [48], replicated
- g_mamba_gain: float32 [3072], replicated
- g_w_mout: float32 [3072, 2048], P('fsdp')
- g_w_aout: float32 [1024, 2048], P('fsdp')
- g_mlp_gain: float32 [2048], replicated
- g_w_gate_up: float32 [2048, 8192], P('fsdp')
- g_w_down: float32 [4096, 2048], P('fsdp')
All inputs are finite; a program needn't handle non-finite values.
Results may differ from a plain program's by a relative error of at most 0.024.
Values may be sent and summed in bfloat16 or wider, within the bound.
No kernel may reach another device: no remote copies, remote signals or barrier semaphores. Data moves between devices by JAX's collectives and lax.ppermute only.
A program may use at most 576 MiB of HBM per device.

v0:
```python
import jax
import jax.numpy as jnp
from jax import lax
from jax.sharding import PartitionSpec as P

MDIM = 64
STATE = 256
QHEADS = 8
KVHEADS = 2
HDIM = 128


EPS = 1e-06
ROPE_BASE = 100000000000.0
HIGH = lax.Precision.HIGHEST
MASKED = -1e30


def with_halo(shard, sides, width):
    for axis, dim in sides:
        size, length = (lax.axis_size(axis), shard.shape[dim])
        up = [(i, (i + 1) % size) for i in range(size - 1)]
        down = [(j, i) for i, j in up]
        last = lax.slice_in_dim(shard, length - width, length, axis=dim)
        first = lax.slice_in_dim(shard, 0, width, axis=dim)
        before = lax.ppermute(last, axis, up)
        after = lax.ppermute(first, axis, down)
        shard = jnp.concatenate([before, shard, after], axis=dim)
    return shard


def carried_in(value, axis, join, neutral, backward):
    count, mine = (lax.axis_size(axis), lax.axis_index(axis))
    pieces = jax.tree.map(lambda part: lax.all_gather(part, axis), value)
    if backward:
        pieces = jax.tree.map(lambda part: part[::-1], pieces)
        mine = count - 1 - mine
    running = jax.tree.map(
        lambda part, zero: jnp.full_like(part, 0) + jnp.asarray(zero, part.dtype), value, neutral
    )

    def step(position, running):
        longer = join(running, jax.tree.map(lambda part: part[position], pieces))
        return jax.tree.map(lambda new, old: jnp.where(position < mine, new, old), longer, running)

    return lax.fori_loop(0, count - 1, step, running)


def norm_rows(values, gain):
    return values * lax.rsqrt(jnp.mean(values * values, axis=-1, keepdims=True) + EPS) * gain


def rotate(values, positions, sign):
    half_dim = values.shape[-1] // 2
    freqs = ROPE_BASE ** (-jnp.arange(half_dim, dtype=jnp.float32) / half_dim)
    angles = positions.astype(jnp.float32)[:, None] * freqs[None, :]
    cosine = jnp.cos(angles)[:, None, :]
    sine = sign * jnp.sin(angles)[:, None, :]
    first = values[..., :half_dim]
    second = values[..., half_dim:]
    return jnp.concatenate(
        [first * cosine - second * sine, second * cosine + first * sine], axis=-1
    )


def dot_last(left, right):
    return lax.dot_general(
        left, right, (((1,), (1,)), ((), ())), preferred_element_type=jnp.float32
    )


def dot_first(left, right):
    return lax.dot_general(
        left, right, (((0,), (0,)), ((), ())), preferred_element_type=jnp.float32
    )


def swiglu(gate, upper):
    return jax.nn.silu(gate) * upper


def chain_step(earlier, later):
    return (earlier[0] * later[0], later[0][:, None, None] * earlier[1] + later[1])


def pick(flag, first, second):
    return (jnp.where(flag, first[0], second[0]), jnp.where(flag, first[1], second[1]))


def mamba_front(xbc, prev_rows, dt_raw, conv_weight, conv_bias, dt_bias, a_log):
    rows = xbc.shape[1]
    taps = conv_weight.shape[0]
    heads = a_log.shape[0]
    inner = heads * MDIM
    extended = jnp.concatenate([prev_rows, xbc], axis=1)
    mixed = (
        sum((conv_weight[tap] * extended[:, tap : tap + rows] for tap in range(taps))) + conv_bias
    )
    active = jax.nn.silu(mixed)
    xs = active[..., :inner].reshape(xbc.shape[0], rows, heads, MDIM)
    bmat = active[..., inner : inner + STATE]
    cmat = active[..., inner + STATE :]
    steps_dt = jax.nn.softplus(dt_raw + dt_bias)
    cumul = jnp.cumsum(steps_dt * -jnp.exp(a_log), axis=1)
    return (xs, bmat, cmat, steps_dt, cumul)


def mamba_summary(xs, bmat, cmat, steps_dt, cumul):
    weights = jnp.exp(cumul[:, -1:, :] - cumul) * steps_dt
    local = jnp.einsum("bsh,bshp,bsn->bhpn", weights, xs, bmat, precision=HIGH)
    return (jnp.exp(cumul[:, -1, :]), local)


def mamba_readout(xs, bmat, cmat, steps_dt, cumul, gate_z, states_in, d_skip, mamba_gain):
    rows = xs.shape[1]
    lower = (jnp.arange(rows)[:, None] >= jnp.arange(rows)[None, :])[None, :, :, None]
    gaps = cumul[:, :, None, :] - cumul[:, None, :, :]
    decays = jnp.where(lower, jnp.exp(jnp.where(lower, gaps, 0.0)), 0.0)
    intersection = jnp.einsum("btn,bsn->bts", cmat, bmat, precision=HIGH)
    mixing = intersection[..., None] * decays * steps_dt[:, None, :, :]
    within = jnp.einsum("btsh,bshp->bthp", mixing, xs, precision=HIGH)
    carried = jnp.exp(cumul)[..., None] * jnp.einsum(
        "btn,bhpn->bthp", cmat, states_in, precision=HIGH
    )
    result = within + carried + d_skip[:, None] * xs
    gated = result.reshape(xs.shape[0], rows, -1) * jax.nn.silu(gate_z)
    return norm_rows(gated, mamba_gain)


def shards(
    tokens,
    norm_gain,
    w_in,
    w_qkv,
    conv_weight,
    conv_bias,
    dt_bias,
    a_log,
    d_skip,
    mamba_gain,
    w_mout,
    w_aout,
    mlp_gain,
    w_gate_up,
    w_down,
    cotangent,
):
    slots = tokens.shape[1]
    half = tokens.shape[2]
    width = tokens.shape[3]
    rows = slots * half
    ctx_size = lax.axis_size("ctx")
    ctx_index = lax.axis_index("ctx")
    is_last = ctx_index == ctx_size - 1
    heads = a_log.shape[0]
    inner = heads * MDIM
    conv_width = conv_weight.shape[1]
    edge = conv_weight.shape[0] - 1
    width_q = QHEADS * HDIM
    width_k = KVHEADS * HDIM
    groups = QHEADS // KVHEADS
    scale = HDIM ** (-0.5)
    in_full, qkv_full, mout_full, aout_full, gu_full, down_full = (
        lax.all_gather(w_in, "fsdp", axis=0, tiled=True),
        lax.all_gather(w_qkv, "fsdp", axis=0, tiled=True),
        lax.all_gather(w_mout, "fsdp", axis=0, tiled=True),
        lax.all_gather(w_aout, "fsdp", axis=0, tiled=True),
        lax.all_gather(w_gate_up, "fsdp", axis=0, tiled=True),
        lax.all_gather(w_down, "fsdp", axis=0, tiled=True),
    )
    hidden_in = tokens.reshape(rows, width).astype(jnp.float32)
    normed, norm_back = jax.vjp(norm_rows, hidden_in, norm_gain)
    normed_low = normed.astype(jnp.bfloat16)
    proj = jnp.dot(normed_low, in_full, preferred_element_type=jnp.float32)
    qkv = jnp.dot(normed_low, qkv_full, preferred_element_type=jnp.float32)
    gate_z = proj[:, :inner].reshape(slots, half, inner)
    xbc = proj[:, inner : inner + conv_width].reshape(slots, half, conv_width)
    dt_raw = proj[:, inner + conv_width :].reshape(slots, half, heads)
    tails = jnp.stack([xbc[1, half - edge :], xbc[0, half - edge :]])
    framed = with_halo(tails, (("ctx", 0),), 1)
    prev_rows = jnp.stack([framed[0], jnp.where(is_last, tails[1], framed[3])])
    front_out, front_back = jax.vjp(
        mamba_front, xbc, prev_rows, dt_raw, conv_weight, conv_bias, dt_bias, a_log
    )
    xs, bmat, cmat, steps_dt, cumul = front_out
    (decay, local), summary_back = jax.vjp(mamba_summary, xs, bmat, cmat, steps_dt, cumul)
    identity = (jnp.ones_like(decay[0]), jnp.zeros_like(local[0]))
    before_low = carried_in((decay[0], local[0]), "ctx", chain_step, identity, False)
    through_low = chain_step(before_low, (decay[0], local[0]))
    own_high = (decay[1], local[1])
    seed_high = pick(is_last, chain_step(through_low, own_high), own_high)
    after_high = carried_in((seed_high[0], seed_high[1]), "ctx", chain_step, identity, True)
    states_in = jnp.stack([before_low[1], jnp.where(is_last, through_low[1], after_high[1])])
    mamba_gated, readout_back = jax.vjp(
        mamba_readout, xs, bmat, cmat, steps_dt, cumul, gate_z, states_in, d_skip, mamba_gain
    )
    gated_low = mamba_gated.reshape(rows, inner).astype(jnp.bfloat16)
    mamba_out = jnp.dot(gated_low, mout_full, preferred_element_type=jnp.float32)
    block_ids = jnp.stack([ctx_index, 2 * ctx_size - 1 - ctx_index])
    positions = (block_ids[:, None] * half + jnp.arange(half, dtype=jnp.int32)[None, :]).reshape(
        rows
    )
    query = rotate(qkv[:, :width_q].reshape(rows, QHEADS, HDIM), positions, 1.0)
    keys = rotate(qkv[:, width_q : width_q + width_k].reshape(rows, KVHEADS, HDIM), positions, 1.0)
    query_low = query.astype(jnp.bfloat16).reshape(rows, KVHEADS, groups, HDIM)
    keys_low = keys.astype(jnp.bfloat16).reshape(slots, half, width_k)
    values_low = qkv[:, width_q + width_k :].astype(jnp.bfloat16).reshape(slots, half, width_k)
    key_all, value_all = (
        lax.all_gather(keys_low, "ctx", axis=0, tiled=True),
        lax.all_gather(values_low, "ctx", axis=0, tiled=True),
    )
    total_keys = key_all.shape[0] * half
    key_flat = key_all.reshape(total_keys, KVHEADS, HDIM)
    value_flat = value_all.reshape(total_keys, KVHEADS, HDIM)
    order = jnp.arange(2 * ctx_size, dtype=jnp.int32)
    owner_block = jnp.where(order % 2 == 0, order // 2, 2 * ctx_size - 1 - order // 2)
    key_pos = (owner_block[:, None] * half + jnp.arange(half, dtype=jnp.int32)[None, :]).reshape(
        total_keys
    )
    visible = (key_pos[None, :] <= positions[:, None])[None, None]

    def attn_scores():
        raw = (
            jnp.einsum("tkgd,skd->kgts", query_low, key_flat, preferred_element_type=jnp.float32)
            * scale
        )
        return jnp.where(visible, raw, MASKED)

    scores = attn_scores()
    top = jnp.max(scores, axis=-1, keepdims=True)
    lse = top + jnp.log(jnp.sum(jnp.exp(scores - top), axis=-1, keepdims=True))
    probs_low = jnp.exp(scores - lse).astype(jnp.bfloat16)
    heads_out = jnp.einsum(
        "kgts,skd->tkgd", probs_low, value_flat, preferred_element_type=jnp.float32
    )
    heads_low = heads_out.reshape(rows, width_q).astype(jnp.bfloat16)
    attn_out = jnp.dot(heads_low, aout_full, preferred_element_type=jnp.float32)
    mixed = hidden_in + mamba_out + attn_out
    normed_two, norm_two_back = jax.vjp(norm_rows, mixed, mlp_gain)
    normed_two_low = normed_two.astype(jnp.bfloat16)
    gate_up = jnp.dot(normed_two_low, gu_full, preferred_element_type=jnp.float32)
    ff = gate_up.shape[1] // 2
    act, act_back = jax.vjp(swiglu, gate_up[:, :ff], gate_up[:, ff:])
    act_low = act.astype(jnp.bfloat16)
    result = mixed + jnp.dot(act_low, down_full, preferred_element_type=jnp.float32)
    output = result.astype(jnp.bfloat16).reshape(tokens.shape)
    in_full, qkv_full, mout_full, aout_full, gu_full, down_full = (
        lax.all_gather(w_in, "fsdp", axis=0, tiled=True),
        lax.all_gather(w_qkv, "fsdp", axis=0, tiled=True),
        lax.all_gather(w_mout, "fsdp", axis=0, tiled=True),
        lax.all_gather(w_aout, "fsdp", axis=0, tiled=True),
        lax.all_gather(w_gate_up, "fsdp", axis=0, tiled=True),
        lax.all_gather(w_down, "fsdp", axis=0, tiled=True),
    )
    upper_low = cotangent.reshape(rows, width)
    upstream = upper_low.astype(jnp.float32)
    d_act = dot_last(upper_low, down_full)
    d_gate, d_upper = act_back(d_act)
    d_gu_low = jnp.concatenate([d_gate, d_upper], axis=1).astype(jnp.bfloat16)
    d_mixed, d_mlp_gain = norm_two_back(dot_last(d_gu_low, gu_full))
    d_mixed = d_mixed + upstream
    branch_low = d_mixed.astype(jnp.bfloat16)
    d_heads = (
        dot_last(branch_low, aout_full).astype(jnp.bfloat16).reshape(rows, KVHEADS, groups, HDIM)
    )
    scores = attn_scores()
    probs = jnp.exp(scores - lse)
    probs_low = probs.astype(jnp.bfloat16)
    d_probs = jnp.einsum("tkgd,skd->kgts", d_heads, value_flat, preferred_element_type=jnp.float32)
    d_value_all = jnp.einsum(
        "kgts,tkgd->skd", probs_low, d_heads, preferred_element_type=jnp.float32
    )
    d_scores = (probs * (d_probs - jnp.sum(probs * d_probs, axis=-1, keepdims=True))).astype(
        jnp.bfloat16
    )
    d_query = (
        jnp.einsum("kgts,skd->tkgd", d_scores, key_flat, preferred_element_type=jnp.float32) * scale
    )
    d_key_all = (
        jnp.einsum("kgts,tkgd->skd", d_scores, query_low, preferred_element_type=jnp.float32)
        * scale
    )
    d_key_own, d_value_own = (
        lax.psum_scatter(
            d_key_all.reshape(2 * ctx_size, half, width_k).astype(jnp.bfloat16),
            "ctx",
            scatter_dimension=0,
            tiled=True,
        ).astype(jnp.float32),
        lax.psum_scatter(
            d_value_all.reshape(2 * ctx_size, half, width_k).astype(jnp.bfloat16),
            "ctx",
            scatter_dimension=0,
            tiled=True,
        ).astype(jnp.float32),
    )
    d_query = rotate(d_query.reshape(rows, QHEADS, HDIM), positions, -1.0).reshape(rows, width_q)
    d_key = rotate(d_key_own.reshape(rows, KVHEADS, HDIM), positions, -1.0).reshape(rows, width_k)
    d_qkv_low = jnp.concatenate(
        [d_query, d_key, d_value_own.reshape(rows, width_k)], axis=1
    ).astype(jnp.bfloat16)
    d_gated = dot_last(branch_low, mout_full).reshape(slots, half, inner)
    r_xs, r_bmat, r_cmat, r_steps, r_cumul, d_gate_z, direct, d_dskip, d_mgain = readout_back(
        d_gated
    )
    before_high = carried_in((decay[1], direct[1]), "ctx", chain_step, identity, False)
    through_high = chain_step(before_high, (decay[1], direct[1]))
    own_low = (decay[0], direct[0])
    seed_low = pick(is_last, chain_step(through_high, own_low), own_low)
    after_low = carried_in((seed_low[0], seed_low[1]), "ctx", chain_step, identity, True)
    exits = jnp.stack([jnp.where(is_last, through_high[1], after_low[1]), before_high[1]])
    d_decay = jnp.sum(exits * states_in, axis=(2, 3))
    s_xs, s_bmat, s_cmat, s_steps, s_cumul = summary_back((d_decay, exits))
    d_xbc, d_prev, d_dt_raw, d_conv_w, d_conv_b, d_dt_bias, d_a_log = front_back(
        (r_xs + s_xs, r_bmat + s_bmat, r_cmat + s_cmat, r_steps + s_steps, r_cumul + s_cumul)
    )
    to_right = jnp.where(is_last, 0.0, d_prev[1])
    returned = with_halo(
        jnp.stack([d_prev[0], to_right]).astype(jnp.bfloat16), (("ctx", 0),), 1
    ).astype(jnp.float32)
    own_edge = jnp.where(is_last, d_prev[1], 0.0) + returned[3]
    d_xbc = d_xbc.at[0, half - edge :].add(own_edge)
    d_xbc = d_xbc.at[1, half - edge :].add(returned[0])
    d_proj_low = jnp.concatenate(
        [
            d_gate_z.reshape(rows, inner),
            d_xbc.reshape(rows, conv_width),
            d_dt_raw.reshape(rows, heads),
        ],
        axis=1,
    ).astype(jnp.bfloat16)
    d_normed = dot_last(d_proj_low, in_full) + dot_last(d_qkv_low, qkv_full)
    d_hidden, d_norm_gain = norm_back(d_normed)
    d_tokens = (d_hidden + d_mixed).astype(jnp.bfloat16).reshape(tokens.shape)

    def shard_sum(term):
        return lax.psum_scatter(
            term.astype(jnp.bfloat16), "fsdp", scatter_dimension=0, tiled=True
        ).astype(jnp.float32)

    shard_in = shard_sum(dot_first(normed_low, d_proj_low))
    shard_qkv = shard_sum(dot_first(normed_low, d_qkv_low))
    shard_mout = shard_sum(dot_first(gated_low, branch_low))
    shard_aout = shard_sum(dot_first(heads_low, branch_low))
    shard_gu = shard_sum(dot_first(normed_two_low, d_gu_low))
    shard_down = shard_sum(dot_first(act_low, upper_low))
    summed = (
        lax.psum(shard_in.astype(jnp.bfloat16), "ctx").astype(jnp.float32),
        lax.psum(shard_qkv.astype(jnp.bfloat16), "ctx").astype(jnp.float32),
        lax.psum(shard_mout.astype(jnp.bfloat16), "ctx").astype(jnp.float32),
        lax.psum(shard_aout.astype(jnp.bfloat16), "ctx").astype(jnp.float32),
        lax.psum(shard_gu.astype(jnp.bfloat16), "ctx").astype(jnp.float32),
        lax.psum(shard_down.astype(jnp.bfloat16), "ctx").astype(jnp.float32),
    )
    small = lax.psum(
        (d_norm_gain, d_conv_w, d_conv_b, d_dt_bias, d_a_log, d_dskip, d_mgain, d_mlp_gain),
        ("ctx", "fsdp"),
    )
    return (
        output,
        d_tokens,
        small[0],
        summed[0],
        summed[1],
        small[1],
        small[2],
        small[3],
        small[4],
        small[5],
        small[6],
        summed[2],
        summed[3],
        small[7],
        summed[4],
        summed[5],
    )


def solution(mesh):
    placed = (
        P("fsdp", "ctx", None, None),
        P(),
        P("fsdp", None),
        P("fsdp", None),
        P(),
        P(),
        P(),
        P(),
        P(),
        P(),
        P("fsdp", None),
        P("fsdp", None),
        P(),
        P("fsdp", None),
        P("fsdp", None),
        P("fsdp", "ctx", None, None),
    )
    return jax.shard_map(
        shards,
        mesh=mesh,
        in_specs=placed,
        out_specs=(
            P("fsdp", "ctx", None, None),
            P("fsdp", "ctx", None, None),
            P(),
            P("fsdp", None),
            P("fsdp", None),
            P(),
            P(),
            P(),
            P(),
            P(),
            P(),
            P("fsdp", None),
            P("fsdp", None),
            P(),
            P("fsdp", None),
            P("fsdp", None),
        ),
        check_vma=False,
    )
```

profile of v0, /device:TPU:16, one launch (start us, length us, event | category | flops | bytes accessed | tf_op | source)
XLA Modules:
  0.0 2919.1 jit_solution(12512038961160354928)
XLA Ops:
  9.8 138.8 %all-gather.19.cloned.1.call-done = bf16[2048,6704]{0,1:T(8,128)(2,1)} async-done(((bf16[256,6704]{0,1:T(8,128)(2,1)}), bf16[2048,6704]{0,1:T(8,128)(2,1)}) %all-gather.19.cloned.1.call-update) | async-done | bytes 27459600 | tf_op jit(solution)/shard_map/all_gather | solution.py:164
  148.6 12.5 fusion.148
  171.5 5.5 collective-permute-start
  187.1 6.6 fusion.31
  208.0 21.4 all-gather.4
  229.4 253.7 %all-gather.21.cloned.1.call-done = f32[16,48,64,256]{3,2,1,0:T(8,128)} async-done(((f32[1,48,64,256]{3,2,1,0:T(8,128)}), f32[16,48,64,256]{3,2,1,0:T(8,128)}) %all-gather.21.cloned.1.call-update) | async-done | bytes 50331664 | tf_op jit(solution)/shard_map/all_gather | solution.py:34
  483.1 41.0 %while.62 = (s32[]{:T(128)}, f32[48]{0:T(128)S(1)}, f32[48,64,256]{2,1,0:T(8,128)S(1)}, s32[]{:T(128)}, f32[16,48]{1,0:T(8,128)S(1)}, /*index=5*/f32[16,48,64,256]{3,2,1,0:T(8,128)}, s32[]{:T(128)}, s32[]{:T(128)}) while((s32[]{:T(128)}, f32[48]{0:T(128)S(1)}, f32[48,64,256]{2,1,0:T(8,128)S(1)}, s32[]{:T(128)}, ...), condition=%wide.region_3.4_spmd.clone, body=%wide.region_2.3_spmd.clone.sunk | while | flops 3145876 | bytes 9438259 | solution.py:46
  524.2 6.3 add_select_fusion.1
  547.9 24.0 all-gather.27.cloned.1.call-done
  594.4 35.0 %all-reduce.13 = f32[768]{0:T(1024)S(1)} all-reduce(f32[768]{0:T(1024)S(1)} %fusion.116), channel_id=2, replica_groups=mesh['ctx'=16,'fsdp'=8] {'ctx'}, use_global_device_ids=true, to_apply=%add.13 | all-reduce | flops 768 | bytes 6144
  630.1 227.1 %all-gather.39.cloned.1.call-done = f32[768,64,256]{2,1,0:T(8,128)} async-done(((f32[48,64,256]{2,1,0:T(8,128)}), f32[768,64,256]{2,1,0:T(8,128)}) %all-gather.39.cloned.1.call-update) | async-done | bytes 50331664 | tf_op jit(solution)/shard_map/all_gather | solution.py:34
  857.2 35.4 %rev.13 = f32[16,48,64,256]{3,2,1,0:T(8,128)} reverse(f32[16,48,64,256]{3,2,1,0:T(8,128)} %bitcast.306), dimensions={0} | reverse | bytes 100663296 | tf_op jit(solution)/shard_map/rev | solution.py:36
  892.5 86.5 %while.63 = (s32[]{:T(128)}, f32[48,64,256]{2,1,0:T(8,128)}, s32[]{:T(128)}, f32[16,48]{1,0:T(8,128)}, f32[16,48,64,256]{3,2,1,0:T(8,128)}, /*index=5*/s32[]{:T(128)}, s32[]{:T(128)}) while((s32[]{:T(128)}, f32[48,64,256]{2,1,0:T(8,128)}, s32[]{:T(128)}, f32[16,48]{1,0:T(8,128)}, f32[16,48,64,256]{3,2,1,0:T(8,128)}, ...), condition=%wide.region_5.6_spmd.clone, body=%wide.region_4.5_spmd.clone.sunk | while | flops 3145732 | bytes 9437865 | solution.py:46
  897.9 5.1 fusion.192
  903.8 5.2 fusion.192
  938.1 5.3 fusion.192
  972.7 6.1 fusion.192
  984.1 7.3 fusion.12
  991.5 7.4 multiply_reduce_fusion.6
  1010.9 8.3 convolution_add_fusion.2
  1022.7 95.4 %all-gather.33.cloned.1.call-done = bf16[2048,8192]{1,0:T(8,128)(2,1)} async-done(((bf16[256,8192]{1,0:T(8,128)(2,1)}), bf16[2048,8192]{1,0:T(8,128)(2,1)}) %all-gather.33.cloned.1.call-update) | async-done | bytes 33554448 | tf_op jit(solution)/shard_map/all_gather | solution.py:168
  1118.1 17.8 fusion.138
  1135.9 70.0 %all-gather.35.cloned.1.call-done = bf16[4096,2048]{1,0:T(8,128)(2,1)} async-done(((bf16[512,2048]{1,0:T(8,128)(2,1)}), bf16[4096,2048]{1,0:T(8,128)(2,1)}) %all-gather.35.cloned.1.call-update) | async-done | bytes 16777232 | tf_op jit(solution)/shard_map/all_gather | solution.py:169
  1205.8 14.9 fusion.41
  1220.8 17.1 multiply_reduce_fusion.12
  1240.0 8.8 fusion.150
  1266.3 6.5 fusion.27
  1282.5 5.4 fusion.4
  1297.5 20.4 all-gather.5
  1317.9 6.8 fusion.36
  1330.9 230.0 %all-gather.37.cloned.1.call-done = f32[16,48,64,256]{3,2,1,0:T(8,128)} async-done(((f32[1,48,64,256]{3,2,1,0:T(8,128)}), f32[16,48,64,256]{3,2,1,0:T(8,128)}) %all-gather.37.cloned.1.call-update) | async-done | bytes 50331664 | tf_op jit(solution)/shard_map/all_gather | solution.py:34
  1560.9 41.1 %while.64 = (s32[]{:T(128)}, f32[48]{0:T(128)S(1)}, f32[48,64,256]{2,1,0:T(8,128)S(1)}, s32[]{:T(128)}, f32[16,48]{1,0:T(8,128)S(1)}, /*index=5*/f32[16,48,64,256]{3,2,1,0:T(8,128)}, s32[]{:T(128)}, s32[]{:T(128)}) while((s32[]{:T(128)}, f32[48]{0:T(128)S(1)}, f32[48,64,256]{2,1,0:T(8,128)S(1)}, s32[]{:T(128)}, ...), condition=%wide.region_14.15_spmd.clone, body=%wide.region_13.14_spmd.clone.sunk | while | flops 3145876 | bytes 9438259 | solution.py:46
  1602.0 5.2 add_select_fusion
  1621.1 15.2 reduce-scatter.9.cloned.1.call-done
  1639.3 72.8 %reduce-scatter.11.cloned.1.call-done = bf16[2,64,256]{2,1,0:T(8,128)(2,1)} async-done(((bf16[32,64,256]{2,1,0:T(8,128)(2,1)}), bf16[2,64,256]{2,1,0:T(8,128)(2,1)}) %reduce-scatter.11.cloned.1.call-update) | async-done | bytes 65552 | tf_op jit(solution)/shard_map/reduce_scatter | solution.py:290
  1712.1 5.6 convolution_convert_fusion.4
  1717.9 11.7 convolution_convert_fusion.3
  1729.6 12.2 convolution_convert_fusion.2
  1742.6 16.5 convolution_convert_fusion
  1763.9 5.5 multiply_reduce_fusion.11
  1771.8 10.5 fusion.53
  1786.3 9.2 fusion.76
  1796.8 34.0 %all-reduce.14 = f32[768]{0:T(1024)S(1)} all-reduce(f32[768]{0:T(1024)S(1)} %fusion.117), channel_id=4, replica_groups=mesh['ctx'=16,'fsdp'=8] {'ctx'}, use_global_device_ids=true, to_apply=%add.14 | all-reduce | flops 768 | bytes 6144
  1830.9 165.7 %all-gather.41.cloned.1.call-done = f32[768,64,256]{2,1,0:T(8,128)} async-done(((f32[48,64,256]{2,1,0:T(8,128)}), f32[768,64,256]{2,1,0:T(8,128)}) %all-gather.41.cloned.1.call-update) | async-done | bytes 50331664 | tf_op jit(solution)/shard_map/all_gather | solution.py:34
  1996.6 34.8 %rev.15 = f32[16,48,64,256]{3,2,1,0:T(8,128)} reverse(f32[16,48,64,256]{3,2,1,0:T(8,128)} %bitcast.305), dimensions={0} | reverse | bytes 100663296 | tf_op jit(solution)/shard_map/rev | solution.py:36
  2031.4 76.3 %while.65 = (s32[]{:T(128)}, f32[48,64,256]{2,1,0:T(8,128)}, s32[]{:T(128)}, f32[16,48]{1,0:T(8,128)S(1)}, f32[16,48,64,256]{3,2,1,0:T(8,128)}, /*index=5*/s32[]{:T(128)}, s32[]{:T(128)}) while((s32[]{:T(128)}, f32[48,64,256]{2,1,0:T(8,128)}, s32[]{:T(128)}, f32[16,48]{1,0:T(8,128)S(1)}, f32[16,48,64,256]{3,2,1,0:T(8,128)}, ...), condition=%wide.region_16.17_spmd.clone, body=%wide.region_15.16_spmd.clone.sunk | while | flops 3145732 | bytes 9437865 | solution.py:46
  2045.6 5.4 fusion.194
  2061.1 5.1 fusion.194
  2066.2 5.1 fusion.194
  2071.3 5.1 fusion.194
  2091.4 6.1 fusion.194
  2097.6 5.1 fusion.194
  2112.9 11.8 fusion.9
  2128.2 8.2 fusion.14
  2140.0 8.4 fusion.79
  2175.1 14.5 convolution_convert_fusion.1
  2189.8 60.3 %reduce-scatter.23.cloned.1.call-done = bf16[512,2048]{1,0:T(8,128)(2,1)} async-done(((bf16[4096,2048]{1,0:T(8,128)(2,1)}), bf16[512,2048]{1,0:T(8,128)(2,1)}) %reduce-scatter.23.cloned.1.call-update) | async-done | bytes 2097168 | tf_op jit(solution)/shard_map/reduce_scatter | solution.py:337
  2250.1 172.6 %reduce-scatter.21.cloned.1.call-done = bf16[256,8192]{1,0:T(8,128)(2,1)} async-done(((bf16[2048,8192]{1,0:T(8,128)(2,1)}), bf16[256,8192]{1,0:T(8,128)(2,1)}) %reduce-scatter.21.cloned.1.call-update) | async-done | bytes 4194320 | tf_op jit(solution)/shard_map/reduce_scatter | solution.py:337
  2422.6 144.6 %reduce-scatter.13.cloned.1.call-done = bf16[256,6704]{0,1:T(8,128)(2,1)} async-done(((bf16[2048,6704]{0,1:T(8,128)(2,1)}), bf16[256,6704]{0,1:T(8,128)(2,1)}) %reduce-scatter.13.cloned.1.call-update) | async-done | bytes 3432464 | tf_op jit(solution)/shard_map/reduce_scatter | solution.py:337
  2568.4 9.4 fusion.38
  2580.2 12.2 fusion.94
  2599.8 152.7 %all-reduce.22.cloned.1.call-done = (bf16[256,6704]{0,1:T(8,128)(2,1)}, bf16[256,1536]{1,0:T(8,128)(2,1)}, bf16[384,2048]{1,0:T(8,128)(2,1)}, bf16[128,2048]{1,0...) async-done(((bf16[256,6704]{0,1:T(8,128)(2,1)}, bf16[256,1536]{1,0:T(8,128)(2,1)}, bf16[384,2048]{1,0:T(8,128)(2,1)}, bf16[128,2048]{1,0:T(8,128)(2,1)}, ...) | async-done | bytes 12607504 | tf_op jit(solution)/shard_map/psum | solution.py:348
  2752.5 6.7 convert_element_type.180
  2769.7 132.3 %all-reduce.20.cloned.1.call-done = (f32[2048]{0:T(1024)}, f32[4,3584]{1,0:T(4,128)}, f32[3584]{0:T(1024)}, f32[48]{0:T(128)}, f32[48]{0:T(128)}, /*index=5*/f32[48]{0:T(128)}, f32[3072]{0:T(1024)}, f32[2048]{0:T(1024)}) async-done(((f32[2048]{0:T(1024)}, f32[4,3584]{1,0:T(4,128)}, f32[3584]{0:T(1024)}, f32[48]{0:T(128)}, f32[48]{0:T(128)}, /*index=5*/f32[48]{0:T(128)}, f32[3072]{0:T(1024)}, ...) | async-done | bytes 100944 | tf_op jit(solution)/shard_map/psum | solution.py:355
  (645 shorter events, 432.0 us)
Async XLA Ops:
  7.2 141.4 %all-gather.19.cloned.1.call-start = ((), (), s32[]{:S(2)}) async-start(), calls=%async_computation.8 | async-start | bytes 30892032 | tf_op jit(solution)/shard_map/all_gather | solution.py:164
  8.0 191.7 %all-gather.25.cloned.1.call-start = ((), (), s32[]{:S(2)}) async-start(), calls=%async_computation.11 | async-start | bytes 7077888 | tf_op jit(solution)/shard_map/all_gather | solution.py:165
  8.7 474.4 %all-gather.21.cloned.1.call-start = ((), (), s32[]{:S(2)}) async-start(), calls=%async_computation.9 | async-start | bytes 53477376 | tf_op jit(solution)/shard_map/all_gather | solution.py:34
  9.1 152.0 %copy-start.124 = (f32[128]{0:T(128)}, f32[128]{0:T(128)S(1)}, u32[]{:S(2)}) copy-start(f32[128]{0:T(128)S(1)} %rsqrt.34) | copy-start | bytes 1540
  9.6 169.2 %copy-start.83 = (f32[3584]{0:T(1024)}, f32[3584]{0:T(1024)S(1)}, u32[]{:S(2)}) copy-start(f32[3584]{0:T(1024)S(1)} %get-tuple-element.547) | copy-start | bytes 43012
  9.6 169.2 %copy-start.85 = (f32[3584]{0:T(1024)}, f32[3584]{0:T(1024)S(1)}, u32[]{:S(2)}) copy-start(f32[3584]{0:T(1024)S(1)} %get-tuple-element.548) | copy-start | bytes 43012
  9.6 169.2 %copy-start.87 = (f32[3584]{0:T(1024)}, f32[3584]{0:T(1024)S(1)}, u32[]{:S(2)}) copy-start(f32[3584]{0:T(1024)S(1)} %get-tuple-element.549) | copy-start | bytes 43012
  9.6 169.2 %copy-start.89 = (f32[3584]{0:T(1024)}, f32[3584]{0:T(1024)S(1)}, u32[]{:S(2)}) copy-start(f32[3584]{0:T(1024)S(1)} %get-tuple-element.550) | copy-start | bytes 43012
  9.6 158.3 %copy-start.130 = (f32[48]{0:T(128)}, f32[48]{0:T(128)S(1)}, u32[]{:S(2)}) copy-start(f32[48]{0:T(128)S(1)} %exponential_negate_fusion) | copy-start | bytes 580
  9.8 151.3 %copy-start.29 = (bf16[128,2048]{1,0:T(8,128)(2,1)}, bf16[128,2048]{1,0:T(8,128)(2,1)S(1)}, u32[]{:S(2)}) copy-start(bf16[128,2048]{1,0:T(8,128)(2,1)S(1)} %fusion.88) | copy-start | bytes 1572868
  165.3 15.7 copy-start.18
  165.3 13.4 copy-start.113
  165.4 6.1 collective-permute-start.1
  168.0 13.1 copy-start.54
  168.8 414.5 %copy-start.50 = (f32[2,64,48]{2,1,0:T(8,128)}, f32[2,64,48]{2,1,0:T(8,128)S(1)}, u32[]{:S(2)}) copy-start(f32[2,64,48]{2,1,0:T(8,128)S(1)} %reduce_window_sum.24) | copy-start | bytes 73732
  168.8 38.6 %copy-start.104 = (f32[2,1,48]{2,1,0:T(1,128)}, f32[2,1,48]{2,1,0:T(1,128)S(1)}, u32[]{:S(2)}) copy-start(f32[2,1,48]{2,1,0:T(1,128)S(1)} %slice.243) | copy-start | bytes 1156
  171.5 7.0 collective-permute-start
  198.4 343.6 %all-gather.29.cloned.1.call-start = ((), (), s32[]{:S(2)}) async-start(), calls=%async_computation.13 | async-start | bytes 1114112 | tf_op jit(solution)/shard_map/all_gather | solution.py:209
  199.7 339.8 %copy-start.60 = (f32[128,64]{1,0:T(8,128)}, f32[128,64]{1,0:T(8,128)S(1)}, u32[]{:S(2)}) copy-start(f32[128,64]{1,0:T(8,128)S(1)} %get-tuple-element.648) | copy-start | bytes 98308
  205.7 366.2 %all-gather.27.cloned.1.call-start = ((), (), s32[]{:S(2)}) async-start(), calls=%async_computation.12 | async-start | bytes 1114112 | tf_op jit(solution)/shard_map/all_gather | solution.py:210
  207.3 649.9 %all-gather.39.cloned.1.call-start = ((), (), s32[]{:S(2)}) async-start(), calls=%async_computation.26 | async-start | bytes 53477376 | tf_op jit(solution)/shard_map/all_gather | solution.py:34
  207.4 275.7 %copy-start.114 = (f32[2,48]{1,0:T(2,128)}, f32[2,48]{1,0:T(2,128)S(1)}, u32[]{:S(2)}) copy-start(f32[2,48]{1,0:T(2,128)S(1)} %exp.69) | copy-start | bytes 1156
  208.0 316.2 %copy-start.117 = (f32[48]{0:T(128)}, f32[48]{0:T(128)S(1)}, u32[]{:S(2)}) copy-start(f32[48]{0:T(128)S(1)} %get-tuple-element.653) | copy-start | bytes 580
  208.0 316.2 %copy-start.120 = (f32[48]{0:T(128)}, f32[48]{0:T(128)S(1)}, u32[]{:S(2)}) copy-start(f32[48]{0:T(128)S(1)} %get-tuple-element.652) | copy-start | bytes 580
  524.1 459.9 %copy-start = (f32[48,64,256]{2,1,0:T(8,128)}, f32[48,64,256]{2,1,0:T(8,128)S(1)}, u32[]{:S(2)}) copy-start(f32[48,64,256]{2,1,0:T(8,128)S(1)} %get-tuple-element.448) | copy-start | bytes 9437188
  530.5 480.4 %all-gather.23.cloned.1.call-start = ((), (), s32[]{:S(2)}) async-start(), calls=%async_computation.10 | async-start | bytes 14155776 | tf_op jit(solution)/shard_map/all_gather | solution.py:166
  531.2 488.0 %all-gather.31.cloned.1.call-start = ((), (), s32[]{:S(2)}) async-start(), calls=%async_computation.14 | async-start | bytes 4718592 | tf_op jit(solution)/shard_map/all_gather | solution.py:167
  532.0 586.1 %all-gather.33.cloned.1.call-start = ((), (), s32[]{:S(2)}) async-start(), calls=%async_computation.15 | async-start | bytes 37748736 | tf_op jit(solution)/shard_map/all_gather | solution.py:168
  532.7 673.1 %all-gather.35.cloned.1.call-start = ((), (), s32[]{:S(2)}) async-start(), calls=%async_computation.16 | async-start | bytes 18874368 | tf_op jit(solution)/shard_map/all_gather | solution.py:169
  533.3 1027.6 %all-gather.37.cloned.1.call-start = ((), (), s32[]{:S(2)}) async-start(), calls=%async_computation.17 | async-start | bytes 53477376 | tf_op jit(solution)/shard_map/all_gather | solution.py:34
  587.9 678.4 %copy-start.75 = (f32[2,64,48]{1,2,0:T(8,128)}, f32[2,64,48]{1,2,0:T(8,128)S(1)}, u32[]{:S(2)}) copy-start(f32[2,64,48]{1,2,0:T(8,128)S(1)} %copy.130) | copy-start | bytes 73732
  594.2 397.2 %copy-start.97 = (f32[2,64,64]{2,1,0:T(8,128)}, f32[2,64,64]{2,1,0:T(8,128)S(1)}, u32[]{:S(2)}) copy-start(f32[2,64,64]{2,1,0:T(8,128)S(1)} %fusion.103) | copy-start | bytes 98308
  892.5 86.5 %copy-start.121 = (f32[48]{0:T(128)S(1)}, f32[48]{0:T(128)}, u32[]{:S(2)}) copy-start(f32[48]{0:T(128)} %copy-done.120) | copy-start | bytes 580
  1019.2 98.9 %copy-start.71 = (f32[2048]{0:T(1024)S(1)}, f32[2048]{0:T(1024)}, u32[]{:S(2)}) copy-start(f32[2048]{0:T(1024)} %param.40) | copy-start | bytes 24580
  1022.7 215.2 %copy-start.7 = (f32[128,2048]{1,0:T(8,128)}, f32[128,2048]{1,0:T(8,128)S(1)}, u32[]{:S(2)}) copy-start(f32[128,2048]{1,0:T(8,128)S(1)} %get-tuple-element.662) | copy-start | bytes 3145732
  1118.1 87.7 %copy-start.44 = (bf16[1,2,64,2048]{3,2,1,0:T(8,128)(2,1)S(1)}, bf16[1,2,64,2048]{3,2,1,0:T(8,128)(2,1)}, u32[]{:S(2)}) copy-start(bf16[1,2,64,2048]{3,2,1,0:T(8,128)(2,1)} %param.43) | copy-start | bytes 1572868
  1277.6 358.7 %reduce-scatter.9.cloned.1.call-start = ((), (), s32[]{:S(2)}) async-start(), calls=%async_computation.18 | async-start | bytes 1114112 | tf_op jit(solution)/shard_map/reduce_scatter | solution.py:284
  1297.4 414.7 %reduce-scatter.11.cloned.1.call-start = ((), (), s32[]{:S(2)}) async-start(), calls=%async_computation.19 | async-start | bytes 1114112 | tf_op jit(solution)/shard_map/reduce_scatter | solution.py:290
  1330.9 665.7 %all-gather.41.cloned.1.call-start = ((), (), s32[]{:S(2)}) async-start(), calls=%async_computation.27 | async-start | bytes 53477376 | tf_op jit(solution)/shard_map/all_gather | solution.py:34
  1560.9 41.1 %copy-start.118 = (f32[48]{0:T(128)S(1)}, f32[48]{0:T(128)}, u32[]{:S(2)}) copy-start(f32[48]{0:T(128)} %copy-done.117) | copy-start | bytes 580
  1607.3 582.4 %reduce-scatter.19.cloned.1.call-start = ((), (), s32[]{:S(2)}) async-start(), calls=%async_computation.23 | async-start | bytes 4718592 | tf_op jit(solution)/shard_map/reduce_scatter | solution.py:337
  1612.6 577.1 %reduce-scatter.15.cloned.1.call-start = ((), (), s32[]{:S(2)}) async-start(), calls=%async_computation.21 | async-start | bytes 7077888 | tf_op jit(solution)/shard_map/reduce_scatter | solution.py:337
  1621.1 96.5 %copy-start.56 = (bf16[16,8,8,128]{3,1,2,0:T(8,128)(2,1)}, bf16[16,8,8,128]{3,1,2,0:T(8,128)(2,1)S(1)}, u32[]{:S(2)}) copy-start(bf16[16,8,8,128]{3,1,2,0:T(8,128)(2,1)S(1)} %copy.234) | copy-start | bytes 786436
  1639.3 78.3 %copy-start.68 = (bf16[16,8,2,128]{3,1,2,0:T(8,128)(2,1)}, bf16[16,8,2,128]{3,1,2,0:T(8,128)(2,1)S(1)}, u32[]{:S(2)}) copy-start(bf16[16,8,2,128]{3,1,2,0:T(8,128)(2,1)S(1)} %copy.235) | copy-start | bytes 196612
  1717.7 472.1 %reduce-scatter.17.cloned.1.call-start = ((), (), s32[]{:S(2)}) async-start(), calls=%async_computation.22 | async-start | bytes 14155776 | tf_op jit(solution)/shard_map/reduce_scatter | solution.py:337
  1729.6 520.5 %reduce-scatter.23.cloned.1.call-start = ((), (), s32[]{:S(2)}) async-start(), calls=%async_computation.25 | async-start | bytes 18874368 | tf_op jit(solution)/shard_map/reduce_scatter | solution.py:337
  1741.9 680.7 %reduce-scatter.21.cloned.1.call-start = ((), (), s32[]{:S(2)}) async-start(), calls=%async_computation.24 | async-start | bytes 37748736 | tf_op jit(solution)/shard_map/reduce_scatter | solution.py:337
  1759.1 808.1 %reduce-scatter.13.cloned.1.call-start = ((), (), s32[]{:S(2)}) async-start(), calls=%async_computation.20 | async-start | bytes 30892032 | tf_op jit(solution)/shard_map/reduce_scatter | solution.py:337
  1771.7 12.9 copy-start.82
  1771.8 14.5 copy-start.76
  2031.4 76.3 %copy-start.119 = (f32[48]{0:T(128)S(1)}, f32[48]{0:T(128)}, u32[]{:S(2)}) copy-start(f32[48]{0:T(128)} %copy-done.117) | copy-start | bytes 580
  2154.2 14.6 collective-permute-start.2
  2157.8 11.0 collective-permute-start.3
  2175.1 14.5 copy-start.47
  2189.6 562.9 %all-reduce.22.cloned.1.call-start = ((), (), s32[]{:S(2)}) async-start(), calls=%async_computation.29 | async-start | bytes 25214976 | tf_op jit(solution)/shard_map/psum | solution.py:348
  2567.3 334.7 %all-reduce.20.cloned.1.call-start = ((), (), s32[]{:S(2)}) async-start(), calls=%async_computation.28 | async-start | bytes 207872 | tf_op jit(solution)/shard_map/psum | solution.py:355
  2568.4 24.0 slice-start.2
  2580.2 12.3 slice-start.3
  2580.2 12.3 copy-start.37
  2580.2 12.3 copy-start.57
  2580.2 12.3 copy-start.69
  2580.2 12.3 copy-start.80
  2580.2 12.3 copy-start.92
  2580.2 12.3 copy-start.125
  (114 other events, 604.3 us)
Sparse Core Ops, SparseCore 0:
  9.7 138.8 all-gather.18
  150.3 42.0 all-gather.24
  198.6 284.5 all-gather.20
  485.7 41.6 all-gather.28
  530.0 41.8 all-gather.26
  573.9 283.2 all-gather.38
  858.9 67.3 all-gather.22
  927.9 32.5 all-gather.30
  962.3 155.7 all-gather.32
  1119.7 86.1 all-gather.34
  1277.7 283.1 all-gather.36
  1564.0 72.2 reduce-scatter.8
  1639.8 72.1 reduce-scatter.10
  1714.1 282.5 all-gather.40
  1998.9 38.4 reduce-scatter.18
  2040.2 41.5 reduce-scatter.14
  2084.1 72.1 reduce-scatter.16
  2158.6 91.4 reduce-scatter.22
  2252.5 170.0 reduce-scatter.20
  2425.1 142.0 reduce-scatter.12
  2572.1 180.3 all-reduce.21
  2760.7 141.2 all-reduce.19
where the time goes:
time: 2930 us; the launch traced here: 2920 us
  waiting for transfers between devices  1960 us (67%)
  other arithmetic  324 us (11%)
  matrix products  283 us (10%)
  local copies, waits for them, and re-layouts  205 us (7%)
  blocking collectives  111 us (4%)
    all_gather x4, waiting for transfers between devices, carried_in(): pieces = jax.tree.map(lambda part: lax.all_gather(part, axis), value)  877 us
    reduce_scatter x6, waiting for transfers between devices, shard_sum(): lax.psum_scatter(term.astype(jnp.bfloat16), 'fsdp', scatter_dimension=0,...  378 us
    select_n x90, other arithmetic, step(): jnp.where(position < mine, new, old)  233 us
    psum x1, waiting for transfers between devices, shards(): lax.psum(shard_in.astype(jnp.bfloat16), 'ctx').astype(jnp.float32)  153 us
    all_gather x1, waiting for transfers between devices, shards(): lax.all_gather(w_in, 'fsdp', axis=0, tiled=True)  139 us
    psum x1, waiting for transfers between devices, shards(): lax.psum((d_norm_gain, d_conv_w, d_conv_b, d_dt_bias, d_a_log, d_dskip, d...  132 us
    all_gather x1, waiting for transfers between devices, shards(): lax.all_gather(w_gate_up, 'fsdp', axis=0, tiled=True)  95.4 us
    reduce_scatter x1, waiting for transfers between devices, shards(): lax.psum_scatter(d_value_all.reshape(2 * ctx_size, half, width_k).astype(...  72.8 us
  transfers between devices with their start and end apart: 26, of which 17 were waited for; matrix products, arithmetic and copies ran while one was open for 24% of the time, Pallas kernels for 0%

commit v1 on v0

v1 whole, which is shorter than its diff:
```python
import jax
import jax.numpy as jnp
from jax import lax
from jax.experimental import pallas as pl
from jax.experimental.pallas import tpu as pltpu
from jax.sharding import PartitionSpec as P

D = 2048
MHEADS = 48
MDIM = 64
STATE = 256
CONV_K = 4
QHEADS = 8
KVHEADS = 2
HDIM = 128
FF = 4096
HALF = 64
INNER = 3072
LENGTH = 2048
SEQS = 8
NC = 16
NF = 8
NZ = 4
LANES = 128
ROWS = 2 * HALF
GROUP = SEQS * ROWS
INNER_F = INNER // NF
HEADS_L = 3
XW = HEADS_L * MDIM
BC_F = 2 * STATE // NF
DT_F = MHEADS // NF
FF_F = FF // NF
CHUNK = 256
CHUNKS = LENGTH // CHUNK
PAIRS = LENGTH // LANES
QROWS = LENGTH // 2
QBLOCK = 128
SHARD = D // NF
SLICE = SHARD // NC
MIX = INNER_F + LANES
QKV = 3 * HDIM
WM_COLS = MIX + QKV
W1_COLS = WM_COLS + INNER_F
MLP_COLS = 2 * FF_F
OUT_ROWS = INNER_F + HDIM
K_AT, V_AT, Q_AT, ATTN = 0, 128, 256, 320
XB = XW + BC_F
B_AT, T_AT, PACK = XW, XB, XB + 16
BOTH = XW + HALF
GATE_SEQS = 4
PART = 16
EPS = 1e-06
ROPE_BASE = 100000000000.0
MASKED = -1e30
SCALE = HDIM ** (-0.5)
BF = jnp.bfloat16
F32 = jnp.float32
PARAMS = pltpu.CompilerParams(vmem_limit_bytes=56 * 1024 * 1024)
SMEM = pl.BlockSpec(memory_space=pltpu.SMEM)


def dot(left, right, left_dim, right_dim):
    return lax.dot_general(
        left, right, (((left_dim,), (right_dim,)), ((), ())), preferred_element_type=F32
    )


def whole(*shape):
    return pl.BlockSpec(shape, lambda *i: (0,) * len(shape))


def cost(flops, moved, transcendentals=0):
    return pl.CostEstimate(
        flops=int(flops), bytes_accessed=int(moved), transcendentals=int(transcendentals)
    )


def shape_of(shape, dtype):
    return jax.ShapeDtypeStruct(shape, dtype)


OTHER_CORE = [(i, i ^ 1) for i in range(NF)]
TO_NEXT = [(i, (i + 2) % NF) for i in range(NF)]
TO_PREV = [(i, (i - 2) % NF) for i in range(NF)]


def send(value, route):
    return lax.ppermute(value, "fsdp", route)


def gather_fsdp(value):
    return lax.all_gather(value, "fsdp", axis=0, tiled=True)


def scatter_fsdp(parts):
    return lax.psum_scatter(parts, "fsdp", scatter_dimension=0, tiled=True).astype(F32)


def ring_pieces(value):
    half = value.shape[0] // 2
    after = send(value, TO_PREV)
    before = send(value, TO_NEXT)
    near = send(value, OTHER_CORE)
    far = jnp.concatenate(
        [send(after[:half], TO_PREV), send(before[half:], TO_NEXT)], axis=0
    )
    near_after = send(after, OTHER_CORE)
    near_before = send(before, OTHER_CORE)
    near_far = send(far, OTHER_CORE)
    return [value, after, far, before, near, near_after, near_far, near_before]


def ring_gather(value, order):
    whole_value = jnp.zeros((NF * value.shape[0],) + value.shape[1:], value.dtype)
    for index, piece in enumerate(ring_pieces(value)):
        whole_value = lax.dynamic_update_slice(
            whole_value, piece, (order[index] * value.shape[0], 0)
        )
    return whole_value


def plus(*terms):
    return sum(term.astype(F32) for term in terms)


def ring_join(mine, other):
    return plus(mine, send(other, OTHER_CORE)).astype(BF)


def ring_scatter(joined):
    size = joined.shape[0] // NZ
    half = size // 2
    own, after, far, before = [joined[i * size : (i + 1) * size] for i in range(NZ)]
    far_next = send(far[:half], TO_NEXT)
    far_prev = send(far[half:], TO_PREV)
    after_two = send(after[half:], TO_NEXT)
    before_one = send(before[:half], TO_PREV)
    after_one = send(plus(after[:half], far_next).astype(BF), TO_NEXT)
    before_two = send(plus(before[half:], far_prev).astype(BF), TO_PREV)
    return plus(
        own,
        jnp.concatenate([after_one, after_two], axis=0),
        jnp.concatenate([before_one, before_two], axis=0),
    )


def after(value, *others):
    return lax.optimization_barrier((value,) + others)[0]


def swap_ctx(value):
    return lax.all_to_all(value, "ctx", 0, 0, tiled=True)


def swap_fsdp(value):
    return lax.all_to_all(value, "fsdp", 0, 0, tiled=True)


def butterfly(value, axis, size):
    bit = 1
    while bit < size:
        value = value + lax.ppermute(value, axis, [(i, i ^ bit) for i in range(size)])
        bit *= 2
    return value


def rotate(values, cosine, sine):
    half = values.shape[-1] // 2
    first = values[:, :half]
    second = values[:, half:]
    return jnp.concatenate(
        [first * cosine - second * sine, second * cosine + first * sine], axis=1
    )


def proj_kernel(n_ref, w_ref, cos_ref, sin_ref, mix_ref, attn_ref):
    acc = jnp.zeros((2 * ROWS, WM_COLS), F32)
    for f in range(NF):
        acc = acc + dot(
            n_ref[:, f * SHARD : (f + 1) * SHARD],
            w_ref[:, f, :, :WM_COLS].reshape(SHARD, WM_COLS),
            1,
            0,
        )
    for j in range(2):
        rows = acc[j * ROWS : (j + 1) * ROWS]
        x_rows = rows[:, :INNER_F].T.astype(BF)
        tail = rows[:, INNER_F:MIX].T
        query = rotate(rows[:, MIX : MIX + HDIM], cos_ref[...], sin_ref[...]).astype(BF)
        key = rotate(
            rows[:, MIX + HDIM : MIX + 2 * HDIM], cos_ref[...], sin_ref[...]
        ).astype(BF)
        value = rows[:, MIX + 2 * HDIM :].astype(BF)
        for p in range(2):
            to = 2 * j + p
            attn_ref[to, K_AT:V_AT] = key
            attn_ref[to, V_AT:Q_AT] = value
            attn_ref[to, Q_AT:] = query[p * HALF : (p + 1) * HALF]
            mix_ref[to, :B_AT] = x_rows[p * XW : (p + 1) * XW]
            mix_ref[to, B_AT:T_AT] = tail[:BC_F].astype(BF)
            steps = tail[BC_F + p * HEADS_L : BC_F + (p + 1) * HEADS_L]
            high = steps.astype(BF).astype(F32)
            mix_ref[to, T_AT:] = jnp.concatenate(
                [high, steps - high, jnp.zeros((16 - 2 * HEADS_L, ROWS), F32)], axis=0
            ).astype(BF)


def packets(rows):
    return pl.BlockSpec((4, rows, LANES), lambda i: (i, 0, 0))


def token_rows(width):
    return pl.BlockSpec((2 * ROWS, width), lambda i: (i, 0))


def project(normed, w_one, cosine, sine):
    return pl.pallas_call(
        proj_kernel,
        grid=(SEQS // 2,),
        in_specs=[
            token_rows(D),
            whole(NC, NF, SLICE, W1_COLS),
            whole(ROWS, HALF),
            whole(ROWS, HALF),
        ],
        out_specs=[packets(PACK), packets(ATTN)],
        out_shape=[shape_of((NC, PACK, LANES), BF), shape_of((NC, ATTN, LANES), BF)],
        compiler_params=PARAMS,
        cost_estimate=cost(2 * GROUP * D * WM_COLS, 10e6),
        name="project",
    )(normed, w_one, cosine, sine)


def proj_z_kernel(n_ref, w_ref, z_ref):
    acc = jnp.zeros((2 * ROWS, INNER_F), F32)
    for f in range(NF):
        acc = acc + dot(
            n_ref[:, f * SHARD : (f + 1) * SHARD],
            w_ref[:, f, :, WM_COLS:].reshape(SHARD, INNER_F),
            1,
            0,
        )
    for j in range(2):
        z_ref[j] = acc[j * ROWS : (j + 1) * ROWS].T


def project_z(normed, w_z):
    return pl.pallas_call(
        proj_z_kernel,
        grid=(SEQS // 2,),
        in_specs=[token_rows(D), whole(NC, NF, SLICE, W1_COLS)],
        out_specs=pl.BlockSpec((2, INNER_F, ROWS), lambda i: (i, 0, 0)),
        out_shape=shape_of((SEQS, INNER_F, ROWS), F32),
        compiler_params=PARAMS,
        cost_estimate=cost(2 * GROUP * D * INNER_F, 8e6),
        name="project_z",
    )(normed, w_z)


def attn_grads_kernel(got_ref, cos_ref, sin_ref, out_ref):
    for j in range(2):
        one = got_ref[2 * j].astype(F32)
        two = got_ref[2 * j + 1].astype(F32)
        both = one + two
        query = jnp.concatenate([one[Q_AT:], two[Q_AT:]], axis=0)
        query = rotate(query, cos_ref[...], -sin_ref[...])
        key = rotate(both[K_AT:V_AT], cos_ref[...], -sin_ref[...])
        out_ref[j * ROWS : (j + 1) * ROWS] = jnp.concatenate(
            [query, key, both[V_AT:Q_AT]], axis=1
        ).astype(BF)


def attn_grads(got, cosine, sine):
    return pl.pallas_call(
        attn_grads_kernel,
        grid=(SEQS // 2,),
        in_specs=[packets(ATTN), whole(ROWS, HALF), whole(ROWS, HALF)],
        out_specs=token_rows(QKV),
        out_shape=shape_of((GROUP, QKV), BF),
        compiler_params=PARAMS,
        cost_estimate=cost(10 * GROUP * QKV, 2e6),
        name="attn_grads",
    )(got, cosine, sine)


def mix_grads_kernel(got_ref, out_ref):
    for j in range(2):
        one = got_ref[2 * j].astype(F32)
        two = got_ref[2 * j + 1].astype(F32)
        x_rows = jnp.concatenate([one[:B_AT], two[:B_AT]], axis=0).T
        tail = jnp.concatenate(
            [
                one[B_AT:T_AT] + two[B_AT:T_AT],
                one[T_AT : T_AT + HEADS_L],
                two[T_AT : T_AT + HEADS_L],
                jnp.zeros((LANES - BC_F - DT_F, ROWS), F32),
            ],
            axis=0,
        ).T
        out_ref[j * ROWS : (j + 1) * ROWS] = jnp.concatenate([x_rows, tail], axis=1).astype(BF)


def mix_grads(got):
    return pl.pallas_call(
        mix_grads_kernel,
        grid=(SEQS // 2,),
        in_specs=[packets(PACK)],
        out_specs=token_rows(MIX),
        out_shape=shape_of((GROUP, MIX), BF),
        compiler_params=PARAMS,
        cost_estimate=cost(4 * GROUP * MIX, 2.2e6),
        name="mix_grads",
    )(got)


def back_kernel(
    spot_ref, mix_ref, dqkv_ref, dz_ref, n_ref, w_ref, mine_ref, other_ref, gain_ref
):
    @pl.when(pl.program_id(0) == 0)
    def _():
        gain_ref[...] = jnp.zeros_like(gain_ref)

    first = spot_ref[NZ] == 0
    grad = jnp.concatenate([mix_ref[...], dqkv_ref[...], dz_ref[...]], axis=1)
    for f in range(NF):
        part = slice(f * SHARD, (f + 1) * SHARD)
        dn = dot(grad, w_ref[:, f].reshape(SHARD, W1_COLS), 1, 1)
        gain_ref[:, part] += jnp.sum(dn * n_ref[:, part].astype(F32), axis=0, keepdims=True)
        dn = dn.astype(BF)
        mine_ref[0, :, part] = jnp.where(first, dn[:ROWS], dn[ROWS:])
        other_ref[0, :, part] = jnp.where(first, dn[ROWS:], dn[:ROWS])


def back_project(spot, mix, dqkv, dz, normed, w_one):
    def rows(width):
        return pl.BlockSpec((2 * ROWS, width), lambda i, spot: (i, 0))

    specs, shapes = ring_specs(D)
    return pl.pallas_call(
        back_kernel,
        grid_spec=pltpu.PrefetchScalarGridSpec(
            num_scalar_prefetch=1,
            grid=(SEQS // 2,),
            in_specs=[
                rows(MIX),
                rows(QKV),
                rows(INNER_F),
                rows(D),
                pl.BlockSpec((NC, NF, SLICE, W1_COLS), lambda i, spot: (0, 0, 0, 0)),
            ],
            out_specs=specs + [pl.BlockSpec((1, D), lambda i, spot: (0, 0))],
        ),
        out_shape=shapes + [shape_of((1, D), F32)],
        compiler_params=PARAMS,
        cost_estimate=cost(2 * GROUP * D * W1_COLS, 18e6),
        name="back_project",
    )(spot, mix, dqkv, dz, normed, w_one)


def column_grad_kernel(left_ref, *refs):
    out_ref = refs[-1]
    first = 0
    for right_ref in refs[:-1]:
        term = dot(left_ref[...], right_ref[...], 0, 0).astype(BF)
        for block in range(out_ref.shape[1]):
            for tile in range(right_ref.shape[1] // LANES):
                out_ref[:, block, first + tile] = term[
                    block * SHARD : (block + 1) * SHARD, tile * LANES : (tile + 1) * LANES
                ].reshape(NC, SLICE, LANES)
        first += right_ref.shape[1] // LANES


def column_grad(left, *rights):
    count, width = left.shape[1] // SHARD, sum(right.shape[1] for right in rights)
    tiles = width // LANES
    many = 2
    return pl.pallas_call(
        column_grad_kernel,
        grid=(count // many,),
        in_specs=[pl.BlockSpec((GROUP, many * SHARD), lambda i: (0, i))]
        + [whole(GROUP, right.shape[1]) for right in rights],
        out_specs=pl.BlockSpec((NC, many, tiles, SLICE, LANES), lambda i: (0, i, 0, 0, 0)),
        out_shape=shape_of((NC, count, tiles, SLICE, LANES), BF),
        compiler_params=PARAMS,
        cost_estimate=cost(
            2 * GROUP * left.shape[1] * width,
            2 * GROUP * (left.shape[1] + width) + 2 * left.shape[1] * width,
        ),
        name="column_grad",
    )(left, *rights)


def channels(count):
    return pl.BlockSpec((count, INNER_F, ROWS), lambda i: (i, 0, 0))


def gate_packets(rows):
    return pl.BlockSpec((2 * GATE_SEQS, rows, LANES), lambda i: (i, 0, 0))


def gate_kernel(got_ref, z_ref, g_ref, sq_ref):
    for j in range(GATE_SEQS):
        ssd = got_ref[2 * j : 2 * j + 2, :XW].reshape(INNER_F, ROWS).astype(F32)
        z = z_ref[j]
        g = ssd * (z * jax.nn.sigmoid(z))
        g_ref[j] = g
        seq = pl.program_id(0) * GATE_SEQS + j
        sq_ref[pl.ds(seq, 1)] = jnp.sum(g * g, axis=0, keepdims=True)


def gate(got, z):
    return pl.pallas_call(
        gate_kernel,
        grid=(SEQS // GATE_SEQS,),
        in_specs=[gate_packets(XW), channels(GATE_SEQS)],
        out_specs=[channels(GATE_SEQS), whole(SEQS, ROWS)],
        out_shape=[shape_of((SEQS, INNER_F, ROWS), F32), shape_of((SEQS, ROWS), F32)],
        compiler_params=PARAMS,
        cost_estimate=cost(8 * GROUP * INNER_F, 4.2e6, GROUP * INNER_F),
        name="gate",
    )(got, z)


def branch_kernel(heads_ref, g_ref, sq_ref, gain_ref, w_ref, gh_ref, out_ref):
    step = pl.program_id(0)
    for j in range(2):
        scale = lax.rsqrt(sq_ref[pl.ds(2 * step + j, 1)] / INNER + EPS)
        gated = (g_ref[j] * scale * gain_ref[...]).T.astype(BF)
        heads = heads_ref[2 * j : 2 * j + 2].reshape(ROWS, HDIM)
        gh_ref[j * ROWS : (j + 1) * ROWS] = jnp.concatenate([gated, heads], axis=1)
    out_ref[...] = dot(gh_ref[...], w_ref[...], 1, 0).astype(BF)


def branch_out(heads, g, squares, gain, w_out):
    return pl.pallas_call(
        branch_kernel,
        grid=(SEQS // 2,),
        in_specs=[
            packets(HALF),
            channels(2),
            whole(SEQS, ROWS),
            whole(INNER_F, 1),
            whole(OUT_ROWS, D),
        ],
        out_specs=[token_rows(OUT_ROWS), token_rows(D)],
        out_shape=[shape_of((GROUP, OUT_ROWS), BF), shape_of((GROUP, D), BF)],
        compiler_params=PARAMS,
        cost_estimate=cost(2 * GROUP * OUT_ROWS * D, 10e6),
        name="branch_out",
    )(heads, g, squares, gain, w_out)


def branch_back_kernel(d_ref, w_ref, g_ref, gain_ref, dg_ref, inner_ref, dh_ref):
    step = pl.program_id(0)
    both = dot(d_ref[...], w_ref[...], 1, 1)
    for j in range(2):
        rows = both[j * ROWS : (j + 1) * ROWS]
        d_gated = rows[:, :INNER_F].T
        dg_ref[j] = d_gated
        inner_ref[pl.ds(2 * step + j, 1)] = jnp.sum(
            d_gated * gain_ref[...] * g_ref[j], axis=0, keepdims=True
        )
        heads = rows[:, INNER_F:].astype(BF)
        dh_ref[2 * j : 2 * j + 2] = heads.reshape(2, HALF, HDIM)


def branch_back(branch, w_out, g, gain):
    return pl.pallas_call(
        branch_back_kernel,
        grid=(SEQS // 2,),
        in_specs=[token_rows(D), whole(OUT_ROWS, D), channels(2), whole(INNER_F, 1)],
        out_specs=[channels(2), whole(SEQS, ROWS), packets(HALF)],
        out_shape=[
            shape_of((SEQS, INNER_F, ROWS), F32),
            shape_of((SEQS, ROWS), F32),
            shape_of((NC, HALF, HDIM), BF),
        ],
        compiler_params=PARAMS,
        cost_estimate=cost(2 * GROUP * OUT_ROWS * D, 10e6),
        name="branch_back",
    )(branch, w_out, g, gain)


def gate_back_kernel(
    got_ref, z_ref, g_ref, dg_ref, dh_ref, sq_ref, inner_ref, gain_ref,
    pack_ref, dz_ref, gain_grad_ref,
):
    index = pl.program_id(0)

    @pl.when(index == 0)
    def _():
        gain_grad_ref[...] = jnp.zeros_like(gain_grad_ref)

    pack_ref[:, XW:] = dh_ref[...]
    for j in range(GATE_SEQS):
        ssd = got_ref[2 * j : 2 * j + 2, :XW].reshape(INNER_F, ROWS).astype(F32)
        z = z_ref[j]
        g = g_ref[j]
        sig = jax.nn.sigmoid(z)
        silu = z * sig
        seq = index * GATE_SEQS + j
        scale = lax.rsqrt(sq_ref[pl.ds(seq, 1)] / INNER + EPS)
        inner = inner_ref[pl.ds(seq, 1)] / INNER
        scaled = dg_ref[j] * scale
        d_g = scaled * gain_ref[...] - g * (scale * scale * scale * inner)
        gain_grad_ref[...] += jnp.sum(scaled * g, axis=1, keepdims=True)
        pack_ref[2 * j : 2 * j + 2, :XW] = (d_g * silu).astype(BF).reshape(2, XW, LANES)
        dz_ref[j * ROWS : (j + 1) * ROWS] = (
            (d_g * ssd * (sig + silu * (1.0 - sig))).T.astype(BF)
        )


def gate_back(got, z, g, dg, dh, squares, inner, gain):
    return pl.pallas_call(
        gate_back_kernel,
        grid=(SEQS // GATE_SEQS,),
        in_specs=[
            gate_packets(XW),
            channels(GATE_SEQS),
            channels(GATE_SEQS),
            channels(GATE_SEQS),
            gate_packets(HALF),
            whole(SEQS, ROWS),
            whole(SEQS, ROWS),
            whole(INNER_F, 1),
        ],
        out_specs=[
            gate_packets(BOTH),
            pl.BlockSpec((GATE_SEQS * ROWS, INNER_F), lambda i: (i, 0)),
            whole(INNER_F, 1),
        ],
        out_shape=[
            shape_of((NC, BOTH, LANES), BF),
            shape_of((GROUP, INNER_F), BF),
            shape_of((INNER_F, 1), F32),
        ],
        compiler_params=PARAMS,
        cost_estimate=cost(20 * GROUP * INNER_F, 8e6, GROUP * INNER_F),
        name="gate_back",
    )(got, z, g, dg, dh, squares, inner, gain)


def act_back_kernel(cot_ref, down_ref, out_ref):
    out_ref[...] = dot(cot_ref[...], down_ref[...], 1, 1)


def act_back(cot, w_down):
    return pl.pallas_call(
        act_back_kernel,
        grid=(SEQS // 2,),
        in_specs=[token_rows(D), whole(FF_F, D)],
        out_specs=token_rows(FF_F),
        out_shape=shape_of((GROUP, FF_F), F32),
        compiler_params=PARAMS,
        cost_estimate=cost(2 * GROUP * D * FF_F, 9e6),
        name="act_back",
    )(cot, w_down)


def mlp_kernel(n_ref, d_act_ref, w_ref, act_ref, dgu_ref, dn_ref):
    acc = jnp.zeros((2 * ROWS, MLP_COLS), F32)
    for f in range(NF):
        acc = acc + dot(
            n_ref[:, f * SHARD : (f + 1) * SHARD], w_ref[:, f].reshape(SHARD, MLP_COLS), 1, 0
        )
    gate_part, upper = acc[:, :FF_F], acc[:, FF_F:]
    sig = jax.nn.sigmoid(gate_part)
    silu = gate_part * sig
    act_ref[...] = (silu * upper).astype(BF)
    d_act = d_act_ref[...]
    d_gu = jnp.concatenate(
        [d_act * upper * (sig + silu * (1.0 - sig)), d_act * silu], axis=1
    ).astype(BF)
    dgu_ref[...] = d_gu
    for f in range(NF):
        dn_ref[:, f * SHARD : (f + 1) * SHARD] = dot(
            d_gu, w_ref[:, f].reshape(SHARD, MLP_COLS), 1, 1
        ).astype(BF)


def mlp(normed, d_act, w_gu):
    return pl.pallas_call(
        mlp_kernel,
        grid=(SEQS // 2,),
        in_specs=[token_rows(D), token_rows(FF_F), whole(NC, NF, SLICE, MLP_COLS)],
        out_specs=[token_rows(FF_F), token_rows(MLP_COLS), token_rows(D)],
        out_shape=[
            shape_of((GROUP, FF_F), BF),
            shape_of((GROUP, MLP_COLS), BF),
            shape_of((GROUP, D), BF),
        ],
        compiler_params=PARAMS,
        cost_estimate=cost(8 * GROUP * D * FF_F, 20e6, GROUP * FF_F),
        name="mlp",
    )(normed, d_act, w_gu)


def ring_specs(width):
    def spec(*_):
        return pl.BlockSpec((1, ROWS, width), lambda i, spot: (spot[i], 0, 0))

    return [spec(), spec()], [shape_of((NZ, ROWS, width), BF)] * 2


def down_kernel(spot_ref, act_ref, down_ref, mine_ref, other_ref):
    rows = dot(act_ref[...], down_ref[...], 1, 0).astype(BF)
    first = spot_ref[NZ] == 0
    mine_ref[0] = jnp.where(first, rows[:ROWS], rows[ROWS:])
    other_ref[0] = jnp.where(first, rows[ROWS:], rows[:ROWS])


def down_out(spot, act, w_down):
    specs, shapes = ring_specs(D)
    return pl.pallas_call(
        down_kernel,
        grid_spec=pltpu.PrefetchScalarGridSpec(
            num_scalar_prefetch=1,
            grid=(SEQS // 2,),
            in_specs=[
                pl.BlockSpec((2 * ROWS, FF_F), lambda i, spot: (i, 0)),
                pl.BlockSpec((FF_F, D), lambda i, spot: (0, 0)),
            ],
            out_specs=specs,
        ),
        out_shape=shapes,
        compiler_params=PARAMS,
        cost_estimate=cost(2 * GROUP * D * FF_F, 8e6),
        name="down_out",
    )(spot, act, w_down)


def lane_of(shape):
    return lax.broadcasted_iota(jnp.int32, shape, 1)


def sources(pair, first):
    if first:
        return 2 * pair, 2 * pair + 1
    return NC - 1 - 2 * pair, NC - 2 - 2 * pair


def assemble(ref, low, high, pair, first):
    one, two = sources(pair, first)
    left = lane_of((high - low, LANES)) < HALF
    return jnp.where(left, ref[one, low:high].astype(F32), ref[two, low:high].astype(F32))


def deal(ref, low, high, pair, first, values):
    one, two = sources(pair, first)
    values = values.astype(BF)
    ref[one, low:high, :HALF] = values[:, :HALF]
    ref[two, low:high, HALF:] = values[:, HALF:]


def taps_of(padded, taps):
    current = padded[:, LANES:]
    total = current * taps[:, CONV_K - 1 : CONV_K] + taps[:, CONV_K : CONV_K + 1]
    inputs = [current]
    for back in range(1, CONV_K):
        moved = pltpu.roll(padded, back, 1)[:, LANES:]
        inputs.append(moved)
        total = total + moved * taps[:, CONV_K - 1 - back : CONV_K - back]
    return inputs[::-1], total


def softplus(values):
    return jnp.maximum(values, 0.0) + jnp.log1p(jnp.exp(-jnp.abs(values)))


def at_pair(pair):
    return pl.ds(pl.multiple_of(pair * LANES, LANES), LANES)


def load_raw(got_ref, raw_ref):
    raw_ref[:, :LANES] = jnp.zeros((XB, LANES), F32)
    half_pairs = PAIRS // 2
    for first in (True, False):

        def load(pair, unused, first=first):
            place = at_pair((pair if first else pair + half_pairs) + 1)
            raw_ref[:, place] = assemble(got_ref, 0, XB, pair, first)
            return unused

        lax.fori_loop(0, half_pairs, load, 0, unroll=True)


def front_kernel(got_ref, taps_ref, heads_ref, x_ref, bc_ref, row_ref, raw_ref):
    load_raw(got_ref, raw_ref)

    def step(part, unused):
        rows = pl.ds(pl.multiple_of(part * PART, PART), PART)
        _, total = taps_of(raw_ref[rows], taps_ref[rows])
        active = (total * jax.nn.sigmoid(total)).astype(BF)

        @pl.when(part < XW // PART)
        def _():
            x_ref[rows] = active

        @pl.when(part >= XW // PART)
        def _():
            bc_ref[pl.ds(pl.multiple_of(part * PART - XW, PART), PART)] = active

        return unused

    lax.fori_loop(0, XB // PART, step, 0)
    half_pairs = PAIRS // 2
    parts = [
        assemble(got_ref, T_AT, PACK, index % half_pairs, index < half_pairs)
        for index in range(PAIRS)
    ]
    parts = jnp.concatenate(parts, axis=1)
    raw = parts[:HEADS_L] + parts[HEADS_L : 2 * HEADS_L] + heads_ref[:HEADS_L, :1]
    steps = softplus(raw)
    pad = jnp.zeros((8 - 2 * HEADS_L, LENGTH), F32)
    sums = jnp.concatenate([steps * heads_ref[HEADS_L : 2 * HEADS_L, :1], steps, pad], axis=0)
    rows = lax.broadcasted_iota(jnp.int32, sums.shape, 0)
    lane = lane_of(sums.shape) % CHUNK
    running = sums
    back = 1
    while back < CHUNK:
        running = running + jnp.where(lane >= back, pltpu.roll(running, back, 1), 0.0)
        back *= 2
    row_ref[:8] = jnp.where(rows < HEADS_L, running, sums)
    row_ref[8:] = jnp.concatenate([raw, jnp.zeros((8 - HEADS_L, LENGTH), F32)], axis=0)


def front(got, taps, heads):
    return pl.pallas_call(
        front_kernel,
        in_specs=[whole(NC, PACK, LANES), whole(XB, 8), whole(8, LANES)],
        out_specs=[whole(XW, LENGTH), whole(BC_F, LENGTH), whole(16, LENGTH)],
        out_shape=[
            shape_of((XW, LENGTH), BF),
            shape_of((BC_F, LENGTH), BF),
            shape_of((16, LENGTH), F32),
        ],
        grid=(1,),
        scratch_shapes=[pltpu.VMEM((XB, LENGTH + LANES), F32)],
        compiler_params=PARAMS,
        cost_estimate=cost(30 * XB * LENGTH, 4e6, XB * LENGTH),
        name="front",
    )(got, taps, heads)


def front_back_kernel(
    got_ref, taps_ref, heads_ref, row_ref, drow_ref, dx_ref, dbc_ref, pack_ref,
    taps_grad_ref, heads_grad_ref, raw_ref, grad_ref,
):
    half_pairs = PAIRS // 2
    load_raw(got_ref, raw_ref)

    grads = drow_ref[...]
    lane = lane_of(grads.shape) % CHUNK
    running = grads
    back = 1
    while back < CHUNK:
        running = running + jnp.where(
            lane < CHUNK - back, pltpu.roll(running, LENGTH - back, 1), 0.0
        )
        back *= 2
    rates = running[:HEADS_L]
    rate = heads_ref[HEADS_L : 2 * HEADS_L, :1]
    d_steps = grads[HEADS_L : 2 * HEADS_L] + rates * rate
    d_dt = d_steps * jax.nn.sigmoid(row_ref[8 : 8 + HEADS_L])
    steps = row_ref[HEADS_L : 2 * HEADS_L]
    heads_grad_ref[...] = jnp.concatenate(
        [
            jnp.sum(d_dt, axis=1, keepdims=True),
            jnp.sum(rates * steps, axis=1, keepdims=True) * rate,
            jnp.zeros((8 - 2 * HEADS_L, 1), F32),
        ],
        axis=0,
    )
    d_dt = jnp.concatenate([d_dt, jnp.zeros((16 - HEADS_L, LENGTH), F32)], axis=0)
    for index in range(PAIRS):
        first = index < half_pairs
        deal(
            pack_ref, T_AT, PACK, index % half_pairs, first,
            d_dt[:, index * LANES : (index + 1) * LANES],
        )

    def step(part, unused):
        rows = pl.ds(pl.multiple_of(part * PART, PART), PART)
        taps = taps_ref[rows]
        inputs, total = taps_of(raw_ref[rows], taps)
        sig = jax.nn.sigmoid(total)

        @pl.when(part < XW // PART)
        def _():
            grad_ref[:, :LENGTH] = dx_ref[rows]

        @pl.when(part >= XW // PART)
        def _():
            grad_ref[:, :LENGTH] = dbc_ref[pl.ds(pl.multiple_of(part * PART - XW, PART), PART)]

        grad = grad_ref[:, :LENGTH] * (sig + total * sig * (1.0 - sig))
        grad_ref[:, :LENGTH] = grad
        padded = grad_ref[...]
        d_raw = grad * taps[:, CONV_K - 1 : CONV_K]
        for ahead in range(1, CONV_K):
            moved = pltpu.roll(padded, LENGTH + LANES - ahead, 1)[:, :LENGTH]
            d_raw = d_raw + moved * taps[:, CONV_K - 1 - ahead : CONV_K - ahead]
        taps_grad_ref[rows] = jnp.concatenate(
            [jnp.sum(grad * moved, axis=1, keepdims=True) for moved in inputs]
            + [jnp.sum(grad, axis=1, keepdims=True)]
            + [jnp.zeros((PART, 8 - CONV_K - 1), F32)],
            axis=1,
        )
        raw_ref[rows, :LENGTH] = d_raw
        return unused

    grad_ref[:, LENGTH:] = jnp.zeros((PART, LANES), F32)
    lax.fori_loop(0, XB // PART, step, 0)
    for first in (True, False):

        def store(pair, unused, first=first):
            place = at_pair(pair if first else pair + half_pairs)
            deal(pack_ref, 0, XB, pair, first, raw_ref[:, place])
            return unused

        lax.fori_loop(0, half_pairs, store, 0, unroll=True)


def front_back(got, taps, heads, rows, drow, dx, dbc):
    return pl.pallas_call(
        front_back_kernel,
        in_specs=[
            whole(NC, PACK, LANES),
            whole(XB, 8),
            whole(8, LANES),
            whole(16, LENGTH),
            whole(8, LENGTH),
            whole(XW, LENGTH),
            whole(BC_F, LENGTH),
        ],
        out_specs=[whole(NC, PACK, LANES), whole(XB, 8), whole(8, 1)],
        out_shape=[
            shape_of((NC, PACK, LANES), BF),
            shape_of((XB, 8), F32),
            shape_of((8, 1), F32),
        ],
        grid=(1,),
        scratch_shapes=[
            pltpu.VMEM((XB, LENGTH + LANES), F32),
            pltpu.VMEM((PART, LENGTH + LANES), F32),
        ],
        compiler_params=PARAMS,
        cost_estimate=cost(60 * XB * LENGTH, 9e6, XB * LENGTH),
        name="front_back",
    )(got, taps, heads, rows, drow, dx, dbc)


def stacked(rows, width):
    return jnp.concatenate(
        [jnp.broadcast_to(row, (MDIM, width)) for row in rows], axis=0
    )


def state_sides(place_ref, bc_ref):
    quarter = STATE // BC_F
    bt = jnp.concatenate([bc_ref[place_ref[j]] for j in range(quarter)], axis=0)
    ct = jnp.concatenate([bc_ref[place_ref[quarter + j]] for j in range(quarter)], axis=0)
    return bt, ct


def chunk_terms(row_ref):
    rows = row_ref[...]
    cols = rows.T
    cum_row = [rows[h : h + 1] for h in range(HEADS_L)]
    dt_row = [rows[HEADS_L + h : HEADS_L + h + 1] for h in range(HEADS_L)]
    cum_col = [cols[:, h : h + 1] for h in range(HEADS_L)]
    dt_col = [cols[:, HEADS_L + h : HEADS_L + h + 1] for h in range(HEADS_L)]
    last = [row[:, CHUNK - 1 :] for row in cum_row]
    return cum_row, dt_row, cum_col, dt_col, last


def later_mask():
    shape = (CHUNK, CHUNK)
    return lax.broadcasted_iota(jnp.int32, shape, 1) >= lax.broadcasted_iota(jnp.int32, shape, 0)


def mamba_fwd_kernel(
    place_ref, x_ref, bc_ref, row_ref, skip_ref, pack_ref, st_out_ref, st_ref
):
    index = pl.program_id(0)

    @pl.when(index == 0)
    def _():
        st_ref[...] = jnp.zeros_like(st_ref)

    x_low = x_ref[...]
    x = x_low.astype(F32)
    bt, ct = state_sides(place_ref, bc_ref)
    st = st_ref[...]
    st_out_ref[0] = st
    cum_row, dt_row, cum_col, dt_col, last = chunk_terms(row_ref)
    inter = dot(bt, ct, 0, 0)
    carried = dot(st.astype(BF), ct, 1, 0)
    later = later_mask()
    within = []
    for h in range(HEADS_L):
        decay = jnp.exp(jnp.where(later, cum_row[h] - cum_col[h], MASKED))
        mixing = (inter * decay * dt_col[h]).astype(BF)
        within.append(dot(x_low[h * MDIM : (h + 1) * MDIM], mixing, 1, 0))
    entering = stacked([jnp.exp(row) for row in cum_row], CHUNK)
    y = jnp.concatenate(within, axis=0) + entering * carried + skip_ref[...] * x
    weights = stacked(
        [jnp.exp(end - row) * step for end, row, step in zip(last, cum_row, dt_row)], CHUNK
    )
    leaving = stacked([jnp.exp(end) for end in last], 1)
    st_ref[...] = st * leaving + dot((x * weights).astype(BF), bt, 1, 1)
    pairs = CHUNK // LANES
    early = index < CHUNKS // 2

    @pl.when(early)
    def _():
        for j in range(pairs):
            deal(pack_ref, 0, XW, pairs * index + j, True, y[:, j * LANES : (j + 1) * LANES])

    @pl.when(jnp.logical_not(early))
    def _():
        for j in range(pairs):
            deal(
                pack_ref, 0, XW, pairs * (index - CHUNKS // 2) + j, False,
                y[:, j * LANES : (j + 1) * LANES],
            )


def mamba_fwd(place, x, bc, rows, skip):
    return pl.pallas_call(
        mamba_fwd_kernel,
        grid=(CHUNKS,),
        in_specs=[
            SMEM,
            pl.BlockSpec((XW, CHUNK), lambda i: (0, i)),
            pl.BlockSpec((NF, BC_F, CHUNK), lambda i: (0, 0, i)),
            pl.BlockSpec((8, CHUNK), lambda i: (0, i)),
            whole(XW, 1),
        ],
        out_specs=[
            whole(NC, XW, LANES),
            pl.BlockSpec((1, XW, STATE), lambda i: (i, 0, 0)),
        ],
        out_shape=[
            shape_of((NC, XW, LANES), BF),
            shape_of((CHUNKS, XW, STATE), F32),
        ],
        scratch_shapes=[pltpu.VMEM((XW, STATE), F32)],
        compiler_params=PARAMS,
        cost_estimate=cost(2 * LENGTH * CHUNK * (STATE + 3 * XW), 7e6, LENGTH * CHUNK * 3),
        name="mamba_fwd",
    )(place, x, bc, rows, skip)


def mamba_bwd_kernel(
    place_ref, x_ref, got_ref, bc_ref, row_ref, st_in_ref, skip_ref,
    dx_ref, mine_ref, other_ref, drow_ref, dskip_ref, dst_ref, dy_ref,
):
    turn = pl.program_id(0)
    index = CHUNKS - 1 - turn
    pairs = CHUNK // LANES

    @pl.when(turn == 0)
    def _():
        dst_ref[...] = jnp.zeros_like(dst_ref)
        dskip_ref[...] = jnp.zeros_like(dskip_ref)

    @pl.when(index < CHUNKS // 2)
    def _():
        for j in range(pairs):
            dy_ref[:, j * LANES : (j + 1) * LANES] = assemble(
                got_ref, 0, XW, pairs * index + j, True
            )

    @pl.when(index >= CHUNKS // 2)
    def _():
        for j in range(pairs):
            dy_ref[:, j * LANES : (j + 1) * LANES] = assemble(
                got_ref, 0, XW, pairs * (index - CHUNKS // 2) + j, False
            )

    x_low = x_ref[...]
    x = x_low.astype(F32)
    dy = dy_ref[...]
    dy_low = dy.astype(BF)
    bt, ct = state_sides(place_ref, bc_ref)
    st = st_in_ref[0]
    dst = dst_ref[...]
    st_low = st.astype(BF)
    dst_low = dst.astype(BF)
    cum_row, dt_row, cum_col, dt_col, last = chunk_terms(row_ref)
    inter = dot(bt, ct, 0, 0)
    later = later_mask()
    entering = stacked([jnp.exp(row) for row in cum_row], CHUNK)
    tail = [jnp.exp(end - row) for end, row in zip(last, cum_row)]
    kept_row = [t * step for t, step in zip(tail, dt_row)]
    weights = stacked(kept_row, CHUNK)
    leaving = stacked([jnp.exp(end) for end in last], 1)
    carried = dot(st_low, ct, 1, 0) * entering
    reach = dot(dst_low, bt, 1, 0)
    dy_in = (dy * entering).astype(BF)
    x_out = (x * weights).astype(BF)
    along = dy * carried
    pulled = x * reach
    kept = jnp.sum(st * dst, axis=1, keepdims=True) * leaving
    d_inter = jnp.zeros((CHUNK, CHUNK), F32)
    dx_parts = []
    row_cum = []
    row_dt = []
    col_cum = []
    col_dt = []
    ends = lane_of((1, CHUNK)) == CHUNK - 1
    for h in range(HEADS_L):
        part = slice(h * MDIM, (h + 1) * MDIM)
        decay = jnp.exp(jnp.where(later, cum_row[h] - cum_col[h], MASKED))
        d_mix = dot(x_low[part], dy_low[part], 0, 0)
        scaled = decay * dt_col[h]
        d_inter = d_inter + d_mix * scaled
        mixing = inter * scaled
        dx_parts.append(dot(dy_low[part], mixing.astype(BF), 1, 1))
        to_dt = jnp.sum(d_mix * (inter * decay), axis=1, keepdims=True)
        q_row = jnp.sum(pulled[part], axis=0, keepdims=True)
        w_q = q_row * kept_row[h]
        d_last = jnp.sum(w_q, axis=1, keepdims=True) + jnp.sum(
            kept[part], axis=0, keepdims=True
        )
        row_cum.append(
            jnp.sum(d_mix * mixing, axis=0, keepdims=True)
            + jnp.sum(along[part], axis=0, keepdims=True)
            - w_q
            + jnp.where(ends, d_last, 0.0)
        )
        row_dt.append(q_row * tail[h])
        col_cum.append(-to_dt * dt_col[h])
        col_dt.append(to_dt)
    dx_ref[...] = jnp.concatenate(dx_parts, axis=0) + weights * reach + skip_ref[...] * dy
    d_low = d_inter.astype(BF)
    dbt = (dot(ct, d_low, 1, 1) + dot(dst_low, x_out, 0, 0)).astype(BF)
    dct = (dot(bt, d_low, 1, 0) + dot(st_low, dy_in, 0, 0)).astype(BF)
    quarter = STATE // BC_F
    parts = [
        grad[j * BC_F : (j + 1) * BC_F] for grad in (dbt, dct) for j in range(quarter)
    ]
    first = place_ref[0] < NZ
    for z in range(NZ):
        one, two = parts[2 * z], parts[2 * z + 1]
        distance = place_ref[2 * z] % NZ
        mine_ref[distance] = jnp.where(first, one, two)
        other_ref[distance] = jnp.where(first, two, one)
    dst_ref[...] = dst * leaving + dot(dy_in, ct, 1, 1)
    dskip_ref[...] += jnp.sum(dy * x, axis=1, keepdims=True)
    pad = jnp.zeros((CHUNK, 8 - 2 * HEADS_L), F32)
    columns = jnp.concatenate(col_cum + col_dt + [pad], axis=1).T
    drow_ref[...] = columns + jnp.concatenate(
        row_cum + row_dt + [jnp.zeros((8 - 2 * HEADS_L, CHUNK), F32)], axis=0
    )


def mamba_bwd(place, x, got, bc, rows, states, skip):
    end = CHUNKS - 1
    return pl.pallas_call(
        mamba_bwd_kernel,
        grid=(CHUNKS,),
        in_specs=[
            SMEM,
            pl.BlockSpec((XW, CHUNK), lambda i: (0, end - i)),
            whole(NC, BOTH, LANES),
            pl.BlockSpec((NF, BC_F, CHUNK), lambda i: (0, 0, end - i)),
            pl.BlockSpec((8, CHUNK), lambda i: (0, end - i)),
            pl.BlockSpec((1, XW, STATE), lambda i: (end - i, 0, 0)),
            whole(XW, 1),
        ],
        out_specs=[
            pl.BlockSpec((XW, CHUNK), lambda i: (0, end - i)),
            pl.BlockSpec((NZ, BC_F, CHUNK), lambda i: (0, 0, end - i)),
            pl.BlockSpec((NZ, BC_F, CHUNK), lambda i: (0, 0, end - i)),
            pl.BlockSpec((8, CHUNK), lambda i: (0, end - i)),
            whole(XW, 1),
        ],
        out_shape=[
            shape_of((XW, LENGTH), F32),
            shape_of((NZ, BC_F, LENGTH), BF),
            shape_of((NZ, BC_F, LENGTH), BF),
            shape_of((8, LENGTH), F32),
            shape_of((XW, 1), F32),
        ],
        scratch_shapes=[pltpu.VMEM((XW, STATE), F32), pltpu.VMEM((XW, CHUNK), F32)],
        compiler_params=PARAMS,
        cost_estimate=cost(
            2 * LENGTH * CHUNK * (3 * STATE + 7 * XW), 12e6, LENGTH * CHUNK * 3
        ),
        name="mamba_bwd",
    )(place, x, got, bc, rows, states, skip)


def position_of(source, odd, inside):
    block = jnp.where(source % 2 == odd, source, 2 * NC - 1 - source)
    return block * HALF + inside


def visible_mask(step, odd):
    key = lax.broadcasted_iota(jnp.int32, (1, LENGTH), 1)
    key_pos = position_of(key // ROWS, (key // HALF) % 2, key % HALF)
    query = lax.broadcasted_iota(jnp.int32, (QBLOCK, 1), 0)
    source = 2 * step + query // HALF
    query_pos = position_of(source, odd, query % HALF)
    return key_pos <= query_pos


def attn_fwd_kernel(odd_ref, q_ref, k_ref, v_ref, o_ref, lse_ref):
    q = q_ref[...].reshape(QBLOCK, HDIM)
    k = k_ref[...].reshape(LENGTH, HDIM)
    v = v_ref[...].reshape(LENGTH, HDIM)
    scores = dot(q, k, 1, 1) * SCALE
    scores = jnp.where(visible_mask(pl.program_id(0), odd_ref[0]), scores, MASKED)
    top = jnp.max(scores, axis=1, keepdims=True)
    grown = jnp.exp(scores - top)
    total = jnp.sum(grown, axis=1, keepdims=True)
    lse_ref[...] = top + jnp.log(total)
    probs = (grown * (1.0 / total)).astype(BF)
    o_ref[...] = dot(probs, v, 1, 0).astype(BF).reshape(2, HALF, HDIM)


def packed_part(at, rows, moving=False):
    block = at // rows
    if moving:
        return pl.BlockSpec((2, rows, HDIM), lambda i: (i, block, 0))
    return pl.BlockSpec((NC, rows, HDIM), lambda i: (0, block, 0))


def attn_fwd(odd, got):
    return pl.pallas_call(
        attn_fwd_kernel,
        grid=(QROWS // QBLOCK,),
        in_specs=[
            SMEM,
            packed_part(Q_AT, HALF, True),
            packed_part(K_AT, ROWS),
            packed_part(V_AT, ROWS),
        ],
        out_specs=[
            pl.BlockSpec((2, HALF, HDIM), lambda i: (i, 0, 0)),
            pl.BlockSpec((QBLOCK, 1), lambda i: (i, 0)),
        ],
        out_shape=[shape_of((NC, HALF, HDIM), BF), shape_of((QROWS, 1), F32)],
        compiler_params=PARAMS,
        cost_estimate=cost(4 * QROWS * LENGTH * HDIM, 3e6, QROWS * LENGTH),
        name="attn_fwd",
    )(odd, got, got, got)


def attn_bwd_kernel(
    odd_ref, q_ref, k_ref, v_ref, do_ref, lse_ref, pack_ref, dk_sum, dv_sum
):
    step = pl.program_id(0)

    @pl.when(step == 0)
    def _():
        dk_sum[...] = jnp.zeros_like(dk_sum)
        dv_sum[...] = jnp.zeros_like(dv_sum)

    q = q_ref[...].reshape(QBLOCK, HDIM)
    k = k_ref[...].reshape(LENGTH, HDIM)
    v = v_ref[...].reshape(LENGTH, HDIM)
    do = do_ref[...].reshape(QBLOCK, HDIM)
    scores = dot(q, k, 1, 1) * SCALE - lse_ref[...]
    probs = jnp.exp(jnp.where(visible_mask(step, odd_ref[0]), scores, MASKED))
    d_probs = dot(do, v, 1, 1)
    dv_sum[...] += dot(probs.astype(BF), do, 0, 0)
    inner = jnp.sum(probs * d_probs, axis=1, keepdims=True)
    d_scores = (probs * (d_probs - inner)).astype(BF)
    pack_ref[pl.ds(2 * step, 2), Q_AT:] = (
        (dot(d_scores, k, 1, 0) * SCALE).astype(BF).reshape(2, HALF, HDIM)
    )
    dk_sum[...] += dot(d_scores, q, 0, 0)

    @pl.when(step == pl.num_programs(0) - 1)
    def _():
        pack_ref[:, K_AT:V_AT] = (dk_sum[...] * SCALE).astype(BF).reshape(NC, ROWS, HDIM)
        pack_ref[:, V_AT:Q_AT] = dv_sum[...].astype(BF).reshape(NC, ROWS, HDIM)


def attn_bwd(odd, got, grads, lse):
    return pl.pallas_call(
        attn_bwd_kernel,
        grid=(QROWS // QBLOCK,),
        in_specs=[
            SMEM,
            packed_part(Q_AT, HALF, True),
            packed_part(K_AT, ROWS),
            packed_part(V_AT, ROWS),
            packed_part(XW, HALF, True),
            pl.BlockSpec((QBLOCK, 1), lambda i: (i, 0)),
        ],
        out_specs=whole(NC, ATTN, LANES),
        out_shape=shape_of((NC, ATTN, LANES), BF),
        scratch_shapes=[pltpu.VMEM((LENGTH, HDIM), F32), pltpu.VMEM((LENGTH, HDIM), F32)],
        compiler_params=PARAMS,
        cost_estimate=cost(10 * QROWS * LENGTH * HDIM, 4e6, QROWS * LENGTH),
        name="attn_bwd",
    )(odd, got, got, got, grads, lse)


def tiles_to_rows(refs):
    tiles = []
    for ref in refs:
        count = ref.shape[0] * SLICE
        for tile in range(ref.shape[1]):
            tiles.append(ref[:, tile].reshape(count, LANES).astype(F32))
    return jnp.concatenate(tiles, axis=1)


def unpack_kernel(*refs):
    refs[-1][...] = tiles_to_rows(refs[:-1])


def unpack_rows(tiles, at, first, rows):
    width = D // LANES
    step = NC // 2
    skip, base = first // LANES, at // width
    return pl.pallas_call(
        unpack_kernel,
        grid=(rows // LANES,),
        in_specs=[
            pl.BlockSpec(
                (step, width, SLICE, LANES),
                lambda i: ((i + skip) % 2, base + (i + skip) // 2, 0, 0),
            )
        ],
        out_specs=pl.BlockSpec((LANES, D), lambda i: (i, 0)),
        out_shape=shape_of((rows, D), F32),
        compiler_params=PARAMS,
        cost_estimate=cost(rows * D, 6 * rows * D),
        name="unpack_rows",
    )(tiles)


def unpack_gate_up(tiles):
    part = FF_F // LANES
    many = NF // 2

    def spec(j):
        return pl.BlockSpec(
            (NC, part, SLICE, LANES), lambda h, q: (0, 2 * (q * many + j) + h, 0, 0)
        )

    return pl.pallas_call(
        unpack_kernel,
        grid=(2, NF // many),
        in_specs=[spec(j) for j in range(many)],
        out_specs=pl.BlockSpec(
            (SHARD, many * FF_F), lambda h, q: (0, h * (NF // many) + q)
        ),
        out_shape=shape_of((SHARD, 2 * FF), F32),
        compiler_params=PARAMS,
        cost_estimate=cost(SHARD * 2 * FF, 6 * SHARD * 2 * FF),
        name="unpack_gate_up",
    )(*[tiles] * many)


def turned(ref, tile):
    return ref[:, tile].reshape(SHARD, LANES).astype(F32).T


def unpack_in_kernel(*refs):
    step = pl.program_id(0)
    steps = NF // 2
    wide = INNER_F // LANES
    out_ref = refs[-1]

    @pl.when(step < 2 * steps)
    def _():
        for index in range(2):
            for tile in range(wide):
                start = index * INNER_F + tile * LANES
                out_ref[start : start + LANES] = turned(refs[index], tile)

    @pl.when(step == 2 * steps)
    def _():
        for f in range(NF):
            tail = turned(refs[2 + f], 0)
            out_ref[f * BC_F : (f + 1) * BC_F] = tail[:BC_F]
            first = NF * BC_F + f * DT_F
            out_ref[first : first + DT_F] = tail[BC_F : BC_F + DT_F]


def unpack_in(tiles, z_at):
    wide = INNER_F // LANES
    half = NF // 2
    each = WM_COLS // LANES

    def spec(j):
        def index(i):
            f = 2 * (jnp.minimum(i, 2 * half - 1) % half) + j
            return (0, jnp.where(i < half, z_at + wide * f, each * f), 0, 0)

        shape = tuple(pl.Element(size) for size in (NC, wide, SLICE, LANES))
        return pl.BlockSpec(shape, index)

    def tail_spec(f):
        return pl.BlockSpec((NC, 1, SLICE, LANES), lambda i: (0, each * f + wide, 0, 0))

    specs = [spec(0), spec(1)]
    specs += [tail_spec(f) for f in range(NF)]
    return pl.pallas_call(
        unpack_in_kernel,
        grid=(2 * half + 1,),
        in_specs=specs,
        out_specs=pl.BlockSpec((2 * INNER_F, SHARD), lambda i: (i, 0)),
        out_shape=shape_of((2 * INNER + 2 * STATE + MHEADS, SHARD), F32),
        compiler_params=PARAMS,
        cost_estimate=cost(SHARD * 6704, 6 * SHARD * 6704),
        name="unpack_in",
    )(*[tiles] * len(specs))


def unpack_qkv_kernel(*refs):
    group = NF // KVHEADS

    def tile(f, index):
        return refs[3 * f + index][:, 0].reshape(SHARD, HDIM).astype(F32)

    parts = [tile(f, 0) for f in range(NF)]
    for index in (1, 2):
        for head in range(KVHEADS):
            parts.append(sum(tile(head * group + j, index) for j in range(group)))
    refs[-1][...] = jnp.concatenate(parts, axis=1)


def unpack_qkv(tiles):
    each, first = WM_COLS // LANES, MIX // LANES
    specs = [
        pl.BlockSpec((NC, 1, SLICE, LANES), lambda i, at=each * f + first + index: (0, at, 0, 0))
        for f in range(NF)
        for index in range(3)
    ]
    width = (QHEADS + 2 * KVHEADS) * HDIM
    return pl.pallas_call(
        unpack_qkv_kernel,
        grid=(1,),
        in_specs=specs,
        out_specs=whole(SHARD, width),
        out_shape=shape_of((SHARD, width), F32),
        compiler_params=PARAMS,
        cost_estimate=cost(SHARD * width, 6 * SHARD * width),
        name="unpack_qkv",
    )(*[tiles] * len(specs))


def norm_scale(values):
    return lax.rsqrt(jnp.mean(values * values, axis=-1, keepdims=True) + EPS)


def norm_back(values, scale, gain, grad):
    pulled = grad * gain
    inner = jnp.mean(pulled * values, axis=-1, keepdims=True)
    d_values = scale * pulled - values * (scale * scale * scale) * inner
    return d_values, jnp.sum(grad * values * scale, axis=0)


def columns_of(weight, start, width):
    part = weight[:, start : start + NF * width]
    return part.reshape(weight.shape[0], NF, width).transpose(1, 0, 2)


def shards(
    tokens,
    norm_gain,
    w_in,
    w_qkv,
    conv_weight,
    conv_bias,
    dt_bias,
    a_log,
    d_skip,
    mamba_gain,
    w_mout,
    w_aout,
    mlp_gain,
    w_gate_up,
    w_down,
    cotangent,
):
    ctx = lax.axis_index("ctx")
    fsdp = lax.axis_index("fsdp")
    parity = ctx % 2
    odd = parity.astype(jnp.int32).reshape(1)
    z_at, core = fsdp // 2, fsdp % 2
    pieces = jnp.arange(NF, dtype=jnp.int32)
    order = ((z_at + pieces % NZ) % NZ) * 2 + (core + pieces // NZ) % 2
    place = ((pieces % 2 + core) % 2) * NZ + (pieces // 2 - z_at) % NZ

    def even_first(rows):
        rows = rows.reshape(2, HALF, D)
        return jnp.where(parity == 1, rows[::-1], rows).reshape(ROWS, D)

    spot = jnp.concatenate([place[::2] % NZ, core.astype(jnp.int32).reshape(1)])

    hidden = even_first(tokens).astype(F32)
    scale_one = norm_scale(hidden)
    normed = ring_gather((hidden * scale_one * norm_gain).astype(BF), order)

    in_rows = lax.dynamic_slice(w_in, (ctx * SLICE, 0), (SLICE, w_in.shape[1]))
    qkv_rows = lax.dynamic_slice(w_qkv, (ctx * SLICE, 0), (SLICE, w_qkv.shape[1]))
    gu_rows = lax.dynamic_slice(w_gate_up, (ctx * SLICE, 0), (SLICE, w_gate_up.shape[1]))
    parts = [
        columns_of(in_rows, INNER, INNER_F),
        columns_of(in_rows, 2 * INNER, BC_F),
        columns_of(in_rows, 2 * INNER + 2 * STATE, DT_F),
        jnp.zeros((NF, SLICE, LANES - BC_F - DT_F), BF),
        columns_of(qkv_rows, 0, HDIM),
    ]
    for start in (QHEADS * HDIM, (QHEADS + KVHEADS) * HDIM):
        pair = qkv_rows[:, start : start + KVHEADS * HDIM].reshape(SLICE, KVHEADS, HDIM)
        parts.append(jnp.repeat(pair.transpose(1, 0, 2), NF // KVHEADS, axis=0))
    parts += [
        columns_of(in_rows, 0, INNER_F),
        columns_of(gu_rows, 0, FF_F),
        columns_of(gu_rows, FF, FF_F),
    ]
    swapped = swap_fsdp(jnp.concatenate(parts, axis=2))
    w_one = lax.all_gather(swapped[..., :W1_COLS], "ctx", axis=0)
    w_out = jnp.concatenate([w_mout, w_aout], axis=0)
    cot_low = even_first(cotangent)

    blocks = jnp.stack([ctx, 2 * NC - 1 - ctx])
    blocks = jnp.where(parity == 1, blocks[::-1], blocks)
    positions = (
        blocks[:, None] * HALF + jnp.arange(HALF, dtype=jnp.int32)[None, :]
    ).reshape(ROWS)
    half_dim = HDIM // 2
    freqs = ROPE_BASE ** (-jnp.arange(half_dim, dtype=F32) / half_dim)
    angles = positions.astype(F32)[:, None] * freqs[None, :]
    cosine, sine = jnp.cos(angles), jnp.sin(angles)
    mix_pack, attn_pack = project(normed, w_one, cosine, sine)
    gate_z = project_z(after(normed, mix_pack), w_one)
    mix_got = after(swap_ctx(mix_pack), gate_z)
    attn_got = swap_ctx(after(attn_pack, mix_got))

    x_start = fsdp * INNER_F + parity * XW
    bc_start = INNER + fsdp * BC_F
    conv_all = jnp.concatenate(
        [conv_weight, conv_bias[None], jnp.zeros((3, conv_bias.shape[0]), F32)], axis=0
    )
    taps = jnp.concatenate(
        [
            lax.dynamic_slice(conv_all, (0, x_start), (8, XW)),
            lax.dynamic_slice(conv_all, (0, bc_start), (8, BC_F)),
        ],
        axis=1,
    ).T
    head = fsdp * DT_F + parity * HEADS_L
    my_bias = lax.dynamic_slice(dt_bias, (head,), (HEADS_L,))
    my_rate = -jnp.exp(lax.dynamic_slice(a_log, (head,), (HEADS_L,)))
    heads_in = jnp.broadcast_to(
        jnp.concatenate([my_bias, my_rate, jnp.zeros((8 - 2 * HEADS_L,), F32)])[:, None],
        (8, LANES),
    )
    my_skip = jnp.repeat(lax.dynamic_slice(d_skip, (head,), (HEADS_L,)), MDIM)[:, None]
    x_act, bc_own, row_terms = front(mix_got, taps, heads_in)
    cot_all = gather_fsdp(after(cot_low, mix_pack))
    bc = jnp.concatenate(ring_pieces(bc_own), axis=0).reshape(NF, BC_F, LENGTH)
    w_gu = lax.all_gather(after(swapped[..., W1_COLS:], cot_all, x_act), "ctx", axis=0)
    bc = after(bc, attn_got)
    ssd_seq, states = mamba_fwd(place, x_act, bc, row_terms, my_skip)
    heads_seq, lse = attn_fwd(odd, after(attn_got, ssd_seq))
    ssd = after(swap_ctx(ssd_seq), heads_seq)
    heads = swap_ctx(after(heads_seq, ssd))

    my_gain = lax.dynamic_slice(mamba_gain, (fsdp * INNER_F,), (INNER_F,))[:, None]
    g, squares = gate(ssd, gate_z)
    squares = after(butterfly(squares, "fsdp", NF), w_gu)
    gated_heads, branches = branch_out(heads, g, squares, my_gain, w_out)
    mixed = hidden + scatter_fsdp(branches)

    scale_two = norm_scale(mixed)
    normed_two = gather_fsdp((mixed * scale_two * mlp_gain).astype(BF))
    d_act = act_back(after(cot_all, branches), w_down)
    act, d_gu, d_normed_two = mlp(normed_two, d_act, w_gu)
    down_mine, down_other = down_out(spot, act, w_down)

    def side_by_side(*terms):
        return jnp.concatenate([term.reshape(NC, -1, LANES) for term in terms], axis=1)

    def total_of(got):
        return jnp.sum(got.astype(F32), axis=0).astype(BF)

    def scatter_ctx(joined):
        part = lax.psum_scatter(joined, "ctx", scatter_dimension=0, tiled=False)
        return lax.optimization_barrier(part)

    def all_ctx(parts):
        joined = jnp.concatenate(parts, axis=0)
        return lax.all_gather(joined.reshape(-1, SLICE, LANES), "ctx", axis=0)

    gu_tiles = MLP_COLS // LANES
    z_tiles = INNER_F // LANES
    mix_tiles = WM_COLS // LANES
    row_tiles = OUT_ROWS // SHARD * (D // LANES)
    packed_one = side_by_side(column_grad(normed_two, d_gu), column_grad(act, cot_all))
    d_normed_two, packed_one, down_mine = lax.optimization_barrier(
        (scatter_fsdp(d_normed_two), packed_one, down_mine)
    )
    sum_one = scatter_ctx(packed_one)
    d_mixed, g_mlp_gain = norm_back(mixed, scale_two, mlp_gain, d_normed_two)
    d_mixed = d_mixed + cot_low.astype(F32)
    branch = ring_gather(d_mixed.astype(BF), order)

    dg, inner, dh = branch_back(branch, w_out, g, my_gain)
    inner = butterfly(inner, "fsdp", NF)
    d_mixers, dz, g_mamba_gain = gate_back(
        ssd, gate_z, g, dg, dh, squares, inner, my_gain
    )
    d_mixers = swap_ctx(d_mixers)
    packed_two = side_by_side(column_grad(gated_heads, branch), column_grad(normed, dz))
    d_mixers, packed_two = lax.optimization_barrier((d_mixers, packed_two))
    sum_two = scatter_ctx(packed_two)
    dx, dbc_mine, dbc_other, drow, dskip = mamba_bwd(
        place, x_act, d_mixers, bc, row_terms, states, my_skip
    )
    dbc_joined = ring_join(
        dbc_mine.reshape(NZ * BC_F, LENGTH), dbc_other.reshape(NZ * BC_F, LENGTH)
    )
    attn_pack = attn_bwd(odd, attn_got, after(d_mixers, dx), lse)
    down_at = NF * gu_tiles
    gu_part = swap_fsdp(after(sum_one, dbc_joined)[: down_at * SLICE].reshape(NF, -1, LANES))
    dbc_own, attn_pack, gu_part = lax.optimization_barrier(
        (ring_scatter(dbc_joined), attn_pack, gu_part)
    )
    all_one = all_ctx([gu_part.reshape(-1, LANES), sum_one[down_at * SLICE :]])
    attn_back = swap_ctx(attn_pack)
    mix_back, g_taps, g_heads = front_back(
        mix_got, taps, heads_in, row_terms, drow, dx, dbc_own
    )
    mix_back = swap_ctx(after(mix_back, attn_back))
    d_qkv = attn_grads(attn_back, cosine, sine)
    mix_back, d_qkv = lax.optimization_barrier((mix_back, d_qkv))
    d_mix = mix_grads(mix_back)
    packed_mix = column_grad(normed, d_mix, d_qkv).reshape(NC, -1, LANES)
    got_mix = swap_ctx(packed_mix)
    mine, other, gain_sum = back_project(
        spot, d_mix, d_qkv, after(dz, packed_mix), normed, w_one
    )
    g_norm_gain = gain_sum[0] / norm_gain

    def joined(mine, other):
        return ring_join(mine.reshape(NZ * ROWS, D), other.reshape(NZ * ROWS, D))

    d_normed = joined(mine, other)
    sum_mix = total_of(after(got_mix, d_normed))
    split = z_tiles * SLICE
    columns = swap_fsdp(
        jnp.concatenate(
            [
                sum_two[row_tiles * SLICE :].reshape(NF, -1, LANES),
                sum_mix.reshape(NF, -1, LANES),
            ],
            axis=1,
        )
    )
    mix_at = NF * mix_tiles
    out_at = mix_at + -mix_at % (D // LANES)
    z_at = out_at + row_tiles
    z_at = z_at + -z_at % z_tiles
    all_two = all_ctx(
        [
            columns[:, split:].reshape(-1, LANES),
            jnp.zeros(((out_at - mix_at) * SLICE, LANES), BF),
            sum_two[: row_tiles * SLICE],
            jnp.zeros(((z_at - out_at - row_tiles) * SLICE, LANES), BF),
            columns[:, :split].reshape(-1, LANES),
        ]
    )
    down = joined(down_mine, after(down_other, mine))
    both = ring_scatter(jnp.concatenate([d_normed, down], axis=1))
    output = even_first((mixed + both[:, D:]).astype(BF)).reshape(tokens.shape)

    g_gate_up = unpack_gate_up(all_one)
    g_down = unpack_rows(all_one, down_at, 0, OUT_ROWS)
    all_two = after(all_two, g_gate_up, g_down, output)
    g_mout = unpack_rows(all_two, out_at, 0, INNER_F)
    g_aout = unpack_rows(all_two, out_at, INNER_F, HDIM)
    g_qkv = unpack_qkv(all_two)
    g_in = unpack_in(all_two, z_at).T
    d_hidden, _ = norm_back(hidden, scale_one, norm_gain, both[:, :D])
    d_tokens = even_first((d_hidden + d_mixed).astype(BF)).reshape(tokens.shape)

    def by_half(values):
        zero = jnp.zeros_like(values)
        return jnp.where(
            parity == 1, jnp.stack([zero, values], axis=-2), jnp.stack([values, zero], axis=-2)
        )

    g_conv = g_taps.T[: CONV_K + 1]
    g_d_skip = jnp.sum(dskip.reshape(HEADS_L, MDIM), axis=1)
    per_head = jnp.stack(
        [g_heads[:HEADS_L, 0], g_heads[HEADS_L : 2 * HEADS_L, 0], g_d_skip]
    )
    own = jnp.concatenate(
        [
            by_half(g_conv[:, :XW]).reshape(-1),
            g_conv[:, XW:].reshape(-1),
            g_mamba_gain[:, 0],
            by_half(per_head).reshape(-1),
        ]
    )
    own_size = own.shape[0]
    own_pad = -(-own_size // LANES) * LANES
    own = jnp.concatenate([own, jnp.zeros((own_pad - own_size,), F32), g_mlp_gain, g_norm_gain])
    own = butterfly(own.reshape(-1, LANES), "ctx", NC).reshape(-1)
    mine = (jnp.arange(NF) == fsdp)[:, None]
    placed = jnp.where(mine, own[None, :own_pad], 0.0).reshape(-1)
    total = butterfly(
        jnp.concatenate([placed, own[own_pad:]]).reshape(-1, LANES), "fsdp", NF
    ).reshape(-1)
    each = total[: NF * own_pad].reshape(NF, own_pad)
    cut = [(CONV_K + 1) * INNER_F]
    cut.append(cut[0] + (CONV_K + 1) * BC_F)
    cut.append(cut[1] + INNER_F)
    conv_x = each[:, : cut[0]].reshape(NF, CONV_K + 1, INNER_F).transpose(1, 0, 2)
    conv_bc = each[:, cut[0] : cut[1]].reshape(NF, CONV_K + 1, BC_F).transpose(1, 0, 2)
    conv = jnp.concatenate(
        [conv_x.reshape(CONV_K + 1, INNER), conv_bc.reshape(CONV_K + 1, 2 * STATE)], axis=1
    )
    per_head = each[:, cut[2] : cut[2] + 3 * DT_F].reshape(NF, 3, DT_F).transpose(1, 0, 2)
    per_head = per_head.reshape(3, MHEADS)
    gains = total[NF * own_pad :].reshape(2, D)
    return (
        output,
        d_tokens,
        gains[1],
        g_in,
        g_qkv,
        conv[:CONV_K],
        conv[CONV_K],
        per_head[0],
        per_head[1],
        per_head[2],
        each[:, cut[1] : cut[2]].reshape(INNER),
        g_mout,
        g_aout,
        gains[0],
        g_gate_up,
        g_down,
    )


def solution(mesh):
    tokens_at = P("fsdp", "ctx", None, None)
    rows_at = P("fsdp", None)
    placed = (
        tokens_at,
        P(),
        rows_at,
        rows_at,
        P(),
        P(),
        P(),
        P(),
        P(),
        P(),
        rows_at,
        rows_at,
        P(),
        rows_at,
        rows_at,
        tokens_at,
    )
    return jax.shard_map(
        shards,
        mesh=mesh,
        in_specs=placed,
        out_specs=(
            tokens_at,
            tokens_at,
            P(),
            rows_at,
            rows_at,
            P(),
            P(),
            P(),
            P(),
            P(),
            P(),
            rows_at,
            rows_at,
            P(),
            rows_at,
            rows_at,
        ),
        check_vma=False,
    )
```

time: 2930 us -> 749 us (0.26)
  waiting for transfers between devices: 1960 us -> 272 us
  matrix products: 283 us -> 0 us
  other arithmetic: 324 us -> 48.4 us
  Pallas kernels: 0 us -> 210 us
  local copies, waits for them, and re-layouts: 205 us -> 55.4 us
  starting transfers between devices: 15.9 us -> 114 us
  blocking collectives: 111 us -> 16.2 us
    all_gather x12 -> x6, waiting for transfers between devices: 1200 us -> 41.7 us  [the longest x2 27.7 us: gather_fsdp(): return lax.all_gather(value, 'fsdp', axis=0, tiled=True)]
    reduce_scatter x8 -> x2, waiting for transfers between devices: 465 us -> 46.3 us  [scatter_fsdp(): lax.psum_scatter(parts, 'fsdp', scatter_dimension=0, tiled=True).astype(F32)]
    psum x2 -> x0, waiting for transfers between devices: 285 us -> none  [the longest x1 153 us: shards(): lax.psum(shard_in.astype(jnp.bfloat16), 'ctx').astype(jnp.float32)]
    dot_general x36 -> x0, matrix products: 283 us -> none  [the longest x6 64.9 us: dot_first(): lax.dot_general(left, right, (((0,), (0,)), ((), ())), preferred_element_...]
    select_n x93 -> x5, other arithmetic: 245 us -> 1.01 us  [the longest x1 0.89 us: even_first(): return jnp.where(parity == 1, rows[::-1], rows).reshape(ROWS, D)]
    pallas_call x0 -> x29, Pallas kernels: none -> 210 us  [the longest x5 35.5 us: column_grad(): pl.pallas_call(column_grad_kernel, grid=(count // many,), in_specs=[pl.Bl...]
    ppermute x4 -> x52, waiting for transfers between devices: 3.44 us -> 100 us  [the longest x39 66.3 us: send(): return lax.ppermute(value, 'fsdp', route)]
    all_to_all x0 -> x10, waiting for transfers between devices: none -> 83.3 us  [the longest x8 71.3 us: swap_ctx(): return lax.all_to_all(value, 'ctx', 0, 0, tiled=True)]
  transfers between devices with their start and end apart: 26 -> 72, of which waited for: 17 -> 38; matrix products, arithmetic and copies ran while one was open for 24% -> 11% of each run, Pallas kernels for 0% -> 22%
where the time goes in v1:
time: 749 us; the launch traced here: 736 us
  waiting for transfers between devices  272 us (36%)
  Pallas kernels  210 us (28%)
  starting transfers between devices  114 us (15%)
  local copies, waits for them, and re-layouts  55.4 us (7%)
  other arithmetic  48.4 us (6%)
  between operations  20.9 us (3%)
  blocking collectives  16.2 us (2%)
    all_to_all x8, waiting for transfers between devices, swap_ctx(): return lax.all_to_all(value, 'ctx', 0, 0, tiled=True)  71.3 us
    ppermute x39, waiting for transfers between devices, send(): return lax.ppermute(value, 'fsdp', route)  66.3 us
    all_to_all x8, starting transfers between devices, swap_ctx(): return lax.all_to_all(value, 'ctx', 0, 0, tiled=True)  53.9 us
    reduce_scatter x2, waiting for transfers between devices, scatter_fsdp(): lax.psum_scatter(parts, 'fsdp', scatter_dimension=0, tiled=True).astype(F32)  46.3 us
    ppermute x39, starting transfers between devices, send(): return lax.ppermute(value, 'fsdp', route)  39.4 us
    pallas_call x5, Pallas kernels, column_grad(): pl.pallas_call(column_grad_kernel, grid=(count // many,), in_specs=[pl.Bl...  35.5 us
    ppermute x13, waiting for transfers between devices, butterfly(): lax.ppermute(value, axis, [(i, i ^ bit) for i in range(size)])  33.8 us
    all_gather x2, waiting for transfers between devices, gather_fsdp(): return lax.all_gather(value, 'fsdp', axis=0, tiled=True)  27.7 us
  transfers between devices with their start and end apart: 72, of which 38 were waited for; matrix products, arithmetic and copies ran while one was open for 11% of the time, Pallas kernels for 22%

profile of v1, /device:TPU:16, one launch (start us, length us, event | category | flops | bytes accessed | tf_op | source)
XLA Modules:
  0.0 736.1 jit_solution(1814438363365960967)
XLA Ops:
  15.0 16.2 %all_to_all.55 = bf16[8,16,2304]{2,1,0:T(8,128)(2,1)S(1)} all-to-all(bf16[8,16,2304]{2,1,0:T(8,128)(2,1)S(1)} %copy.115), channel_id=1, replica_groups=mesh['ctx'=16,'fsdp'=8] {'fsdp'}, dimensions={0} | all-to-all | bytes 1179648 | tf_op jit(solution)/shard_map/all_to_all | solution.py:156
  41.1 10.2 %collective-permute-done = bf16[128,2048]{1,0:T(8,128)(2,1)S(1)} collective-permute-done((bf16[128,2048]{1,0:T(8,128)(2,1)S(1)}, bf16[128,2048]{1,0:T(8,128)(2,1)S(1)}, u32[]{:S(2)}, u32[]{:S(2)}) %collective-permute-start) | collective-permute-done | bytes 524320 | tf_op jit(solution)/shard_map/ppermute | solution.py:88
  60.9 6.7 collective-permute-done.3
  73.8 14.0 %all-gather.17.cloned.1.call-done = bf16[128,16,1280]{2,1,0:T(8,128)(2,1)} async-done(((bf16[8,16,1280]{2,1,0:T(8,128)(2,1)}), bf16[128,16,1280]{2,1,0:T(8,128)(2,1)}) %all-gather.17.cloned.1.call-update) | async-done | bytes 5242896 | tf_op jit(solution)/shard_map/all_gather | solution.py:1422
  87.7 9.5 %project.1 = (bf16[16,272,128]{2,1,0:T(8,128)(2,1)}, bf16[16,320,128]{2,1,0:T(8,128)(2,1)}) custom-call(bf16[1024,2048]{1,0:T(8,128)(2,1)} %constant_dynamic-update-slice_fusion.25.n_ref.left_ref, bf16[16,8,16,1280]{3,2,1,0:T(8,128)(2,1)} %bitcast.165, f32[128,64]{1,0:T(8,128)} %get-tuple-element.172.cos_ref, f32[128,64]{1,0:T(8,128)} %get-tuple-element.171.sin_ref), custom_call_target="tpu_custom_call" | custom-call | flops 3758096384 | bytes 10000000 | tf_op jit(solution)/shard_map/project/pallas_call | solution.py:217
  97.4 5.7 all-to-all-start.1
  105.2 7.9 %project_z.1.z_ref = f32[8,384,128]{2,1,0:T(8,128)} custom-call(bf16[1024,2048]{1,0:T(8,128)(2,1)} %constant_dynamic-update-slice_fusion.25.n_ref.left_ref, bf16[16,8,16,1280]{3,2,1,0:T(8,128)(2,1)} %bitcast.166), custom_call_target="tpu_custom_call" | custom-call | flops 1610612736 | bytes 8000000 | tf_op jit(solution)/shard_map/project_z/pallas_call | solution.py:248
  113.1 5.8 all-to-all-done.1.got_ref
  120.0 6.4 front.1
  133.8 7.2 all-to-all-start.2
  142.8 3.5 collective-permute-start.9
  154.4 9.3 %all-to-all-done.2.q_ref.k_ref.v_ref = bf16[16,320,128]{2,1,0:T(8,128)(2,1)S(1)} async-done(((bf16[16,320,128]{2,1,0:T(8,128)(2,1)}), bf16[16,320,128]{2,1,0:T(8,128)(2,1)S(1)}, u32[]{:S(2)}, u32[]{:S(2)}) %all-to-all-start.2) | async-done | bytes 1310752 | tf_op jit(solution)/shard_map/all_to_all | solution.py:152
  163.7 8.9 %mamba_fwd.1 = (bf16[16,192,128]{2,1,0:T(8,128)(2,1)}, f32[8,192,256]{2,1,0:T(8,128)}) custom-call(s32[8]{0:T(128)} %get-tuple-element.188.place_ref, bf16[192,2048]{1,0:T(8,128)(2,1)} %get-tuple-element.84.x_ref, bf16[8,64,2048]{2,1,0:T(8,128)(2,1)} %bitcast.29.bc_ref, f32[16,2048]{1,0:T(8,128)} %get-tuple-element.87.row_ref, ...), custom_call_target="tpu_custom_call" | custom-call | flops 872415232 | bytes 7000000 | tf_op jit(solution)/shard_map/mamba_fwd/pallas_call | solution.py:930
  172.7 6.6 all-to-all-start.3
  179.3 9.2 %attn_fwd.1 = (bf16[16,64,128]{2,1,0:T(8,128)(2,1)}, f32[1024,1]{1,0:T(8,128)}) custom-call(s32[1]{0:T(128)} %bitcast.2.odd_ref, bf16[16,320,128]{2,1,0:T(8,128)(2,1)} %copy-done.15, bf16[16,320,128]{2,1,0:T(8,128)(2,1)} %copy-done.15, bf16[16,320,128]{2,1,0:T(8,128)(2,1)} %copy-done.15), custom_call_target="tpu_custom_call" | custom-call | flops 1073741824 | bytes 3000000 | tf_op jit(solution)/shard_map/attn_fwd/pallas_call | solution.py:1132
  188.5 11.5 %all-to-all-done.3.got_ref = bf16[16,192,128]{2,1,0:T(8,128)(2,1)S(1)} async-done(((bf16[16,192,128]{2,1,0:T(8,128)(2,1)}), bf16[16,192,128]{2,1,0:T(8,128)(2,1)S(1)}, u32[]{:S(2)}, u32[]{:S(2)}) %all-to-all-start.3) | async-done | bytes 786464 | tf_op jit(solution)/shard_map/all_to_all | solution.py:152
  203.6 6.1 all-to-all-start.4
  220.5 7.2 branch_out.1
  227.8 37.0 %reduce-scatter.9.cloned.1.call-done = bf16[128,2048]{1,0:T(8,128)(2,1)} async-done(((bf16[1024,2048]{1,0:T(8,128)(2,1)}), bf16[128,2048]{1,0:T(8,128)(2,1)}) %reduce-scatter.9.cloned.1.call-update) | async-done | bytes 524304 | tf_op jit(solution)/shard_map/reduce_scatter | solution.py:96
  268.3 6.5 act_back.1.d_act_ref
  274.8 24.6 %all-gather.11.cloned.1.call-done.n_ref.left_ref = bf16[1024,2048]{1,0:T(8,128)(2,1)} async-done(((bf16[128,2048]{1,0:T(8,128)(2,1)}), bf16[1024,2048]{1,0:T(8,128)(2,1)}) %all-gather.11.cloned.1.call-update) | async-done | bytes 4194320 | tf_op jit(solution)/shard_map/all_gather | solution.py:92
  299.4 13.9 %mlp.1 = (bf16[1024,512]{1,0:T(8,128)(2,1)}, bf16[1024,1024]{1,0:T(8,128)(2,1)}, bf16[1024,2048]{1,0:T(8,128)(2,1)}) custom-call(bf16[1024,2048]{1,0:T(8,128)(2,1)} %all-gather.11.cloned.1.call-done.n_ref.left_ref, f32[1024,512]{1,0:T(8,128)} %act_back.1.d_act_ref, bf16[16,8,16,1024]{3,2,1,0:T(8,128)(2,1)} %bitcast.215), custom_call_target="tpu_custom_call" | custom-call | flops 8589934592 | bytes 20000000 | tf_op jit(solution)/shard_map/mlp/pallas_call | solution.py:582
  314.7 6.9 down_out.1
  321.6 6.4 column_grad.6
  328.0 8.7 %column_grad.5 = bf16[16,8,8,16,128]{4,3,2,1,0:T(8,128)(2,1)} custom-call(bf16[1024,2048]{1,0:T(8,128)(2,1)} %all-gather.11.cloned.1.call-done.n_ref.left_ref, bf16[1024,1024]{1,0:T(8,128)(2,1)} %get-tuple-element.101.refs_0_), custom_call_target="tpu_custom_call" | custom-call | flops 4294967296 | bytes 10485760 | tf_op jit(solution)/shard_map/column_grad/pallas_call | solution.py:377
  336.7 5.6 pad_maximum_fusion
  342.3 9.3 %reduce-scatter.11.cloned.1.call-done = bf16[128,2048]{1,0:T(8,128)(2,1)} async-done(((bf16[1024,2048]{1,0:T(8,128)(2,1)}), bf16[128,2048]{1,0:T(8,128)(2,1)}) %reduce-scatter.11.cloned.1.call-update) | async-done | bytes 524304 | tf_op jit(solution)/shard_map/reduce_scatter | solution.py:96
  357.8 10.3 %collective-permute-done.19 = bf16[128,2048]{1,0:T(8,128)(2,1)S(1)} collective-permute-done((bf16[128,2048]{1,0:T(8,128)(2,1)S(1)}, bf16[128,2048]{1,0:T(8,128)(2,1)S(1)}, u32[]{:S(2)}, u32[]{:S(2)}) %collective-permute-start.19) | collective-permute-done | bytes 524320 | tf_op jit(solution)/shard_map/ppermute | solution.py:88
  368.1 3.8 collective-permute-start.20
  372.7 5.1 collective-permute-done.20
  377.9 4.0 collective-permute-done.22
  386.1 7.0 branch_back.1
  395.2 3.6 collective-permute-done.28
  398.9 5.1 collective-permute-done.29
  404.6 4.9 gate_back.1
  409.5 7.5 %all-to-all-start.5 = ((bf16[16,256,128]{2,1,0:T(8,128)(2,1)}), bf16[16,256,128]{2,1,0:T(8,128)(2,1)S(1)}, u32[]{:S(2)}, u32[]{:S(2)}) async-start(bf16[16,256,128]{2,1,0:T(8,128)(2,1)} %get-tuple-element.108), calls=%async_computation.7 | async-start | bytes 2097152 | tf_op jit(solution)/shard_map/all_to_all | solution.py:152
  417.1 6.2 column_grad.7
  423.3 6.1 column_grad.8
  429.4 3.6 pad_maximum_fusion.1
  435.0 14.3 %mamba_bwd.1 = (f32[192,2048]{1,0:T(8,128)}, bf16[4,64,2048]{2,1,0:T(8,128)(2,1)}, bf16[4,64,2048]{2,1,0:T(8,128)(2,1)}, f32[8,2048]{1,0:T(8,128)}, f32[192,1]{1,0:T(8,128)}) custom-call(s32[8]{0:T(128)} %get-tuple-element.188.place_ref, bf16[192,2048]{1,0:T(8,128)(2,1)} %get-tuple-element.84.x_ref, bf16[16,256,128]{2,1,0:T(8,128)(2,1)} %copy-done.16, ...), custom_call_target="tpu_custom_call" | custom-call | flops 2214592512 | bytes 12000000 | tf_op jit(solution)/shard_map/mamba_bwd/pallas_call | solution.py:1061
  464.2 11.6 %attn_bwd.1 = bf16[16,320,128]{2,1,0:T(8,128)(2,1)} custom-call(s32[1]{0:T(128)} %bitcast.2.odd_ref, bf16[16,320,128]{2,1,0:T(8,128)(2,1)} %copy-done.15, bf16[16,320,128]{2,1,0:T(8,128)(2,1)} %copy-done.15, bf16[16,320,128]{2,1,0:T(8,128)(2,1)} %copy-done.15, bf16[16,256,128]{2,1,0:T(8,128)(2,1)} %copy-done.16, f32[1024,1]{1,0:T(8,128)} %get-tuple-element.118.lse_ref), custom_call_target="tpu_custom_call" | custom-call | flops 2684354560 | bytes 4000000 | tf_op jit(solution)/shard_map/attn_bwd/pallas_call | solution.py:1184
  482.8 5.6 all-to-all-done.6
  489.1 6.2 all-to-all-start.7
  495.4 11.1 %front_back.1 = (bf16[16,272,128]{2,1,0:T(8,128)(2,1)}, f32[256,8]{1,0:T(8,128)}, f32[8,1]{1,0:T(8,128)}) custom-call(bf16[16,272,128]{2,1,0:T(8,128)(2,1)} %copy-done.6, f32[256,8]{1,0:T(8,128)} %bitcast.179, f32[8,128]{1,0:T(8,128)} %broadcast_in_dim.74.heads_ref, f32[16,2048]{1,0:T(8,128)} %get-tuple-element.87.row_ref, ...), custom_call_target="tpu_custom_call" | custom-call | flops 31457280 | bytes 9000000 | tf_op jit(solution)/shard_map/front_back/pallas_call | solution.py:825
  506.4 7.2 all-to-all-done.7.got_ref
  513.6 6.5 all-to-all-start.8
  520.1 4.1 attn_grads.1.refs_1_.dqkv_ref
  524.2 9.5 %all-to-all-done.8.got_ref = bf16[16,272,128]{2,1,0:T(8,128)(2,1)} async-done(((bf16[16,272,128]{2,1,0:T(8,128)(2,1)}), bf16[16,272,128]{2,1,0:T(8,128)(2,1)}, u32[]{:S(2)}, u32[]{:S(2)}) %all-to-all-start.8) | async-done | bytes 1114144 | tf_op jit(solution)/shard_map/all_to_all | solution.py:152
  533.7 3.6 mix_grads.1.refs_0_.mix_ref
  537.3 8.2 %column_grad.9 = bf16[16,8,7,16,128]{4,3,2,1,0:T(8,128)(2,1)} custom-call(bf16[1024,2048]{1,0:T(8,128)(2,1)} %constant_dynamic-update-slice_fusion.25.n_ref.left_ref, bf16[1024,512]{1,0:T(8,128)(2,1)} %mix_grads.1.refs_0_.mix_ref, bf16[1024,384]{1,0:T(8,128)(2,1)} %attn_grads.1.refs_1_.dqkv_ref), custom_call_target="tpu_custom_call" | custom-call | flops 3758096384 | bytes 9699328 | tf_op jit(solution)/shard_map/column_grad/pallas_call | solution.py:377
  545.5 8.0 %all-to-all-start.9 = ((bf16[16,896,128]{2,1,0:T(8,128)(2,1)}), bf16[16,896,128]{2,1,0:T(8,128)(2,1)}, u32[]{:S(2)}, u32[]{:S(2)}) async-start(bf16[16,896,128]{2,1,0:T(8,128)(2,1)} %bitcast.169), calls=%async_computation.11 | async-start | bytes 7340032 | tf_op jit(solution)/shard_map/all_to_all | solution.py:152
  553.5 11.6 %back_project.1 = (bf16[4,128,2048]{2,1,0:T(8,128)(2,1)}, bf16[4,128,2048]{2,1,0:T(8,128)(2,1)}, f32[1,2048]{1,0:T(1,128)}) custom-call(s32[5]{0:T(128)} %pad_add_fusion.1.spot_ref, bf16[1024,512]{1,0:T(8,128)(2,1)} %mix_grads.1.refs_0_.mix_ref, bf16[1024,384]{1,0:T(8,128)(2,1)} %attn_grads.1.refs_1_.dqkv_ref, ...), custom_call_target="tpu_custom_call" | custom-call | flops 5368709120 | bytes 18000000 | tf_op jit(solution)/shard_map/back_project/pallas_call | solution.py:339
  573.9 27.0 %all-to-all-done.9 = bf16[16,896,128]{2,1,0:T(8,128)(2,1)} async-done(((bf16[16,896,128]{2,1,0:T(8,128)(2,1)}), bf16[16,896,128]{2,1,0:T(8,128)(2,1)}, u32[]{:S(2)}, u32[]{:S(2)}) %all-to-all-start.9) | async-done | bytes 3670048 | tf_op jit(solution)/shard_map/all_to_all | solution.py:152
  609.3 6.5 all-to-all-done.10
  628.2 3.6 collective-permute-done.46
  632.0 3.9 collective-permute-done.47
  635.8 8.1 %collective-permute-start.48 = (f32[53,128]{1,0:T(8,128)S(1)}, f32[53,128]{1,0:T(8,128)S(1)}, u32[]{:S(2)}, u32[]{:S(2)}) collective-permute-start(f32[53,128]{1,0:T(8,128)S(1)} %add.328), channel_id=1, source_target_pairs={{0,64},{8,72},{16,80},{24,88},{32,96},{40,104},{48,112},{56,120},{... | collective-permute-start | bytes 81416 | tf_op jit(solution)/shard_map/ppermute | solution.py:162
  648.2 4.7 collective-permute-done.50
  666.1 9.4 %collective-permute-done.39 = bf16[64,4096]{1,0:T(8,128)(2,1)} collective-permute-done((bf16[64,4096]{1,0:T(8,128)(2,1)}, bf16[64,4096]{1,0:T(8,128)(2,1)}, u32[]{:S(2)}, u32[]{:S(2)}) %collective-permute-start.39) | collective-permute-done | bytes 524320 | tf_op jit(solution)/shard_map/ppermute | solution.py:88
  686.8 9.7 %collective-permute-done.40 = bf16[64,4096]{1,0:T(8,128)(2,1)} collective-permute-done((bf16[64,4096]{1,0:T(8,128)(2,1)}, bf16[64,4096]{1,0:T(8,128)(2,1)}, u32[]{:S(2)}, u32[]{:S(2)}) %collective-permute-start.40) | collective-permute-done | bytes 524320 | tf_op jit(solution)/shard_map/ppermute | solution.py:88
  701.6 4.2 unpack_rows.3
  705.8 5.9 unpack_gate_up.1
  711.7 8.7 %unpack_in.1 = f32[6704,256]{1,0:T(8,128)} custom-call(bf16[16,120,16,128]{3,2,1,0:T(8,128)(2,1)} %all-gather.13.cloned.1.call-done.refs_0_.refs_1_.refs_2_.refs_3_.refs_4_.refs_5_.refs_6_.refs_7_.refs_8_.refs_9_.refs_10_.refs_11_.refs_12_.refs_13_.refs_14_.refs_15_.refs_16_.refs_17_.refs_18_.refs_19_.refs_20_.refs_21_.refs_22_.refs_23_, ...), custom_call_target="tpu_custom_call" | custom-call | flops 1716224 | bytes 10297344 | tf_op jit(solution)/shard_map/unpack_in/pallas_call | solution.py:1305
  720.4 3.6 unpack_rows.4
  (371 shorter events, 174.4 us)
Async XLA Ops:
  7.2 80.6 %all-gather.17.cloned.1.call-start = ((), (), s32[]{:S(2)}) async-start(), calls=%async_computation.21 | async-start | bytes 5570560 | tf_op jit(solution)/shard_map/all_gather | solution.py:1422
  32.0 97.5 %all-gather.9.cloned.1.call-start = ((), (), s32[]{:S(2)}) async-start(), calls=%async_computation.15 | async-start | bytes 4718592 | tf_op jit(solution)/shard_map/all_gather | solution.py:92
  37.8 13.6 %collective-permute-start = (bf16[128,2048]{1,0:T(8,128)(2,1)S(1)}, bf16[128,2048]{1,0:T(8,128)(2,1)S(1)}, u32[]{:S(2)}, u32[]{:S(2)}) collective-permute-start(bf16[128,2048]{1,0:T(8,128)(2,1)S(1)} %get-tuple-element.184), channel_id=1, source_target_pairs={{0,6},{1,7},{2,0},{3,1},{4,2},{5,3},{6,4},{7,5},{8,14},{9,15},{10,... | collective-permute-start | bytes 1572872 | tf_op jit(solution)/shard_map/ppermute | solution.py:88
  38.9 20.4 %collective-permute-start.2 = (bf16[128,2048]{1,0:T(8,128)(2,1)S(1)}, bf16[128,2048]{1,0:T(8,128)(2,1)S(1)}, u32[]{:S(2)}, u32[]{:S(2)}) collective-permute-start(bf16[128,2048]{1,0:T(8,128)(2,1)S(1)} %get-tuple-element.184), channel_id=1, source_target_pairs={{0,2},{1,3},{2,4},{3,5},{4,6},{5,7},{6,0},{7,1},{8,10},{9,11},{10,... | collective-permute-start | bytes 1572872 | tf_op jit(solution)/shard_map/ppermute | solution.py:88
  39.8 29.6 %collective-permute-start.4 = (bf16[128,2048]{1,0:T(8,128)(2,1)S(1)}, bf16[128,2048]{1,0:T(8,128)(2,1)}, u32[]{:S(2)}, u32[]{:S(2)}) collective-permute-start(bf16[128,2048]{1,0:T(8,128)(2,1)S(1)} %get-tuple-element.184), channel_id=1, source_target_pairs={{0,1},{1,0},{2,3},{3,2},{4,5},{5,4},{6,7},{7,6},{8,9},{9,8},{10,11... | collective-permute-start | bytes 1572872 | tf_op jit(solution)/shard_map/ppermute | solution.py:88
  51.4 9.5 %collective-permute-start.1 = (bf16[64,2048]{1,0:T(8,128)(2,1)S(1)}, bf16[64,2048]{1,0:T(8,128)(2,1)S(1)}, u32[]{:S(2)}, u32[]{:S(2)}) collective-permute-start(bf16[64,2048]{1,0:T(8,128)(2,1)S(1)} %slice.308), channel_id=1, source_target_pairs={{0,6},{1,7},{2,0},{3,1},{4,2},{5,3},{6,4},{7,5},{8,14},{9,15},{10,... | collective-permute-start | bytes 786440 | tf_op jit(solution)/shard_map/ppermute | solution.py:88
  59.4 8.2 %collective-permute-start.3 = (bf16[64,2048]{1,0:T(8,128)(2,1)S(1)}, bf16[64,2048]{1,0:T(8,128)(2,1)S(1)}, u32[]{:S(2)}, u32[]{:S(2)}) collective-permute-start(bf16[64,2048]{1,0:T(8,128)(2,1)S(1)} %slice.309), channel_id=1, source_target_pairs={{0,2},{1,3},{2,4},{3,5},{4,6},{5,7},{6,0},{7,1},{8,10},{9,11},{10,... | collective-permute-start | bytes 786440 | tf_op jit(solution)/shard_map/ppermute | solution.py:88
  59.5 11.8 %collective-permute-start.5 = (bf16[128,2048]{1,0:T(8,128)(2,1)S(1)}, bf16[128,2048]{1,0:T(8,128)(2,1)S(1)}, u32[]{:S(2)}, u32[]{:S(2)}) collective-permute-start(bf16[128,2048]{1,0:T(8,128)(2,1)S(1)} %collective-permute-done), channel_id=1, source_target_pairs={{0,1},{1,0},{2,3},{3,2},{4,5},{5,4},{6,7},{7,6},{8,9},{9,8},{10,11... | collective-permute-start | bytes 1572872 | tf_op jit(solution)/shard_map/ppermute | solution.py:88
  59.6 13.4 %collective-permute-start.7 = (bf16[128,2048]{1,0:T(8,128)(2,1)S(1)}, bf16[128,2048]{1,0:T(8,128)(2,1)S(1)}, u32[]{:S(2)}, u32[]{:S(2)}) collective-permute-start(bf16[128,2048]{1,0:T(8,128)(2,1)S(1)} %collective-permute-done.2), channel_id=1, source_target_pairs={{0,1},{1,0},{2,3},{3,2},{4,5},{5,4},{6,7},{7,6},{8,9},{9,8},{10,11... | collective-permute-start | bytes 1572872 | tf_op jit(solution)/shard_map/ppermute | solution.py:88
  67.6 4.5 collective-permute-start.6
  97.4 21.5 %all-to-all-start.1 = ((bf16[16,272,128]{2,1,0:T(8,128)(2,1)}), bf16[16,272,128]{2,1,0:T(8,128)(2,1)S(1)}, u32[]{:S(2)}, u32[]{:S(2)}) async-start(bf16[16,272,128]{2,1,0:T(8,128)(2,1)} %get-tuple-element.80), calls=%async_computation.1 | async-start | bytes 2228224 | tf_op jit(solution)/shard_map/all_to_all | solution.py:152
  103.1 116.7 %all-gather.19.cloned.1.call-start = ((), (), s32[]{:S(2)}) async-start(), calls=%async_computation.22 | async-start | bytes 4456448 | tf_op jit(solution)/shard_map/all_gather | solution.py:1463
  129.5 13.2 %collective-permute-start.10 = (bf16[64,2048]{1,0:T(8,128)(2,1)}, bf16[64,2048]{1,0:T(8,128)(2,1)S(1)}, u32[]{:S(2)}, u32[]{:S(2)}) collective-permute-start(bf16[64,2048]{1,0:T(8,128)(2,1)} %get-tuple-element.85), channel_id=1, source_target_pairs={{0,2},{1,3},{2,4},{3,5},{4,6},{5,7},{6,0},{7,1},{8,10},{9,11},{10,... | collective-permute-start | bytes 786440 | tf_op jit(solution)/shard_map/ppermute | solution.py:88
  130.0 12.8 %collective-permute-start.8 = (bf16[64,2048]{1,0:T(8,128)(2,1)}, bf16[64,2048]{1,0:T(8,128)(2,1)S(1)}, u32[]{:S(2)}, u32[]{:S(2)}) collective-permute-start(bf16[64,2048]{1,0:T(8,128)(2,1)} %get-tuple-element.85), channel_id=1, source_target_pairs={{0,6},{1,7},{2,0},{3,1},{4,2},{5,3},{6,4},{7,5},{8,14},{9,15},{10,... | collective-permute-start | bytes 786440 | tf_op jit(solution)/shard_map/ppermute | solution.py:88
  133.8 17.7 %collective-permute-start.12 = (bf16[64,2048]{1,0:T(8,128)(2,1)}, bf16[64,2048]{1,0:T(8,128)(2,1)S(1)}, u32[]{:S(2)}, u32[]{:S(2)}) collective-permute-start(bf16[64,2048]{1,0:T(8,128)(2,1)} %get-tuple-element.85), channel_id=1, source_target_pairs={{0,1},{1,0},{2,3},{3,2},{4,5},{5,4},{6,7},{7,6},{8,9},{9,8},{10,11... | collective-permute-start | bytes 786440 | tf_op jit(solution)/shard_map/ppermute | solution.py:88
  133.8 30.0 %all-to-all-start.2 = ((bf16[16,320,128]{2,1,0:T(8,128)(2,1)}), bf16[16,320,128]{2,1,0:T(8,128)(2,1)S(1)}, u32[]{:S(2)}, u32[]{:S(2)}) async-start(bf16[16,320,128]{2,1,0:T(8,128)(2,1)} %get-tuple-element.83), calls=%async_computation.2 | async-start | bytes 2621440 | tf_op jit(solution)/shard_map/all_to_all | solution.py:152
  142.7 6.6 collective-permute-start.11
  142.8 6.5 collective-permute-start.9
  146.3 5.9 collective-permute-start.13
  146.3 7.4 %collective-permute-start.15 = (bf16[64,2048]{1,0:T(8,128)(2,1)S(1)}, bf16[64,2048]{1,0:T(8,128)(2,1)S(1)}, u32[]{:S(2)}, u32[]{:S(2)}) collective-permute-start(bf16[64,2048]{1,0:T(8,128)(2,1)S(1)} %collective-permute-done.10), channel_id=1, source_target_pairs={{0,1},{1,0},{2,3},{3,2},{4,5},{5,4},{6,7},{7,6},{8,9},{9,8},{10,11... | collective-permute-start | bytes 786440 | tf_op jit(solution)/shard_map/ppermute | solution.py:88
  172.7 27.4 %all-to-all-start.3 = ((bf16[16,192,128]{2,1,0:T(8,128)(2,1)}), bf16[16,192,128]{2,1,0:T(8,128)(2,1)S(1)}, u32[]{:S(2)}, u32[]{:S(2)}) async-start(bf16[16,192,128]{2,1,0:T(8,128)(2,1)} %get-tuple-element.88), calls=%async_computation.3 | async-start | bytes 1572864 | tf_op jit(solution)/shard_map/all_to_all | solution.py:152
  203.6 6.1 collective-permute-start.16
  203.6 16.1 %all-to-all-start.4 = ((bf16[16,64,128]{2,1,0:T(8,128)(2,1)}), bf16[16,64,128]{2,1,0:T(8,128)(2,1)S(1)}, u32[]{:S(2)}, u32[]{:S(2)}) async-start(bf16[16,64,128]{2,1,0:T(8,128)(2,1)} %get-tuple-element.92), calls=%async_computation.4 | async-start | bytes 524288 | tf_op jit(solution)/shard_map/all_to_all | solution.py:152
  209.7 55.1 %reduce-scatter.9.cloned.1.call-start = ((), (), s32[]{:S(2)}) async-start(), calls=%async_computation.16 | async-start | bytes 4718592 | tf_op jit(solution)/shard_map/reduce_scatter | solution.py:96
  214.1 5.1 collective-permute-start.18
  227.7 71.7 %all-gather.11.cloned.1.call-start = ((), (), s32[]{:S(2)}) async-start(), calls=%async_computation.17 | async-start | bytes 4718592 | tf_op jit(solution)/shard_map/all_gather | solution.py:92
  268.3 83.3 %reduce-scatter.11.cloned.1.call-start = ((), (), s32[]{:S(2)}) async-start(), calls=%async_computation.18 | async-start | bytes 4718592 | tf_op jit(solution)/shard_map/reduce_scatter | solution.py:96
  313.4 162.4 %reduce-scatter.13.cloned.1.call-start = ((), (), s32[]{:S(2)}) async-start(), calls=%async_computation.23 | async-start | bytes 6684672
  355.7 12.4 %collective-permute-start.19 = (bf16[128,2048]{1,0:T(8,128)(2,1)S(1)}, bf16[128,2048]{1,0:T(8,128)(2,1)S(1)}, u32[]{:S(2)}, u32[]{:S(2)}) collective-permute-start(bf16[128,2048]{1,0:T(8,128)(2,1)S(1)} %get-tuple-element.186), channel_id=1, source_target_pairs={{0,6},{1,7},{2,0},{3,1},{4,2},{5,3},{6,4},{7,5},{8,14},{9,15},{10,... | collective-permute-start | bytes 1572872 | tf_op jit(solution)/shard_map/ppermute | solution.py:88
  355.8 16.1 %collective-permute-start.21 = (bf16[128,2048]{1,0:T(8,128)(2,1)S(1)}, bf16[128,2048]{1,0:T(8,128)(2,1)S(1)}, u32[]{:S(2)}, u32[]{:S(2)}) collective-permute-start(bf16[128,2048]{1,0:T(8,128)(2,1)S(1)} %get-tuple-element.186), channel_id=1, source_target_pairs={{0,2},{1,3},{2,4},{3,5},{4,6},{5,7},{6,0},{7,1},{8,10},{9,11},{10,... | collective-permute-start | bytes 1572872 | tf_op jit(solution)/shard_map/ppermute | solution.py:88
  368.1 9.7 %collective-permute-start.20 = (bf16[64,2048]{1,0:T(8,128)(2,1)S(1)}, bf16[64,2048]{1,0:T(8,128)(2,1)S(1)}, u32[]{:S(2)}, u32[]{:S(2)}) collective-permute-start(bf16[64,2048]{1,0:T(8,128)(2,1)S(1)} %slice.314), channel_id=1, source_target_pairs={{0,6},{1,7},{2,0},{3,1},{4,2},{5,3},{6,4},{7,5},{8,14},{9,15},{10,... | collective-permute-start | bytes 786440 | tf_op jit(solution)/shard_map/ppermute | solution.py:88
  371.9 10.3 %collective-permute-start.23 = (bf16[128,2048]{1,0:T(8,128)(2,1)S(1)}, bf16[128,2048]{1,0:T(8,128)(2,1)S(1)}, u32[]{:S(2)}, u32[]{:S(2)}) collective-permute-start(bf16[128,2048]{1,0:T(8,128)(2,1)S(1)} %get-tuple-element.186), channel_id=1, source_target_pairs={{0,1},{1,0},{2,3},{3,2},{4,5},{5,4},{6,7},{7,6},{8,9},{9,8},{10,11... | collective-permute-start | bytes 1572872 | tf_op jit(solution)/shard_map/ppermute | solution.py:88
  371.9 10.0 %collective-permute-start.22 = (bf16[64,2048]{1,0:T(8,128)(2,1)S(1)}, bf16[64,2048]{1,0:T(8,128)(2,1)S(1)}, u32[]{:S(2)}, u32[]{:S(2)}) collective-permute-start(bf16[64,2048]{1,0:T(8,128)(2,1)S(1)} %slice.315), channel_id=1, source_target_pairs={{0,2},{1,3},{2,4},{3,5},{4,6},{5,7},{6,0},{7,1},{8,10},{9,11},{10,... | collective-permute-start | bytes 786440 | tf_op jit(solution)/shard_map/ppermute | solution.py:88
  372.0 10.2 %collective-permute-start.24 = (bf16[128,2048]{1,0:T(8,128)(2,1)S(1)}, bf16[128,2048]{1,0:T(8,128)(2,1)S(1)}, u32[]{:S(2)}, u32[]{:S(2)}) collective-permute-start(bf16[128,2048]{1,0:T(8,128)(2,1)S(1)} %collective-permute-done.19), channel_id=1, source_target_pairs={{0,1},{1,0},{2,3},{3,2},{4,5},{5,4},{6,7},{7,6},{8,9},{9,8},{10,11... | collective-permute-start | bytes 1572872 | tf_op jit(solution)/shard_map/ppermute | solution.py:88
  372.6 11.4 %collective-permute-start.26 = (bf16[128,2048]{1,0:T(8,128)(2,1)S(1)}, bf16[128,2048]{1,0:T(8,128)(2,1)S(1)}, u32[]{:S(2)}, u32[]{:S(2)}) collective-permute-start(bf16[128,2048]{1,0:T(8,128)(2,1)S(1)} %collective-permute-done.21), channel_id=1, source_target_pairs={{0,1},{1,0},{2,3},{3,2},{4,5},{5,4},{6,7},{7,6},{8,9},{9,8},{10,11... | collective-permute-start | bytes 1572872 | tf_op jit(solution)/shard_map/ppermute | solution.py:88
  398.9 5.1 collective-permute-start.29
  409.5 24.6 %all-to-all-start.5 = ((bf16[16,256,128]{2,1,0:T(8,128)(2,1)}), bf16[16,256,128]{2,1,0:T(8,128)(2,1)S(1)}, u32[]{:S(2)}, u32[]{:S(2)}) async-start(bf16[16,256,128]{2,1,0:T(8,128)(2,1)} %get-tuple-element.108), calls=%async_computation.7 | async-start | bytes 2097152 | tf_op jit(solution)/shard_map/all_to_all | solution.py:152
  416.9 148.3 %reduce-scatter.15.cloned.1.call-start = ((), (), s32[]{:S(2)}) async-start(), calls=%async_computation.24 | async-start | bytes 3899392
  454.0 6.9 collective-permute-start.31
  454.1 6.7 collective-permute-start.35
  457.3 23.7 %collective-permute-start.33 = (bf16[32,2048]{1,0:T(8,128)(2,1)S(1)}, bf16[32,2048]{1,0:T(8,128)(2,1)S(1)}, u32[]{:S(2)}, u32[]{:S(2)}) collective-permute-start(bf16[32,2048]{1,0:T(8,128)(2,1)S(1)} %get-tuple-element.163), channel_id=1, source_target_pairs={{0,2},{1,3},{2,4},{3,5},{4,6},{5,7},{6,0},{7,1},{8,10},{9,11},{10,... | collective-permute-start | bytes 393224 | tf_op jit(solution)/shard_map/ppermute | solution.py:88
  457.3 23.7 %collective-permute-start.34 = (bf16[32,2048]{1,0:T(8,128)(2,1)S(1)}, bf16[32,2048]{1,0:T(8,128)(2,1)S(1)}, u32[]{:S(2)}, u32[]{:S(2)}) collective-permute-start(bf16[32,2048]{1,0:T(8,128)(2,1)S(1)} %get-tuple-element.161), channel_id=1, source_target_pairs={{0,6},{1,7},{2,0},{3,1},{4,2},{5,3},{6,4},{7,5},{8,14},{9,15},{10,... | collective-permute-start | bytes 393224 | tf_op jit(solution)/shard_map/ppermute | solution.py:88
  460.9 20.0 %collective-permute-start.32 = (bf16[32,2048]{1,0:T(8,128)(2,1)S(1)}, bf16[32,2048]{1,0:T(8,128)(2,1)S(1)}, u32[]{:S(2)}, u32[]{:S(2)}) collective-permute-start(bf16[32,2048]{1,0:T(8,128)(2,1)S(1)} %get-tuple-element.166), channel_id=1, source_target_pairs={{0,2},{1,3},{2,4},{3,5},{4,6},{5,7},{6,0},{7,1},{8,10},{9,11},{10,... | collective-permute-start | bytes 393224 | tf_op jit(solution)/shard_map/ppermute | solution.py:88
  461.0 20.0 %collective-permute-start.36 = (bf16[32,2048]{1,0:T(8,128)(2,1)S(1)}, bf16[32,2048]{1,0:T(8,128)(2,1)S(1)}, u32[]{:S(2)}, u32[]{:S(2)}) collective-permute-start(bf16[32,2048]{1,0:T(8,128)(2,1)S(1)} %get-tuple-element.165), channel_id=1, source_target_pairs={{0,6},{1,7},{2,0},{3,1},{4,2},{5,3},{6,4},{7,5},{8,14},{9,15},{10,... | collective-permute-start | bytes 393224 | tf_op jit(solution)/shard_map/ppermute | solution.py:88
  477.5 10.9 %all-to-all-start.6 = ((bf16[8,128,128]{2,1,0:T(8,128)(2,1)}), bf16[8,128,128]{2,1,0:T(8,128)(2,1)S(1)}, u32[]{:S(2)}, u32[]{:S(2)}) async-start(bf16[8,128,128]{2,1,0:T(8,128)(2,1)} %bitcast.42), calls=%async_computation.8 | async-start | bytes 524288 | tf_op jit(solution)/shard_map/all_to_all | solution.py:156
  480.9 220.8 %all-gather.15.cloned.1.call-start = ((), (), s32[]{:S(2)}) async-start(), calls=%async_computation.20 | async-start | bytes 6684672 | tf_op jit(solution)/shard_map/all_gather | solution.py:1494
  489.1 24.5 %all-to-all-start.7 = ((bf16[16,320,128]{2,1,0:T(8,128)(2,1)}), bf16[16,320,128]{2,1,0:T(8,128)(2,1)S(1)}, u32[]{:S(2)}, u32[]{:S(2)}) async-start(bf16[16,320,128]{2,1,0:T(8,128)(2,1)} %attn_bwd.1), calls=%async_computation.9 | async-start | bytes 2621440 | tf_op jit(solution)/shard_map/all_to_all | solution.py:152
  513.6 20.1 %all-to-all-start.8 = ((bf16[16,272,128]{2,1,0:T(8,128)(2,1)}), bf16[16,272,128]{2,1,0:T(8,128)(2,1)}, u32[]{:S(2)}, u32[]{:S(2)}) async-start(bf16[16,272,128]{2,1,0:T(8,128)(2,1)} %get-tuple-element.124), calls=%async_computation.10 | async-start | bytes 2228224 | tf_op jit(solution)/shard_map/all_to_all | solution.py:152
  545.5 55.4 %all-to-all-start.9 = ((bf16[16,896,128]{2,1,0:T(8,128)(2,1)}), bf16[16,896,128]{2,1,0:T(8,128)(2,1)}, u32[]{:S(2)}, u32[]{:S(2)}) async-start(bf16[16,896,128]{2,1,0:T(8,128)(2,1)} %bitcast.169), calls=%async_computation.11 | async-start | bytes 7340032 | tf_op jit(solution)/shard_map/all_to_all | solution.py:152
  565.1 4.4 collective-permute-start.37
  604.2 11.6 %all-to-all-start.10 = ((bf16[8,160,128]{2,1,0:T(8,128)(2,1)}), bf16[8,160,128]{2,1,0:T(8,128)(2,1)S(1)}, u32[]{:S(2)}, u32[]{:S(2)}) async-start(bf16[8,160,128]{2,1,0:T(8,128)(2,1)} %pad_maximum_fusion.5), calls=%async_computation.12 | async-start | bytes 655360 | tf_op jit(solution)/shard_map/all_to_all | solution.py:156
  607.7 104.0 %all-gather.13.cloned.1.call-start = ((), (), s32[]{:S(2)}) async-start(), calls=%async_computation.19 | async-start | bytes 8355840 | tf_op jit(solution)/shard_map/all_gather | solution.py:1494
  626.5 5.4 collective-permute-start.46
  628.2 25.2 %collective-permute-start.38 = (bf16[512,2048]{1,0:T(8,128)(2,1)}, bf16[512,2048]{1,0:T(8,128)(2,1)}, u32[]{:S(2)}, u32[]{:S(2)}) collective-permute-start(bf16[512,2048]{1,0:T(8,128)(2,1)} %bitcast.216), channel_id=1, source_target_pairs={{0,1},{1,0},{2,3},{3,2},{4,5},{5,4},{6,7},{7,6},{8,9},{9,8},{10,11... | collective-permute-start | bytes 6291464 | tf_op jit(solution)/shard_map/ppermute | solution.py:88
  631.9 3.9 collective-permute-start.47
  635.8 10.5 %collective-permute-start.48 = (f32[53,128]{1,0:T(8,128)S(1)}, f32[53,128]{1,0:T(8,128)S(1)}, u32[]{:S(2)}, u32[]{:S(2)}) collective-permute-start(f32[53,128]{1,0:T(8,128)S(1)} %add.328), channel_id=1, source_target_pairs={{0,64},{8,72},{16,80},{24,88},{32,96},{40,104},{48,112},{56,120},{... | collective-permute-start | bytes 81416 | tf_op jit(solution)/shard_map/ppermute | solution.py:162
  647.9 5.0 collective-permute-start.50
  652.9 9.5 %collective-permute-start.51 = (f32[200,128]{1,0:T(8,128)S(1)}, f32[200,128]{1,0:T(8,128)S(1)}, u32[]{:S(2)}, u32[]{:S(2)}) collective-permute-start(f32[200,128]{1,0:T(8,128)S(1)} %fusion.39), channel_id=1, source_target_pairs={{0,4},{1,5},{2,6},{3,7},{4,0},{5,1},{6,2},{7,3},{8,12},{9,13},{10,... | collective-permute-start | bytes 307208 | tf_op jit(solution)/shard_map/ppermute | solution.py:162
  659.1 16.4 %collective-permute-start.39 = (bf16[64,4096]{1,0:T(8,128)(2,1)}, bf16[64,4096]{1,0:T(8,128)(2,1)}, u32[]{:S(2)}, u32[]{:S(2)}) collective-permute-start(bf16[64,4096]{1,0:T(8,128)(2,1)} %get-tuple-element.150), channel_id=1, source_target_pairs={{0,2},{1,3},{2,4},{3,5},{4,6},{5,7},{6,0},{7,1},{8,10},{9,11},{10,... | collective-permute-start | bytes 1572872 | tf_op jit(solution)/shard_map/ppermute | solution.py:88
  660.3 15.3 %collective-permute-start.43 = (bf16[64,4096]{1,0:T(8,128)(2,1)}, bf16[64,4096]{1,0:T(8,128)(2,1)}, u32[]{:S(2)}, u32[]{:S(2)}) collective-permute-start(bf16[64,4096]{1,0:T(8,128)(2,1)} %get-tuple-element.152), channel_id=1, source_target_pairs={{0,6},{1,7},{2,0},{3,1},{4,2},{5,3},{6,4},{7,5},{8,14},{9,15},{10,... | collective-permute-start | bytes 1572872 | tf_op jit(solution)/shard_map/ppermute | solution.py:88
  662.8 24.0 %collective-permute-start.41 = (bf16[64,4096]{1,0:T(8,128)(2,1)}, bf16[64,4096]{1,0:T(8,128)(2,1)}, u32[]{:S(2)}, u32[]{:S(2)}) collective-permute-start(bf16[64,4096]{1,0:T(8,128)(2,1)} %get-tuple-element.151), channel_id=1, source_target_pairs={{0,2},{1,3},{2,4},{3,5},{4,6},{5,7},{6,0},{7,1},{8,10},{9,11},{10,... | collective-permute-start | bytes 1572872 | tf_op jit(solution)/shard_map/ppermute | solution.py:88
  662.9 23.9 %collective-permute-start.42 = (bf16[64,4096]{1,0:T(8,128)(2,1)}, bf16[64,4096]{1,0:T(8,128)(2,1)}, u32[]{:S(2)}, u32[]{:S(2)}) collective-permute-start(bf16[64,4096]{1,0:T(8,128)(2,1)} %get-tuple-element.149), channel_id=1, source_target_pairs={{0,6},{1,7},{2,0},{3,1},{4,2},{5,3},{6,4},{7,5},{8,14},{9,15},{10,... | collective-permute-start | bytes 1572872 | tf_op jit(solution)/shard_map/ppermute | solution.py:88
  678.1 18.3 %collective-permute-start.40 = (bf16[64,4096]{1,0:T(8,128)(2,1)}, bf16[64,4096]{1,0:T(8,128)(2,1)}, u32[]{:S(2)}, u32[]{:S(2)}) collective-permute-start(bf16[64,4096]{1,0:T(8,128)(2,1)} %get-tuple-element.154), channel_id=1, source_target_pairs={{0,2},{1,3},{2,4},{3,5},{4,6},{5,7},{6,0},{7,1},{8,10},{9,11},{10,... | collective-permute-start | bytes 1572872 | tf_op jit(solution)/shard_map/ppermute | solution.py:88
  679.9 16.5 %collective-permute-start.44 = (bf16[64,4096]{1,0:T(8,128)(2,1)}, bf16[64,4096]{1,0:T(8,128)(2,1)}, u32[]{:S(2)}, u32[]{:S(2)}) collective-permute-start(bf16[64,4096]{1,0:T(8,128)(2,1)} %get-tuple-element.153), channel_id=1, source_target_pairs={{0,6},{1,7},{2,0},{3,1},{4,2},{5,3},{6,4},{7,5},{8,14},{9,15},{10,... | collective-permute-start | bytes 1572872 | tf_op jit(solution)/shard_map/ppermute | solution.py:88
  (38 other events, 403.2 us)
Sparse Core Ops, SparseCore 0:
  32.1 55.5 all-gather.16
  97.4 32.0 all-gather.8
  132.2 67.9 all-gather.18
  227.8 36.9 reduce-scatter.8
  268.4 31.0 all-gather.10
  313.5 38.0 reduce-scatter.10
  355.6 84.1 reduce-scatter.12
  443.8 80.9 reduce-scatter.14
  527.0 96.6 all-gather.14
  626.3 67.4 all-gather.12

commit v2 on v1

--- a/solution.py
+++ b/solution.py
@@ -127,16 +127,22 @@
     return plus(mine, send(other, OTHER_CORE)).astype(BF)
 
 
-def ring_scatter(joined):
+def ring_first(joined):
     size = joined.shape[0] // NZ
     half = size // 2
     own, after, far, before = [joined[i * size : (i + 1) * size] for i in range(NZ)]
-    far_next = send(far[:half], TO_NEXT)
-    far_prev = send(far[half:], TO_PREV)
-    after_two = send(after[half:], TO_NEXT)
-    before_one = send(before[:half], TO_PREV)
-    after_one = send(plus(after[:half], far_next).astype(BF), TO_NEXT)
-    before_two = send(plus(before[half:], far_prev).astype(BF), TO_PREV)
+    sent = (
+        send(far[:half], TO_NEXT),
+        send(far[half:], TO_PREV),
+        send(after[half:], TO_NEXT),
+        send(before[:half], TO_PREV),
+    )
+    return own, after[:half], before[half:], *sent
+
+
+def ring_last(own, after, before, far_next, far_prev, after_two, before_one):
+    after_one = send(plus(after, far_next).astype(BF), TO_NEXT)
+    before_two = send(plus(before, far_prev).astype(BF), TO_PREV)
     return plus(
         own,
         jnp.concatenate([after_one, after_two], axis=0),
@@ -144,8 +150,12 @@
     )
 
 
-def after(value, *others):
-    return lax.optimization_barrier((value,) + others)[0]
+def ring_scatter(joined):
+    return ring_last(*ring_first(joined))
+
+
+def together(*values):
+    return lax.optimization_barrier(values)
 
 
 def swap_ctx(value):
@@ -156,11 +166,14 @@
     return lax.all_to_all(value, "fsdp", 0, 0, tiled=True)
 
 
-def butterfly(value, axis, size):
-    bit = 1
-    while bit < size:
-        value = value + lax.ppermute(value, axis, [(i, i ^ bit) for i in range(size)])
-        bit *= 2
+def exchange(value, axis, bit):
+    size = lax.axis_size(axis)
+    return value + lax.ppermute(value, axis, [(i, i ^ bit) for i in range(size)])
+
+
+def butterfly(value, axis, bits):
+    for bit in bits:
+        value = exchange(value, axis, bit)
     return value
 
 
@@ -1284,21 +1297,21 @@
             out_ref[first : first + DT_F] = tail[BC_F : BC_F + DT_F]
 
 
-def unpack_in(tiles, z_at):
+def unpack_in(tiles):
     wide = INNER_F // LANES
     half = NF // 2
-    each = WM_COLS // LANES
+    each = W1_COLS // LANES
 
     def spec(j):
         def index(i):
             f = 2 * (jnp.minimum(i, 2 * half - 1) % half) + j
-            return (0, jnp.where(i < half, z_at + wide * f, each * f), 0, 0)
+            return (0, each * f + jnp.where(i < half, 0, wide), 0, 0)
 
         shape = tuple(pl.Element(size) for size in (NC, wide, SLICE, LANES))
         return pl.BlockSpec(shape, index)
 
     def tail_spec(f):
-        return pl.BlockSpec((NC, 1, SLICE, LANES), lambda i: (0, each * f + wide, 0, 0))
+        return pl.BlockSpec((NC, 1, SLICE, LANES), lambda i: (0, each * f + 2 * wide, 0, 0))
 
     specs = [spec(0), spec(1)]
     specs += [tail_spec(f) for f in range(NF)]
@@ -1328,7 +1341,7 @@
 
 
 def unpack_qkv(tiles):
-    each, first = WM_COLS // LANES, MIX // LANES
+    each, first = W1_COLS // LANES, (INNER_F + MIX) // LANES
     specs = [
         pl.BlockSpec((NC, 1, SLICE, LANES), lambda i, at=each * f + first + index: (0, at, 0, 0))
         for f in range(NF)
@@ -1418,8 +1431,11 @@
         columns_of(gu_rows, 0, FF_F),
         columns_of(gu_rows, FF, FF_F),
     ]
-    swapped = swap_fsdp(jnp.concatenate(parts, axis=2))
-    w_one = lax.all_gather(swapped[..., :W1_COLS], "ctx", axis=0)
+    swapped, gu_swapped = together(
+        swap_fsdp(jnp.concatenate(parts[:-2], axis=2)), jnp.concatenate(parts[-2:], axis=2)
+    )
+    w_one = lax.all_gather(swapped, "ctx", axis=0)
+    normed, gu_swapped = together(normed, swap_fsdp(gu_swapped))
     w_out = jnp.concatenate([w_mout, w_aout], axis=0)
     cot_low = even_first(cotangent)
 
@@ -1433,9 +1449,12 @@
     angles = positions.astype(F32)[:, None] * freqs[None, :]
     cosine, sine = jnp.cos(angles), jnp.sin(angles)
     mix_pack, attn_pack = project(normed, w_one, cosine, sine)
-    gate_z = project_z(after(normed, mix_pack), w_one)
-    mix_got = after(swap_ctx(mix_pack), gate_z)
-    attn_got = swap_ctx(after(attn_pack, mix_got))
+    mix_pack, cot_low, normed = together(mix_pack, cot_low, normed)
+    cot_all = gather_fsdp(cot_low)
+    mix_got, gate_z, attn_pack = together(
+        swap_ctx(mix_pack), project_z(normed, w_one), attn_pack
+    )
+    attn_got = swap_ctx(attn_pack)
 
     x_start = fsdp * INNER_F + parity * XW
     bc_start = INNER + fsdp * BC_F
@@ -1458,24 +1477,26 @@
     )
     my_skip = jnp.repeat(lax.dynamic_slice(d_skip, (head,), (HEADS_L,)), MDIM)[:, None]
     x_act, bc_own, row_terms = front(mix_got, taps, heads_in)
-    cot_all = gather_fsdp(after(cot_low, mix_pack))
+    bc_own, gu_swapped = together(bc_own, gu_swapped)
+    w_gu = lax.all_gather(gu_swapped, "ctx", axis=0)
     bc = jnp.concatenate(ring_pieces(bc_own), axis=0).reshape(NF, BC_F, LENGTH)
-    w_gu = lax.all_gather(after(swapped[..., W1_COLS:], cot_all, x_act), "ctx", axis=0)
-    bc = after(bc, attn_got)
     ssd_seq, states = mamba_fwd(place, x_act, bc, row_terms, my_skip)
-    heads_seq, lse = attn_fwd(odd, after(attn_got, ssd_seq))
-    ssd = after(swap_ctx(ssd_seq), heads_seq)
-    heads = swap_ctx(after(heads_seq, ssd))
+    ssd_seq, attn_got, cot_all = together(ssd_seq, attn_got, cot_all)
+    heads_seq, lse = attn_fwd(odd, attn_got)
+    ssd, heads_seq = together(swap_ctx(ssd_seq), heads_seq)
+    heads = swap_ctx(heads_seq)
 
     my_gain = lax.dynamic_slice(mamba_gain, (fsdp * INNER_F,), (INNER_F,))[:, None]
     g, squares = gate(ssd, gate_z)
-    squares = after(butterfly(squares, "fsdp", NF), w_gu)
+    squares, w_gu = together(butterfly(squares, "fsdp", (1, 2, 4)), w_gu)
     gated_heads, branches = branch_out(heads, g, squares, my_gain, w_out)
+    branches, cot_all = together(branches, cot_all)
     mixed = hidden + scatter_fsdp(branches)
 
     scale_two = norm_scale(mixed)
-    normed_two = gather_fsdp((mixed * scale_two * mlp_gain).astype(BF))
-    d_act = act_back(after(cot_all, branches), w_down)
+    normed_two, d_act = together(
+        gather_fsdp((mixed * scale_two * mlp_gain).astype(BF)), act_back(cot_all, w_down)
+    )
     act, d_gu, d_normed_two = mlp(normed_two, d_act, w_gu)
     down_mine, down_other = down_out(spot, act, w_down)
 
@@ -1494,12 +1515,10 @@
         return lax.all_gather(joined.reshape(-1, SLICE, LANES), "ctx", axis=0)
 
     gu_tiles = MLP_COLS // LANES
-    z_tiles = INNER_F // LANES
-    mix_tiles = WM_COLS // LANES
     row_tiles = OUT_ROWS // SHARD * (D // LANES)
     packed_one = side_by_side(column_grad(normed_two, d_gu), column_grad(act, cot_all))
-    d_normed_two, packed_one, down_mine = lax.optimization_barrier(
-        (scatter_fsdp(d_normed_two), packed_one, down_mine)
+    d_normed_two, packed_one, down_mine, down_other = together(
+        scatter_fsdp(d_normed_two), packed_one, down_mine, down_other
     )
     sum_one = scatter_ctx(packed_one)
     d_mixed, g_mlp_gain = norm_back(mixed, scale_two, mlp_gain, d_normed_two)
@@ -1507,7 +1526,7 @@
     branch = ring_gather(d_mixed.astype(BF), order)
 
     dg, inner, dh = branch_back(branch, w_out, g, my_gain)
-    inner = butterfly(inner, "fsdp", NF)
+    inner = butterfly(inner, "fsdp", (1, 2, 4))
     d_mixers, dz, g_mamba_gain = gate_back(
         ssd, gate_z, g, dg, dh, squares, inner, my_gain
     )
@@ -1521,70 +1540,51 @@
     dbc_joined = ring_join(
         dbc_mine.reshape(NZ * BC_F, LENGTH), dbc_other.reshape(NZ * BC_F, LENGTH)
     )
-    attn_pack = attn_bwd(odd, attn_got, after(d_mixers, dx), lse)
+    dx, d_mixers = together(dx, d_mixers)
+    dbc_joined, sum_one = together(dbc_joined, sum_one)
     down_at = NF * gu_tiles
-    gu_part = swap_fsdp(after(sum_one, dbc_joined)[: down_at * SLICE].reshape(NF, -1, LANES))
-    dbc_own, attn_pack, gu_part = lax.optimization_barrier(
-        (ring_scatter(dbc_joined), attn_pack, gu_part)
-    )
-    all_one = all_ctx([gu_part.reshape(-1, LANES), sum_one[down_at * SLICE :]])
+    out_at = down_at + row_tiles
+    gu_part = swap_fsdp(sum_one[: down_at * SLICE].reshape(NF, -1, LANES))
+    dbc_own, attn_pack, gu_part, down_other = together(
+        ring_scatter(dbc_joined), attn_bwd(odd, attn_got, d_mixers, lse), gu_part, down_other
+    )
     attn_back = swap_ctx(attn_pack)
-    mix_back, g_taps, g_heads = front_back(
+    mix_pack, g_taps, g_heads = front_back(
         mix_got, taps, heads_in, row_terms, drow, dx, dbc_own
     )
-    mix_back = swap_ctx(after(mix_back, attn_back))
-    d_qkv = attn_grads(attn_back, cosine, sine)
-    mix_back, d_qkv = lax.optimization_barrier((mix_back, d_qkv))
-    d_mix = mix_grads(mix_back)
-    packed_mix = column_grad(normed, d_mix, d_qkv).reshape(NC, -1, LANES)
-    got_mix = swap_ctx(packed_mix)
-    mine, other, gain_sum = back_project(
-        spot, d_mix, d_qkv, after(dz, packed_mix), normed, w_one
-    )
-    g_norm_gain = gain_sum[0] / norm_gain
-
+    mix_pack, attn_back = together(mix_pack, attn_back)
     def joined(mine, other):
         return ring_join(mine.reshape(NZ * ROWS, D), other.reshape(NZ * ROWS, D))
 
-    d_normed = joined(mine, other)
-    sum_mix = total_of(after(got_mix, d_normed))
-    split = z_tiles * SLICE
+    mix_back, d_qkv, sum_two, down = together(
+        swap_ctx(mix_pack),
+        attn_grads(attn_back, cosine, sine),
+        sum_two,
+        ring_scatter(joined(down_mine, down_other)),
+    )
+    output = even_first((mixed + down).astype(BF)).reshape(tokens.shape)
+    all_one = all_ctx(
+        [
+            gu_part.reshape(-1, LANES),
+            sum_one[down_at * SLICE :],
+            sum_two[: row_tiles * SLICE],
+        ]
+    )
+    d_mix = mix_grads(mix_back)
+    packed_mix, dz = together(column_grad(normed, d_mix, d_qkv).reshape(NC, -1, LANES), dz)
+    mine, other, gain_sum = back_project(spot, d_mix, d_qkv, dz, normed, w_one)
+    g_norm_gain = gain_sum[0] / norm_gain
+
+    got_mix, d_normed = together(swap_ctx(packed_mix), joined(mine, other))
     columns = swap_fsdp(
         jnp.concatenate(
             [
                 sum_two[row_tiles * SLICE :].reshape(NF, -1, LANES),
-                sum_mix.reshape(NF, -1, LANES),
+                total_of(got_mix).reshape(NF, -1, LANES),
             ],
             axis=1,
         )
     )
-    mix_at = NF * mix_tiles
-    out_at = mix_at + -mix_at % (D // LANES)
-    z_at = out_at + row_tiles
-    z_at = z_at + -z_at % z_tiles
-    all_two = all_ctx(
-        [
-            columns[:, split:].reshape(-1, LANES),
-            jnp.zeros(((out_at - mix_at) * SLICE, LANES), BF),
-            sum_two[: row_tiles * SLICE],
-            jnp.zeros(((z_at - out_at - row_tiles) * SLICE, LANES), BF),
-            columns[:, :split].reshape(-1, LANES),
-        ]
-    )
-    down = joined(down_mine, after(down_other, mine))
-    both = ring_scatter(jnp.concatenate([d_normed, down], axis=1))
-    output = even_first((mixed + both[:, D:]).astype(BF)).reshape(tokens.shape)
-
-    g_gate_up = unpack_gate_up(all_one)
-    g_down = unpack_rows(all_one, down_at, 0, OUT_ROWS)
-    all_two = after(all_two, g_gate_up, g_down, output)
-    g_mout = unpack_rows(all_two, out_at, 0, INNER_F)
-    g_aout = unpack_rows(all_two, out_at, INNER_F, HDIM)
-    g_qkv = unpack_qkv(all_two)
-    g_in = unpack_in(all_two, z_at).T
-    d_hidden, _ = norm_back(hidden, scale_one, norm_gain, both[:, :D])
-    d_tokens = even_first((d_hidden + d_mixed).astype(BF)).reshape(tokens.shape)
-
     def by_half(values):
         zero = jnp.zeros_like(values)
         return jnp.where(
@@ -1607,12 +1607,30 @@
     own_size = own.shape[0]
     own_pad = -(-own_size // LANES) * LANES
     own = jnp.concatenate([own, jnp.zeros((own_pad - own_size,), F32), g_mlp_gain, g_norm_gain])
-    own = butterfly(own.reshape(-1, LANES), "ctx", NC).reshape(-1)
+
+    own, columns, all_one = together(own.reshape(-1, LANES), columns, all_one)
+    all_two = all_ctx([columns.reshape(-1, LANES)])
+    own, *d_normed = together(butterfly(own, "ctx", (1, 2, 4)), *ring_first(d_normed))
+    own = butterfly(own, "ctx", (8,)).reshape(-1)
     mine = (jnp.arange(NF) == fsdp)[:, None]
     placed = jnp.where(mine, own[None, :own_pad], 0.0).reshape(-1)
-    total = butterfly(
-        jnp.concatenate([placed, own[own_pad:]]).reshape(-1, LANES), "fsdp", NF
-    ).reshape(-1)
+    total = jnp.concatenate([placed, own[own_pad:]]).reshape(-1, LANES)
+    total, d_normed = together(butterfly(total, "fsdp", (1,)), ring_last(*d_normed))
+
+    g_gate_up = unpack_gate_up(all_one)
+    g_down = unpack_rows(all_one, down_at, 0, OUT_ROWS)
+    g_mout = unpack_rows(all_one, out_at, 0, INNER_F)
+    g_aout = unpack_rows(all_one, out_at, INNER_F, HDIM)
+    total = butterfly(total, "fsdp", (2,))
+    total, g_gate_up, g_down, g_mout, g_aout = together(
+        total, g_gate_up, g_down, g_mout, g_aout
+    )
+    g_qkv = unpack_qkv(all_two)
+    g_in = unpack_in(all_two).T
+    d_hidden, _ = norm_back(hidden, scale_one, norm_gain, d_normed)
+    d_tokens = even_first((d_hidden + d_mixed).astype(BF)).reshape(tokens.shape)
+
+    total = butterfly(total, "fsdp", (4,)).reshape(-1)
     each = total[: NF * own_pad].reshape(NF, own_pad)
     cut = [(CONV_K + 1) * INNER_F]
     cut.append(cut[0] + (CONV_K + 1) * BC_F)

time: 749 us -> 732 us (0.977)
  starting transfers between devices: 114 us -> 146 us
  waiting for transfers between devices: 272 us -> 245 us
  blocking collectives: 16.2 us -> 0 us
  local copies, waits for them, and re-layouts: 55.4 us -> 47.2 us
    all_to_all x8, waiting for transfers between devices: 71.3 us -> 51.8 us  [swap_ctx(): return lax.all_to_all(value, 'ctx', 0, 0, tiled=True)]
    all_to_all x1 -> x0, blocking collectives: 16.2 us -> none  [swap_fsdp(): return lax.all_to_all(value, 'fsdp', 0, 0, tiled=True)]
    all_gather x2, waiting for transfers between devices: 0.01 us -> 16.1 us  [all_ctx(): return lax.all_gather(joined.reshape(-1, SLICE, LANES), 'ctx', axis=0)]
    ppermute x39 -> x45, waiting for transfers between devices: 66.3 us -> 50.8 us  [send(): return lax.ppermute(value, 'fsdp', route)]
    ppermute x39 -> x45, starting transfers between devices: 39.4 us -> 51.7 us  [send(): return lax.ppermute(value, 'fsdp', route)]
    all_to_all x2 -> x4, starting transfers between devices: 6.85 us -> 18.8 us  [swap_fsdp(): return lax.all_to_all(value, 'fsdp', 0, 0, tiled=True)]
    all_to_all x2 -> x4, waiting for transfers between devices: 12.1 us -> 20.1 us  [swap_fsdp(): return lax.all_to_all(value, 'fsdp', 0, 0, tiled=True)]
    ppermute x13, waiting for transfers between devices: 33.8 us -> 26.2 us  [exchange(): lax.ppermute(value, axis, [(i, i ^ bit) for i in range(size)])]
  transfers between devices with their start and end apart: 72 -> 80, of which waited for: 38 -> 35; matrix products, arithmetic and copies ran while one was open for 11% -> 11% of each run, Pallas kernels for 22% -> 23%
where the time goes in v2:
time: 732 us; the launch traced here: 720 us
  waiting for transfers between devices  245 us (33%)
  Pallas kernels  210 us (29%)
  starting transfers between devices  146 us (20%)
  other arithmetic  50.9 us (7%)
  local copies, waits for them, and re-layouts  47.2 us (6%)
  between operations  21 us (3%)
    all_to_all x8, starting transfers between devices, swap_ctx(): return lax.all_to_all(value, 'ctx', 0, 0, tiled=True)  54.5 us
    all_to_all x8, waiting for transfers between devices, swap_ctx(): return lax.all_to_all(value, 'ctx', 0, 0, tiled=True)  51.8 us
    ppermute x45, starting transfers between devices, send(): return lax.ppermute(value, 'fsdp', route)  51.7 us
    ppermute x45, waiting for transfers between devices, send(): return lax.ppermute(value, 'fsdp', route)  50.8 us
    reduce_scatter x2, waiting for transfers between devices, scatter_fsdp(): lax.psum_scatter(parts, 'fsdp', scatter_dimension=0, tiled=True).astype(F32)  46.9 us
    pallas_call x5, Pallas kernels, column_grad(): pl.pallas_call(column_grad_kernel, grid=(count // many,), in_specs=[pl.Bl...  35.4 us
    ppermute x13, waiting for transfers between devices, exchange(): lax.ppermute(value, axis, [(i, i ^ bit) for i in range(size)])  26.2 us
    all_gather x2, waiting for transfers between devices, gather_fsdp(): return lax.all_gather(value, 'fsdp', axis=0, tiled=True)  24.7 us
  transfers between devices with their start and end apart: 80, of which 35 were waited for; matrix products, arithmetic and copies ran while one was open for 11% of the time, Pallas kernels for 23%

profile of v2, /device:TPU:16, one launch (start us, length us, event | category | flops | bytes accessed | tf_op | source)
XLA Modules:
  0.0 720.1 jit_solution(9967577035082955785)
XLA Ops:
  14.3 5.4 all-to-all-start
  20.9 7.1 all-to-all-done
  37.3 9.9 %collective-permute-done = bf16[128,2048]{1,0:T(8,128)(2,1)S(1)} collective-permute-done((bf16[128,2048]{1,0:T(8,128)(2,1)S(1)}, bf16[128,2048]{1,0:T(8,128)(2,1)S(1)}, u32[]{:S(2)}, u32[]{:S(2)}) %collective-permute-start) | collective-permute-done | bytes 524320 | tf_op jit(solution)/shard_map/ppermute | solution.py:88
  56.6 3.4 all-to-all-start.1
  64.4 8.5 %collective-permute-done.3 = bf16[64,2048]{1,0:T(8,128)(2,1)S(1)} collective-permute-done((bf16[64,2048]{1,0:T(8,128)(2,1)S(1)}, bf16[64,2048]{1,0:T(8,128)(2,1)S(1)}, u32[]{:S(2)}, u32[]{:S(2)}) %collective-permute-start.3) | collective-permute-done | bytes 262176 | tf_op jit(solution)/shard_map/ppermute | solution.py:88
  77.9 6.5 all-gather.17.cloned.1.call-done
  84.5 9.5 %project.1 = (bf16[16,272,128]{2,1,0:T(8,128)(2,1)}, bf16[16,320,128]{2,1,0:T(8,128)(2,1)}) custom-call(bf16[1024,2048]{1,0:T(8,128)(2,1)} %constant_dynamic-update-slice_fusion.25.n_ref.left_ref, bf16[16,8,16,1280]{3,2,1,0:T(8,128)(2,1)} %bitcast.155, f32[128,64]{1,0:T(8,128)} %get-tuple-element.252.cos_ref, f32[128,64]{1,0:T(8,128)} %get-tuple-element.251.sin_ref), custom_call_target="tpu_custom_call" | custom-call | flops 3758096384 | bytes 10000000 | tf_op jit(solution)/shard_map/project/pallas_call | solution.py:230
  94.1 5.7 all-to-all-start.2
  101.2 7.9 %project_z.1.z_ref = f32[8,384,128]{2,1,0:T(8,128)} custom-call(bf16[1024,2048]{1,0:T(8,128)(2,1)} %constant_dynamic-update-slice_fusion.25.n_ref.left_ref, bf16[16,8,16,1280]{3,2,1,0:T(8,128)(2,1)} %bitcast.156), custom_call_target="tpu_custom_call" | custom-call | flops 1610612736 | bytes 8000000 | tf_op jit(solution)/shard_map/project_z/pallas_call | solution.py:261
  109.1 6.6 all-to-all-done.2.got_ref
  116.7 6.4 front.1
  127.9 6.2 all-to-all-start.3
  145.3 8.5 %mamba_fwd.1 = (bf16[16,192,128]{2,1,0:T(8,128)(2,1)}, f32[8,192,256]{2,1,0:T(8,128)}) custom-call(s32[8]{0:T(128)} %fusion.13.place_ref, bf16[192,2048]{1,0:T(8,128)(2,1)} %get-tuple-element.124.x_ref, bf16[8,64,2048]{2,1,0:T(8,128)(2,1)} %bitcast.200, f32[16,2048]{1,0:T(8,128)} %get-tuple-element.128.row_ref, f32[192,1]{1,0:T(8,128)} %broadcast_in_dim_reshape.4.skip_ref), custom_call_target="tpu_custom_call" | custom-call | flops 872415232 | bytes 7000000 | tf_op jit(solution)/shard_map/mamba_fwd/pallas_call | solution.py:943
  157.2 6.1 all-to-all-start.4
  163.2 9.2 %attn_fwd.1 = (bf16[16,64,128]{2,1,0:T(8,128)(2,1)}, f32[1024,1]{1,0:T(8,128)}) custom-call(s32[1]{0:T(128)} %bitcast.31.odd_ref, bf16[16,320,128]{2,1,0:T(8,128)(2,1)} %copy-done.11, bf16[16,320,128]{2,1,0:T(8,128)(2,1)} %copy-done.11, bf16[16,320,128]{2,1,0:T(8,128)(2,1)} %copy-done.11), custom_call_target="tpu_custom_call" | custom-call | flops 1073741824 | bytes 3000000 | tf_op jit(solution)/shard_map/attn_fwd/pallas_call | solution.py:1145
  172.4 8.8 %all-to-all-done.4.got_ref = bf16[16,192,128]{2,1,0:T(8,128)(2,1)S(1)} async-done(((bf16[16,192,128]{2,1,0:T(8,128)(2,1)}), bf16[16,192,128]{2,1,0:T(8,128)(2,1)S(1)}, u32[]{:S(2)}, u32[]{:S(2)}) %all-to-all-start.4) | async-done | bytes 786464 | tf_op jit(solution)/shard_map/all_to_all | solution.py:162
  184.8 6.1 all-to-all-start.5
  201.7 7.2 branch_out.1
  208.9 37.6 %reduce-scatter.9.cloned.1.call-done = bf16[128,2048]{1,0:T(8,128)(2,1)} async-done(((bf16[1024,2048]{1,0:T(8,128)(2,1)}), bf16[128,2048]{1,0:T(8,128)(2,1)}) %reduce-scatter.9.cloned.1.call-update) | async-done | bytes 524304 | tf_op jit(solution)/shard_map/reduce_scatter | solution.py:96
  250.0 6.5 act_back.1.d_act_ref
  256.5 24.7 %all-gather.11.cloned.1.call-done.n_ref.left_ref = bf16[1024,2048]{1,0:T(8,128)(2,1)} async-done(((bf16[128,2048]{1,0:T(8,128)(2,1)}), bf16[1024,2048]{1,0:T(8,128)(2,1)}) %all-gather.11.cloned.1.call-update) | async-done | bytes 4194320 | tf_op jit(solution)/shard_map/all_gather | solution.py:92
  281.2 13.9 %mlp.1 = (bf16[1024,512]{1,0:T(8,128)(2,1)}, bf16[1024,1024]{1,0:T(8,128)(2,1)}, bf16[1024,2048]{1,0:T(8,128)(2,1)}) custom-call(bf16[1024,2048]{1,0:T(8,128)(2,1)} %all-gather.11.cloned.1.call-done.n_ref.left_ref, f32[1024,512]{1,0:T(8,128)} %act_back.1.d_act_ref, bf16[16,8,16,1024]{3,2,1,0:T(8,128)(2,1)} %bitcast.206), custom_call_target="tpu_custom_call" | custom-call | flops 8589934592 | bytes 20000000 | tf_op jit(solution)/shard_map/mlp/pallas_call | solution.py:595
  296.5 6.2 column_grad.6
  302.7 7.1 down_out.1
  309.8 8.7 %column_grad.5 = bf16[16,8,8,16,128]{4,3,2,1,0:T(8,128)(2,1)} custom-call(bf16[1024,2048]{1,0:T(8,128)(2,1)} %all-gather.11.cloned.1.call-done.n_ref.left_ref, bf16[1024,1024]{1,0:T(8,128)(2,1)} %get-tuple-element.150.refs_0_), custom_call_target="tpu_custom_call" | custom-call | flops 4294967296 | bytes 10485760 | tf_op jit(solution)/shard_map/column_grad/pallas_call | solution.py:390
  318.5 5.6 pad_maximum_fusion
  324.1 9.3 %reduce-scatter.11.cloned.1.call-done = bf16[128,2048]{1,0:T(8,128)(2,1)} async-done(((bf16[1024,2048]{1,0:T(8,128)(2,1)}), bf16[128,2048]{1,0:T(8,128)(2,1)}) %reduce-scatter.11.cloned.1.call-update) | async-done | bytes 524304 | tf_op jit(solution)/shard_map/reduce_scatter | solution.py:96
  338.2 10.3 %collective-permute-done.19 = bf16[128,2048]{1,0:T(8,128)(2,1)S(1)} collective-permute-done((bf16[128,2048]{1,0:T(8,128)(2,1)S(1)}, bf16[128,2048]{1,0:T(8,128)(2,1)S(1)}, u32[]{:S(2)}, u32[]{:S(2)}) %collective-permute-start.19) | collective-permute-done | bytes 524320 | tf_op jit(solution)/shard_map/ppermute | solution.py:88
  348.5 3.8 collective-permute-start.20
  353.1 5.1 collective-permute-done.20
  358.3 4.0 collective-permute-done.22
  366.4 7.2 %branch_back.1 = (f32[8,384,128]{2,1,0:T(8,128)}, f32[8,128]{1,0:T(8,128)}, bf16[16,64,128]{2,1,0:T(8,128)(2,1)}) custom-call(bf16[1024,2048]{1,0:T(8,128)(2,1)} %copy-done.1, bf16[512,2048]{1,0:T(8,128)(2,1)} %copy-done.7, f32[8,384,128]{2,1,0:T(8,128)} %get-tuple-element.138.g_ref, f32[384,1]{1,0:T(8,128)} %broadcast_in_dim.79.gain_ref), custom_call_target="tpu_custom_call" | custom-call | flops 2147483648 | bytes 10000000 | tf_op jit(solution)/shard_map/branch_back/pallas_call | solution.py:481
  375.8 3.6 collective-permute-done.28
  379.4 5.1 collective-permute-done.29
  385.1 4.9 gate_back.1
  390.0 7.2 all-to-all-start.6
  397.4 6.2 column_grad.7
  403.6 6.1 column_grad.8
  409.7 3.6 pad_maximum_fusion.1
  414.0 14.3 %mamba_bwd.1 = (f32[192,2048]{1,0:T(8,128)}, bf16[4,64,2048]{2,1,0:T(8,128)(2,1)}, bf16[4,64,2048]{2,1,0:T(8,128)(2,1)}, f32[8,2048]{1,0:T(8,128)}, f32[192,1]{1,0:T(8,128)}) custom-call(s32[8]{0:T(128)} %fusion.13.place_ref, bf16[192,2048]{1,0:T(8,128)(2,1)} %get-tuple-element.124.x_ref, bf16[16,256,128]{2,1,0:T(8,128)(2,1)} %all-to-all-done.6.got_ref.do_ref, ...), custom_call_target="tpu_custom_call" | custom-call | flops 2214592512 | bytes 12000000 | tf_op jit(solution)/shard_map/mamba_bwd/pallas_call | solution.py:1074
  447.8 11.7 %attn_bwd.1 = bf16[16,320,128]{2,1,0:T(8,128)(2,1)} custom-call(s32[1]{0:T(128)} %bitcast.31.odd_ref, bf16[16,320,128]{2,1,0:T(8,128)(2,1)} %copy-done.11, bf16[16,320,128]{2,1,0:T(8,128)(2,1)} %copy-done.11, bf16[16,320,128]{2,1,0:T(8,128)(2,1)} %copy-done.11, bf16[16,256,128]{2,1,0:T(8,128)(2,1)} %all-to-all-done.6.got_ref.do_ref, ...), custom_call_target="tpu_custom_call" | custom-call | flops 2684354560 | bytes 4000000 | tf_op jit(solution)/shard_map/attn_bwd/pallas_call | solution.py:1197
  460.2 3.4 all-to-all-start.7
  465.7 5.4 all-to-all-done.7
  471.1 6.5 all-to-all-start.8
  486.2 11.0 %front_back.1 = (bf16[16,272,128]{2,1,0:T(8,128)(2,1)}, f32[256,8]{1,0:T(8,128)}, f32[8,1]{1,0:T(8,128)}) custom-call(bf16[16,272,128]{2,1,0:T(8,128)(2,1)} %copy-done.3, f32[256,8]{1,0:T(8,128)} %bitcast.169, f32[8,128]{1,0:T(8,128)} %broadcast_in_dim.71.heads_ref, f32[16,2048]{1,0:T(8,128)} %get-tuple-element.128.row_ref, ...), custom_call_target="tpu_custom_call" | custom-call | flops 31457280 | bytes 9000000 | tf_op jit(solution)/shard_map/front_back/pallas_call | solution.py:838
  497.2 7.2 %all-to-all-start.9 = ((bf16[16,272,128]{2,1,0:T(8,128)(2,1)}), bf16[16,272,128]{2,1,0:T(8,128)(2,1)}, u32[]{:S(2)}, u32[]{:S(2)}) async-start(bf16[16,272,128]{2,1,0:T(8,128)(2,1)} %get-tuple-element.177), calls=%async_computation.11 | async-start | bytes 2228224 | tf_op jit(solution)/shard_map/all_to_all | solution.py:162
  515.2 4.1 attn_grads.1.refs_1_.dqkv_ref
  522.7 3.6 mix_grads.1.refs_0_.mix_ref
  526.3 8.2 %column_grad.9 = bf16[16,8,7,16,128]{4,3,2,1,0:T(8,128)(2,1)} custom-call(bf16[1024,2048]{1,0:T(8,128)(2,1)} %constant_dynamic-update-slice_fusion.25.n_ref.left_ref, bf16[1024,512]{1,0:T(8,128)(2,1)} %mix_grads.1.refs_0_.mix_ref, bf16[1024,384]{1,0:T(8,128)(2,1)} %attn_grads.1.refs_1_.dqkv_ref), custom_call_target="tpu_custom_call" | custom-call | flops 3758096384 | bytes 9699328 | tf_op jit(solution)/shard_map/column_grad/pallas_call | solution.py:390
  534.5 9.4 %all-to-all-start.10 = ((bf16[16,896,128]{2,1,0:T(8,128)(2,1)}), bf16[16,896,128]{2,1,0:T(8,128)(2,1)}, u32[]{:S(2)}, u32[]{:S(2)}) async-start(bf16[16,896,128]{2,1,0:T(8,128)(2,1)} %bitcast.159), calls=%async_computation.12 | async-start | bytes 7340032 | tf_op jit(solution)/shard_map/all_to_all | solution.py:162
  544.0 11.8 %back_project.1 = (bf16[4,128,2048]{2,1,0:T(8,128)(2,1)}, bf16[4,128,2048]{2,1,0:T(8,128)(2,1)}, f32[1,2048]{1,0:T(1,128)}) custom-call(s32[5]{0:T(128)} %pad_add_fusion.1.spot_ref, bf16[1024,512]{1,0:T(8,128)(2,1)} %mix_grads.1.refs_0_.mix_ref, bf16[1024,384]{1,0:T(8,128)(2,1)} %attn_grads.1.refs_1_.dqkv_ref, ...), custom_call_target="tpu_custom_call" | custom-call | flops 5368709120 | bytes 18000000 | tf_op jit(solution)/shard_map/back_project/pallas_call | solution.py:352
  556.6 3.7 collective-permute-done.44
  560.3 4.4 fusion
  564.8 32.4 %all-to-all-done.10 = bf16[16,896,128]{2,1,0:T(8,128)(2,1)} async-done(((bf16[16,896,128]{2,1,0:T(8,128)(2,1)}), bf16[16,896,128]{2,1,0:T(8,128)(2,1)}, u32[]{:S(2)}, u32[]{:S(2)}) %all-to-all-start.10) | async-done | bytes 3670048 | tf_op jit(solution)/shard_map/all_to_all | solution.py:162
  600.5 6.5 all-to-all-start.11
  607.6 7.7 %all-to-all-done.11 = bf16[8,160,128]{2,1,0:T(8,128)(2,1)S(1)} async-done(((bf16[8,160,128]{2,1,0:T(8,128)(2,1)}), bf16[8,160,128]{2,1,0:T(8,128)(2,1)S(1)}, u32[]{:S(2)}, u32[]{:S(2)}) %all-to-all-start.11) | async-done | bytes 327712 | tf_op jit(solution)/shard_map/all_to_all | solution.py:166
  615.3 16.1 %all-gather.13.cloned.1.call-done.refs_0_.refs_1_.refs_2_.refs_3_ = bf16[16,128,16,128]{3,2,1,0:T(8,128)(2,1)} async-done(((bf16[1,128,16,128]{3,2,1,0:T(8,128)(2,1)}), bf16[16,128,16,128]{3,2,1,0:T(8,128)(2,1)}) %all-gather.13.cloned.1.call-update) | async-done | bytes 8388624 | tf_op jit(solution)/shard_map/all_gather | solution.py:1515
  643.3 4.4 collective-permute-start.46
  657.2 7.1 collective-permute-start.52
  669.4 3.6 unpack_rows.4
  673.1 4.2 unpack_rows.3
  677.3 6.0 unpack_gate_up.1
  692.6 3.9 collective-permute-done.57
  701.4 8.7 %unpack_in.1 = f32[6704,256]{1,0:T(8,128)} custom-call(bf16[16,80,16,128]{3,2,1,0:T(8,128)(2,1)} %all-gather.15.cloned.1.call-done.refs_0_.refs_1_.refs_2_.refs_3_.refs_4_.refs_5_.refs_6_.refs_7_.refs_8_.refs_9_.refs_10_.refs_11_.refs_12_.refs_13_.refs_14_.refs_15_.refs_16_.refs_17_.refs_18_.refs_19_.refs_20_.refs_21_.refs_22_.refs_23_, ...), custom_call_target="tpu_custom_call" | custom-call | flops 1716224 | bytes 10297344 | tf_op jit(solution)/shard_map/unpack_in/pallas_call | solution.py:1318
  (393 shorter events, 178.3 us)
Async XLA Ops:
  14.3 13.7 %all-to-all-start = ((bf16[8,16,1280]{2,1,0:T(8,128)(2,1)}), bf16[8,16,1280]{2,1,0:T(8,128)(2,1)S(1)}, u32[]{:S(2)}, u32[]{:S(2)}) async-start(bf16[8,16,1280]{2,1,0:T(8,128)(2,1)} %copy.115), calls=%async_computation | async-start | bytes 655360 | tf_op jit(solution)/shard_map/all_to_all | solution.py:166
  19.7 64.7 %all-gather.17.cloned.1.call-start = ((), (), s32[]{:S(2)}) async-start(), calls=%async_computation.22 | async-start | bytes 5570560 | tf_op jit(solution)/shard_map/all_gather | solution.py:1437
  33.9 13.2 %collective-permute-start = (bf16[128,2048]{1,0:T(8,128)(2,1)S(1)}, bf16[128,2048]{1,0:T(8,128)(2,1)S(1)}, u32[]{:S(2)}, u32[]{:S(2)}) collective-permute-start(bf16[128,2048]{1,0:T(8,128)(2,1)S(1)} %get-tuple-element.264), channel_id=1, source_target_pairs={{0,6},{1,7},{2,0},{3,1},{4,2},{5,3},{6,4},{7,5},{8,14},{9,15},{10,... | collective-permute-start | bytes 1572872 | tf_op jit(solution)/shard_map/ppermute | solution.py:88
  35.1 25.0 %collective-permute-start.2 = (bf16[128,2048]{1,0:T(8,128)(2,1)S(1)}, bf16[128,2048]{1,0:T(8,128)(2,1)S(1)}, u32[]{:S(2)}, u32[]{:S(2)}) collective-permute-start(bf16[128,2048]{1,0:T(8,128)(2,1)S(1)} %get-tuple-element.264), channel_id=1, source_target_pairs={{0,2},{1,3},{2,4},{3,5},{4,6},{5,7},{6,0},{7,1},{8,10},{9,11},{10,... | collective-permute-start | bytes 1572872 | tf_op jit(solution)/shard_map/ppermute | solution.py:88
  36.0 38.7 %collective-permute-start.4 = (bf16[128,2048]{1,0:T(8,128)(2,1)S(1)}, bf16[128,2048]{1,0:T(8,128)(2,1)S(1)}, u32[]{:S(2)}, u32[]{:S(2)}) collective-permute-start(bf16[128,2048]{1,0:T(8,128)(2,1)S(1)} %get-tuple-element.264), channel_id=1, source_target_pairs={{0,1},{1,0},{2,3},{3,2},{4,5},{5,4},{6,7},{7,6},{8,9},{9,8},{10,11... | collective-permute-start | bytes 1572872 | tf_op jit(solution)/shard_map/ppermute | solution.py:88
  47.9 15.6 %collective-permute-start.1 = (bf16[64,2048]{1,0:T(8,128)(2,1)}, bf16[64,2048]{1,0:T(8,128)(2,1)}, u32[]{:S(2)}, u32[]{:S(2)}) collective-permute-start(bf16[64,2048]{1,0:T(8,128)(2,1)} %slice.321), channel_id=1, source_target_pairs={{0,6},{1,7},{2,0},{3,1},{4,2},{5,3},{6,4},{7,5},{8,14},{9,15},{10,... | collective-permute-start | bytes 786440 | tf_op jit(solution)/shard_map/ppermute | solution.py:88
  56.6 21.3 %all-to-all-start.1 = ((bf16[8,16,1024]{2,1,0:T(8,128)(2,1)}), bf16[8,16,1024]{2,1,0:T(8,128)(2,1)S(1)}, u32[]{:S(2)}, u32[]{:S(2)}) async-start(bf16[8,16,1024]{2,1,0:T(8,128)(2,1)} %copy.116), calls=%async_computation.1 | async-start | bytes 524288 | tf_op jit(solution)/shard_map/all_to_all | solution.py:166
  60.0 97.1 %all-gather.9.cloned.1.call-start = ((), (), s32[]{:S(2)}) async-start(), calls=%async_computation.16 | async-start | bytes 4718592 | tf_op jit(solution)/shard_map/all_gather | solution.py:92
  60.1 12.7 %collective-permute-start.3 = (bf16[64,2048]{1,0:T(8,128)(2,1)S(1)}, bf16[64,2048]{1,0:T(8,128)(2,1)S(1)}, u32[]{:S(2)}, u32[]{:S(2)}) collective-permute-start(bf16[64,2048]{1,0:T(8,128)(2,1)S(1)} %slice.322), channel_id=1, source_target_pairs={{0,2},{1,3},{2,4},{3,5},{4,6},{5,7},{6,0},{7,1},{8,10},{9,11},{10,... | collective-permute-start | bytes 786440 | tf_op jit(solution)/shard_map/ppermute | solution.py:88
  62.1 13.4 %collective-permute-start.5 = (bf16[128,2048]{1,0:T(8,128)(2,1)S(1)}, bf16[128,2048]{1,0:T(8,128)(2,1)S(1)}, u32[]{:S(2)}, u32[]{:S(2)}) collective-permute-start(bf16[128,2048]{1,0:T(8,128)(2,1)S(1)} %collective-permute-done), channel_id=1, source_target_pairs={{0,1},{1,0},{2,3},{3,2},{4,5},{5,4},{6,7},{7,6},{8,9},{9,8},{10,11... | collective-permute-start | bytes 1572872 | tf_op jit(solution)/shard_map/ppermute | solution.py:88
  62.1 15.0 %collective-permute-start.7 = (bf16[128,2048]{1,0:T(8,128)(2,1)S(1)}, bf16[128,2048]{1,0:T(8,128)(2,1)S(1)}, u32[]{:S(2)}, u32[]{:S(2)}) collective-permute-start(bf16[128,2048]{1,0:T(8,128)(2,1)S(1)} %collective-permute-done.2), channel_id=1, source_target_pairs={{0,1},{1,0},{2,3},{3,2},{4,5},{5,4},{6,7},{7,6},{8,9},{9,8},{10,11... | collective-permute-start | bytes 1572872 | tf_op jit(solution)/shard_map/ppermute | solution.py:88
  94.1 21.5 %all-to-all-start.2 = ((bf16[16,272,128]{2,1,0:T(8,128)(2,1)}), bf16[16,272,128]{2,1,0:T(8,128)(2,1)S(1)}, u32[]{:S(2)}, u32[]{:S(2)}) async-start(bf16[16,272,128]{2,1,0:T(8,128)(2,1)} %get-tuple-element.120), calls=%async_computation.2 | async-start | bytes 2228224 | tf_op jit(solution)/shard_map/all_to_all | solution.py:162
  99.8 101.1 %all-gather.19.cloned.1.call-start = ((), (), s32[]{:S(2)}) async-start(), calls=%async_computation.23 | async-start | bytes 4456448 | tf_op jit(solution)/shard_map/all_gather | solution.py:1481
  123.1 12.0 %collective-permute-start.10 = (bf16[64,2048]{1,0:T(8,128)(2,1)}, bf16[64,2048]{1,0:T(8,128)(2,1)S(1)}, u32[]{:S(2)}, u32[]{:S(2)}) collective-permute-start(bf16[64,2048]{1,0:T(8,128)(2,1)} %get-tuple-element.127), channel_id=1, source_target_pairs={{0,2},{1,3},{2,4},{3,5},{4,6},{5,7},{6,0},{7,1},{8,10},{9,11},{10,... | collective-permute-start | bytes 786440 | tf_op jit(solution)/shard_map/ppermute | solution.py:88
  124.7 11.1 %collective-permute-start.8 = (bf16[64,2048]{1,0:T(8,128)(2,1)}, bf16[64,2048]{1,0:T(8,128)(2,1)S(1)}, u32[]{:S(2)}, u32[]{:S(2)}) collective-permute-start(bf16[64,2048]{1,0:T(8,128)(2,1)} %get-tuple-element.127), channel_id=1, source_target_pairs={{0,6},{1,7},{2,0},{3,1},{4,2},{5,3},{6,4},{7,5},{8,14},{9,15},{10,... | collective-permute-start | bytes 786440 | tf_op jit(solution)/shard_map/ppermute | solution.py:88
  127.9 14.6 %collective-permute-start.12 = (bf16[64,2048]{1,0:T(8,128)(2,1)}, bf16[64,2048]{1,0:T(8,128)(2,1)S(1)}, u32[]{:S(2)}, u32[]{:S(2)}) collective-permute-start(bf16[64,2048]{1,0:T(8,128)(2,1)} %get-tuple-element.127), channel_id=1, source_target_pairs={{0,1},{1,0},{2,3},{3,2},{4,5},{5,4},{6,7},{7,6},{8,9},{9,8},{10,11... | collective-permute-start | bytes 786440 | tf_op jit(solution)/shard_map/ppermute | solution.py:88
  127.9 29.2 %all-to-all-start.3 = ((bf16[16,320,128]{2,1,0:T(8,128)(2,1)}), bf16[16,320,128]{2,1,0:T(8,128)(2,1)S(1)}, u32[]{:S(2)}, u32[]{:S(2)}) async-start(bf16[16,320,128]{2,1,0:T(8,128)(2,1)} %get-tuple-element.130), calls=%async_computation.3 | async-start | bytes 2621440 | tf_op jit(solution)/shard_map/all_to_all | solution.py:162
  135.1 7.1 collective-permute-start.11
  135.8 6.5 collective-permute-start.9
  157.2 24.0 %all-to-all-start.4 = ((bf16[16,192,128]{2,1,0:T(8,128)(2,1)}), bf16[16,192,128]{2,1,0:T(8,128)(2,1)S(1)}, u32[]{:S(2)}, u32[]{:S(2)}) async-start(bf16[16,192,128]{2,1,0:T(8,128)(2,1)} %get-tuple-element.132), calls=%async_computation.4 | async-start | bytes 1572864 | tf_op jit(solution)/shard_map/all_to_all | solution.py:162
  184.8 16.2 %all-to-all-start.5 = ((bf16[16,64,128]{2,1,0:T(8,128)(2,1)}), bf16[16,64,128]{2,1,0:T(8,128)(2,1)S(1)}, u32[]{:S(2)}, u32[]{:S(2)}) async-start(bf16[16,64,128]{2,1,0:T(8,128)(2,1)} %get-tuple-element.135), calls=%async_computation.5 | async-start | bytes 524288 | tf_op jit(solution)/shard_map/all_to_all | solution.py:162
  190.9 55.6 %reduce-scatter.9.cloned.1.call-start = ((), (), s32[]{:S(2)}) async-start(), calls=%async_computation.17 | async-start | bytes 4718592 | tf_op jit(solution)/shard_map/reduce_scatter | solution.py:96
  208.9 72.3 %all-gather.11.cloned.1.call-start = ((), (), s32[]{:S(2)}) async-start(), calls=%async_computation.18 | async-start | bytes 4718592 | tf_op jit(solution)/shard_map/all_gather | solution.py:92
  250.0 83.4 %reduce-scatter.11.cloned.1.call-start = ((), (), s32[]{:S(2)}) async-start(), calls=%async_computation.19 | async-start | bytes 4718592 | tf_op jit(solution)/shard_map/reduce_scatter | solution.py:96
  295.2 139.1 %reduce-scatter.13.cloned.1.call-start = ((), (), s32[]{:S(2)}) async-start(), calls=%async_computation.24 | async-start | bytes 6684672
  336.1 12.4 %collective-permute-start.19 = (bf16[128,2048]{1,0:T(8,128)(2,1)S(1)}, bf16[128,2048]{1,0:T(8,128)(2,1)S(1)}, u32[]{:S(2)}, u32[]{:S(2)}) collective-permute-start(bf16[128,2048]{1,0:T(8,128)(2,1)S(1)} %get-tuple-element.266), channel_id=1, source_target_pairs={{0,6},{1,7},{2,0},{3,1},{4,2},{5,3},{6,4},{7,5},{8,14},{9,15},{10,... | collective-permute-start | bytes 1572872 | tf_op jit(solution)/shard_map/ppermute | solution.py:88
  336.2 16.1 %collective-permute-start.21 = (bf16[128,2048]{1,0:T(8,128)(2,1)S(1)}, bf16[128,2048]{1,0:T(8,128)(2,1)S(1)}, u32[]{:S(2)}, u32[]{:S(2)}) collective-permute-start(bf16[128,2048]{1,0:T(8,128)(2,1)S(1)} %get-tuple-element.266), channel_id=1, source_target_pairs={{0,2},{1,3},{2,4},{3,5},{4,6},{5,7},{6,0},{7,1},{8,10},{9,11},{10,... | collective-permute-start | bytes 1572872 | tf_op jit(solution)/shard_map/ppermute | solution.py:88
  348.5 9.7 %collective-permute-start.20 = (bf16[64,2048]{1,0:T(8,128)(2,1)S(1)}, bf16[64,2048]{1,0:T(8,128)(2,1)S(1)}, u32[]{:S(2)}, u32[]{:S(2)}) collective-permute-start(bf16[64,2048]{1,0:T(8,128)(2,1)S(1)} %slice.325), channel_id=1, source_target_pairs={{0,6},{1,7},{2,0},{3,1},{4,2},{5,3},{6,4},{7,5},{8,14},{9,15},{10,... | collective-permute-start | bytes 786440 | tf_op jit(solution)/shard_map/ppermute | solution.py:88
  352.3 10.3 %collective-permute-start.23 = (bf16[128,2048]{1,0:T(8,128)(2,1)S(1)}, bf16[128,2048]{1,0:T(8,128)(2,1)S(1)}, u32[]{:S(2)}, u32[]{:S(2)}) collective-permute-start(bf16[128,2048]{1,0:T(8,128)(2,1)S(1)} %get-tuple-element.266), channel_id=1, source_target_pairs={{0,1},{1,0},{2,3},{3,2},{4,5},{5,4},{6,7},{7,6},{8,9},{9,8},{10,11... | collective-permute-start | bytes 1572872 | tf_op jit(solution)/shard_map/ppermute | solution.py:88
  352.3 10.0 %collective-permute-start.22 = (bf16[64,2048]{1,0:T(8,128)(2,1)S(1)}, bf16[64,2048]{1,0:T(8,128)(2,1)S(1)}, u32[]{:S(2)}, u32[]{:S(2)}) collective-permute-start(bf16[64,2048]{1,0:T(8,128)(2,1)S(1)} %slice.326), channel_id=1, source_target_pairs={{0,2},{1,3},{2,4},{3,5},{4,6},{5,7},{6,0},{7,1},{8,10},{9,11},{10,... | collective-permute-start | bytes 786440 | tf_op jit(solution)/shard_map/ppermute | solution.py:88
  352.4 10.2 %collective-permute-start.24 = (bf16[128,2048]{1,0:T(8,128)(2,1)S(1)}, bf16[128,2048]{1,0:T(8,128)(2,1)S(1)}, u32[]{:S(2)}, u32[]{:S(2)}) collective-permute-start(bf16[128,2048]{1,0:T(8,128)(2,1)S(1)} %collective-permute-done.19), channel_id=1, source_target_pairs={{0,1},{1,0},{2,3},{3,2},{4,5},{5,4},{6,7},{7,6},{8,9},{9,8},{10,11... | collective-permute-start | bytes 1572872 | tf_op jit(solution)/shard_map/ppermute | solution.py:88
  353.0 11.4 %collective-permute-start.26 = (bf16[128,2048]{1,0:T(8,128)(2,1)S(1)}, bf16[128,2048]{1,0:T(8,128)(2,1)S(1)}, u32[]{:S(2)}, u32[]{:S(2)}) collective-permute-start(bf16[128,2048]{1,0:T(8,128)(2,1)S(1)} %collective-permute-done.21), channel_id=1, source_target_pairs={{0,1},{1,0},{2,3},{3,2},{4,5},{5,4},{6,7},{7,6},{8,9},{9,8},{10,11... | collective-permute-start | bytes 1572872 | tf_op jit(solution)/shard_map/ppermute | solution.py:88
  390.0 24.0 %all-to-all-start.6 = ((bf16[16,256,128]{2,1,0:T(8,128)(2,1)}), bf16[16,256,128]{2,1,0:T(8,128)(2,1)}, u32[]{:S(2)}, u32[]{:S(2)}) async-start(bf16[16,256,128]{2,1,0:T(8,128)(2,1)} %get-tuple-element.158), calls=%async_computation.8 | async-start | bytes 2097152 | tf_op jit(solution)/shard_map/all_to_all | solution.py:162
  397.2 118.0 %reduce-scatter.15.cloned.1.call-start = ((), (), s32[]{:S(2)}) async-start(), calls=%async_computation.25 | async-start | bytes 3899392
  436.1 6.7 collective-permute-start.31
  436.1 6.7 collective-permute-start.35
  439.3 24.3 %collective-permute-start.33 = (bf16[32,2048]{1,0:T(8,128)(2,1)}, bf16[32,2048]{1,0:T(8,128)(2,1)S(1)}, u32[]{:S(2)}, u32[]{:S(2)}) collective-permute-start(bf16[32,2048]{1,0:T(8,128)(2,1)} %get-tuple-element.243), channel_id=1, source_target_pairs={{0,2},{1,3},{2,4},{3,5},{4,6},{5,7},{6,0},{7,1},{8,10},{9,11},{10,... | collective-permute-start | bytes 393224 | tf_op jit(solution)/shard_map/ppermute | solution.py:88
  439.3 24.3 %collective-permute-start.34 = (bf16[32,2048]{1,0:T(8,128)(2,1)}, bf16[32,2048]{1,0:T(8,128)(2,1)}, u32[]{:S(2)}, u32[]{:S(2)}) collective-permute-start(bf16[32,2048]{1,0:T(8,128)(2,1)} %get-tuple-element.241), channel_id=1, source_target_pairs={{0,6},{1,7},{2,0},{3,1},{4,2},{5,3},{6,4},{7,5},{8,14},{9,15},{10,... | collective-permute-start | bytes 393224 | tf_op jit(solution)/shard_map/ppermute | solution.py:88
  444.6 19.1 %collective-permute-start.32 = (bf16[32,2048]{1,0:T(8,128)(2,1)}, bf16[32,2048]{1,0:T(8,128)(2,1)}, u32[]{:S(2)}, u32[]{:S(2)}) collective-permute-start(bf16[32,2048]{1,0:T(8,128)(2,1)} %get-tuple-element.246), channel_id=1, source_target_pairs={{0,2},{1,3},{2,4},{3,5},{4,6},{5,7},{6,0},{7,1},{8,10},{9,11},{10,... | collective-permute-start | bytes 393224 | tf_op jit(solution)/shard_map/ppermute | solution.py:88
  444.6 19.1 %collective-permute-start.36 = (bf16[32,2048]{1,0:T(8,128)(2,1)}, bf16[32,2048]{1,0:T(8,128)(2,1)}, u32[]{:S(2)}, u32[]{:S(2)}) collective-permute-start(bf16[32,2048]{1,0:T(8,128)(2,1)} %get-tuple-element.245), channel_id=1, source_target_pairs={{0,6},{1,7},{2,0},{3,1},{4,2},{5,3},{6,4},{7,5},{8,14},{9,15},{10,... | collective-permute-start | bytes 393224 | tf_op jit(solution)/shard_map/ppermute | solution.py:88
  460.2 10.9 %all-to-all-start.7 = ((bf16[8,128,128]{2,1,0:T(8,128)(2,1)}), bf16[8,128,128]{2,1,0:T(8,128)(2,1)S(1)}, u32[]{:S(2)}, u32[]{:S(2)}) async-start(bf16[8,128,128]{2,1,0:T(8,128)(2,1)} %bitcast.42), calls=%async_computation.9 | async-start | bytes 524288 | tf_op jit(solution)/shard_map/all_to_all | solution.py:166
  471.1 6.5 collective-permute-start.37
  471.1 26.1 %all-to-all-start.8 = ((bf16[16,320,128]{2,1,0:T(8,128)(2,1)}), bf16[16,320,128]{2,1,0:T(8,128)(2,1)}, u32[]{:S(2)}, u32[]{:S(2)}) async-start(bf16[16,320,128]{2,1,0:T(8,128)(2,1)} %attn_bwd.1), calls=%async_computation.10 | async-start | bytes 2621440 | tf_op jit(solution)/shard_map/all_to_all | solution.py:162
  483.0 25.1 %collective-permute-start.38 = (bf16[64,2048]{1,0:T(8,128)(2,1)}, bf16[64,2048]{1,0:T(8,128)(2,1)}, u32[]{:S(2)}, u32[]{:S(2)}) collective-permute-start(bf16[64,2048]{1,0:T(8,128)(2,1)} %get-tuple-element.236), channel_id=1, source_target_pairs={{0,2},{1,3},{2,4},{3,5},{4,6},{5,7},{6,0},{7,1},{8,10},{9,11},{10,... | collective-permute-start | bytes 786440 | tf_op jit(solution)/shard_map/ppermute | solution.py:88
  483.6 24.4 %collective-permute-start.42 = (bf16[64,2048]{1,0:T(8,128)(2,1)}, bf16[64,2048]{1,0:T(8,128)(2,1)}, u32[]{:S(2)}, u32[]{:S(2)}) collective-permute-start(bf16[64,2048]{1,0:T(8,128)(2,1)} %get-tuple-element.234), channel_id=1, source_target_pairs={{0,6},{1,7},{2,0},{3,1},{4,2},{5,3},{6,4},{7,5},{8,14},{9,15},{10,... | collective-permute-start | bytes 786440 | tf_op jit(solution)/shard_map/ppermute | solution.py:88
  497.2 24.7 %all-to-all-start.9 = ((bf16[16,272,128]{2,1,0:T(8,128)(2,1)}), bf16[16,272,128]{2,1,0:T(8,128)(2,1)}, u32[]{:S(2)}, u32[]{:S(2)}) async-start(bf16[16,272,128]{2,1,0:T(8,128)(2,1)} %get-tuple-element.177), calls=%async_computation.11 | async-start | bytes 2228224 | tf_op jit(solution)/shard_map/all_to_all | solution.py:162
  504.5 126.9 %all-gather.13.cloned.1.call-start = ((), (), s32[]{:S(2)}) async-start(), calls=%async_computation.20 | async-start | bytes 8912896 | tf_op jit(solution)/shard_map/all_gather | solution.py:1515
  504.5 14.8 %collective-permute-start.40 = (bf16[64,2048]{1,0:T(8,128)(2,1)}, bf16[64,2048]{1,0:T(8,128)(2,1)}, u32[]{:S(2)}, u32[]{:S(2)}) collective-permute-start(bf16[64,2048]{1,0:T(8,128)(2,1)} %get-tuple-element.235), channel_id=1, source_target_pairs={{0,2},{1,3},{2,4},{3,5},{4,6},{5,7},{6,0},{7,1},{8,10},{9,11},{10,... | collective-permute-start | bytes 786440 | tf_op jit(solution)/shard_map/ppermute | solution.py:88
  504.9 14.4 %collective-permute-start.41 = (bf16[64,2048]{1,0:T(8,128)(2,1)}, bf16[64,2048]{1,0:T(8,128)(2,1)}, u32[]{:S(2)}, u32[]{:S(2)}) collective-permute-start(bf16[64,2048]{1,0:T(8,128)(2,1)} %get-tuple-element.233), channel_id=1, source_target_pairs={{0,6},{1,7},{2,0},{3,1},{4,2},{5,3},{6,4},{7,5},{8,14},{9,15},{10,... | collective-permute-start | bytes 786440 | tf_op jit(solution)/shard_map/ppermute | solution.py:88
  510.1 9.2 %collective-permute-start.39 = (bf16[64,2048]{1,0:T(8,128)(2,1)}, bf16[64,2048]{1,0:T(8,128)(2,1)}, u32[]{:S(2)}, u32[]{:S(2)}) collective-permute-start(bf16[64,2048]{1,0:T(8,128)(2,1)} %get-tuple-element.238), channel_id=1, source_target_pairs={{0,2},{1,3},{2,4},{3,5},{4,6},{5,7},{6,0},{7,1},{8,10},{9,11},{10,... | collective-permute-start | bytes 786440 | tf_op jit(solution)/shard_map/ppermute | solution.py:88
  510.1 9.2 %collective-permute-start.43 = (bf16[64,2048]{1,0:T(8,128)(2,1)}, bf16[64,2048]{1,0:T(8,128)(2,1)}, u32[]{:S(2)}, u32[]{:S(2)}) collective-permute-start(bf16[64,2048]{1,0:T(8,128)(2,1)} %get-tuple-element.237), channel_id=1, source_target_pairs={{0,6},{1,7},{2,0},{3,1},{4,2},{5,3},{6,4},{7,5},{8,14},{9,15},{10,... | collective-permute-start | bytes 786440 | tf_op jit(solution)/shard_map/ppermute | solution.py:88
  534.5 62.6 %all-to-all-start.10 = ((bf16[16,896,128]{2,1,0:T(8,128)(2,1)}), bf16[16,896,128]{2,1,0:T(8,128)(2,1)}, u32[]{:S(2)}, u32[]{:S(2)}) async-start(bf16[16,896,128]{2,1,0:T(8,128)(2,1)} %bitcast.159), calls=%async_computation.12 | async-start | bytes 7340032 | tf_op jit(solution)/shard_map/all_to_all | solution.py:162
  600.5 14.7 %all-to-all-start.11 = ((bf16[8,160,128]{2,1,0:T(8,128)(2,1)}), bf16[8,160,128]{2,1,0:T(8,128)(2,1)S(1)}, u32[]{:S(2)}, u32[]{:S(2)}) async-start(bf16[8,160,128]{2,1,0:T(8,128)(2,1)} %pad_maximum_fusion.3), calls=%async_computation.13 | async-start | bytes 655360 | tf_op jit(solution)/shard_map/all_to_all | solution.py:166
  607.0 94.3 %all-gather.15.cloned.1.call-start = ((), (), s32[]{:S(2)}) async-start(), calls=%async_computation.21 | async-start | bytes 5570560 | tf_op jit(solution)/shard_map/all_gather | solution.py:1515
  632.9 21.4 %collective-permute-start.48 = (bf16[64,2048]{1,0:T(8,128)(2,1)S(1)}, bf16[64,2048]{1,0:T(8,128)(2,1)S(1)}, u32[]{:S(2)}, u32[]{:S(2)}) collective-permute-start(bf16[64,2048]{1,0:T(8,128)(2,1)S(1)} %get-tuple-element.230), channel_id=1, source_target_pairs={{0,2},{1,3},{2,4},{3,5},{4,6},{5,7},{6,0},{7,1},{8,10},{9,11},{10,... | collective-permute-start | bytes 786440 | tf_op jit(solution)/shard_map/ppermute | solution.py:88
  634.9 19.4 %collective-permute-start.49 = (bf16[64,2048]{1,0:T(8,128)(2,1)S(1)}, bf16[64,2048]{1,0:T(8,128)(2,1)S(1)}, u32[]{:S(2)}, u32[]{:S(2)}) collective-permute-start(bf16[64,2048]{1,0:T(8,128)(2,1)S(1)} %get-tuple-element.229), channel_id=1, source_target_pairs={{0,6},{1,7},{2,0},{3,1},{4,2},{5,3},{6,4},{7,5},{8,14},{9,15},{10,... | collective-permute-start | bytes 786440 | tf_op jit(solution)/shard_map/ppermute | solution.py:88
  636.2 18.1 %collective-permute-start.50 = (bf16[64,2048]{1,0:T(8,128)(2,1)S(1)}, bf16[64,2048]{1,0:T(8,128)(2,1)S(1)}, u32[]{:S(2)}, u32[]{:S(2)}) collective-permute-start(bf16[64,2048]{1,0:T(8,128)(2,1)S(1)} %get-tuple-element.228), channel_id=1, source_target_pairs={{0,2},{1,3},{2,4},{3,5},{4,6},{5,7},{6,0},{7,1},{8,10},{9,11},{10,... | collective-permute-start | bytes 786440 | tf_op jit(solution)/shard_map/ppermute | solution.py:88
  637.0 17.3 %collective-permute-start.51 = (bf16[64,2048]{1,0:T(8,128)(2,1)S(1)}, bf16[64,2048]{1,0:T(8,128)(2,1)S(1)}, u32[]{:S(2)}, u32[]{:S(2)}) collective-permute-start(bf16[64,2048]{1,0:T(8,128)(2,1)S(1)} %get-tuple-element.227), channel_id=1, source_target_pairs={{0,6},{1,7},{2,0},{3,1},{4,2},{5,3},{6,4},{7,5},{8,14},{9,15},{10,... | collective-permute-start | bytes 786440 | tf_op jit(solution)/shard_map/ppermute | solution.py:88
  643.3 6.2 collective-permute-start.46
  655.1 28.2 %collective-permute-start.55 = (bf16[64,2048]{1,0:T(8,128)(2,1)}, bf16[64,2048]{1,0:T(8,128)(2,1)}, u32[]{:S(2)}, u32[]{:S(2)}) collective-permute-start(bf16[64,2048]{1,0:T(8,128)(2,1)} %add_convert_fusion.1), channel_id=1, source_target_pairs={{0,6},{1,7},{2,0},{3,1},{4,2},{5,3},{6,4},{7,5},{8,14},{9,15},{10,... | collective-permute-start | bytes 786440 | tf_op jit(solution)/shard_map/ppermute | solution.py:88
  657.2 9.9 %collective-permute-start.52 = (f32[53,128]{1,0:T(8,128)S(1)}, f32[53,128]{1,0:T(8,128)S(1)}, u32[]{:S(2)}, u32[]{:S(2)}) collective-permute-start(f32[53,128]{1,0:T(8,128)S(1)} %add.336), channel_id=1, source_target_pairs={{0,64},{8,72},{16,80},{24,88},{32,96},{40,104},{48,112},{56,120},{... | collective-permute-start | bytes 81416 | tf_op jit(solution)/shard_map/ppermute | solution.py:171
  665.1 18.2 %collective-permute-start.54 = (bf16[64,2048]{1,0:T(8,128)(2,1)}, bf16[64,2048]{1,0:T(8,128)(2,1)}, u32[]{:S(2)}, u32[]{:S(2)}) collective-permute-start(bf16[64,2048]{1,0:T(8,128)(2,1)} %add_convert_fusion.2), channel_id=1, source_target_pairs={{0,2},{1,3},{2,4},{3,5},{4,6},{5,7},{6,0},{7,1},{8,10},{9,11},{10,... | collective-permute-start | bytes 786440 | tf_op jit(solution)/shard_map/ppermute | solution.py:88
  667.3 16.0 %collective-permute-start.53 = (f32[200,128]{1,0:T(8,128)S(1)}, f32[200,128]{1,0:T(8,128)S(1)}, u32[]{:S(2)}, u32[]{:S(2)}) collective-permute-start(f32[200,128]{1,0:T(8,128)S(1)} %maximum_bitcast_fusion), channel_id=1, source_target_pairs={{0,1},{1,0},{2,3},{3,2},{4,5},{5,4},{6,7},{7,6},{8,9},{9,8},{10,11... | collective-permute-start | bytes 307208 | tf_op jit(solution)/shard_map/ppermute | solution.py:171
  690.3 6.2 collective-permute-start.57
  (50 other events, 437.1 us)
Sparse Core Ops, SparseCore 0:
  28.8 55.5 all-gather.16
  94.1 32.0 all-gather.8
  129.0 62.9 all-gather.18
  209.0 37.4 reduce-scatter.8
  250.1 31.0 all-gather.10
  295.3 38.0 reduce-scatter.10
  337.4 82.8 reduce-scatter.12
  428.5 86.6 reduce-scatter.14
  522.8 108.4 all-gather.12
  633.9 64.9 all-gather.14

commit v3 on v2

--- a/solution.py
+++ b/solution.py
@@ -1,3 +1,5 @@
+import functools
+
 import jax
 import jax.numpy as jnp
 from jax import lax
@@ -21,6 +23,7 @@
 NC = 16
 NF = 8
 NZ = 4
+NY = 4
 LANES = 128
 ROWS = 2 * HALF
 GROUP = SEQS * ROWS
@@ -48,6 +51,7 @@
 B_AT, T_AT, PACK = XW, XB, XB + 16
 BOTH = XW + HALF
 GATE_SEQS = 4
+IN_SEQS = 4
 PART = 16
 EPS = 1e-06
 ROPE_BASE = 100000000000.0
@@ -370,25 +374,32 @@
     )(spot, mix, dqkv, dz, normed, w_one)
 
 
-def column_grad_kernel(left_ref, *refs):
+def column_grad_kernel(by_y, left_ref, *refs):
     out_ref = refs[-1]
     first = 0
     for right_ref in refs[:-1]:
         term = dot(left_ref[...], right_ref[...], 0, 0).astype(BF)
         for block in range(out_ref.shape[1]):
             for tile in range(right_ref.shape[1] // LANES):
-                out_ref[:, block, first + tile] = term[
+                part = term[
                     block * SHARD : (block + 1) * SHARD, tile * LANES : (tile + 1) * LANES
-                ].reshape(NC, SLICE, LANES)
+                ]
+                if by_y:
+                    part = part.reshape(NC // NY, NY, SLICE, LANES)
+                    for y in range(NY):
+                        rows = slice(y * NC // NY, (y + 1) * NC // NY)
+                        out_ref[rows, block, first + tile] = part[:, y]
+                else:
+                    out_ref[:, block, first + tile] = part.reshape(NC, SLICE, LANES)
         first += right_ref.shape[1] // LANES
 
 
-def column_grad(left, *rights):
+def column_grad(left, *rights, by_y=False):
     count, width = left.shape[1] // SHARD, sum(right.shape[1] for right in rights)
     tiles = width // LANES
     many = 2
     return pl.pallas_call(
-        column_grad_kernel,
+        functools.partial(column_grad_kernel, by_y),
         grid=(count // many,),
         in_specs=[pl.BlockSpec((GROUP, many * SHARD), lambda i: (0, i))]
         + [whole(GROUP, right.shape[1]) for right in rights],
@@ -1227,23 +1238,48 @@
     refs[-1][...] = tiles_to_rows(refs[:-1])
 
 
-def unpack_rows(tiles, at, first, rows):
+def unpack_rows_kernel(tiles_ref, down_ref, mout_ref, aout_ref):
+    step = pl.program_id(0)
+    rows = tiles_to_rows([tiles_ref])
+    last = pl.num_programs(0) - 1
+
+    @pl.when(step < FF_F // LANES)
+    def _():
+        down_ref[...] = rows
+
+    @pl.when((step >= FF_F // LANES) & (step < last))
+    def _():
+        mout_ref[...] = rows
+
+    @pl.when(step == last)
+    def _():
+        aout_ref[...] = rows
+
+
+def unpack_rows(tiles, at):
     width = D // LANES
-    step = NC // 2
-    skip, base = first // LANES, at // width
-    return pl.pallas_call(
-        unpack_kernel,
-        grid=(rows // LANES,),
+    base = at // width
+    downs, outs = FF_F // LANES, INNER_F // LANES
+
+    def rows(index):
+        return pl.BlockSpec((LANES, D), index)
+
+    return pl.pallas_call(
+        unpack_rows_kernel,
+        grid=((FF_F + OUT_ROWS) // LANES,),
         in_specs=[
             pl.BlockSpec(
-                (step, width, SLICE, LANES),
-                lambda i: ((i + skip) % 2, base + (i + skip) // 2, 0, 0),
+                (NC // 2, width, SLICE, LANES), lambda i: (i % 2, base + i // 2, 0, 0)
             )
         ],
-        out_specs=pl.BlockSpec((LANES, D), lambda i: (i, 0)),
-        out_shape=shape_of((rows, D), F32),
-        compiler_params=PARAMS,
-        cost_estimate=cost(rows * D, 6 * rows * D),
+        out_specs=[
+            rows(lambda i: (jnp.minimum(i, downs - 1), 0)),
+            rows(lambda i: (jnp.clip(i - downs, 0, outs - 1), 0)),
+            rows(lambda i: (0, 0)),
+        ],
+        out_shape=[shape_of((FF_F, D), F32), shape_of((INNER_F, D), F32), shape_of((HDIM, D), F32)],
+        compiler_params=PARAMS,
+        cost_estimate=cost((FF_F + OUT_ROWS) * D, 6 * (FF_F + OUT_ROWS) * D),
         name="unpack_rows",
     )(tiles)
 
@@ -1277,13 +1313,13 @@
 
 def unpack_in_kernel(*refs):
     step = pl.program_id(0)
-    steps = NF // 2
+    steps = NF // IN_SEQS
     wide = INNER_F // LANES
     out_ref = refs[-1]
 
     @pl.when(step < 2 * steps)
     def _():
-        for index in range(2):
+        for index in range(IN_SEQS):
             for tile in range(wide):
                 start = index * INNER_F + tile * LANES
                 out_ref[start : start + LANES] = turned(refs[index], tile)
@@ -1291,7 +1327,7 @@
     @pl.when(step == 2 * steps)
     def _():
         for f in range(NF):
-            tail = turned(refs[2 + f], 0)
+            tail = turned(refs[IN_SEQS + f], 0)
             out_ref[f * BC_F : (f + 1) * BC_F] = tail[:BC_F]
             first = NF * BC_F + f * DT_F
             out_ref[first : first + DT_F] = tail[BC_F : BC_F + DT_F]
@@ -1299,12 +1335,12 @@
 
 def unpack_in(tiles):
     wide = INNER_F // LANES
-    half = NF // 2
+    half = NF // IN_SEQS
     each = W1_COLS // LANES
 
     def spec(j):
         def index(i):
-            f = 2 * (jnp.minimum(i, 2 * half - 1) % half) + j
+            f = IN_SEQS * (jnp.minimum(i, 2 * half - 1) % half) + j
             return (0, each * f + jnp.where(i < half, 0, wide), 0, 0)
 
         shape = tuple(pl.Element(size) for size in (NC, wide, SLICE, LANES))
@@ -1313,13 +1349,13 @@
     def tail_spec(f):
         return pl.BlockSpec((NC, 1, SLICE, LANES), lambda i: (0, each * f + 2 * wide, 0, 0))
 
-    specs = [spec(0), spec(1)]
+    specs = [spec(j) for j in range(IN_SEQS)]
     specs += [tail_spec(f) for f in range(NF)]
     return pl.pallas_call(
         unpack_in_kernel,
         grid=(2 * half + 1,),
         in_specs=specs,
-        out_specs=pl.BlockSpec((2 * INNER_F, SHARD), lambda i: (i, 0)),
+        out_specs=pl.BlockSpec((IN_SEQS * INNER_F, SHARD), lambda i: (i, 0)),
         out_shape=shape_of((2 * INNER + 2 * STATE + MHEADS, SHARD), F32),
         compiler_params=PARAMS,
         cost_estimate=cost(SHARD * 6704, 6 * SHARD * 6704),
@@ -1415,7 +1451,6 @@
 
     in_rows = lax.dynamic_slice(w_in, (ctx * SLICE, 0), (SLICE, w_in.shape[1]))
     qkv_rows = lax.dynamic_slice(w_qkv, (ctx * SLICE, 0), (SLICE, w_qkv.shape[1]))
-    gu_rows = lax.dynamic_slice(w_gate_up, (ctx * SLICE, 0), (SLICE, w_gate_up.shape[1]))
     parts = [
         columns_of(in_rows, INNER, INNER_F),
         columns_of(in_rows, 2 * INNER, BC_F),
@@ -1428,11 +1463,11 @@
         parts.append(jnp.repeat(pair.transpose(1, 0, 2), NF // KVHEADS, axis=0))
     parts += [
         columns_of(in_rows, 0, INNER_F),
-        columns_of(gu_rows, 0, FF_F),
-        columns_of(gu_rows, FF, FF_F),
     ]
-    swapped, gu_swapped = together(
-        swap_fsdp(jnp.concatenate(parts[:-2], axis=2)), jnp.concatenate(parts[-2:], axis=2)
+    swapped, w_gate_up = together(swap_fsdp(jnp.concatenate(parts, axis=2)), w_gate_up)
+    gu_rows = lax.dynamic_slice(w_gate_up, (ctx * SLICE, 0), (SLICE, w_gate_up.shape[1]))
+    gu_swapped = jnp.concatenate(
+        [columns_of(gu_rows, 0, FF_F), columns_of(gu_rows, FF, FF_F)], axis=2
     )
     w_one = lax.all_gather(swapped, "ctx", axis=0)
     normed, gu_swapped = together(normed, swap_fsdp(gu_swapped))
@@ -1506,8 +1541,14 @@
     def total_of(got):
         return jnp.sum(got.astype(F32), axis=0).astype(BF)
 
-    def scatter_ctx(joined):
-        part = lax.psum_scatter(joined, "ctx", scatter_dimension=0, tiled=False)
+    along_y = [[x * NY + y for y in range(NY)] for x in range(NC // NY)]
+    along_x = [[x * NY + y for x in range(NC // NY)] for y in range(NY)]
+
+    def scatter_ctx(joined, groups):
+        joined = joined.reshape(len(groups[0]), -1, LANES)
+        part = lax.psum_scatter(
+            joined, "ctx", scatter_dimension=0, axis_index_groups=groups, tiled=False
+        )
         return lax.optimization_barrier(part)
 
     def all_ctx(parts):
@@ -1516,11 +1557,13 @@
 
     gu_tiles = MLP_COLS // LANES
     row_tiles = OUT_ROWS // SHARD * (D // LANES)
-    packed_one = side_by_side(column_grad(normed_two, d_gu), column_grad(act, cot_all))
-    d_normed_two, packed_one, down_mine, down_other = together(
-        scatter_fsdp(d_normed_two), packed_one, down_mine, down_other
-    )
-    sum_one = scatter_ctx(packed_one)
+    got_down = swap_ctx(column_grad(act, cot_all).reshape(NC, -1, LANES))
+    packed_gu = column_grad(normed_two, d_gu, by_y=True)
+    d_normed_two, packed_gu, down_mine, down_other, got_down = together(
+        scatter_fsdp(d_normed_two), packed_gu, down_mine, down_other, got_down
+    )
+    sum_gu = scatter_ctx(packed_gu, along_y)
+    sum_down = total_of(got_down)
     d_mixed, g_mlp_gain = norm_back(mixed, scale_two, mlp_gain, d_normed_two)
     d_mixed = d_mixed + cot_low.astype(F32)
     branch = ring_gather(d_mixed.astype(BF), order)
@@ -1530,10 +1573,14 @@
     d_mixers, dz, g_mamba_gain = gate_back(
         ssd, gate_z, g, dg, dh, squares, inner, my_gain
     )
+    d_mixers, sum_gu = together(d_mixers, sum_gu)
+    sum_gu = scatter_ctx(sum_gu, along_x)
     d_mixers = swap_ctx(d_mixers)
-    packed_two = side_by_side(column_grad(gated_heads, branch), column_grad(normed, dz))
-    d_mixers, packed_two = lax.optimization_barrier((d_mixers, packed_two))
-    sum_two = scatter_ctx(packed_two)
+    packed_two = side_by_side(
+        column_grad(gated_heads, branch, by_y=True), column_grad(normed, dz, by_y=True)
+    )
+    d_mixers, packed_two, sum_gu = together(d_mixers, packed_two, sum_gu)
+    sum_two = scatter_ctx(packed_two, along_y)
     dx, dbc_mine, dbc_other, drow, dskip = mamba_bwd(
         place, x_act, d_mixers, bc, row_terms, states, my_skip
     )
@@ -1541,41 +1588,39 @@
         dbc_mine.reshape(NZ * BC_F, LENGTH), dbc_other.reshape(NZ * BC_F, LENGTH)
     )
     dx, d_mixers = together(dx, d_mixers)
-    dbc_joined, sum_one = together(dbc_joined, sum_one)
     down_at = NF * gu_tiles
     out_at = down_at + row_tiles
-    gu_part = swap_fsdp(sum_one[: down_at * SLICE].reshape(NF, -1, LANES))
-    dbc_own, attn_pack, gu_part, down_other = together(
-        ring_scatter(dbc_joined), attn_bwd(odd, attn_got, d_mixers, lse), gu_part, down_other
-    )
+    gu_part = swap_fsdp(sum_gu.reshape(NF, -1, LANES))
+    dbc_joined, gu_part = together(dbc_joined, gu_part)
+    dbc_own, attn_pack, sum_two = together(
+        ring_scatter(dbc_joined), attn_bwd(odd, attn_got, d_mixers, lse), sum_two
+    )
+    sum_two = scatter_ctx(sum_two, along_x)
     attn_back = swap_ctx(attn_pack)
     mix_pack, g_taps, g_heads = front_back(
         mix_got, taps, heads_in, row_terms, drow, dx, dbc_own
     )
-    mix_pack, attn_back = together(mix_pack, attn_back)
-    def joined(mine, other):
-        return ring_join(mine.reshape(NZ * ROWS, D), other.reshape(NZ * ROWS, D))
-
-    mix_back, d_qkv, sum_two, down = together(
-        swap_ctx(mix_pack),
-        attn_grads(attn_back, cosine, sine),
-        sum_two,
-        ring_scatter(joined(down_mine, down_other)),
-    )
-    output = even_first((mixed + down).astype(BF)).reshape(tokens.shape)
+    mix_pack, attn_back, sum_two = together(mix_pack, attn_back, sum_two)
     all_one = all_ctx(
         [
             gu_part.reshape(-1, LANES),
-            sum_one[down_at * SLICE :],
+            sum_down,
             sum_two[: row_tiles * SLICE],
         ]
     )
+    mix_back, d_qkv = together(swap_ctx(mix_pack), attn_grads(attn_back, cosine, sine))
     d_mix = mix_grads(mix_back)
     packed_mix, dz = together(column_grad(normed, d_mix, d_qkv).reshape(NC, -1, LANES), dz)
     mine, other, gain_sum = back_project(spot, d_mix, d_qkv, dz, normed, w_one)
     g_norm_gain = gain_sum[0] / norm_gain
 
-    got_mix, d_normed = together(swap_ctx(packed_mix), joined(mine, other))
+    def joined(mine, other):
+        return ring_join(mine.reshape(NZ * ROWS, D), other.reshape(NZ * ROWS, D))
+
+    mine, down_other = together(mine, down_other)
+    got_mix, d_normed, down = together(
+        swap_ctx(packed_mix), joined(mine, other), joined(down_mine, down_other)
+    )
     columns = swap_fsdp(
         jnp.concatenate(
             [
@@ -1610,17 +1655,18 @@
 
     own, columns, all_one = together(own.reshape(-1, LANES), columns, all_one)
     all_two = all_ctx([columns.reshape(-1, LANES)])
-    own, *d_normed = together(butterfly(own, "ctx", (1, 2, 4)), *ring_first(d_normed))
+    both = jnp.concatenate([d_normed, down], axis=1)
+    own, *both = together(butterfly(own, "ctx", (1, 2, 4)), *ring_first(both))
     own = butterfly(own, "ctx", (8,)).reshape(-1)
     mine = (jnp.arange(NF) == fsdp)[:, None]
     placed = jnp.where(mine, own[None, :own_pad], 0.0).reshape(-1)
     total = jnp.concatenate([placed, own[own_pad:]]).reshape(-1, LANES)
-    total, d_normed = together(butterfly(total, "fsdp", (1,)), ring_last(*d_normed))
+    total, both = together(butterfly(total, "fsdp", (1,)), ring_last(*both))
+    d_normed, down = both[:, :D], both[:, D:]
+    output = even_first((mixed + down).astype(BF)).reshape(tokens.shape)
 
     g_gate_up = unpack_gate_up(all_one)
-    g_down = unpack_rows(all_one, down_at, 0, OUT_ROWS)
-    g_mout = unpack_rows(all_one, out_at, 0, INNER_F)
-    g_aout = unpack_rows(all_one, out_at, INNER_F, HDIM)
+    g_down, g_mout, g_aout = unpack_rows(all_one, down_at)
     total = butterfly(total, "fsdp", (2,))
     total, g_gate_up, g_down, g_mout, g_aout = together(
         total, g_gate_up, g_down, g_mout, g_aout

time: 732 us -> 731 us (level)
  starting transfers between devices: 146 us -> 109 us
  waiting for transfers between devices: 245 us -> 280 us
  blocking collectives: 0 us -> 13.5 us
  other arithmetic: 50.9 us -> 43.1 us
    all_to_all x8 -> x9, waiting for transfers between devices: 51.8 us -> 85.6 us  [swap_ctx(): return lax.all_to_all(value, 'ctx', 0, 0, tiled=True)]
    ppermute x13, starting transfers between devices: 20 us -> 3.36 us  [exchange(): lax.ppermute(value, axis, [(i, i ^ bit) for i in range(size)])]
    all_gather x2, waiting for transfers between devices: 16.1 us -> 0.01 us  [all_ctx(): return lax.all_gather(joined.reshape(-1, SLICE, LANES), 'ctx', axis=0)]
    reduce_scatter x0 -> x4, waiting for transfers between devices: none -> 15.6 us  [scatter_ctx(): lax.psum_scatter(joined, 'ctx', scatter_dimension=0, axis_index_groups=gr...]
    all_to_all x0 -> x1, blocking collectives: none -> 13.5 us  [swap_fsdp(): return lax.all_to_all(value, 'fsdp', 0, 0, tiled=True)]
    ppermute x13, waiting for transfers between devices: 26.2 us -> 39.1 us  [exchange(): lax.ppermute(value, axis, [(i, i ^ bit) for i in range(size)])]
    ppermute x45 -> x39, starting transfers between devices: 51.7 us -> 39.7 us  [send(): return lax.ppermute(value, 'fsdp', route)]
    all_to_all x4 -> x3, starting transfers between devices: 18.8 us -> 10.4 us  [swap_fsdp(): return lax.all_to_all(value, 'fsdp', 0, 0, tiled=True)]
  transfers between devices with their start and end apart: 80 -> 76, of which waited for: 35 -> 35; matrix products, arithmetic and copies ran while one was open for 11% -> 10% of each run, Pallas kernels for 23% -> 23%
where the time goes in v3:
time: 731 us; the launch traced here: 719 us
  waiting for transfers between devices  280 us (38%)
  Pallas kernels  206 us (28%)
  starting transfers between devices  109 us (15%)
  local copies, waits for them, and re-layouts  46.2 us (6%)
  other arithmetic  43.1 us (6%)
  between operations  21 us (3%)
  blocking collectives  13.5 us (2%)
    all_to_all x9, waiting for transfers between devices, swap_ctx(): return lax.all_to_all(value, 'ctx', 0, 0, tiled=True)  85.6 us
    all_to_all x9, starting transfers between devices, swap_ctx(): return lax.all_to_all(value, 'ctx', 0, 0, tiled=True)  54.9 us
    reduce_scatter x2, waiting for transfers between devices, scatter_fsdp(): lax.psum_scatter(parts, 'fsdp', scatter_dimension=0, tiled=True).astype(F32)  45.7 us
    ppermute x39, waiting for transfers between devices, send(): return lax.ppermute(value, 'fsdp', route)  45.2 us
    ppermute x39, starting transfers between devices, send(): return lax.ppermute(value, 'fsdp', route)  39.7 us
    ppermute x13, waiting for transfers between devices, exchange(): lax.ppermute(value, axis, [(i, i ^ bit) for i in range(size)])  39.1 us
    pallas_call x5, Pallas kernels, column_grad(): pl.pallas_call(functools.partial(column_grad_kernel, by_y), grid=(count /...  35.5 us
    all_gather x2, waiting for transfers between devices, gather_fsdp(): return lax.all_gather(value, 'fsdp', axis=0, tiled=True)  24.6 us
  transfers between devices with their start and end apart: 76, of which 35 were waited for; matrix products, arithmetic and copies ran while one was open for 10% of the time, Pallas kernels for 23%

profile of v3, /device:TPU:16, one launch (start us, length us, event | category | flops | bytes accessed | tf_op | source)
XLA Modules:
  0.0 718.6 jit_solution(322958686373897398)
XLA Ops:
  13.6 13.5 %all_to_all.65 = bf16[8,16,1280]{2,1,0:T(8,128)(2,1)} all-to-all(bf16[8,16,1280]{2,1,0:T(8,128)(2,1)S(1)} %copy.115), channel_id=1, replica_groups=mesh['ctx'=16,'fsdp'=8] {'fsdp'}, dimensions={0} | all-to-all | bytes 655360 | tf_op jit(solution)/shard_map/all_to_all | solution.py:170
  42.3 3.6 collective-permute-done
  57.6 8.5 %collective-permute-done.3 = bf16[64,2048]{1,0:T(8,128)(2,1)S(1)} collective-permute-done((bf16[64,2048]{1,0:T(8,128)(2,1)S(1)}, bf16[64,2048]{1,0:T(8,128)(2,1)S(1)}, u32[]{:S(2)}, u32[]{:S(2)}) %collective-permute-start.3) | collective-permute-done | bytes 262176 | tf_op jit(solution)/shard_map/ppermute | solution.py:92
  71.2 11.6 %all-gather.17.cloned.1.call-done = bf16[128,16,1280]{2,1,0:T(8,128)(2,1)} async-done(((bf16[8,16,1280]{2,1,0:T(8,128)(2,1)}), bf16[128,16,1280]{2,1,0:T(8,128)(2,1)}) %all-gather.17.cloned.1.call-update) | async-done | bytes 5242896 | tf_op jit(solution)/shard_map/all_gather | solution.py:1472
  82.8 9.4 %project.1 = (bf16[16,272,128]{2,1,0:T(8,128)(2,1)}, bf16[16,320,128]{2,1,0:T(8,128)(2,1)}) custom-call(bf16[1024,2048]{1,0:T(8,128)(2,1)} %constant_dynamic-update-slice_fusion.27.n_ref.left_ref, bf16[16,8,16,1280]{3,2,1,0:T(8,128)(2,1)} %bitcast.160, f32[128,64]{1,0:T(8,128)} %get-tuple-element.262.cos_ref, f32[128,64]{1,0:T(8,128)} %get-tuple-element.261.sin_ref), custom_call_target="tpu_custom_call" | custom-call | flops 3758096384 | bytes 10000000 | tf_op jit(solution)/shard_map/project/pallas_call | solution.py:234
  92.4 5.7 all-to-all-start.2
  99.6 7.8 %project_z.1.z_ref = f32[8,384,128]{2,1,0:T(8,128)} custom-call(bf16[1024,2048]{1,0:T(8,128)(2,1)} %constant_dynamic-update-slice_fusion.27.n_ref.left_ref, bf16[16,8,16,1280]{3,2,1,0:T(8,128)(2,1)} %bitcast.161), custom_call_target="tpu_custom_call" | custom-call | flops 1610612736 | bytes 8000000 | tf_op jit(solution)/shard_map/project_z/pallas_call | solution.py:265
  107.4 6.6 all-to-all-done.2.got_ref
  115.0 6.4 front.1
  126.2 6.2 all-to-all-start.3
  142.7 8.5 %mamba_fwd.1 = (bf16[16,192,128]{2,1,0:T(8,128)(2,1)}, f32[8,192,256]{2,1,0:T(8,128)}) custom-call(s32[8]{0:T(128)} %fusion.13.place_ref, bf16[192,2048]{1,0:T(8,128)(2,1)} %get-tuple-element.132.x_ref, bf16[8,64,2048]{2,1,0:T(8,128)(2,1)} %bitcast.205, f32[16,2048]{1,0:T(8,128)} %get-tuple-element.136.row_ref, f32[192,1]{1,0:T(8,128)} %broadcast_in_dim_reshape.4.skip_ref), custom_call_target="tpu_custom_call" | custom-call | flops 872415232 | bytes 7000000 | tf_op jit(solution)/shard_map/mamba_fwd/pallas_call | solution.py:954
  151.1 4.3 all-to-all-done.3.q_ref.k_ref.v_ref
  155.5 6.1 all-to-all-start.4
  161.6 9.2 %attn_fwd.1 = (bf16[16,64,128]{2,1,0:T(8,128)(2,1)}, f32[1024,1]{1,0:T(8,128)}) custom-call(s32[1]{0:T(128)} %bitcast.31.odd_ref, bf16[16,320,128]{2,1,0:T(8,128)(2,1)} %copy-done.11, bf16[16,320,128]{2,1,0:T(8,128)(2,1)} %copy-done.11, bf16[16,320,128]{2,1,0:T(8,128)(2,1)} %copy-done.11), custom_call_target="tpu_custom_call" | custom-call | flops 1073741824 | bytes 3000000 | tf_op jit(solution)/shard_map/attn_fwd/pallas_call | solution.py:1156
  170.8 8.8 %all-to-all-done.4.got_ref = bf16[16,192,128]{2,1,0:T(8,128)(2,1)S(1)} async-done(((bf16[16,192,128]{2,1,0:T(8,128)(2,1)}), bf16[16,192,128]{2,1,0:T(8,128)(2,1)S(1)}, u32[]{:S(2)}, u32[]{:S(2)}) %all-to-all-start.4) | async-done | bytes 786464 | tf_op jit(solution)/shard_map/all_to_all | solution.py:166
  183.2 6.3 all-to-all-start.5
  200.3 7.2 %branch_out.1 = (bf16[1024,512]{1,0:T(8,128)(2,1)}, bf16[1024,2048]{1,0:T(8,128)(2,1)}) custom-call(bf16[16,64,128]{2,1,0:T(8,128)(2,1)} %copy-done.19, f32[8,384,128]{2,1,0:T(8,128)} %get-tuple-element.146.g_ref, f32[8,128]{1,0:T(8,128)} %add.305.sq_ref, f32[384,1]{1,0:T(8,128)} %broadcast_in_dim.79.gain_ref, bf16[512,2048]{1,0:T(8,128)(2,1)} %copy-done.7), custom_call_target="tpu_custom_call" | custom-call | flops 2147483648 | bytes 10000000 | tf_op jit(solution)/shard_map/branch_out/pallas_call | solution.py:459
  207.5 37.0 %reduce-scatter.7.cloned.1.call-done = bf16[128,2048]{1,0:T(8,128)(2,1)} async-done(((bf16[1024,2048]{1,0:T(8,128)(2,1)}), bf16[128,2048]{1,0:T(8,128)(2,1)}) %reduce-scatter.7.cloned.1.call-update) | async-done | bytes 524304 | tf_op jit(solution)/shard_map/reduce_scatter | solution.py:100
  248.0 6.5 act_back.1.d_act_ref
  254.5 24.6 %all-gather.11.cloned.1.call-done.n_ref.left_ref = bf16[1024,2048]{1,0:T(8,128)(2,1)} async-done(((bf16[128,2048]{1,0:T(8,128)(2,1)}), bf16[1024,2048]{1,0:T(8,128)(2,1)}) %all-gather.11.cloned.1.call-update) | async-done | bytes 4194320 | tf_op jit(solution)/shard_map/all_gather | solution.py:96
  279.1 13.9 %mlp.1 = (bf16[1024,512]{1,0:T(8,128)(2,1)}, bf16[1024,1024]{1,0:T(8,128)(2,1)}, bf16[1024,2048]{1,0:T(8,128)(2,1)}) custom-call(bf16[1024,2048]{1,0:T(8,128)(2,1)} %all-gather.11.cloned.1.call-done.n_ref.left_ref, f32[1024,512]{1,0:T(8,128)} %act_back.1.d_act_ref, bf16[16,8,16,1024]{3,2,1,0:T(8,128)(2,1)} %bitcast.211), custom_call_target="tpu_custom_call" | custom-call | flops 8589934592 | bytes 20000000 | tf_op jit(solution)/shard_map/mlp/pallas_call | solution.py:606
  293.1 6.3 column_grad.6
  299.4 7.4 %all-to-all-start.6 = ((bf16[16,512,128]{2,1,0:T(8,128)(2,1)}), bf16[16,512,128]{2,1,0:T(8,128)(2,1)}, u32[]{:S(2)}, u32[]{:S(2)}) async-start(bf16[16,512,128]{2,1,0:T(8,128)(2,1)} %bitcast.170), calls=%async_computation.8 | async-start | bytes 4194304 | tf_op jit(solution)/shard_map/all_to_all | solution.py:166
  307.9 6.9 down_out.1
  314.8 8.5 %column_grad.5 = bf16[16,8,8,16,128]{4,3,2,1,0:T(8,128)(2,1)} custom-call(bf16[1024,2048]{1,0:T(8,128)(2,1)} %all-gather.11.cloned.1.call-done.n_ref.left_ref, bf16[1024,1024]{1,0:T(8,128)(2,1)} %get-tuple-element.158.refs_0_), custom_call_target="tpu_custom_call" | custom-call | flops 4294967296 | bytes 10485760 | tf_op jit(solution)/shard_map/column_grad/pallas_call | solution.py:401
  323.4 8.7 %reduce-scatter.9.cloned.1.call-done = bf16[128,2048]{1,0:T(8,128)(2,1)} async-done(((bf16[1024,2048]{1,0:T(8,128)(2,1)}), bf16[128,2048]{1,0:T(8,128)(2,1)}) %reduce-scatter.9.cloned.1.call-update) | async-done | bytes 524304 | tf_op jit(solution)/shard_map/reduce_scatter | solution.py:100
  341.3 9.9 %collective-permute-done.19 = bf16[128,2048]{1,0:T(8,128)(2,1)S(1)} collective-permute-done((bf16[128,2048]{1,0:T(8,128)(2,1)S(1)}, bf16[128,2048]{1,0:T(8,128)(2,1)S(1)}, u32[]{:S(2)}, u32[]{:S(2)}) %collective-permute-start.19) | collective-permute-done | bytes 524320 | tf_op jit(solution)/shard_map/ppermute | solution.py:92
  354.0 3.6 collective-permute-done.20
  357.7 5.5 collective-permute-done.22
  367.3 7.1 branch_back.1
  376.6 3.6 collective-permute-done.28
  380.2 5.1 collective-permute-done.29
  385.9 4.9 gate_back.1
  390.8 7.2 all-to-all-start.7
  398.2 6.2 column_grad.7
  404.4 6.1 column_grad.8
  410.5 3.6 pad_maximum_fusion
  414.1 5.5 reduce-scatter.13.cloned.1.call-done
  419.6 14.2 %mamba_bwd.1 = (f32[192,2048]{1,0:T(8,128)}, bf16[4,64,2048]{2,1,0:T(8,128)(2,1)}, bf16[4,64,2048]{2,1,0:T(8,128)(2,1)}, f32[8,2048]{1,0:T(8,128)}, f32[192,1]{1,0:T(8,128)}) custom-call(s32[8]{0:T(128)} %fusion.13.place_ref, bf16[192,2048]{1,0:T(8,128)(2,1)} %get-tuple-element.132.x_ref, bf16[16,256,128]{2,1,0:T(8,128)(2,1)} %all-to-all-done.7.got_ref.do_ref, ...), custom_call_target="tpu_custom_call" | custom-call | flops 2214592512 | bytes 12000000 | tf_op jit(solution)/shard_map/mamba_bwd/pallas_call | solution.py:1085
  440.5 4.5 all-to-all-done.8
  457.3 11.6 %attn_bwd.1 = bf16[16,320,128]{2,1,0:T(8,128)(2,1)} custom-call(s32[1]{0:T(128)} %bitcast.31.odd_ref, bf16[16,320,128]{2,1,0:T(8,128)(2,1)} %copy-done.11, bf16[16,320,128]{2,1,0:T(8,128)(2,1)} %copy-done.11, bf16[16,320,128]{2,1,0:T(8,128)(2,1)} %copy-done.11, bf16[16,256,128]{2,1,0:T(8,128)(2,1)} %all-to-all-done.7.got_ref.do_ref, ...), custom_call_target="tpu_custom_call" | custom-call | flops 2684354560 | bytes 4000000 | tf_op jit(solution)/shard_map/attn_bwd/pallas_call | solution.py:1208
  470.7 5.5 all-to-all-start.9
  478.1 11.0 %front_back.1 = (bf16[16,272,128]{2,1,0:T(8,128)(2,1)}, f32[256,8]{1,0:T(8,128)}, f32[8,1]{1,0:T(8,128)}) custom-call(bf16[16,272,128]{2,1,0:T(8,128)(2,1)} %copy-done.3, f32[256,8]{1,0:T(8,128)} %bitcast.174, f32[8,128]{1,0:T(8,128)} %broadcast_in_dim.71.heads_ref, f32[16,2048]{1,0:T(8,128)} %get-tuple-element.136.row_ref, ...), custom_call_target="tpu_custom_call" | custom-call | flops 31457280 | bytes 9000000 | tf_op jit(solution)/shard_map/front_back/pallas_call | solution.py:849
  489.2 10.1 %reduce-scatter.17.cloned.1.call-done = bf16[1,896,128]{2,1,0:T(8,128)(2,1)} async-done(((bf16[4,896,128]{2,1,0:T(8,128)(2,1)}), bf16[1,896,128]{2,1,0:T(8,128)(2,1)}) %reduce-scatter.17.cloned.1.call-update) | async-done | bytes 229392 | tf_op jit(solution)/shard_map/reduce_scatter | solution.py:1549
  501.0 5.7 all-to-all-start.10
  506.7 4.0 attn_grads.1.refs_1_.dqkv_ref
  510.8 19.1 %all-to-all-done.10.got_ref = bf16[16,272,128]{2,1,0:T(8,128)(2,1)} async-done(((bf16[16,272,128]{2,1,0:T(8,128)(2,1)}), bf16[16,272,128]{2,1,0:T(8,128)(2,1)}, u32[]{:S(2)}, u32[]{:S(2)}) %all-to-all-start.10) | async-done | bytes 1114144 | tf_op jit(solution)/shard_map/all_to_all | solution.py:166
  529.8 3.6 mix_grads.1.refs_0_.mix_ref
  533.5 8.3 %column_grad.9 = bf16[16,8,7,16,128]{4,3,2,1,0:T(8,128)(2,1)} custom-call(bf16[1024,2048]{1,0:T(8,128)(2,1)} %constant_dynamic-update-slice_fusion.27.n_ref.left_ref, bf16[1024,512]{1,0:T(8,128)(2,1)} %mix_grads.1.refs_0_.mix_ref, bf16[1024,384]{1,0:T(8,128)(2,1)} %attn_grads.1.refs_1_.dqkv_ref), custom_call_target="tpu_custom_call" | custom-call | flops 3758096384 | bytes 9699328 | tf_op jit(solution)/shard_map/column_grad/pallas_call | solution.py:401
  541.8 4.8 all-to-all-start.11
  546.7 11.8 %back_project.1 = (bf16[4,128,2048]{2,1,0:T(8,128)(2,1)}, bf16[4,128,2048]{2,1,0:T(8,128)(2,1)}, f32[1,2048]{1,0:T(1,128)}) custom-call(s32[5]{0:T(128)} %pad_add_fusion.1.spot_ref, bf16[1024,512]{1,0:T(8,128)(2,1)} %mix_grads.1.refs_0_.mix_ref, bf16[1024,384]{1,0:T(8,128)(2,1)} %attn_grads.1.refs_1_.dqkv_ref, ...), custom_call_target="tpu_custom_call" | custom-call | flops 5368709120 | bytes 18000000 | tf_op jit(solution)/shard_map/back_project/pallas_call | solution.py:356
  563.0 4.5 fusion
  567.5 3.8 fusion.1
  571.3 43.8 %all-to-all-done.11 = bf16[16,896,128]{2,1,0:T(8,128)(2,1)} async-done(((bf16[16,896,128]{2,1,0:T(8,128)(2,1)}), bf16[16,896,128]{2,1,0:T(8,128)(2,1)}, u32[]{:S(2)}, u32[]{:S(2)}) %all-to-all-start.11) | async-done | bytes 3670048 | tf_op jit(solution)/shard_map/all_to_all | solution.py:166
  618.5 3.6 all-to-all-start.12
  622.6 7.7 %all-to-all-done.12 = bf16[8,160,128]{2,1,0:T(8,128)(2,1)S(1)} async-done(((bf16[8,160,128]{2,1,0:T(8,128)(2,1)}), bf16[8,160,128]{2,1,0:T(8,128)(2,1)S(1)}, u32[]{:S(2)}, u32[]{:S(2)}) %all-to-all-start.12) | async-done | bytes 327712 | tf_op jit(solution)/shard_map/all_to_all | solution.py:170
  644.4 5.6 collective-permute-done.40
  653.9 5.7 collective-permute-done.44
  665.9 3.6 collective-permute-done.46
  669.7 8.3 %unpack_rows.1 = (f32[512,2048]{1,0:T(8,128)}, f32[384,2048]{1,0:T(8,128)}, f32[128,2048]{1,0:T(8,128)}) custom-call(bf16[16,128,16,128]{3,2,1,0:T(8,128)(2,1)} %all-gather.13.cloned.1.call-done.refs_0_.refs_1_.refs_2_.refs_3_.tiles_ref), custom_call_target="tpu_custom_call" | custom-call | flops 2097152 | bytes 12582912 | tf_op jit(solution)/shard_map/unpack_rows/pallas_call | solution.py:1267
  678.0 6.0 unpack_gate_up.1
  687.0 4.1 collective-permute-done.50
  692.5 5.0 collective-permute-done.51
  702.3 6.3 unpack_in.1
  (384 shorter events, 157.5 us)
Async XLA Ops:
  7.2 75.7 %all-gather.17.cloned.1.call-start = ((), (), s32[]{:S(2)}) async-start(), calls=%async_computation.29 | async-start | bytes 5570560 | tf_op jit(solution)/shard_map/all_gather | solution.py:1472
  32.3 13.6 %collective-permute-start = (bf16[128,2048]{1,0:T(8,128)(2,1)S(1)}, bf16[128,2048]{1,0:T(8,128)(2,1)S(1)}, u32[]{:S(2)}, u32[]{:S(2)}) collective-permute-start(bf16[128,2048]{1,0:T(8,128)(2,1)S(1)} %get-tuple-element.274), channel_id=1, source_target_pairs={{0,6},{1,7},{2,0},{3,1},{4,2},{5,3},{6,4},{7,5},{8,14},{9,15},{10,... | collective-permute-start | bytes 1572872 | tf_op jit(solution)/shard_map/ppermute | solution.py:92
  33.5 19.9 %collective-permute-start.2 = (bf16[128,2048]{1,0:T(8,128)(2,1)S(1)}, bf16[128,2048]{1,0:T(8,128)(2,1)S(1)}, u32[]{:S(2)}, u32[]{:S(2)}) collective-permute-start(bf16[128,2048]{1,0:T(8,128)(2,1)S(1)} %get-tuple-element.274), channel_id=1, source_target_pairs={{0,2},{1,3},{2,4},{3,5},{4,6},{5,7},{6,0},{7,1},{8,10},{9,11},{10,... | collective-permute-start | bytes 1572872 | tf_op jit(solution)/shard_map/ppermute | solution.py:92
  34.3 33.5 %collective-permute-start.4 = (bf16[128,2048]{1,0:T(8,128)(2,1)S(1)}, bf16[128,2048]{1,0:T(8,128)(2,1)S(1)}, u32[]{:S(2)}, u32[]{:S(2)}) collective-permute-start(bf16[128,2048]{1,0:T(8,128)(2,1)S(1)} %get-tuple-element.274), channel_id=1, source_target_pairs={{0,1},{1,0},{2,3},{3,2},{4,5},{5,4},{6,7},{7,6},{8,9},{9,8},{10,11... | collective-permute-start | bytes 1572872 | tf_op jit(solution)/shard_map/ppermute | solution.py:92
  46.6 10.0 %collective-permute-start.1 = (bf16[64,2048]{1,0:T(8,128)(2,1)}, bf16[64,2048]{1,0:T(8,128)(2,1)}, u32[]{:S(2)}, u32[]{:S(2)}) collective-permute-start(bf16[64,2048]{1,0:T(8,128)(2,1)} %slice.284), channel_id=1, source_target_pairs={{0,6},{1,7},{2,0},{3,1},{4,2},{5,3},{6,4},{7,5},{8,14},{9,15},{10,... | collective-permute-start | bytes 786440 | tf_op jit(solution)/shard_map/ppermute | solution.py:92
  49.9 21.3 %all-to-all-start.1 = ((bf16[8,16,1024]{2,1,0:T(8,128)(2,1)}), bf16[8,16,1024]{2,1,0:T(8,128)(2,1)S(1)}, u32[]{:S(2)}, u32[]{:S(2)}) async-start(bf16[8,16,1024]{2,1,0:T(8,128)(2,1)} %copy.116), calls=%async_computation.1 | async-start | bytes 524288 | tf_op jit(solution)/shard_map/all_to_all | solution.py:170
  53.3 102.2 %all-gather.9.cloned.1.call-start = ((), (), s32[]{:S(2)}) async-start(), calls=%async_computation.19 | async-start | bytes 4718592 | tf_op jit(solution)/shard_map/all_gather | solution.py:96
  53.4 12.7 %collective-permute-start.3 = (bf16[64,2048]{1,0:T(8,128)(2,1)S(1)}, bf16[64,2048]{1,0:T(8,128)(2,1)S(1)}, u32[]{:S(2)}, u32[]{:S(2)}) collective-permute-start(bf16[64,2048]{1,0:T(8,128)(2,1)S(1)} %slice.285), channel_id=1, source_target_pairs={{0,2},{1,3},{2,4},{3,5},{4,6},{5,7},{6,0},{7,1},{8,10},{9,11},{10,... | collective-permute-start | bytes 786440 | tf_op jit(solution)/shard_map/ppermute | solution.py:92
  55.3 13.4 %collective-permute-start.5 = (bf16[128,2048]{1,0:T(8,128)(2,1)S(1)}, bf16[128,2048]{1,0:T(8,128)(2,1)S(1)}, u32[]{:S(2)}, u32[]{:S(2)}) collective-permute-start(bf16[128,2048]{1,0:T(8,128)(2,1)S(1)} %collective-permute-done), channel_id=1, source_target_pairs={{0,1},{1,0},{2,3},{3,2},{4,5},{5,4},{6,7},{7,6},{8,9},{9,8},{10,11... | collective-permute-start | bytes 1572872 | tf_op jit(solution)/shard_map/ppermute | solution.py:92
  55.3 15.0 %collective-permute-start.7 = (bf16[128,2048]{1,0:T(8,128)(2,1)S(1)}, bf16[128,2048]{1,0:T(8,128)(2,1)S(1)}, u32[]{:S(2)}, u32[]{:S(2)}) collective-permute-start(bf16[128,2048]{1,0:T(8,128)(2,1)S(1)} %collective-permute-done.2), channel_id=1, source_target_pairs={{0,1},{1,0},{2,3},{3,2},{4,5},{5,4},{6,7},{7,6},{8,9},{9,8},{10,11... | collective-permute-start | bytes 1572872 | tf_op jit(solution)/shard_map/ppermute | solution.py:92
  92.4 21.5 %all-to-all-start.2 = ((bf16[16,272,128]{2,1,0:T(8,128)(2,1)}), bf16[16,272,128]{2,1,0:T(8,128)(2,1)S(1)}, u32[]{:S(2)}, u32[]{:S(2)}) async-start(bf16[16,272,128]{2,1,0:T(8,128)(2,1)} %get-tuple-element.128), calls=%async_computation.2 | async-start | bytes 2228224 | tf_op jit(solution)/shard_map/all_to_all | solution.py:166
  98.2 101.4 %all-gather.19.cloned.1.call-start = ((), (), s32[]{:S(2)}) async-start(), calls=%async_computation.30 | async-start | bytes 4456448 | tf_op jit(solution)/shard_map/all_gather | solution.py:1516
  121.5 11.1 %collective-permute-start.10 = (bf16[64,2048]{1,0:T(8,128)(2,1)}, bf16[64,2048]{1,0:T(8,128)(2,1)S(1)}, u32[]{:S(2)}, u32[]{:S(2)}) collective-permute-start(bf16[64,2048]{1,0:T(8,128)(2,1)} %get-tuple-element.135), channel_id=1, source_target_pairs={{0,2},{1,3},{2,4},{3,5},{4,6},{5,7},{6,0},{7,1},{8,10},{9,11},{10,... | collective-permute-start | bytes 786440 | tf_op jit(solution)/shard_map/ppermute | solution.py:92
  123.0 10.2 %collective-permute-start.8 = (bf16[64,2048]{1,0:T(8,128)(2,1)}, bf16[64,2048]{1,0:T(8,128)(2,1)S(1)}, u32[]{:S(2)}, u32[]{:S(2)}) collective-permute-start(bf16[64,2048]{1,0:T(8,128)(2,1)} %get-tuple-element.135), channel_id=1, source_target_pairs={{0,6},{1,7},{2,0},{3,1},{4,2},{5,3},{6,4},{7,5},{8,14},{9,15},{10,... | collective-permute-start | bytes 786440 | tf_op jit(solution)/shard_map/ppermute | solution.py:92
  126.2 13.6 %collective-permute-start.12 = (bf16[64,2048]{1,0:T(8,128)(2,1)}, bf16[64,2048]{1,0:T(8,128)(2,1)S(1)}, u32[]{:S(2)}, u32[]{:S(2)}) collective-permute-start(bf16[64,2048]{1,0:T(8,128)(2,1)} %get-tuple-element.135), channel_id=1, source_target_pairs={{0,1},{1,0},{2,3},{3,2},{4,5},{5,4},{6,7},{7,6},{8,9},{9,8},{10,11... | collective-permute-start | bytes 786440 | tf_op jit(solution)/shard_map/ppermute | solution.py:92
  126.2 29.3 %all-to-all-start.3 = ((bf16[16,320,128]{2,1,0:T(8,128)(2,1)}), bf16[16,320,128]{2,1,0:T(8,128)(2,1)S(1)}, u32[]{:S(2)}, u32[]{:S(2)}) async-start(bf16[16,320,128]{2,1,0:T(8,128)(2,1)} %get-tuple-element.138), calls=%async_computation.3 | async-start | bytes 2621440 | tf_op jit(solution)/shard_map/all_to_all | solution.py:166
  132.5 7.1 collective-permute-start.11
  133.2 6.5 collective-permute-start.9
  136.1 5.2 collective-permute-start.15
  155.5 24.1 %all-to-all-start.4 = ((bf16[16,192,128]{2,1,0:T(8,128)(2,1)}), bf16[16,192,128]{2,1,0:T(8,128)(2,1)S(1)}, u32[]{:S(2)}, u32[]{:S(2)}) async-start(bf16[16,192,128]{2,1,0:T(8,128)(2,1)} %get-tuple-element.140), calls=%async_computation.4 | async-start | bytes 1572864 | tf_op jit(solution)/shard_map/all_to_all | solution.py:166
  183.2 6.3 collective-permute-start.16
  183.2 16.3 %all-to-all-start.5 = ((bf16[16,64,128]{2,1,0:T(8,128)(2,1)}), bf16[16,64,128]{2,1,0:T(8,128)(2,1)S(1)}, u32[]{:S(2)}, u32[]{:S(2)}) async-start(bf16[16,64,128]{2,1,0:T(8,128)(2,1)} %get-tuple-element.143), calls=%async_computation.5 | async-start | bytes 524288 | tf_op jit(solution)/shard_map/all_to_all | solution.py:166
  189.5 55.0 %reduce-scatter.7.cloned.1.call-start = ((), (), s32[]{:S(2)}) async-start(), calls=%async_computation.20 | async-start | bytes 4718592 | tf_op jit(solution)/shard_map/reduce_scatter | solution.py:100
  193.9 5.1 collective-permute-start.18
  207.5 71.6 %all-gather.11.cloned.1.call-start = ((), (), s32[]{:S(2)}) async-start(), calls=%async_computation.21 | async-start | bytes 4718592 | tf_op jit(solution)/shard_map/all_gather | solution.py:96
  248.0 84.1 %reduce-scatter.9.cloned.1.call-start = ((), (), s32[]{:S(2)}) async-start(), calls=%async_computation.22 | async-start | bytes 4718592 | tf_op jit(solution)/shard_map/reduce_scatter | solution.py:100
  299.4 36.8 %all-to-all-start.6 = ((bf16[16,512,128]{2,1,0:T(8,128)(2,1)}), bf16[16,512,128]{2,1,0:T(8,128)(2,1)}, u32[]{:S(2)}, u32[]{:S(2)}) async-start(bf16[16,512,128]{2,1,0:T(8,128)(2,1)} %bitcast.170), calls=%async_computation.8 | async-start | bytes 4194304 | tf_op jit(solution)/shard_map/all_to_all | solution.py:166
  306.8 84.0 %reduce-scatter.11.cloned.1.call-start = ((), (), s32[]{:S(2)}) async-start(), calls=%async_computation.23 | async-start | bytes 5242880 | tf_op jit(solution)/shard_map/reduce_scatter | solution.py:1549
  336.2 83.4 %reduce-scatter.13.cloned.1.call-start = ((), (), s32[]{:S(2)}) async-start(), calls=%async_computation.24 | async-start | bytes 1310720 | tf_op jit(solution)/shard_map/reduce_scatter | solution.py:1549
  339.2 12.0 %collective-permute-start.19 = (bf16[128,2048]{1,0:T(8,128)(2,1)S(1)}, bf16[128,2048]{1,0:T(8,128)(2,1)S(1)}, u32[]{:S(2)}, u32[]{:S(2)}) collective-permute-start(bf16[128,2048]{1,0:T(8,128)(2,1)S(1)} %get-tuple-element.276), channel_id=1, source_target_pairs={{0,6},{1,7},{2,0},{3,1},{4,2},{5,3},{6,4},{7,5},{8,14},{9,15},{10,... | collective-permute-start | bytes 1572872 | tf_op jit(solution)/shard_map/ppermute | solution.py:92
  340.0 13.1 %collective-permute-start.21 = (bf16[128,2048]{1,0:T(8,128)(2,1)S(1)}, bf16[128,2048]{1,0:T(8,128)(2,1)S(1)}, u32[]{:S(2)}, u32[]{:S(2)}) collective-permute-start(bf16[128,2048]{1,0:T(8,128)(2,1)S(1)} %get-tuple-element.276), channel_id=1, source_target_pairs={{0,2},{1,3},{2,4},{3,5},{4,6},{5,7},{6,0},{7,1},{8,10},{9,11},{10,... | collective-permute-start | bytes 1572872 | tf_op jit(solution)/shard_map/ppermute | solution.py:92
  351.2 6.4 collective-permute-start.20
  353.1 10.3 %collective-permute-start.23 = (bf16[128,2048]{1,0:T(8,128)(2,1)S(1)}, bf16[128,2048]{1,0:T(8,128)(2,1)S(1)}, u32[]{:S(2)}, u32[]{:S(2)}) collective-permute-start(bf16[128,2048]{1,0:T(8,128)(2,1)S(1)} %get-tuple-element.276), channel_id=1, source_target_pairs={{0,1},{1,0},{2,3},{3,2},{4,5},{5,4},{6,7},{7,6},{8,9},{9,8},{10,11... | collective-permute-start | bytes 1572872 | tf_op jit(solution)/shard_map/ppermute | solution.py:92
  353.2 10.0 %collective-permute-start.22 = (bf16[64,2048]{1,0:T(8,128)(2,1)S(1)}, bf16[64,2048]{1,0:T(8,128)(2,1)S(1)}, u32[]{:S(2)}, u32[]{:S(2)}) collective-permute-start(bf16[64,2048]{1,0:T(8,128)(2,1)S(1)} %slice.289), channel_id=1, source_target_pairs={{0,2},{1,3},{2,4},{3,5},{4,6},{5,7},{6,0},{7,1},{8,10},{9,11},{10,... | collective-permute-start | bytes 786440 | tf_op jit(solution)/shard_map/ppermute | solution.py:92
  353.4 10.1 %collective-permute-start.24 = (bf16[128,2048]{1,0:T(8,128)(2,1)S(1)}, bf16[128,2048]{1,0:T(8,128)(2,1)S(1)}, u32[]{:S(2)}, u32[]{:S(2)}) collective-permute-start(bf16[128,2048]{1,0:T(8,128)(2,1)S(1)} %collective-permute-done.19), channel_id=1, source_target_pairs={{0,1},{1,0},{2,3},{3,2},{4,5},{5,4},{6,7},{7,6},{8,9},{9,8},{10,11... | collective-permute-start | bytes 1572872 | tf_op jit(solution)/shard_map/ppermute | solution.py:92
  353.8 11.4 %collective-permute-start.26 = (bf16[128,2048]{1,0:T(8,128)(2,1)S(1)}, bf16[128,2048]{1,0:T(8,128)(2,1)S(1)}, u32[]{:S(2)}, u32[]{:S(2)}) collective-permute-start(bf16[128,2048]{1,0:T(8,128)(2,1)S(1)} %collective-permute-done.21), channel_id=1, source_target_pairs={{0,1},{1,0},{2,3},{3,2},{4,5},{5,4},{6,7},{7,6},{8,9},{9,8},{10,11... | collective-permute-start | bytes 1572872 | tf_op jit(solution)/shard_map/ppermute | solution.py:92
  390.8 28.8 %all-to-all-start.7 = ((bf16[16,256,128]{2,1,0:T(8,128)(2,1)}), bf16[16,256,128]{2,1,0:T(8,128)(2,1)}, u32[]{:S(2)}, u32[]{:S(2)}) async-start(bf16[16,256,128]{2,1,0:T(8,128)(2,1)} %get-tuple-element.168), calls=%async_computation.10 | async-start | bytes 2097152 | tf_op jit(solution)/shard_map/all_to_all | solution.py:166
  398.0 72.7 %reduce-scatter.15.cloned.1.call-start = ((), (), s32[]{:S(2)}) async-start(), calls=%async_computation.25 | async-start | bytes 4587520 | tf_op jit(solution)/shard_map/reduce_scatter | solution.py:1549
  434.1 10.9 %all-to-all-start.8 = ((bf16[8,128,128]{2,1,0:T(8,128)(2,1)}), bf16[8,128,128]{2,1,0:T(8,128)(2,1)S(1)}, u32[]{:S(2)}, u32[]{:S(2)}) async-start(bf16[8,128,128]{2,1,0:T(8,128)(2,1)} %bitcast.43), calls=%async_computation.12 | async-start | bytes 524288 | tf_op jit(solution)/shard_map/all_to_all | solution.py:170
  437.5 61.8 %reduce-scatter.17.cloned.1.call-start = ((), (), s32[]{:S(2)}) async-start(), calls=%async_computation.26 | async-start | bytes 1146880 | tf_op jit(solution)/shard_map/reduce_scatter | solution.py:1549
  446.1 6.5 collective-permute-start.31
  446.8 5.9 collective-permute-start.35
  449.4 19.4 %collective-permute-start.33 = (bf16[32,2048]{1,0:T(8,128)(2,1)S(1)}, bf16[32,2048]{1,0:T(8,128)(2,1)S(1)}, u32[]{:S(2)}, u32[]{:S(2)}) collective-permute-start(bf16[32,2048]{1,0:T(8,128)(2,1)S(1)} %get-tuple-element.253), channel_id=1, source_target_pairs={{0,2},{1,3},{2,4},{3,5},{4,6},{5,7},{6,0},{7,1},{8,10},{9,11},{10,... | collective-permute-start | bytes 393224 | tf_op jit(solution)/shard_map/ppermute | solution.py:92
  449.4 19.4 %collective-permute-start.34 = (bf16[32,2048]{1,0:T(8,128)(2,1)S(1)}, bf16[32,2048]{1,0:T(8,128)(2,1)S(1)}, u32[]{:S(2)}, u32[]{:S(2)}) collective-permute-start(bf16[32,2048]{1,0:T(8,128)(2,1)S(1)} %get-tuple-element.251), channel_id=1, source_target_pairs={{0,6},{1,7},{2,0},{3,1},{4,2},{5,3},{6,4},{7,5},{8,14},{9,15},{10,... | collective-permute-start | bytes 393224 | tf_op jit(solution)/shard_map/ppermute | solution.py:92
  453.7 15.2 %collective-permute-start.32 = (bf16[32,2048]{1,0:T(8,128)(2,1)S(1)}, bf16[32,2048]{1,0:T(8,128)(2,1)S(1)}, u32[]{:S(2)}, u32[]{:S(2)}) collective-permute-start(bf16[32,2048]{1,0:T(8,128)(2,1)S(1)} %get-tuple-element.256), channel_id=1, source_target_pairs={{0,2},{1,3},{2,4},{3,5},{4,6},{5,7},{6,0},{7,1},{8,10},{9,11},{10,... | collective-permute-start | bytes 393224 | tf_op jit(solution)/shard_map/ppermute | solution.py:92
  454.1 14.7 %collective-permute-start.36 = (bf16[32,2048]{1,0:T(8,128)(2,1)S(1)}, bf16[32,2048]{1,0:T(8,128)(2,1)S(1)}, u32[]{:S(2)}, u32[]{:S(2)}) collective-permute-start(bf16[32,2048]{1,0:T(8,128)(2,1)S(1)} %get-tuple-element.255), channel_id=1, source_target_pairs={{0,6},{1,7},{2,0},{3,1},{4,2},{5,3},{6,4},{7,5},{8,14},{9,15},{10,... | collective-permute-start | bytes 393224 | tf_op jit(solution)/shard_map/ppermute | solution.py:92
  470.7 28.5 %all-to-all-start.9 = ((bf16[16,320,128]{2,1,0:T(8,128)(2,1)}), bf16[16,320,128]{2,1,0:T(8,128)(2,1)}, u32[]{:S(2)}, u32[]{:S(2)}) async-start(bf16[16,320,128]{2,1,0:T(8,128)(2,1)} %attn_bwd.1), calls=%async_computation.14 | async-start | bytes 2621440 | tf_op jit(solution)/shard_map/all_to_all | solution.py:166
  476.2 154.1 %all-gather.13.cloned.1.call-start = ((), (), s32[]{:S(2)}) async-start(), calls=%async_computation.27 | async-start | bytes 8912896 | tf_op jit(solution)/shard_map/all_gather | solution.py:1556
  501.0 28.8 %all-to-all-start.10 = ((bf16[16,272,128]{2,1,0:T(8,128)(2,1)}), bf16[16,272,128]{2,1,0:T(8,128)(2,1)}, u32[]{:S(2)}, u32[]{:S(2)}) async-start(bf16[16,272,128]{2,1,0:T(8,128)(2,1)} %get-tuple-element.192), calls=%async_computation.16 | async-start | bytes 2228224 | tf_op jit(solution)/shard_map/all_to_all | solution.py:166
  541.8 73.3 %all-to-all-start.11 = ((bf16[16,896,128]{2,1,0:T(8,128)(2,1)}), bf16[16,896,128]{2,1,0:T(8,128)(2,1)}, u32[]{:S(2)}, u32[]{:S(2)}) async-start(bf16[16,896,128]{2,1,0:T(8,128)(2,1)} %bitcast.164), calls=%async_computation.17 | async-start | bytes 7340032 | tf_op jit(solution)/shard_map/all_to_all | solution.py:166
  558.5 8.9 %collective-permute-start.37 = (bf16[512,2048]{1,0:T(8,128)(2,1)}, bf16[512,2048]{1,0:T(8,128)(2,1)}, u32[]{:S(2)}, u32[]{:S(2)}) collective-permute-start(bf16[512,2048]{1,0:T(8,128)(2,1)} %bitcast.212), channel_id=1, source_target_pairs={{0,1},{1,0},{2,3},{3,2},{4,5},{5,4},{6,7},{7,6},{8,9},{9,8},{10,11... | collective-permute-start | bytes 6291464 | tf_op jit(solution)/shard_map/ppermute | solution.py:92
  618.5 11.8 %all-to-all-start.12 = ((bf16[8,160,128]{2,1,0:T(8,128)(2,1)}), bf16[8,160,128]{2,1,0:T(8,128)(2,1)S(1)}, u32[]{:S(2)}, u32[]{:S(2)}) async-start(bf16[8,160,128]{2,1,0:T(8,128)(2,1)} %pad_maximum_fusion.2), calls=%async_computation.18 | async-start | bytes 655360 | tf_op jit(solution)/shard_map/all_to_all | solution.py:170
  622.0 80.2 %all-gather.15.cloned.1.call-start = ((), (), s32[]{:S(2)}) async-start(), calls=%async_computation.28 | async-start | bytes 5570560 | tf_op jit(solution)/shard_map/all_gather | solution.py:1556
  633.9 20.0 %collective-permute-start.42 = (bf16[64,4096]{1,0:T(8,128)(2,1)S(1)}, bf16[64,4096]{1,0:T(8,128)(2,1)S(1)}, u32[]{:S(2)}, u32[]{:S(2)}) collective-permute-start(bf16[64,4096]{1,0:T(8,128)(2,1)S(1)} %get-tuple-element.242), channel_id=1, source_target_pairs={{0,2},{1,3},{2,4},{3,5},{4,6},{5,7},{6,0},{7,1},{8,10},{9,11},{10,... | collective-permute-start | bytes 1572872 | tf_op jit(solution)/shard_map/ppermute | solution.py:92
  634.5 19.4 %collective-permute-start.43 = (bf16[64,4096]{1,0:T(8,128)(2,1)S(1)}, bf16[64,4096]{1,0:T(8,128)(2,1)S(1)}, u32[]{:S(2)}, u32[]{:S(2)}) collective-permute-start(bf16[64,4096]{1,0:T(8,128)(2,1)S(1)} %get-tuple-element.241), channel_id=1, source_target_pairs={{0,6},{1,7},{2,0},{3,1},{4,2},{5,3},{6,4},{7,5},{8,14},{9,15},{10,... | collective-permute-start | bytes 1572872 | tf_op jit(solution)/shard_map/ppermute | solution.py:92
  637.2 22.4 %collective-permute-start.44 = (bf16[64,4096]{1,0:T(8,128)(2,1)S(1)}, bf16[64,4096]{1,0:T(8,128)(2,1)S(1)}, u32[]{:S(2)}, u32[]{:S(2)}) collective-permute-start(bf16[64,4096]{1,0:T(8,128)(2,1)S(1)} %get-tuple-element.240), channel_id=1, source_target_pairs={{0,2},{1,3},{2,4},{3,5},{4,6},{5,7},{6,0},{7,1},{8,10},{9,11},{10,... | collective-permute-start | bytes 1572872 | tf_op jit(solution)/shard_map/ppermute | solution.py:92
  637.2 22.4 %collective-permute-start.45 = (bf16[64,4096]{1,0:T(8,128)(2,1)S(1)}, bf16[64,4096]{1,0:T(8,128)(2,1)S(1)}, u32[]{:S(2)}, u32[]{:S(2)}) collective-permute-start(bf16[64,4096]{1,0:T(8,128)(2,1)S(1)} %get-tuple-element.239), channel_id=1, source_target_pairs={{0,6},{1,7},{2,0},{3,1},{4,2},{5,3},{6,4},{7,5},{8,14},{9,15},{10,... | collective-permute-start | bytes 1572872 | tf_op jit(solution)/shard_map/ppermute | solution.py:92
  644.4 5.6 collective-permute-start.40
  660.6 23.5 %collective-permute-start.49 = (bf16[64,4096]{1,0:T(8,128)(2,1)}, bf16[64,4096]{1,0:T(8,128)(2,1)}, u32[]{:S(2)}, u32[]{:S(2)}) collective-permute-start(bf16[64,4096]{1,0:T(8,128)(2,1)} %add_convert_fusion.1), channel_id=1, source_target_pairs={{0,6},{1,7},{2,0},{3,1},{4,2},{5,3},{6,4},{7,5},{8,14},{9,15},{10,... | collective-permute-start | bytes 1572872 | tf_op jit(solution)/shard_map/ppermute | solution.py:92
  663.5 6.0 collective-permute-start.46
  665.9 18.2 %collective-permute-start.48 = (bf16[64,4096]{1,0:T(8,128)(2,1)}, bf16[64,4096]{1,0:T(8,128)(2,1)}, u32[]{:S(2)}, u32[]{:S(2)}) collective-permute-start(bf16[64,4096]{1,0:T(8,128)(2,1)} %add_convert_fusion.2), channel_id=1, source_target_pairs={{0,2},{1,3},{2,4},{3,5},{4,6},{5,7},{6,0},{7,1},{8,10},{9,11},{10,... | collective-permute-start | bytes 1572872 | tf_op jit(solution)/shard_map/ppermute | solution.py:92
  669.6 14.5 %collective-permute-start.47 = (f32[200,128]{1,0:T(8,128)S(1)}, f32[200,128]{1,0:T(8,128)S(1)}, u32[]{:S(2)}, u32[]{:S(2)}) collective-permute-start(f32[200,128]{1,0:T(8,128)S(1)} %maximum_bitcast_fusion), channel_id=1, source_target_pairs={{0,1},{1,0},{2,3},{3,2},{4,5},{5,4},{6,7},{7,6},{8,9},{9,8},{10,11... | collective-permute-start | bytes 307208 | tf_op jit(solution)/shard_map/ppermute | solution.py:175
  685.8 5.4 collective-permute-start.50
  691.2 6.2 collective-permute-start.51
  (46 other events, 372.3 us)
Sparse Core Ops, SparseCore 0:
  27.2 55.5 all-gather.16
  92.4 32.0 all-gather.8
  127.3 62.9 all-gather.18
  207.6 36.8 reduce-scatter.6
  248.1 30.9 all-gather.10
  293.2 38.8 reduce-scatter.8
  336.3 43.9 reduce-scatter.10
  390.9 28.6 reduce-scatter.12
  422.6 38.9 reduce-scatter.14
  470.8 28.3 reduce-scatter.16
  502.0 111.9 all-gather.12
  631.2 54.7 all-gather.14

commit v4 on v3

--- a/solution.py
+++ b/solution.py
@@ -1238,16 +1238,27 @@
     refs[-1][...] = tiles_to_rows(refs[:-1])
 
 
-def unpack_rows_kernel(tiles_ref, down_ref, mout_ref, aout_ref):
+def unpack_down(tiles, at):
+    width = D // LANES
+    base = at // width
+    return pl.pallas_call(
+        unpack_kernel,
+        grid=(FF_F // SHARD,),
+        in_specs=[pl.BlockSpec((NC, width, SLICE, LANES), lambda i: (0, base + i, 0, 0))],
+        out_specs=pl.BlockSpec((SHARD, D), lambda i: (i, 0)),
+        out_shape=shape_of((FF_F, D), F32),
+        compiler_params=PARAMS,
+        cost_estimate=cost(FF_F * D, 6 * FF_F * D),
+        name="unpack_down",
+    )(tiles)
+
+
+def unpack_out_kernel(tiles_ref, mout_ref, aout_ref):
     step = pl.program_id(0)
+    last = pl.num_programs(0) - 1
     rows = tiles_to_rows([tiles_ref])
-    last = pl.num_programs(0) - 1
-
-    @pl.when(step < FF_F // LANES)
-    def _():
-        down_ref[...] = rows
-
-    @pl.when((step >= FF_F // LANES) & (step < last))
+
+    @pl.when(step < last)
     def _():
         mout_ref[...] = rows
 
@@ -1256,31 +1267,26 @@
         aout_ref[...] = rows
 
 
-def unpack_rows(tiles, at):
+def unpack_out(tiles, at):
     width = D // LANES
     base = at // width
-    downs, outs = FF_F // LANES, INNER_F // LANES
-
-    def rows(index):
-        return pl.BlockSpec((LANES, D), index)
-
-    return pl.pallas_call(
-        unpack_rows_kernel,
-        grid=((FF_F + OUT_ROWS) // LANES,),
+    outs = INNER_F // LANES
+    return pl.pallas_call(
+        unpack_out_kernel,
+        grid=(OUT_ROWS // LANES,),
         in_specs=[
             pl.BlockSpec(
                 (NC // 2, width, SLICE, LANES), lambda i: (i % 2, base + i // 2, 0, 0)
             )
         ],
         out_specs=[
-            rows(lambda i: (jnp.minimum(i, downs - 1), 0)),
-            rows(lambda i: (jnp.clip(i - downs, 0, outs - 1), 0)),
-            rows(lambda i: (0, 0)),
-        ],
-        out_shape=[shape_of((FF_F, D), F32), shape_of((INNER_F, D), F32), shape_of((HDIM, D), F32)],
-        compiler_params=PARAMS,
-        cost_estimate=cost((FF_F + OUT_ROWS) * D, 6 * (FF_F + OUT_ROWS) * D),
-        name="unpack_rows",
+            pl.BlockSpec((LANES, D), lambda i: (jnp.minimum(i, outs - 1), 0)),
+            pl.BlockSpec((LANES, D), lambda i: (0, 0)),
+        ],
+        out_shape=[shape_of((INNER_F, D), F32), shape_of((HDIM, D), F32)],
+        compiler_params=PARAMS,
+        cost_estimate=cost(OUT_ROWS * D, 6 * OUT_ROWS * D),
+        name="unpack_out",
     )(tiles)
 
 
@@ -1589,26 +1595,21 @@
     )
     dx, d_mixers = together(dx, d_mixers)
     down_at = NF * gu_tiles
-    out_at = down_at + row_tiles
     gu_part = swap_fsdp(sum_gu.reshape(NF, -1, LANES))
     dbc_joined, gu_part = together(dbc_joined, gu_part)
+    all_one = all_ctx([gu_part.reshape(-1, LANES), sum_down])
     dbc_own, attn_pack, sum_two = together(
         ring_scatter(dbc_joined), attn_bwd(odd, attn_got, d_mixers, lse), sum_two
     )
-    sum_two = scatter_ctx(sum_two, along_x)
     attn_back = swap_ctx(attn_pack)
     mix_pack, g_taps, g_heads = front_back(
         mix_got, taps, heads_in, row_terms, drow, dx, dbc_own
     )
-    mix_pack, attn_back, sum_two = together(mix_pack, attn_back, sum_two)
-    all_one = all_ctx(
-        [
-            gu_part.reshape(-1, LANES),
-            sum_down,
-            sum_two[: row_tiles * SLICE],
-        ]
-    )
-    mix_back, d_qkv = together(swap_ctx(mix_pack), attn_grads(attn_back, cosine, sine))
+    mix_pack, attn_back = together(mix_pack, attn_back)
+    mix_back, d_qkv, sum_two = together(
+        swap_ctx(mix_pack), attn_grads(attn_back, cosine, sine), sum_two
+    )
+    sum_two = scatter_ctx(sum_two, along_x)
     d_mix = mix_grads(mix_back)
     packed_mix, dz = together(column_grad(normed, d_mix, d_qkv).reshape(NC, -1, LANES), dz)
     mine, other, gain_sum = back_project(spot, d_mix, d_qkv, dz, normed, w_one)
@@ -1617,9 +1618,13 @@
     def joined(mine, other):
         return ring_join(mine.reshape(NZ * ROWS, D), other.reshape(NZ * ROWS, D))
 
-    mine, down_other = together(mine, down_other)
-    got_mix, d_normed, down = together(
-        swap_ctx(packed_mix), joined(mine, other), joined(down_mine, down_other)
+    mine, down_other, all_one = together(mine, down_other, all_one)
+    got_mix, d_normed, down, g_gate_up, g_down = together(
+        swap_ctx(packed_mix),
+        joined(mine, other),
+        joined(down_mine, down_other),
+        unpack_gate_up(all_one),
+        unpack_down(all_one, down_at),
     )
     columns = swap_fsdp(
         jnp.concatenate(
@@ -1653,8 +1658,9 @@
     own_pad = -(-own_size // LANES) * LANES
     own = jnp.concatenate([own, jnp.zeros((own_pad - own_size,), F32), g_mlp_gain, g_norm_gain])
 
-    own, columns, all_one = together(own.reshape(-1, LANES), columns, all_one)
-    all_two = all_ctx([columns.reshape(-1, LANES)])
+    own, columns = together(own.reshape(-1, LANES), columns)
+    out_at = NF * W1_COLS // LANES
+    all_two = all_ctx([columns.reshape(-1, LANES), sum_two[: row_tiles * SLICE]])
     both = jnp.concatenate([d_normed, down], axis=1)
     own, *both = together(butterfly(own, "ctx", (1, 2, 4)), *ring_first(both))
     own = butterfly(own, "ctx", (8,)).reshape(-1)
@@ -1665,18 +1671,13 @@
     d_normed, down = both[:, :D], both[:, D:]
     output = even_first((mixed + down).astype(BF)).reshape(tokens.shape)
 
-    g_gate_up = unpack_gate_up(all_one)
-    g_down, g_mout, g_aout = unpack_rows(all_one, down_at)
-    total = butterfly(total, "fsdp", (2,))
-    total, g_gate_up, g_down, g_mout, g_aout = together(
-        total, g_gate_up, g_down, g_mout, g_aout
-    )
+    g_mout, g_aout = unpack_out(all_two, out_at)
     g_qkv = unpack_qkv(all_two)
     g_in = unpack_in(all_two).T
     d_hidden, _ = norm_back(hidden, scale_one, norm_gain, d_normed)
     d_tokens = even_first((d_hidden + d_mixed).astype(BF)).reshape(tokens.shape)
 
-    total = butterfly(total, "fsdp", (4,)).reshape(-1)
+    total = butterfly(total, "fsdp", (2, 4)).reshape(-1)
     each = total[: NF * own_pad].reshape(NF, own_pad)
     cut = [(CONV_K + 1) * INNER_F]
     cut.append(cut[0] + (CONV_K + 1) * BC_F)

time: 731 us -> 736 us (level)
    all_to_all x9, waiting for transfers between devices: 85.6 us -> 54 us  [swap_ctx(): return lax.all_to_all(value, 'ctx', 0, 0, tiled=True)]
    reduce_scatter x4, waiting for transfers between devices: 15.6 us -> 43.1 us  [scatter_ctx(): lax.psum_scatter(joined, 'ctx', scatter_dimension=0, axis_index_groups=gr...]
  transfers between devices with their start and end apart: 76 -> 76, of which waited for: 35 -> 37; matrix products, arithmetic and copies ran while one was open for 10% -> 9% of each run, Pallas kernels for 23% -> 22%
where the time goes in v4:
time: 736 us; the launch traced here: 724 us
  waiting for transfers between devices  281 us (38%)
  Pallas kernels  206 us (28%)
  starting transfers between devices  114 us (15%)
  local copies, waits for them, and re-layouts  44.4 us (6%)
  other arithmetic  44.1 us (6%)
  between operations  20.9 us (3%)
  blocking collectives  13.5 us (2%)
    all_to_all x9, starting transfers between devices, swap_ctx(): return lax.all_to_all(value, 'ctx', 0, 0, tiled=True)  57.9 us
    all_to_all x9, waiting for transfers between devices, swap_ctx(): return lax.all_to_all(value, 'ctx', 0, 0, tiled=True)  54 us
    ppermute x39, waiting for transfers between devices, send(): return lax.ppermute(value, 'fsdp', route)  50.7 us
    reduce_scatter x2, waiting for transfers between devices, scatter_fsdp(): lax.psum_scatter(parts, 'fsdp', scatter_dimension=0, tiled=True).astype(F32)  45.6 us
    reduce_scatter x4, waiting for transfers between devices, scatter_ctx(): lax.psum_scatter(joined, 'ctx', scatter_dimension=0, axis_index_groups=gr...  43.1 us
    ppermute x39, starting transfers between devices, send(): return lax.ppermute(value, 'fsdp', route)  39.8 us
    ppermute x13, waiting for transfers between devices, exchange(): lax.ppermute(value, axis, [(i, i ^ bit) for i in range(size)])  38.8 us
    pallas_call x5, Pallas kernels, column_grad(): pl.pallas_call(functools.partial(column_grad_kernel, by_y), grid=(count /...  35.4 us
  transfers between devices with their start and end apart: 76, of which 37 were waited for; matrix products, arithmetic and copies ran while one was open for 9% of the time, Pallas kernels for 22%

profile of v4, /device:TPU:16, one launch (start us, length us, event | category | flops | bytes accessed | tf_op | source)
XLA Modules:
  0.0 723.5 jit_solution(15624914009438757574)
XLA Ops:
  13.6 13.5 %all_to_all.65 = bf16[8,16,1280]{2,1,0:T(8,128)(2,1)} all-to-all(bf16[8,16,1280]{2,1,0:T(8,128)(2,1)S(1)} %copy.115), channel_id=1, replica_groups=mesh['ctx'=16,'fsdp'=8] {'fsdp'}, dimensions={0} | all-to-all | bytes 655360 | tf_op jit(solution)/shard_map/all_to_all | solution.py:170
  42.3 3.6 collective-permute-done
  57.6 8.5 %collective-permute-done.3 = bf16[64,2048]{1,0:T(8,128)(2,1)S(1)} collective-permute-done((bf16[64,2048]{1,0:T(8,128)(2,1)S(1)}, bf16[64,2048]{1,0:T(8,128)(2,1)S(1)}, u32[]{:S(2)}, u32[]{:S(2)}) %collective-permute-start.3) | collective-permute-done | bytes 262176 | tf_op jit(solution)/shard_map/ppermute | solution.py:92
  71.2 11.6 %all-gather.17.cloned.1.call-done = bf16[128,16,1280]{2,1,0:T(8,128)(2,1)} async-done(((bf16[8,16,1280]{2,1,0:T(8,128)(2,1)}), bf16[128,16,1280]{2,1,0:T(8,128)(2,1)}) %all-gather.17.cloned.1.call-update) | async-done | bytes 5242896 | tf_op jit(solution)/shard_map/all_gather | solution.py:1478
  82.8 9.4 %project.1 = (bf16[16,272,128]{2,1,0:T(8,128)(2,1)}, bf16[16,320,128]{2,1,0:T(8,128)(2,1)}) custom-call(bf16[1024,2048]{1,0:T(8,128)(2,1)} %constant_dynamic-update-slice_fusion.27.n_ref.left_ref, bf16[16,8,16,1280]{3,2,1,0:T(8,128)(2,1)} %bitcast.161, f32[128,64]{1,0:T(8,128)} %get-tuple-element.254.cos_ref, f32[128,64]{1,0:T(8,128)} %get-tuple-element.253.sin_ref), custom_call_target="tpu_custom_call" | custom-call | flops 3758096384 | bytes 10000000 | tf_op jit(solution)/shard_map/project/pallas_call | solution.py:234
  92.4 5.7 all-to-all-start.2
  99.6 7.8 %project_z.1.z_ref = f32[8,384,128]{2,1,0:T(8,128)} custom-call(bf16[1024,2048]{1,0:T(8,128)(2,1)} %constant_dynamic-update-slice_fusion.27.n_ref.left_ref, bf16[16,8,16,1280]{3,2,1,0:T(8,128)(2,1)} %bitcast.162), custom_call_target="tpu_custom_call" | custom-call | flops 1610612736 | bytes 8000000 | tf_op jit(solution)/shard_map/project_z/pallas_call | solution.py:265
  107.3 6.6 all-to-all-done.2.got_ref
  115.0 6.4 front.1
  126.2 6.2 all-to-all-start.3
  142.7 8.5 %mamba_fwd.1 = (bf16[16,192,128]{2,1,0:T(8,128)(2,1)}, f32[8,192,256]{2,1,0:T(8,128)}) custom-call(s32[8]{0:T(128)} %fusion.13.place_ref, bf16[192,2048]{1,0:T(8,128)(2,1)} %get-tuple-element.128.x_ref, bf16[8,64,2048]{2,1,0:T(8,128)(2,1)} %bitcast.207, f32[16,2048]{1,0:T(8,128)} %get-tuple-element.132.row_ref, f32[192,1]{1,0:T(8,128)} %broadcast_in_dim_reshape.4.skip_ref), custom_call_target="tpu_custom_call" | custom-call | flops 872415232 | bytes 7000000 | tf_op jit(solution)/shard_map/mamba_fwd/pallas_call | solution.py:954
  151.1 4.3 all-to-all-done.3.q_ref.k_ref.v_ref
  155.4 6.2 all-to-all-start.4
  161.6 9.2 %attn_fwd.1 = (bf16[16,64,128]{2,1,0:T(8,128)(2,1)}, f32[1024,1]{1,0:T(8,128)}) custom-call(s32[1]{0:T(128)} %bitcast.31.odd_ref, bf16[16,320,128]{2,1,0:T(8,128)(2,1)} %copy-done.11, bf16[16,320,128]{2,1,0:T(8,128)(2,1)} %copy-done.11, bf16[16,320,128]{2,1,0:T(8,128)(2,1)} %copy-done.11), custom_call_target="tpu_custom_call" | custom-call | flops 1073741824 | bytes 3000000 | tf_op jit(solution)/shard_map/attn_fwd/pallas_call | solution.py:1156
  170.7 8.8 %all-to-all-done.4.got_ref = bf16[16,192,128]{2,1,0:T(8,128)(2,1)S(1)} async-done(((bf16[16,192,128]{2,1,0:T(8,128)(2,1)}), bf16[16,192,128]{2,1,0:T(8,128)(2,1)S(1)}, u32[]{:S(2)}, u32[]{:S(2)}) %all-to-all-start.4) | async-done | bytes 786464 | tf_op jit(solution)/shard_map/all_to_all | solution.py:166
  183.2 6.3 all-to-all-start.5
  200.3 7.2 branch_out.1
  207.5 37.0 %reduce-scatter.7.cloned.1.call-done = bf16[128,2048]{1,0:T(8,128)(2,1)} async-done(((bf16[1024,2048]{1,0:T(8,128)(2,1)}), bf16[128,2048]{1,0:T(8,128)(2,1)}) %reduce-scatter.7.cloned.1.call-update) | async-done | bytes 524304 | tf_op jit(solution)/shard_map/reduce_scatter | solution.py:100
  248.0 6.5 act_back.1.d_act_ref
  254.5 24.6 %all-gather.11.cloned.1.call-done.n_ref.left_ref = bf16[1024,2048]{1,0:T(8,128)(2,1)} async-done(((bf16[128,2048]{1,0:T(8,128)(2,1)}), bf16[1024,2048]{1,0:T(8,128)(2,1)}) %all-gather.11.cloned.1.call-update) | async-done | bytes 4194320 | tf_op jit(solution)/shard_map/all_gather | solution.py:96
  279.1 13.9 %mlp.1 = (bf16[1024,512]{1,0:T(8,128)(2,1)}, bf16[1024,1024]{1,0:T(8,128)(2,1)}, bf16[1024,2048]{1,0:T(8,128)(2,1)}) custom-call(bf16[1024,2048]{1,0:T(8,128)(2,1)} %all-gather.11.cloned.1.call-done.n_ref.left_ref, f32[1024,512]{1,0:T(8,128)} %act_back.1.d_act_ref, bf16[16,8,16,1024]{3,2,1,0:T(8,128)(2,1)} %bitcast.213), custom_call_target="tpu_custom_call" | custom-call | flops 8589934592 | bytes 20000000 | tf_op jit(solution)/shard_map/mlp/pallas_call | solution.py:606
  293.0 6.3 column_grad.6
  299.4 7.4 %all-to-all-start.6 = ((bf16[16,512,128]{2,1,0:T(8,128)(2,1)}), bf16[16,512,128]{2,1,0:T(8,128)(2,1)}, u32[]{:S(2)}, u32[]{:S(2)}) async-start(bf16[16,512,128]{2,1,0:T(8,128)(2,1)} %bitcast.171), calls=%async_computation.8 | async-start | bytes 4194304 | tf_op jit(solution)/shard_map/all_to_all | solution.py:166
  307.9 7.0 down_out.1
  314.9 8.5 %column_grad.5 = bf16[16,8,8,16,128]{4,3,2,1,0:T(8,128)(2,1)} custom-call(bf16[1024,2048]{1,0:T(8,128)(2,1)} %all-gather.11.cloned.1.call-done.n_ref.left_ref, bf16[1024,1024]{1,0:T(8,128)(2,1)} %get-tuple-element.154.refs_0_), custom_call_target="tpu_custom_call" | custom-call | flops 4294967296 | bytes 10485760 | tf_op jit(solution)/shard_map/column_grad/pallas_call | solution.py:401
  323.4 8.6 %reduce-scatter.9.cloned.1.call-done = bf16[128,2048]{1,0:T(8,128)(2,1)} async-done(((bf16[1024,2048]{1,0:T(8,128)(2,1)}), bf16[128,2048]{1,0:T(8,128)(2,1)}) %reduce-scatter.9.cloned.1.call-update) | async-done | bytes 524304 | tf_op jit(solution)/shard_map/reduce_scatter | solution.py:100
  341.2 9.9 %collective-permute-done.19 = bf16[128,2048]{1,0:T(8,128)(2,1)S(1)} collective-permute-done((bf16[128,2048]{1,0:T(8,128)(2,1)S(1)}, bf16[128,2048]{1,0:T(8,128)(2,1)S(1)}, u32[]{:S(2)}, u32[]{:S(2)}) %collective-permute-start.19) | collective-permute-done | bytes 524320 | tf_op jit(solution)/shard_map/ppermute | solution.py:92
  353.9 3.6 collective-permute-done.20
  357.6 5.5 collective-permute-done.22
  367.3 7.1 branch_back.1
  376.5 3.6 collective-permute-done.28
  380.1 5.1 collective-permute-done.29
  385.8 4.9 gate_back.1
  390.7 7.2 all-to-all-start.7
  398.1 6.2 column_grad.7
  404.3 6.1 column_grad.8
  410.4 3.6 pad_maximum_fusion
  414.0 5.6 reduce-scatter.13.cloned.1.call-done
  419.6 14.3 %mamba_bwd.1 = (f32[192,2048]{1,0:T(8,128)}, bf16[4,64,2048]{2,1,0:T(8,128)(2,1)}, bf16[4,64,2048]{2,1,0:T(8,128)(2,1)}, f32[8,2048]{1,0:T(8,128)}, f32[192,1]{1,0:T(8,128)}) custom-call(s32[8]{0:T(128)} %fusion.13.place_ref, bf16[192,2048]{1,0:T(8,128)(2,1)} %get-tuple-element.128.x_ref, bf16[16,256,128]{2,1,0:T(8,128)(2,1)} %all-to-all-done.7.got_ref.do_ref, ...), custom_call_target="tpu_custom_call" | custom-call | flops 2214592512 | bytes 12000000 | tf_op jit(solution)/shard_map/mamba_bwd/pallas_call | solution.py:1085
  442.4 4.5 all-to-all-done.8
  460.1 11.6 %attn_bwd.1 = bf16[16,320,128]{2,1,0:T(8,128)(2,1)} custom-call(s32[1]{0:T(128)} %bitcast.31.odd_ref, bf16[16,320,128]{2,1,0:T(8,128)(2,1)} %copy-done.11, bf16[16,320,128]{2,1,0:T(8,128)(2,1)} %copy-done.11, bf16[16,320,128]{2,1,0:T(8,128)(2,1)} %copy-done.11, bf16[16,256,128]{2,1,0:T(8,128)(2,1)} %all-to-all-done.7.got_ref.do_ref, ...), custom_call_target="tpu_custom_call" | custom-call | flops 2684354560 | bytes 4000000 | tf_op jit(solution)/shard_map/attn_bwd/pallas_call | solution.py:1208
  473.5 5.4 all-to-all-start.9
  478.9 11.0 %front_back.1 = (bf16[16,272,128]{2,1,0:T(8,128)(2,1)}, f32[256,8]{1,0:T(8,128)}, f32[8,1]{1,0:T(8,128)}) custom-call(bf16[16,272,128]{2,1,0:T(8,128)(2,1)} %copy-done.3, f32[256,8]{1,0:T(8,128)} %bitcast.176, f32[8,128]{1,0:T(8,128)} %broadcast_in_dim.71.heads_ref, f32[16,2048]{1,0:T(8,128)} %get-tuple-element.132.row_ref, ...), custom_call_target="tpu_custom_call" | custom-call | flops 31457280 | bytes 9000000 | tf_op jit(solution)/shard_map/front_back/pallas_call | solution.py:849
  489.9 10.1 %all-to-all-done.9.got_ref = bf16[16,320,128]{2,1,0:T(8,128)(2,1)} async-done(((bf16[16,320,128]{2,1,0:T(8,128)(2,1)}), bf16[16,320,128]{2,1,0:T(8,128)(2,1)}, u32[]{:S(2)}, u32[]{:S(2)}) %all-to-all-start.9) | async-done | bytes 1310752 | tf_op jit(solution)/shard_map/all_to_all | solution.py:166
  500.0 7.2 all-to-all-start.10
  507.1 4.2 attn_grads.1.refs_1_.dqkv_ref
  511.3 21.2 %all-to-all-done.10.got_ref = bf16[16,272,128]{2,1,0:T(8,128)(2,1)} async-done(((bf16[16,272,128]{2,1,0:T(8,128)(2,1)}), bf16[16,272,128]{2,1,0:T(8,128)(2,1)}, u32[]{:S(2)}, u32[]{:S(2)}) %all-to-all-start.10) | async-done | bytes 1114144 | tf_op jit(solution)/shard_map/all_to_all | solution.py:166
  532.5 3.6 mix_grads.1.refs_0_.mix_ref
  536.2 8.2 %column_grad.9 = bf16[16,8,7,16,128]{4,3,2,1,0:T(8,128)(2,1)} custom-call(bf16[1024,2048]{1,0:T(8,128)(2,1)} %constant_dynamic-update-slice_fusion.27.n_ref.left_ref, bf16[1024,512]{1,0:T(8,128)(2,1)} %mix_grads.1.refs_0_.mix_ref, bf16[1024,384]{1,0:T(8,128)(2,1)} %attn_grads.1.refs_1_.dqkv_ref), custom_call_target="tpu_custom_call" | custom-call | flops 3758096384 | bytes 9699328 | tf_op jit(solution)/shard_map/column_grad/pallas_call | solution.py:401
  544.4 6.4 all-to-all-start.11
  550.9 11.8 %back_project.1 = (bf16[4,128,2048]{2,1,0:T(8,128)(2,1)}, bf16[4,128,2048]{2,1,0:T(8,128)(2,1)}, f32[1,2048]{1,0:T(1,128)}) custom-call(s32[5]{0:T(128)} %pad_add_fusion.1.spot_ref, bf16[1024,512]{1,0:T(8,128)(2,1)} %mix_grads.1.refs_0_.mix_ref, bf16[1024,384]{1,0:T(8,128)(2,1)} %attn_grads.1.refs_1_.dqkv_ref, ...), custom_call_target="tpu_custom_call" | custom-call | flops 5368709120 | bytes 18000000 | tf_op jit(solution)/shard_map/back_project/pallas_call | solution.py:356
  564.1 37.5 %reduce-scatter.17.cloned.1.call-done = bf16[1,896,128]{2,1,0:T(8,128)(2,1)} async-done(((bf16[4,896,128]{2,1,0:T(8,128)(2,1)}), bf16[1,896,128]{2,1,0:T(8,128)(2,1)}) %reduce-scatter.17.cloned.1.call-update) | async-done | bytes 229392 | tf_op jit(solution)/shard_map/reduce_scatter | solution.py:1555
  605.9 6.0 unpack_gate_up.1
  612.0 4.0 fusion.1
  615.9 3.8 fusion
  623.2 4.5 all-to-all-start.12
  628.2 7.7 %all-to-all-done.12 = bf16[8,160,128]{2,1,0:T(8,128)(2,1)S(1)} async-done(((bf16[8,160,128]{2,1,0:T(8,128)(2,1)}), bf16[8,160,128]{2,1,0:T(8,128)(2,1)S(1)}, u32[]{:S(2)}, u32[]{:S(2)}) %all-to-all-start.12) | async-done | bytes 327712 | tf_op jit(solution)/shard_map/all_to_all | solution.py:170
  650.9 4.8 collective-permute-done.40
  659.5 5.7 collective-permute-done.44
  671.6 3.6 collective-permute-done.46
  679.0 5.5 collective-permute-done.48
  692.8 5.0 collective-permute-done.51
  702.6 6.3 unpack_in.1
  708.9 4.6 unpack_out.1
  (384 shorter events, 166.4 us)
Async XLA Ops:
  7.2 75.7 %all-gather.17.cloned.1.call-start = ((), (), s32[]{:S(2)}) async-start(), calls=%async_computation.29 | async-start | bytes 5570560 | tf_op jit(solution)/shard_map/all_gather | solution.py:1478
  32.3 13.6 %collective-permute-start = (bf16[128,2048]{1,0:T(8,128)(2,1)S(1)}, bf16[128,2048]{1,0:T(8,128)(2,1)S(1)}, u32[]{:S(2)}, u32[]{:S(2)}) collective-permute-start(bf16[128,2048]{1,0:T(8,128)(2,1)S(1)} %get-tuple-element.266), channel_id=1, source_target_pairs={{0,6},{1,7},{2,0},{3,1},{4,2},{5,3},{6,4},{7,5},{8,14},{9,15},{10,... | collective-permute-start | bytes 1572872 | tf_op jit(solution)/shard_map/ppermute | solution.py:92
  33.5 19.9 %collective-permute-start.2 = (bf16[128,2048]{1,0:T(8,128)(2,1)S(1)}, bf16[128,2048]{1,0:T(8,128)(2,1)S(1)}, u32[]{:S(2)}, u32[]{:S(2)}) collective-permute-start(bf16[128,2048]{1,0:T(8,128)(2,1)S(1)} %get-tuple-element.266), channel_id=1, source_target_pairs={{0,2},{1,3},{2,4},{3,5},{4,6},{5,7},{6,0},{7,1},{8,10},{9,11},{10,... | collective-permute-start | bytes 1572872 | tf_op jit(solution)/shard_map/ppermute | solution.py:92
  34.3 33.5 %collective-permute-start.4 = (bf16[128,2048]{1,0:T(8,128)(2,1)S(1)}, bf16[128,2048]{1,0:T(8,128)(2,1)S(1)}, u32[]{:S(2)}, u32[]{:S(2)}) collective-permute-start(bf16[128,2048]{1,0:T(8,128)(2,1)S(1)} %get-tuple-element.266), channel_id=1, source_target_pairs={{0,1},{1,0},{2,3},{3,2},{4,5},{5,4},{6,7},{7,6},{8,9},{9,8},{10,11... | collective-permute-start | bytes 1572872 | tf_op jit(solution)/shard_map/ppermute | solution.py:92
  46.6 10.0 %collective-permute-start.1 = (bf16[64,2048]{1,0:T(8,128)(2,1)}, bf16[64,2048]{1,0:T(8,128)(2,1)}, u32[]{:S(2)}, u32[]{:S(2)}) collective-permute-start(bf16[64,2048]{1,0:T(8,128)(2,1)} %slice.284), channel_id=1, source_target_pairs={{0,6},{1,7},{2,0},{3,1},{4,2},{5,3},{6,4},{7,5},{8,14},{9,15},{10,... | collective-permute-start | bytes 786440 | tf_op jit(solution)/shard_map/ppermute | solution.py:92
  49.9 21.3 %all-to-all-start.1 = ((bf16[8,16,1024]{2,1,0:T(8,128)(2,1)}), bf16[8,16,1024]{2,1,0:T(8,128)(2,1)S(1)}, u32[]{:S(2)}, u32[]{:S(2)}) async-start(bf16[8,16,1024]{2,1,0:T(8,128)(2,1)} %copy.116), calls=%async_computation.1 | async-start | bytes 524288 | tf_op jit(solution)/shard_map/all_to_all | solution.py:170
  53.3 102.1 %all-gather.9.cloned.1.call-start = ((), (), s32[]{:S(2)}) async-start(), calls=%async_computation.19 | async-start | bytes 4718592 | tf_op jit(solution)/shard_map/all_gather | solution.py:96
  53.4 12.7 %collective-permute-start.3 = (bf16[64,2048]{1,0:T(8,128)(2,1)S(1)}, bf16[64,2048]{1,0:T(8,128)(2,1)S(1)}, u32[]{:S(2)}, u32[]{:S(2)}) collective-permute-start(bf16[64,2048]{1,0:T(8,128)(2,1)S(1)} %slice.285), channel_id=1, source_target_pairs={{0,2},{1,3},{2,4},{3,5},{4,6},{5,7},{6,0},{7,1},{8,10},{9,11},{10,... | collective-permute-start | bytes 786440 | tf_op jit(solution)/shard_map/ppermute | solution.py:92
  55.3 13.4 %collective-permute-start.5 = (bf16[128,2048]{1,0:T(8,128)(2,1)S(1)}, bf16[128,2048]{1,0:T(8,128)(2,1)S(1)}, u32[]{:S(2)}, u32[]{:S(2)}) collective-permute-start(bf16[128,2048]{1,0:T(8,128)(2,1)S(1)} %collective-permute-done), channel_id=1, source_target_pairs={{0,1},{1,0},{2,3},{3,2},{4,5},{5,4},{6,7},{7,6},{8,9},{9,8},{10,11... | collective-permute-start | bytes 1572872 | tf_op jit(solution)/shard_map/ppermute | solution.py:92
  55.3 15.0 %collective-permute-start.7 = (bf16[128,2048]{1,0:T(8,128)(2,1)S(1)}, bf16[128,2048]{1,0:T(8,128)(2,1)S(1)}, u32[]{:S(2)}, u32[]{:S(2)}) collective-permute-start(bf16[128,2048]{1,0:T(8,128)(2,1)S(1)} %collective-permute-done.2), channel_id=1, source_target_pairs={{0,1},{1,0},{2,3},{3,2},{4,5},{5,4},{6,7},{7,6},{8,9},{9,8},{10,11... | collective-permute-start | bytes 1572872 | tf_op jit(solution)/shard_map/ppermute | solution.py:92
  92.4 21.5 %all-to-all-start.2 = ((bf16[16,272,128]{2,1,0:T(8,128)(2,1)}), bf16[16,272,128]{2,1,0:T(8,128)(2,1)S(1)}, u32[]{:S(2)}, u32[]{:S(2)}) async-start(bf16[16,272,128]{2,1,0:T(8,128)(2,1)} %get-tuple-element.124), calls=%async_computation.2 | async-start | bytes 2228224 | tf_op jit(solution)/shard_map/all_to_all | solution.py:166
  98.2 101.4 %all-gather.19.cloned.1.call-start = ((), (), s32[]{:S(2)}) async-start(), calls=%async_computation.30 | async-start | bytes 4456448 | tf_op jit(solution)/shard_map/all_gather | solution.py:1522
  121.4 11.0 %collective-permute-start.10 = (bf16[64,2048]{1,0:T(8,128)(2,1)}, bf16[64,2048]{1,0:T(8,128)(2,1)S(1)}, u32[]{:S(2)}, u32[]{:S(2)}) collective-permute-start(bf16[64,2048]{1,0:T(8,128)(2,1)} %get-tuple-element.131), channel_id=1, source_target_pairs={{0,2},{1,3},{2,4},{3,5},{4,6},{5,7},{6,0},{7,1},{8,10},{9,11},{10,... | collective-permute-start | bytes 786440 | tf_op jit(solution)/shard_map/ppermute | solution.py:92
  123.0 10.1 %collective-permute-start.8 = (bf16[64,2048]{1,0:T(8,128)(2,1)}, bf16[64,2048]{1,0:T(8,128)(2,1)S(1)}, u32[]{:S(2)}, u32[]{:S(2)}) collective-permute-start(bf16[64,2048]{1,0:T(8,128)(2,1)} %get-tuple-element.131), channel_id=1, source_target_pairs={{0,6},{1,7},{2,0},{3,1},{4,2},{5,3},{6,4},{7,5},{8,14},{9,15},{10,... | collective-permute-start | bytes 786440 | tf_op jit(solution)/shard_map/ppermute | solution.py:92
  126.2 13.6 %collective-permute-start.12 = (bf16[64,2048]{1,0:T(8,128)(2,1)}, bf16[64,2048]{1,0:T(8,128)(2,1)S(1)}, u32[]{:S(2)}, u32[]{:S(2)}) collective-permute-start(bf16[64,2048]{1,0:T(8,128)(2,1)} %get-tuple-element.131), channel_id=1, source_target_pairs={{0,1},{1,0},{2,3},{3,2},{4,5},{5,4},{6,7},{7,6},{8,9},{9,8},{10,11... | collective-permute-start | bytes 786440 | tf_op jit(solution)/shard_map/ppermute | solution.py:92
  126.2 29.2 %all-to-all-start.3 = ((bf16[16,320,128]{2,1,0:T(8,128)(2,1)}), bf16[16,320,128]{2,1,0:T(8,128)(2,1)S(1)}, u32[]{:S(2)}, u32[]{:S(2)}) async-start(bf16[16,320,128]{2,1,0:T(8,128)(2,1)} %get-tuple-element.134), calls=%async_computation.3 | async-start | bytes 2621440 | tf_op jit(solution)/shard_map/all_to_all | solution.py:166
  132.5 7.1 collective-permute-start.11
  133.2 6.5 collective-permute-start.9
  136.1 5.2 collective-permute-start.15
  155.4 24.2 %all-to-all-start.4 = ((bf16[16,192,128]{2,1,0:T(8,128)(2,1)}), bf16[16,192,128]{2,1,0:T(8,128)(2,1)S(1)}, u32[]{:S(2)}, u32[]{:S(2)}) async-start(bf16[16,192,128]{2,1,0:T(8,128)(2,1)} %get-tuple-element.136), calls=%async_computation.4 | async-start | bytes 1572864 | tf_op jit(solution)/shard_map/all_to_all | solution.py:166
  183.2 6.3 collective-permute-start.16
  183.2 16.3 %all-to-all-start.5 = ((bf16[16,64,128]{2,1,0:T(8,128)(2,1)}), bf16[16,64,128]{2,1,0:T(8,128)(2,1)S(1)}, u32[]{:S(2)}, u32[]{:S(2)}) async-start(bf16[16,64,128]{2,1,0:T(8,128)(2,1)} %get-tuple-element.139), calls=%async_computation.5 | async-start | bytes 524288 | tf_op jit(solution)/shard_map/all_to_all | solution.py:166
  189.5 55.0 %reduce-scatter.7.cloned.1.call-start = ((), (), s32[]{:S(2)}) async-start(), calls=%async_computation.20 | async-start | bytes 4718592 | tf_op jit(solution)/shard_map/reduce_scatter | solution.py:100
  193.8 5.1 collective-permute-start.18
  207.5 71.6 %all-gather.11.cloned.1.call-start = ((), (), s32[]{:S(2)}) async-start(), calls=%async_computation.21 | async-start | bytes 4718592 | tf_op jit(solution)/shard_map/all_gather | solution.py:96
  247.9 84.1 %reduce-scatter.9.cloned.1.call-start = ((), (), s32[]{:S(2)}) async-start(), calls=%async_computation.22 | async-start | bytes 4718592 | tf_op jit(solution)/shard_map/reduce_scatter | solution.py:100
  299.4 36.8 %all-to-all-start.6 = ((bf16[16,512,128]{2,1,0:T(8,128)(2,1)}), bf16[16,512,128]{2,1,0:T(8,128)(2,1)}, u32[]{:S(2)}, u32[]{:S(2)}) async-start(bf16[16,512,128]{2,1,0:T(8,128)(2,1)} %bitcast.171), calls=%async_computation.8 | async-start | bytes 4194304 | tf_op jit(solution)/shard_map/all_to_all | solution.py:166
  306.7 84.0 %reduce-scatter.11.cloned.1.call-start = ((), (), s32[]{:S(2)}) async-start(), calls=%async_computation.23 | async-start | bytes 5242880 | tf_op jit(solution)/shard_map/reduce_scatter | solution.py:1555
  336.2 83.4 %reduce-scatter.13.cloned.1.call-start = ((), (), s32[]{:S(2)}) async-start(), calls=%async_computation.24 | async-start | bytes 1310720 | tf_op jit(solution)/shard_map/reduce_scatter | solution.py:1555
  339.1 12.0 %collective-permute-start.19 = (bf16[128,2048]{1,0:T(8,128)(2,1)S(1)}, bf16[128,2048]{1,0:T(8,128)(2,1)S(1)}, u32[]{:S(2)}, u32[]{:S(2)}) collective-permute-start(bf16[128,2048]{1,0:T(8,128)(2,1)S(1)} %get-tuple-element.268), channel_id=1, source_target_pairs={{0,6},{1,7},{2,0},{3,1},{4,2},{5,3},{6,4},{7,5},{8,14},{9,15},{10,... | collective-permute-start | bytes 1572872 | tf_op jit(solution)/shard_map/ppermute | solution.py:92
  340.0 13.1 %collective-permute-start.21 = (bf16[128,2048]{1,0:T(8,128)(2,1)S(1)}, bf16[128,2048]{1,0:T(8,128)(2,1)S(1)}, u32[]{:S(2)}, u32[]{:S(2)}) collective-permute-start(bf16[128,2048]{1,0:T(8,128)(2,1)S(1)} %get-tuple-element.268), channel_id=1, source_target_pairs={{0,2},{1,3},{2,4},{3,5},{4,6},{5,7},{6,0},{7,1},{8,10},{9,11},{10,... | collective-permute-start | bytes 1572872 | tf_op jit(solution)/shard_map/ppermute | solution.py:92
  351.1 6.4 collective-permute-start.20
  353.1 10.3 %collective-permute-start.23 = (bf16[128,2048]{1,0:T(8,128)(2,1)S(1)}, bf16[128,2048]{1,0:T(8,128)(2,1)S(1)}, u32[]{:S(2)}, u32[]{:S(2)}) collective-permute-start(bf16[128,2048]{1,0:T(8,128)(2,1)S(1)} %get-tuple-element.268), channel_id=1, source_target_pairs={{0,1},{1,0},{2,3},{3,2},{4,5},{5,4},{6,7},{7,6},{8,9},{9,8},{10,11... | collective-permute-start | bytes 1572872 | tf_op jit(solution)/shard_map/ppermute | solution.py:92
  353.1 10.0 %collective-permute-start.22 = (bf16[64,2048]{1,0:T(8,128)(2,1)S(1)}, bf16[64,2048]{1,0:T(8,128)(2,1)S(1)}, u32[]{:S(2)}, u32[]{:S(2)}) collective-permute-start(bf16[64,2048]{1,0:T(8,128)(2,1)S(1)} %slice.289), channel_id=1, source_target_pairs={{0,2},{1,3},{2,4},{3,5},{4,6},{5,7},{6,0},{7,1},{8,10},{9,11},{10,... | collective-permute-start | bytes 786440 | tf_op jit(solution)/shard_map/ppermute | solution.py:92
  353.3 10.1 %collective-permute-start.24 = (bf16[128,2048]{1,0:T(8,128)(2,1)S(1)}, bf16[128,2048]{1,0:T(8,128)(2,1)S(1)}, u32[]{:S(2)}, u32[]{:S(2)}) collective-permute-start(bf16[128,2048]{1,0:T(8,128)(2,1)S(1)} %collective-permute-done.19), channel_id=1, source_target_pairs={{0,1},{1,0},{2,3},{3,2},{4,5},{5,4},{6,7},{7,6},{8,9},{9,8},{10,11... | collective-permute-start | bytes 1572872 | tf_op jit(solution)/shard_map/ppermute | solution.py:92
  353.8 11.4 %collective-permute-start.26 = (bf16[128,2048]{1,0:T(8,128)(2,1)S(1)}, bf16[128,2048]{1,0:T(8,128)(2,1)S(1)}, u32[]{:S(2)}, u32[]{:S(2)}) collective-permute-start(bf16[128,2048]{1,0:T(8,128)(2,1)S(1)} %collective-permute-done.21), channel_id=1, source_target_pairs={{0,1},{1,0},{2,3},{3,2},{4,5},{5,4},{6,7},{7,6},{8,9},{9,8},{10,11... | collective-permute-start | bytes 1572872 | tf_op jit(solution)/shard_map/ppermute | solution.py:92
  390.7 28.9 %all-to-all-start.7 = ((bf16[16,256,128]{2,1,0:T(8,128)(2,1)}), bf16[16,256,128]{2,1,0:T(8,128)(2,1)}, u32[]{:S(2)}, u32[]{:S(2)}) async-start(bf16[16,256,128]{2,1,0:T(8,128)(2,1)} %get-tuple-element.164), calls=%async_computation.10 | async-start | bytes 2097152 | tf_op jit(solution)/shard_map/all_to_all | solution.py:166
  397.9 75.6 %reduce-scatter.15.cloned.1.call-start = ((), (), s32[]{:S(2)}) async-start(), calls=%async_computation.25 | async-start | bytes 4587520 | tf_op jit(solution)/shard_map/reduce_scatter | solution.py:1555
  433.9 5.6 collective-permute-start.30
  436.0 10.9 %all-to-all-start.8 = ((bf16[8,128,128]{2,1,0:T(8,128)(2,1)}), bf16[8,128,128]{2,1,0:T(8,128)(2,1)S(1)}, u32[]{:S(2)}, u32[]{:S(2)}) async-start(bf16[8,128,128]{2,1,0:T(8,128)(2,1)} %bitcast.43), calls=%async_computation.12 | async-start | bytes 524288 | tf_op jit(solution)/shard_map/all_to_all | solution.py:170
  439.4 123.3 %all-gather.13.cloned.1.call-start = ((), (), s32[]{:S(2)}) async-start(), calls=%async_computation.27 | async-start | bytes 6684672 | tf_op jit(solution)/shard_map/all_gather | solution.py:1562
  448.8 6.5 collective-permute-start.31
  449.5 5.9 collective-permute-start.35
  452.2 19.5 %collective-permute-start.33 = (bf16[32,2048]{1,0:T(8,128)(2,1)S(1)}, bf16[32,2048]{1,0:T(8,128)(2,1)S(1)}, u32[]{:S(2)}, u32[]{:S(2)}) collective-permute-start(bf16[32,2048]{1,0:T(8,128)(2,1)S(1)} %get-tuple-element.245), channel_id=1, source_target_pairs={{0,2},{1,3},{2,4},{3,5},{4,6},{5,7},{6,0},{7,1},{8,10},{9,11},{10,... | collective-permute-start | bytes 393224 | tf_op jit(solution)/shard_map/ppermute | solution.py:92
  452.2 19.5 %collective-permute-start.34 = (bf16[32,2048]{1,0:T(8,128)(2,1)S(1)}, bf16[32,2048]{1,0:T(8,128)(2,1)S(1)}, u32[]{:S(2)}, u32[]{:S(2)}) collective-permute-start(bf16[32,2048]{1,0:T(8,128)(2,1)S(1)} %get-tuple-element.243), channel_id=1, source_target_pairs={{0,6},{1,7},{2,0},{3,1},{4,2},{5,3},{6,4},{7,5},{8,14},{9,15},{10,... | collective-permute-start | bytes 393224 | tf_op jit(solution)/shard_map/ppermute | solution.py:92
  456.4 15.2 %collective-permute-start.32 = (bf16[32,2048]{1,0:T(8,128)(2,1)S(1)}, bf16[32,2048]{1,0:T(8,128)(2,1)S(1)}, u32[]{:S(2)}, u32[]{:S(2)}) collective-permute-start(bf16[32,2048]{1,0:T(8,128)(2,1)S(1)} %get-tuple-element.248), channel_id=1, source_target_pairs={{0,2},{1,3},{2,4},{3,5},{4,6},{5,7},{6,0},{7,1},{8,10},{9,11},{10,... | collective-permute-start | bytes 393224 | tf_op jit(solution)/shard_map/ppermute | solution.py:92
  456.9 14.7 %collective-permute-start.36 = (bf16[32,2048]{1,0:T(8,128)(2,1)S(1)}, bf16[32,2048]{1,0:T(8,128)(2,1)S(1)}, u32[]{:S(2)}, u32[]{:S(2)}) collective-permute-start(bf16[32,2048]{1,0:T(8,128)(2,1)S(1)} %get-tuple-element.247), channel_id=1, source_target_pairs={{0,6},{1,7},{2,0},{3,1},{4,2},{5,3},{6,4},{7,5},{8,14},{9,15},{10,... | collective-permute-start | bytes 393224 | tf_op jit(solution)/shard_map/ppermute | solution.py:92
  473.5 26.5 %all-to-all-start.9 = ((bf16[16,320,128]{2,1,0:T(8,128)(2,1)}), bf16[16,320,128]{2,1,0:T(8,128)(2,1)}, u32[]{:S(2)}, u32[]{:S(2)}) async-start(bf16[16,320,128]{2,1,0:T(8,128)(2,1)} %attn_bwd.1), calls=%async_computation.14 | async-start | bytes 2621440 | tf_op jit(solution)/shard_map/all_to_all | solution.py:166
  500.0 32.6 %all-to-all-start.10 = ((bf16[16,272,128]{2,1,0:T(8,128)(2,1)}), bf16[16,272,128]{2,1,0:T(8,128)(2,1)}, u32[]{:S(2)}, u32[]{:S(2)}) async-start(bf16[16,272,128]{2,1,0:T(8,128)(2,1)} %get-tuple-element.187), calls=%async_computation.15 | async-start | bytes 2228224 | tf_op jit(solution)/shard_map/all_to_all | solution.py:166
  544.4 75.4 %all-to-all-start.11 = ((bf16[16,896,128]{2,1,0:T(8,128)(2,1)}), bf16[16,896,128]{2,1,0:T(8,128)(2,1)}, u32[]{:S(2)}, u32[]{:S(2)}) async-start(bf16[16,896,128]{2,1,0:T(8,128)(2,1)} %bitcast.165), calls=%async_computation.17 | async-start | bytes 7340032 | tf_op jit(solution)/shard_map/all_to_all | solution.py:166
  550.9 50.7 %reduce-scatter.17.cloned.1.call-start = ((), (), s32[]{:S(2)}) async-start(), calls=%async_computation.26 | async-start | bytes 1146880 | tf_op jit(solution)/shard_map/reduce_scatter | solution.py:1555
  562.7 49.3 %collective-permute-start.37 = (bf16[512,2048]{1,0:T(8,128)(2,1)}, bf16[512,2048]{1,0:T(8,128)(2,1)}, u32[]{:S(2)}, u32[]{:S(2)}) collective-permute-start(bf16[512,2048]{1,0:T(8,128)(2,1)} %bitcast.215), channel_id=1, source_target_pairs={{0,1},{1,0},{2,3},{3,2},{4,5},{5,4},{6,7},{7,6},{8,9},{9,8},{10,11... | collective-permute-start | bytes 6291464 | tf_op jit(solution)/shard_map/ppermute | solution.py:92
  562.8 53.2 %collective-permute-start.38 = (bf16[512,2048]{1,0:T(8,128)(2,1)}, bf16[512,2048]{1,0:T(8,128)(2,1)}, u32[]{:S(2)}, u32[]{:S(2)}) collective-permute-start(bf16[512,2048]{1,0:T(8,128)(2,1)} %bitcast.214), channel_id=1, source_target_pairs={{0,1},{1,0},{2,3},{3,2},{4,5},{5,4},{6,7},{7,6},{8,9},{9,8},{10,11... | collective-permute-start | bytes 6291464 | tf_op jit(solution)/shard_map/ppermute | solution.py:92
  623.2 12.7 %all-to-all-start.12 = ((bf16[8,160,128]{2,1,0:T(8,128)(2,1)}), bf16[8,160,128]{2,1,0:T(8,128)(2,1)S(1)}, u32[]{:S(2)}, u32[]{:S(2)}) async-start(bf16[8,160,128]{2,1,0:T(8,128)(2,1)} %pad_maximum_fusion.3), calls=%async_computation.18 | async-start | bytes 655360 | tf_op jit(solution)/shard_map/all_to_all | solution.py:170
  627.6 74.9 %all-gather.15.cloned.1.call-start = ((), (), s32[]{:S(2)}) async-start(), calls=%async_computation.28 | async-start | bytes 7798784 | tf_op jit(solution)/shard_map/all_gather | solution.py:1562
  639.5 20.0 %collective-permute-start.42 = (bf16[64,4096]{1,0:T(8,128)(2,1)S(1)}, bf16[64,4096]{1,0:T(8,128)(2,1)S(1)}, u32[]{:S(2)}, u32[]{:S(2)}) collective-permute-start(bf16[64,4096]{1,0:T(8,128)(2,1)S(1)} %get-tuple-element.234), channel_id=1, source_target_pairs={{0,2},{1,3},{2,4},{3,5},{4,6},{5,7},{6,0},{7,1},{8,10},{9,11},{10,... | collective-permute-start | bytes 1572872 | tf_op jit(solution)/shard_map/ppermute | solution.py:92
  640.1 19.4 %collective-permute-start.43 = (bf16[64,4096]{1,0:T(8,128)(2,1)S(1)}, bf16[64,4096]{1,0:T(8,128)(2,1)S(1)}, u32[]{:S(2)}, u32[]{:S(2)}) collective-permute-start(bf16[64,4096]{1,0:T(8,128)(2,1)S(1)} %get-tuple-element.233), channel_id=1, source_target_pairs={{0,6},{1,7},{2,0},{3,1},{4,2},{5,3},{6,4},{7,5},{8,14},{9,15},{10,... | collective-permute-start | bytes 1572872 | tf_op jit(solution)/shard_map/ppermute | solution.py:92
  642.8 22.4 %collective-permute-start.44 = (bf16[64,4096]{1,0:T(8,128)(2,1)S(1)}, bf16[64,4096]{1,0:T(8,128)(2,1)S(1)}, u32[]{:S(2)}, u32[]{:S(2)}) collective-permute-start(bf16[64,4096]{1,0:T(8,128)(2,1)S(1)} %get-tuple-element.232), channel_id=1, source_target_pairs={{0,2},{1,3},{2,4},{3,5},{4,6},{5,7},{6,0},{7,1},{8,10},{9,11},{10,... | collective-permute-start | bytes 1572872 | tf_op jit(solution)/shard_map/ppermute | solution.py:92
  642.8 22.4 %collective-permute-start.45 = (bf16[64,4096]{1,0:T(8,128)(2,1)S(1)}, bf16[64,4096]{1,0:T(8,128)(2,1)S(1)}, u32[]{:S(2)}, u32[]{:S(2)}) collective-permute-start(bf16[64,4096]{1,0:T(8,128)(2,1)S(1)} %get-tuple-element.231), channel_id=1, source_target_pairs={{0,6},{1,7},{2,0},{3,1},{4,2},{5,3},{6,4},{7,5},{8,14},{9,15},{10,... | collective-permute-start | bytes 1572872 | tf_op jit(solution)/shard_map/ppermute | solution.py:92
  650.2 5.5 collective-permute-start.40
  666.2 12.8 %collective-permute-start.49 = (bf16[64,4096]{1,0:T(8,128)(2,1)}, bf16[64,4096]{1,0:T(8,128)(2,1)}, u32[]{:S(2)}, u32[]{:S(2)}) collective-permute-start(bf16[64,4096]{1,0:T(8,128)(2,1)} %add_convert_fusion.1), channel_id=1, source_target_pairs={{0,6},{1,7},{2,0},{3,1},{4,2},{5,3},{6,4},{7,5},{8,14},{9,15},{10,... | collective-permute-start | bytes 1572872 | tf_op jit(solution)/shard_map/ppermute | solution.py:92
  669.2 6.0 collective-permute-start.46
  671.6 13.0 %collective-permute-start.48 = (bf16[64,4096]{1,0:T(8,128)(2,1)}, bf16[64,4096]{1,0:T(8,128)(2,1)}, u32[]{:S(2)}, u32[]{:S(2)}) collective-permute-start(bf16[64,4096]{1,0:T(8,128)(2,1)} %add_convert_fusion.2), channel_id=1, source_target_pairs={{0,2},{1,3},{2,4},{3,5},{4,6},{5,7},{6,0},{7,1},{8,10},{9,11},{10,... | collective-permute-start | bytes 1572872 | tf_op jit(solution)/shard_map/ppermute | solution.py:92
  691.5 6.2 collective-permute-start.51
  (45 other events, 326.5 us)
Sparse Core Ops, SparseCore 0:
  27.2 55.5 all-gather.16
  92.4 32.0 all-gather.8
  127.3 62.8 all-gather.18
  207.6 36.8 reduce-scatter.6
  248.1 30.9 all-gather.10
  293.2 38.8 reduce-scatter.8
  336.3 43.9 reduce-scatter.10
  390.8 28.6 reduce-scatter.12
  422.6 38.8 reduce-scatter.14
  463.5 82.1 all-gather.12
  562.9 38.7 reduce-scatter.16
  636.8 64.4 all-gather.14

commit v5 on v3

--- a/solution.py
+++ b/solution.py
@@ -144,9 +144,13 @@
     return own, after[:half], before[half:], *sent
 
 
-def ring_last(own, after, before, far_next, far_prev, after_two, before_one):
+def ring_second(own, after, before, far_next, far_prev, after_two, before_one):
     after_one = send(plus(after, far_next).astype(BF), TO_NEXT)
     before_two = send(plus(before, far_prev).astype(BF), TO_PREV)
+    return own, after_one, after_two, before_one, before_two
+
+
+def ring_last(own, after_one, after_two, before_one, before_two):
     return plus(
         own,
         jnp.concatenate([after_one, after_two], axis=0),
@@ -155,7 +159,7 @@
 
 
 def ring_scatter(joined):
-    return ring_last(*ring_first(joined))
+    return ring_last(*ring_second(*ring_first(joined)))
 
 
 def together(*values):
@@ -1621,6 +1625,31 @@
     got_mix, d_normed, down = together(
         swap_ctx(packed_mix), joined(mine, other), joined(down_mine, down_other)
     )
+    def by_half(values):
+        zero = jnp.zeros_like(values)
+        return jnp.where(
+            parity == 1, jnp.stack([zero, values], axis=-2), jnp.stack([values, zero], axis=-2)
+        )
+
+    g_conv = g_taps.T[: CONV_K + 1]
+    g_d_skip = jnp.sum(dskip.reshape(HEADS_L, MDIM), axis=1)
+    per_head = jnp.stack(
+        [g_heads[:HEADS_L, 0], g_heads[HEADS_L : 2 * HEADS_L, 0], g_d_skip]
+    )
+    own = jnp.concatenate(
+        [
+            by_half(g_conv[:, :XW]).reshape(-1),
+            g_conv[:, XW:].reshape(-1),
+            g_mamba_gain[:, 0],
+            by_half(per_head).reshape(-1),
+        ]
+    )
+    own_size = own.shape[0]
+    own_pad = -(-own_size // LANES) * LANES
+    own = jnp.concatenate([own, jnp.zeros((own_pad - own_size,), F32), g_mlp_gain, g_norm_gain])
+
+    own, got_mix = together(own.reshape(-1, LANES), got_mix)
+    own = butterfly(own, "ctx", (1, 2))
     columns = swap_fsdp(
         jnp.concatenate(
             [
@@ -1630,53 +1659,30 @@
             axis=1,
         )
     )
-    def by_half(values):
-        zero = jnp.zeros_like(values)
-        return jnp.where(
-            parity == 1, jnp.stack([zero, values], axis=-2), jnp.stack([values, zero], axis=-2)
-        )
-
-    g_conv = g_taps.T[: CONV_K + 1]
-    g_d_skip = jnp.sum(dskip.reshape(HEADS_L, MDIM), axis=1)
-    per_head = jnp.stack(
-        [g_heads[:HEADS_L, 0], g_heads[HEADS_L : 2 * HEADS_L, 0], g_d_skip]
-    )
-    own = jnp.concatenate(
-        [
-            by_half(g_conv[:, :XW]).reshape(-1),
-            g_conv[:, XW:].reshape(-1),
-            g_mamba_gain[:, 0],
-            by_half(per_head).reshape(-1),
-        ]
-    )
-    own_size = own.shape[0]
-    own_pad = -(-own_size // LANES) * LANES
-    own = jnp.concatenate([own, jnp.zeros((own_pad - own_size,), F32), g_mlp_gain, g_norm_gain])
-
-    own, columns, all_one = together(own.reshape(-1, LANES), columns, all_one)
+    columns, all_one = together(columns, all_one)
     all_two = all_ctx([columns.reshape(-1, LANES)])
     both = jnp.concatenate([d_normed, down], axis=1)
-    own, *both = together(butterfly(own, "ctx", (1, 2, 4)), *ring_first(both))
+    own, *both = together(butterfly(own, "ctx", (4,)), *ring_first(both))
     own = butterfly(own, "ctx", (8,)).reshape(-1)
     mine = (jnp.arange(NF) == fsdp)[:, None]
     placed = jnp.where(mine, own[None, :own_pad], 0.0).reshape(-1)
     total = jnp.concatenate([placed, own[own_pad:]]).reshape(-1, LANES)
-    total, both = together(butterfly(total, "fsdp", (1,)), ring_last(*both))
+    total, g_gate_up, g_down, g_mout, g_aout, *both = together(
+        butterfly(total, "fsdp", (1,)),
+        unpack_gate_up(all_one),
+        *unpack_rows(all_one, down_at),
+        *ring_second(*both),
+    )
+    both = ring_last(*both)
     d_normed, down = both[:, :D], both[:, D:]
     output = even_first((mixed + down).astype(BF)).reshape(tokens.shape)
 
-    g_gate_up = unpack_gate_up(all_one)
-    g_down, g_mout, g_aout = unpack_rows(all_one, down_at)
-    total = butterfly(total, "fsdp", (2,))
-    total, g_gate_up, g_down, g_mout, g_aout = together(
-        total, g_gate_up, g_down, g_mout, g_aout
-    )
     g_qkv = unpack_qkv(all_two)
     g_in = unpack_in(all_two).T
     d_hidden, _ = norm_back(hidden, scale_one, norm_gain, d_normed)
     d_tokens = even_first((d_hidden + d_mixed).astype(BF)).reshape(tokens.shape)
 
-    total = butterfly(total, "fsdp", (4,)).reshape(-1)
+    total = butterfly(total, "fsdp", (2, 4)).reshape(-1)
     each = total[: NF * own_pad].reshape(NF, own_pad)
     cut = [(CONV_K + 1) * INNER_F]
     cut.append(cut[0] + (CONV_K + 1) * BC_F)

time: 731 us -> 729 us (level)
  blocking collectives: 13.5 us -> 25.3 us
  waiting for transfers between devices: 280 us -> 271 us
    all_to_all x1 -> x2, blocking collectives: 13.5 us -> 25.3 us  [swap_fsdp(): return lax.all_to_all(value, 'fsdp', 0, 0, tiled=True)]
    all_to_all x3 -> x2, waiting for transfers between devices: 12.2 us -> 4.49 us  [swap_fsdp(): return lax.all_to_all(value, 'fsdp', 0, 0, tiled=True)]
  transfers between devices with their start and end apart: 76 -> 75, of which waited for: 35 -> 35; matrix products, arithmetic and copies ran while one was open for 10% -> 10% of each run, Pallas kernels for 23% -> 23%
where the time goes in v5:
time: 729 us; the launch traced here: 717 us
  waiting for transfers between devices  271 us (37%)
  Pallas kernels  206 us (28%)
  starting transfers between devices  106 us (15%)
  local copies, waits for them, and re-layouts  45.4 us (6%)
  other arithmetic  43 us (6%)
  blocking collectives  25.3 us (3%)
  between operations  20.9 us (3%)
    all_to_all x9, waiting for transfers between devices, swap_ctx(): return lax.all_to_all(value, 'ctx', 0, 0, tiled=True)  85.6 us
    all_to_all x9, starting transfers between devices, swap_ctx(): return lax.all_to_all(value, 'ctx', 0, 0, tiled=True)  54.8 us
    reduce_scatter x2, waiting for transfers between devices, scatter_fsdp(): lax.psum_scatter(parts, 'fsdp', scatter_dimension=0, tiled=True).astype(F32)  45.6 us
    ppermute x39, waiting for transfers between devices, send(): return lax.ppermute(value, 'fsdp', route)  44.4 us
    ppermute x39, starting transfers between devices, send(): return lax.ppermute(value, 'fsdp', route)  39.8 us
    ppermute x13, waiting for transfers between devices, exchange(): lax.ppermute(value, axis, [(i, i ^ bit) for i in range(size)])  38.6 us
    pallas_call x5, Pallas kernels, column_grad(): pl.pallas_call(functools.partial(column_grad_kernel, by_y), grid=(count /...  35.5 us
    all_to_all x2, blocking collectives, swap_fsdp(): return lax.all_to_all(value, 'fsdp', 0, 0, tiled=True)  25.3 us
  transfers between devices with their start and end apart: 75, of which 35 were waited for; matrix products, arithmetic and copies ran while one was open for 10% of the time, Pallas kernels for 23%

profile of v5, /device:TPU:16, one launch (start us, length us, event | category | flops | bytes accessed | tf_op | source)
XLA Modules:
  0.0 716.9 jit_solution(3321018062368668616)
XLA Ops:
  13.6 13.5 %all_to_all.65 = bf16[8,16,1280]{2,1,0:T(8,128)(2,1)} all-to-all(bf16[8,16,1280]{2,1,0:T(8,128)(2,1)S(1)} %copy.115), channel_id=1, replica_groups=mesh['ctx'=16,'fsdp'=8] {'fsdp'}, dimensions={0} | all-to-all | bytes 655360 | tf_op jit(solution)/shard_map/all_to_all | solution.py:174
  42.3 3.6 collective-permute-done
  49.9 3.4 all-to-all-start.1
  57.6 8.5 %collective-permute-done.3 = bf16[64,2048]{1,0:T(8,128)(2,1)S(1)} collective-permute-done((bf16[64,2048]{1,0:T(8,128)(2,1)S(1)}, bf16[64,2048]{1,0:T(8,128)(2,1)S(1)}, u32[]{:S(2)}, u32[]{:S(2)}) %collective-permute-start.3) | collective-permute-done | bytes 262176 | tf_op jit(solution)/shard_map/ppermute | solution.py:92
  71.2 11.6 %all-gather.17.cloned.1.call-done = bf16[128,16,1280]{2,1,0:T(8,128)(2,1)} async-done(((bf16[8,16,1280]{2,1,0:T(8,128)(2,1)}), bf16[128,16,1280]{2,1,0:T(8,128)(2,1)}) %all-gather.17.cloned.1.call-update) | async-done | bytes 5242896 | tf_op jit(solution)/shard_map/all_gather | solution.py:1476
  82.8 9.4 %project.1 = (bf16[16,272,128]{2,1,0:T(8,128)(2,1)}, bf16[16,320,128]{2,1,0:T(8,128)(2,1)}) custom-call(bf16[1024,2048]{1,0:T(8,128)(2,1)} %constant_dynamic-update-slice_fusion.27.n_ref.left_ref, bf16[16,8,16,1280]{3,2,1,0:T(8,128)(2,1)} %bitcast.160, f32[128,64]{1,0:T(8,128)} %get-tuple-element.270.cos_ref, f32[128,64]{1,0:T(8,128)} %get-tuple-element.269.sin_ref), custom_call_target="tpu_custom_call" | custom-call | flops 3758096384 | bytes 10000000 | tf_op jit(solution)/shard_map/project/pallas_call | solution.py:238
  92.4 5.7 all-to-all-start.2
  99.6 7.8 %project_z.1.z_ref = f32[8,384,128]{2,1,0:T(8,128)} custom-call(bf16[1024,2048]{1,0:T(8,128)(2,1)} %constant_dynamic-update-slice_fusion.27.n_ref.left_ref, bf16[16,8,16,1280]{3,2,1,0:T(8,128)(2,1)} %bitcast.161), custom_call_target="tpu_custom_call" | custom-call | flops 1610612736 | bytes 8000000 | tf_op jit(solution)/shard_map/project_z/pallas_call | solution.py:269
  107.4 6.6 all-to-all-done.2.got_ref
  115.0 6.4 front.1
  126.2 6.2 all-to-all-start.3
  142.7 8.5 %mamba_fwd.1 = (bf16[16,192,128]{2,1,0:T(8,128)(2,1)}, f32[8,192,256]{2,1,0:T(8,128)}) custom-call(s32[8]{0:T(128)} %fusion.14.place_ref, bf16[192,2048]{1,0:T(8,128)(2,1)} %get-tuple-element.136.x_ref, bf16[8,64,2048]{2,1,0:T(8,128)(2,1)} %bitcast.205, f32[16,2048]{1,0:T(8,128)} %get-tuple-element.140.row_ref, f32[192,1]{1,0:T(8,128)} %broadcast_in_dim_reshape.4.skip_ref), custom_call_target="tpu_custom_call" | custom-call | flops 872415232 | bytes 7000000 | tf_op jit(solution)/shard_map/mamba_fwd/pallas_call | solution.py:958
  151.2 4.3 all-to-all-done.3.q_ref.k_ref.v_ref
  155.5 6.1 all-to-all-start.4
  161.6 9.2 %attn_fwd.1 = (bf16[16,64,128]{2,1,0:T(8,128)(2,1)}, f32[1024,1]{1,0:T(8,128)}) custom-call(s32[1]{0:T(128)} %bitcast.31.odd_ref, bf16[16,320,128]{2,1,0:T(8,128)(2,1)} %copy-done.11, bf16[16,320,128]{2,1,0:T(8,128)(2,1)} %copy-done.11, bf16[16,320,128]{2,1,0:T(8,128)(2,1)} %copy-done.11), custom_call_target="tpu_custom_call" | custom-call | flops 1073741824 | bytes 3000000 | tf_op jit(solution)/shard_map/attn_fwd/pallas_call | solution.py:1160
  170.8 8.8 %all-to-all-done.4.got_ref = bf16[16,192,128]{2,1,0:T(8,128)(2,1)S(1)} async-done(((bf16[16,192,128]{2,1,0:T(8,128)(2,1)}), bf16[16,192,128]{2,1,0:T(8,128)(2,1)S(1)}, u32[]{:S(2)}, u32[]{:S(2)}) %all-to-all-start.4) | async-done | bytes 786464 | tf_op jit(solution)/shard_map/all_to_all | solution.py:170
  183.2 6.3 all-to-all-start.5
  200.3 7.2 %branch_out.1 = (bf16[1024,512]{1,0:T(8,128)(2,1)}, bf16[1024,2048]{1,0:T(8,128)(2,1)}) custom-call(bf16[16,64,128]{2,1,0:T(8,128)(2,1)} %copy-done.18, f32[8,384,128]{2,1,0:T(8,128)} %get-tuple-element.150.g_ref, f32[8,128]{1,0:T(8,128)} %add.305.sq_ref, f32[384,1]{1,0:T(8,128)} %broadcast_in_dim.79.gain_ref, bf16[512,2048]{1,0:T(8,128)(2,1)} %copy-done.7), custom_call_target="tpu_custom_call" | custom-call | flops 2147483648 | bytes 10000000 | tf_op jit(solution)/shard_map/branch_out/pallas_call | solution.py:463
  207.5 37.0 %reduce-scatter.7.cloned.1.call-done = bf16[128,2048]{1,0:T(8,128)(2,1)} async-done(((bf16[1024,2048]{1,0:T(8,128)(2,1)}), bf16[128,2048]{1,0:T(8,128)(2,1)}) %reduce-scatter.7.cloned.1.call-update) | async-done | bytes 524304 | tf_op jit(solution)/shard_map/reduce_scatter | solution.py:100
  248.0 6.5 act_back.1.d_act_ref
  254.5 24.7 %all-gather.11.cloned.1.call-done.n_ref.left_ref = bf16[1024,2048]{1,0:T(8,128)(2,1)} async-done(((bf16[128,2048]{1,0:T(8,128)(2,1)}), bf16[1024,2048]{1,0:T(8,128)(2,1)}) %all-gather.11.cloned.1.call-update) | async-done | bytes 4194320 | tf_op jit(solution)/shard_map/all_gather | solution.py:96
  279.2 13.9 %mlp.1 = (bf16[1024,512]{1,0:T(8,128)(2,1)}, bf16[1024,1024]{1,0:T(8,128)(2,1)}, bf16[1024,2048]{1,0:T(8,128)(2,1)}) custom-call(bf16[1024,2048]{1,0:T(8,128)(2,1)} %all-gather.11.cloned.1.call-done.n_ref.left_ref, f32[1024,512]{1,0:T(8,128)} %act_back.1.d_act_ref, bf16[16,8,16,1024]{3,2,1,0:T(8,128)(2,1)} %bitcast.211), custom_call_target="tpu_custom_call" | custom-call | flops 8589934592 | bytes 20000000 | tf_op jit(solution)/shard_map/mlp/pallas_call | solution.py:610
  293.2 6.3 column_grad.6
  299.5 7.4 %all-to-all-start.6 = ((bf16[16,512,128]{2,1,0:T(8,128)(2,1)}), bf16[16,512,128]{2,1,0:T(8,128)(2,1)}, u32[]{:S(2)}, u32[]{:S(2)}) async-start(bf16[16,512,128]{2,1,0:T(8,128)(2,1)} %bitcast.170), calls=%async_computation.8 | async-start | bytes 4194304 | tf_op jit(solution)/shard_map/all_to_all | solution.py:170
  308.0 7.0 down_out.1
  315.0 8.5 %column_grad.5 = bf16[16,8,8,16,128]{4,3,2,1,0:T(8,128)(2,1)} custom-call(bf16[1024,2048]{1,0:T(8,128)(2,1)} %all-gather.11.cloned.1.call-done.n_ref.left_ref, bf16[1024,1024]{1,0:T(8,128)(2,1)} %get-tuple-element.162.refs_0_), custom_call_target="tpu_custom_call" | custom-call | flops 4294967296 | bytes 10485760 | tf_op jit(solution)/shard_map/column_grad/pallas_call | solution.py:405
  323.5 8.6 %reduce-scatter.9.cloned.1.call-done = bf16[128,2048]{1,0:T(8,128)(2,1)} async-done(((bf16[1024,2048]{1,0:T(8,128)(2,1)}), bf16[128,2048]{1,0:T(8,128)(2,1)}) %reduce-scatter.9.cloned.1.call-update) | async-done | bytes 524304 | tf_op jit(solution)/shard_map/reduce_scatter | solution.py:100
  341.4 9.9 %collective-permute-done.19 = bf16[128,2048]{1,0:T(8,128)(2,1)S(1)} collective-permute-done((bf16[128,2048]{1,0:T(8,128)(2,1)S(1)}, bf16[128,2048]{1,0:T(8,128)(2,1)S(1)}, u32[]{:S(2)}, u32[]{:S(2)}) %collective-permute-start.19) | collective-permute-done | bytes 524320 | tf_op jit(solution)/shard_map/ppermute | solution.py:92
  354.2 3.5 collective-permute-done.20
  357.7 5.6 collective-permute-done.22
  367.5 7.1 branch_back.1
  376.8 3.6 collective-permute-done.28
  380.4 5.1 collective-permute-done.29
  386.1 4.8 gate_back.1
  390.9 7.1 all-to-all-start.7
  398.3 6.2 column_grad.7
  404.5 6.1 column_grad.8
  410.6 3.6 pad_maximum_fusion
  414.2 5.5 reduce-scatter.13.cloned.1.call-done
  419.7 14.3 %mamba_bwd.1 = (f32[192,2048]{1,0:T(8,128)}, bf16[4,64,2048]{2,1,0:T(8,128)(2,1)}, bf16[4,64,2048]{2,1,0:T(8,128)(2,1)}, f32[8,2048]{1,0:T(8,128)}, f32[192,1]{1,0:T(8,128)}) custom-call(s32[8]{0:T(128)} %fusion.14.place_ref, bf16[192,2048]{1,0:T(8,128)(2,1)} %get-tuple-element.136.x_ref, bf16[16,256,128]{2,1,0:T(8,128)(2,1)} %all-to-all-done.7.got_ref.do_ref, ...), custom_call_target="tpu_custom_call" | custom-call | flops 2214592512 | bytes 12000000 | tf_op jit(solution)/shard_map/mamba_bwd/pallas_call | solution.py:1089
  434.2 3.4 all-to-all-start.8
  440.6 4.5 all-to-all-done.8
  457.4 11.6 %attn_bwd.1 = bf16[16,320,128]{2,1,0:T(8,128)(2,1)} custom-call(s32[1]{0:T(128)} %bitcast.31.odd_ref, bf16[16,320,128]{2,1,0:T(8,128)(2,1)} %copy-done.11, bf16[16,320,128]{2,1,0:T(8,128)(2,1)} %copy-done.11, bf16[16,320,128]{2,1,0:T(8,128)(2,1)} %copy-done.11, bf16[16,256,128]{2,1,0:T(8,128)(2,1)} %all-to-all-done.7.got_ref.do_ref, ...), custom_call_target="tpu_custom_call" | custom-call | flops 2684354560 | bytes 4000000 | tf_op jit(solution)/shard_map/attn_bwd/pallas_call | solution.py:1212
  470.8 5.5 all-to-all-start.9
  478.2 11.0 %front_back.1 = (bf16[16,272,128]{2,1,0:T(8,128)(2,1)}, f32[256,8]{1,0:T(8,128)}, f32[8,1]{1,0:T(8,128)}) custom-call(bf16[16,272,128]{2,1,0:T(8,128)(2,1)} %copy-done.3, f32[256,8]{1,0:T(8,128)} %bitcast.174, f32[8,128]{1,0:T(8,128)} %broadcast_in_dim.71.heads_ref, f32[16,2048]{1,0:T(8,128)} %get-tuple-element.140.row_ref, ...), custom_call_target="tpu_custom_call" | custom-call | flops 31457280 | bytes 9000000 | tf_op jit(solution)/shard_map/front_back/pallas_call | solution.py:853
  489.3 10.1 %reduce-scatter.17.cloned.1.call-done = bf16[1,896,128]{2,1,0:T(8,128)(2,1)} async-done(((bf16[4,896,128]{2,1,0:T(8,128)(2,1)}), bf16[1,896,128]{2,1,0:T(8,128)(2,1)}) %reduce-scatter.17.cloned.1.call-update) | async-done | bytes 229392 | tf_op jit(solution)/shard_map/reduce_scatter | solution.py:1553
  501.1 5.7 all-to-all-start.10
  506.8 4.0 attn_grads.1.refs_1_.dqkv_ref
  510.9 19.1 %all-to-all-done.10.got_ref = bf16[16,272,128]{2,1,0:T(8,128)(2,1)} async-done(((bf16[16,272,128]{2,1,0:T(8,128)(2,1)}), bf16[16,272,128]{2,1,0:T(8,128)(2,1)}, u32[]{:S(2)}, u32[]{:S(2)}) %all-to-all-start.10) | async-done | bytes 1114144 | tf_op jit(solution)/shard_map/all_to_all | solution.py:170
  530.0 3.6 mix_grads.1.refs_0_.mix_ref
  533.6 8.3 %column_grad.9 = bf16[16,8,7,16,128]{4,3,2,1,0:T(8,128)(2,1)} custom-call(bf16[1024,2048]{1,0:T(8,128)(2,1)} %constant_dynamic-update-slice_fusion.27.n_ref.left_ref, bf16[1024,512]{1,0:T(8,128)(2,1)} %mix_grads.1.refs_0_.mix_ref, bf16[1024,384]{1,0:T(8,128)(2,1)} %attn_grads.1.refs_1_.dqkv_ref), custom_call_target="tpu_custom_call" | custom-call | flops 3758096384 | bytes 9699328 | tf_op jit(solution)/shard_map/column_grad/pallas_call | solution.py:405
  541.9 4.8 all-to-all-start.11
  546.8 11.8 %back_project.1 = (bf16[4,128,2048]{2,1,0:T(8,128)(2,1)}, bf16[4,128,2048]{2,1,0:T(8,128)(2,1)}, f32[1,2048]{1,0:T(1,128)}) custom-call(s32[5]{0:T(128)} %pad_add_fusion.1.spot_ref, bf16[1024,512]{1,0:T(8,128)(2,1)} %mix_grads.1.refs_0_.mix_ref, bf16[1024,384]{1,0:T(8,128)(2,1)} %attn_grads.1.refs_1_.dqkv_ref, ...), custom_call_target="tpu_custom_call" | custom-call | flops 5368709120 | bytes 18000000 | tf_op jit(solution)/shard_map/back_project/pallas_call | solution.py:360
  563.2 4.5 fusion
  567.7 3.8 fusion.1
  571.5 43.7 %all-to-all-done.11 = bf16[16,896,128]{2,1,0:T(8,128)(2,1)} async-done(((bf16[16,896,128]{2,1,0:T(8,128)(2,1)}), bf16[16,896,128]{2,1,0:T(8,128)(2,1)}, u32[]{:S(2)}, u32[]{:S(2)}) %all-to-all-start.11) | async-done | bytes 3670048 | tf_op jit(solution)/shard_map/all_to_all | solution.py:170
  617.9 11.9 %all_to_all.66 = bf16[8,160,128]{2,1,0:T(8,128)(2,1)} all-to-all(bf16[8,160,128]{2,1,0:T(8,128)(2,1)S(1)} %pad_maximum_fusion.2), channel_id=1, replica_groups=mesh['ctx'=16,'fsdp'=8] {'fsdp'}, dimensions={0} | all-to-all | bytes 655360 | tf_op jit(solution)/shard_map/all_to_all | solution.py:174
  643.0 5.7 collective-permute-done.40
  652.6 6.1 collective-permute-done.44
  664.8 3.8 collective-permute-done.46
  670.1 8.3 %unpack_rows.1 = (f32[512,2048]{1,0:T(8,128)}, f32[384,2048]{1,0:T(8,128)}, f32[128,2048]{1,0:T(8,128)}) custom-call(bf16[16,128,16,128]{3,2,1,0:T(8,128)(2,1)} %all-gather.13.cloned.1.call-done.refs_0_.refs_1_.refs_2_.refs_3_.tiles_ref), custom_call_target="tpu_custom_call" | custom-call | flops 2097152 | bytes 12582912 | tf_op jit(solution)/shard_map/unpack_rows/pallas_call | solution.py:1271
  678.4 6.0 unpack_gate_up.1
  690.8 5.0 collective-permute-done.51
  700.6 6.3 unpack_in.1
  (379 shorter events, 151.9 us)
Async XLA Ops:
  7.2 75.7 %all-gather.17.cloned.1.call-start = ((), (), s32[]{:S(2)}) async-start(), calls=%async_computation.29 | async-start | bytes 5570560 | tf_op jit(solution)/shard_map/all_gather | solution.py:1476
  32.3 13.6 %collective-permute-start = (bf16[128,2048]{1,0:T(8,128)(2,1)S(1)}, bf16[128,2048]{1,0:T(8,128)(2,1)S(1)}, u32[]{:S(2)}, u32[]{:S(2)}) collective-permute-start(bf16[128,2048]{1,0:T(8,128)(2,1)S(1)} %get-tuple-element.282), channel_id=1, source_target_pairs={{0,6},{1,7},{2,0},{3,1},{4,2},{5,3},{6,4},{7,5},{8,14},{9,15},{10,... | collective-permute-start | bytes 1572872 | tf_op jit(solution)/shard_map/ppermute | solution.py:92
  33.5 19.9 %collective-permute-start.2 = (bf16[128,2048]{1,0:T(8,128)(2,1)S(1)}, bf16[128,2048]{1,0:T(8,128)(2,1)S(1)}, u32[]{:S(2)}, u32[]{:S(2)}) collective-permute-start(bf16[128,2048]{1,0:T(8,128)(2,1)S(1)} %get-tuple-element.282), channel_id=1, source_target_pairs={{0,2},{1,3},{2,4},{3,5},{4,6},{5,7},{6,0},{7,1},{8,10},{9,11},{10,... | collective-permute-start | bytes 1572872 | tf_op jit(solution)/shard_map/ppermute | solution.py:92
  34.3 33.5 %collective-permute-start.4 = (bf16[128,2048]{1,0:T(8,128)(2,1)S(1)}, bf16[128,2048]{1,0:T(8,128)(2,1)S(1)}, u32[]{:S(2)}, u32[]{:S(2)}) collective-permute-start(bf16[128,2048]{1,0:T(8,128)(2,1)S(1)} %get-tuple-element.282), channel_id=1, source_target_pairs={{0,1},{1,0},{2,3},{3,2},{4,5},{5,4},{6,7},{7,6},{8,9},{9,8},{10,11... | collective-permute-start | bytes 1572872 | tf_op jit(solution)/shard_map/ppermute | solution.py:92
  46.6 10.0 %collective-permute-start.1 = (bf16[64,2048]{1,0:T(8,128)(2,1)}, bf16[64,2048]{1,0:T(8,128)(2,1)}, u32[]{:S(2)}, u32[]{:S(2)}) collective-permute-start(bf16[64,2048]{1,0:T(8,128)(2,1)} %slice.284), channel_id=1, source_target_pairs={{0,6},{1,7},{2,0},{3,1},{4,2},{5,3},{6,4},{7,5},{8,14},{9,15},{10,... | collective-permute-start | bytes 786440 | tf_op jit(solution)/shard_map/ppermute | solution.py:92
  49.9 21.3 %all-to-all-start.1 = ((bf16[8,16,1024]{2,1,0:T(8,128)(2,1)}), bf16[8,16,1024]{2,1,0:T(8,128)(2,1)S(1)}, u32[]{:S(2)}, u32[]{:S(2)}) async-start(bf16[8,16,1024]{2,1,0:T(8,128)(2,1)} %copy.116), calls=%async_computation.1 | async-start | bytes 524288 | tf_op jit(solution)/shard_map/all_to_all | solution.py:174
  53.3 102.2 %all-gather.9.cloned.1.call-start = ((), (), s32[]{:S(2)}) async-start(), calls=%async_computation.19 | async-start | bytes 4718592 | tf_op jit(solution)/shard_map/all_gather | solution.py:96
  53.4 12.7 %collective-permute-start.3 = (bf16[64,2048]{1,0:T(8,128)(2,1)S(1)}, bf16[64,2048]{1,0:T(8,128)(2,1)S(1)}, u32[]{:S(2)}, u32[]{:S(2)}) collective-permute-start(bf16[64,2048]{1,0:T(8,128)(2,1)S(1)} %slice.285), channel_id=1, source_target_pairs={{0,2},{1,3},{2,4},{3,5},{4,6},{5,7},{6,0},{7,1},{8,10},{9,11},{10,... | collective-permute-start | bytes 786440 | tf_op jit(solution)/shard_map/ppermute | solution.py:92
  55.3 13.4 %collective-permute-start.5 = (bf16[128,2048]{1,0:T(8,128)(2,1)S(1)}, bf16[128,2048]{1,0:T(8,128)(2,1)S(1)}, u32[]{:S(2)}, u32[]{:S(2)}) collective-permute-start(bf16[128,2048]{1,0:T(8,128)(2,1)S(1)} %collective-permute-done), channel_id=1, source_target_pairs={{0,1},{1,0},{2,3},{3,2},{4,5},{5,4},{6,7},{7,6},{8,9},{9,8},{10,11... | collective-permute-start | bytes 1572872 | tf_op jit(solution)/shard_map/ppermute | solution.py:92
  55.3 15.0 %collective-permute-start.7 = (bf16[128,2048]{1,0:T(8,128)(2,1)S(1)}, bf16[128,2048]{1,0:T(8,128)(2,1)S(1)}, u32[]{:S(2)}, u32[]{:S(2)}) collective-permute-start(bf16[128,2048]{1,0:T(8,128)(2,1)S(1)} %collective-permute-done.2), channel_id=1, source_target_pairs={{0,1},{1,0},{2,3},{3,2},{4,5},{5,4},{6,7},{7,6},{8,9},{9,8},{10,11... | collective-permute-start | bytes 1572872 | tf_op jit(solution)/shard_map/ppermute | solution.py:92
  92.4 21.5 %all-to-all-start.2 = ((bf16[16,272,128]{2,1,0:T(8,128)(2,1)}), bf16[16,272,128]{2,1,0:T(8,128)(2,1)S(1)}, u32[]{:S(2)}, u32[]{:S(2)}) async-start(bf16[16,272,128]{2,1,0:T(8,128)(2,1)} %get-tuple-element.132), calls=%async_computation.2 | async-start | bytes 2228224 | tf_op jit(solution)/shard_map/all_to_all | solution.py:170
  98.2 101.4 %all-gather.19.cloned.1.call-start = ((), (), s32[]{:S(2)}) async-start(), calls=%async_computation.30 | async-start | bytes 4456448 | tf_op jit(solution)/shard_map/all_gather | solution.py:1520
  121.5 11.1 %collective-permute-start.10 = (bf16[64,2048]{1,0:T(8,128)(2,1)}, bf16[64,2048]{1,0:T(8,128)(2,1)S(1)}, u32[]{:S(2)}, u32[]{:S(2)}) collective-permute-start(bf16[64,2048]{1,0:T(8,128)(2,1)} %get-tuple-element.139), channel_id=1, source_target_pairs={{0,2},{1,3},{2,4},{3,5},{4,6},{5,7},{6,0},{7,1},{8,10},{9,11},{10,... | collective-permute-start | bytes 786440 | tf_op jit(solution)/shard_map/ppermute | solution.py:92
  123.0 10.2 %collective-permute-start.8 = (bf16[64,2048]{1,0:T(8,128)(2,1)}, bf16[64,2048]{1,0:T(8,128)(2,1)S(1)}, u32[]{:S(2)}, u32[]{:S(2)}) collective-permute-start(bf16[64,2048]{1,0:T(8,128)(2,1)} %get-tuple-element.139), channel_id=1, source_target_pairs={{0,6},{1,7},{2,0},{3,1},{4,2},{5,3},{6,4},{7,5},{8,14},{9,15},{10,... | collective-permute-start | bytes 786440 | tf_op jit(solution)/shard_map/ppermute | solution.py:92
  126.2 13.6 %collective-permute-start.12 = (bf16[64,2048]{1,0:T(8,128)(2,1)}, bf16[64,2048]{1,0:T(8,128)(2,1)S(1)}, u32[]{:S(2)}, u32[]{:S(2)}) collective-permute-start(bf16[64,2048]{1,0:T(8,128)(2,1)} %get-tuple-element.139), channel_id=1, source_target_pairs={{0,1},{1,0},{2,3},{3,2},{4,5},{5,4},{6,7},{7,6},{8,9},{9,8},{10,11... | collective-permute-start | bytes 786440 | tf_op jit(solution)/shard_map/ppermute | solution.py:92
  126.2 29.3 %all-to-all-start.3 = ((bf16[16,320,128]{2,1,0:T(8,128)(2,1)}), bf16[16,320,128]{2,1,0:T(8,128)(2,1)S(1)}, u32[]{:S(2)}, u32[]{:S(2)}) async-start(bf16[16,320,128]{2,1,0:T(8,128)(2,1)} %get-tuple-element.142), calls=%async_computation.3 | async-start | bytes 2621440 | tf_op jit(solution)/shard_map/all_to_all | solution.py:170
  132.5 7.1 collective-permute-start.11
  133.2 6.5 collective-permute-start.9
  136.2 5.2 collective-permute-start.15
  155.5 24.1 %all-to-all-start.4 = ((bf16[16,192,128]{2,1,0:T(8,128)(2,1)}), bf16[16,192,128]{2,1,0:T(8,128)(2,1)S(1)}, u32[]{:S(2)}, u32[]{:S(2)}) async-start(bf16[16,192,128]{2,1,0:T(8,128)(2,1)} %get-tuple-element.144), calls=%async_computation.4 | async-start | bytes 1572864 | tf_op jit(solution)/shard_map/all_to_all | solution.py:170
  183.2 6.3 collective-permute-start.16
  183.2 16.3 %all-to-all-start.5 = ((bf16[16,64,128]{2,1,0:T(8,128)(2,1)}), bf16[16,64,128]{2,1,0:T(8,128)(2,1)S(1)}, u32[]{:S(2)}, u32[]{:S(2)}) async-start(bf16[16,64,128]{2,1,0:T(8,128)(2,1)} %get-tuple-element.147), calls=%async_computation.5 | async-start | bytes 524288 | tf_op jit(solution)/shard_map/all_to_all | solution.py:170
  189.5 55.0 %reduce-scatter.7.cloned.1.call-start = ((), (), s32[]{:S(2)}) async-start(), calls=%async_computation.20 | async-start | bytes 4718592 | tf_op jit(solution)/shard_map/reduce_scatter | solution.py:100
  193.8 5.1 collective-permute-start.18
  207.5 71.7 %all-gather.11.cloned.1.call-start = ((), (), s32[]{:S(2)}) async-start(), calls=%async_computation.21 | async-start | bytes 4718592 | tf_op jit(solution)/shard_map/all_gather | solution.py:96
  248.0 84.1 %reduce-scatter.9.cloned.1.call-start = ((), (), s32[]{:S(2)}) async-start(), calls=%async_computation.22 | async-start | bytes 4718592 | tf_op jit(solution)/shard_map/reduce_scatter | solution.py:100
  299.5 36.8 %all-to-all-start.6 = ((bf16[16,512,128]{2,1,0:T(8,128)(2,1)}), bf16[16,512,128]{2,1,0:T(8,128)(2,1)}, u32[]{:S(2)}, u32[]{:S(2)}) async-start(bf16[16,512,128]{2,1,0:T(8,128)(2,1)} %bitcast.170), calls=%async_computation.8 | async-start | bytes 4194304 | tf_op jit(solution)/shard_map/all_to_all | solution.py:170
  306.9 84.1 %reduce-scatter.11.cloned.1.call-start = ((), (), s32[]{:S(2)}) async-start(), calls=%async_computation.23 | async-start | bytes 5242880 | tf_op jit(solution)/shard_map/reduce_scatter | solution.py:1553
  336.3 83.4 %reduce-scatter.13.cloned.1.call-start = ((), (), s32[]{:S(2)}) async-start(), calls=%async_computation.24 | async-start | bytes 1310720 | tf_op jit(solution)/shard_map/reduce_scatter | solution.py:1553
  339.3 12.0 %collective-permute-start.19 = (bf16[128,2048]{1,0:T(8,128)(2,1)S(1)}, bf16[128,2048]{1,0:T(8,128)(2,1)S(1)}, u32[]{:S(2)}, u32[]{:S(2)}) collective-permute-start(bf16[128,2048]{1,0:T(8,128)(2,1)S(1)} %get-tuple-element.284), channel_id=1, source_target_pairs={{0,6},{1,7},{2,0},{3,1},{4,2},{5,3},{6,4},{7,5},{8,14},{9,15},{10,... | collective-permute-start | bytes 1572872 | tf_op jit(solution)/shard_map/ppermute | solution.py:92
  340.1 13.2 %collective-permute-start.21 = (bf16[128,2048]{1,0:T(8,128)(2,1)S(1)}, bf16[128,2048]{1,0:T(8,128)(2,1)S(1)}, u32[]{:S(2)}, u32[]{:S(2)}) collective-permute-start(bf16[128,2048]{1,0:T(8,128)(2,1)S(1)} %get-tuple-element.284), channel_id=1, source_target_pairs={{0,2},{1,3},{2,4},{3,5},{4,6},{5,7},{6,0},{7,1},{8,10},{9,11},{10,... | collective-permute-start | bytes 1572872 | tf_op jit(solution)/shard_map/ppermute | solution.py:92
  351.3 6.4 collective-permute-start.20
  353.3 10.3 %collective-permute-start.23 = (bf16[128,2048]{1,0:T(8,128)(2,1)S(1)}, bf16[128,2048]{1,0:T(8,128)(2,1)S(1)}, u32[]{:S(2)}, u32[]{:S(2)}) collective-permute-start(bf16[128,2048]{1,0:T(8,128)(2,1)S(1)} %get-tuple-element.284), channel_id=1, source_target_pairs={{0,1},{1,0},{2,3},{3,2},{4,5},{5,4},{6,7},{7,6},{8,9},{9,8},{10,11... | collective-permute-start | bytes 1572872 | tf_op jit(solution)/shard_map/ppermute | solution.py:92
  353.4 10.0 %collective-permute-start.22 = (bf16[64,2048]{1,0:T(8,128)(2,1)S(1)}, bf16[64,2048]{1,0:T(8,128)(2,1)S(1)}, u32[]{:S(2)}, u32[]{:S(2)}) collective-permute-start(bf16[64,2048]{1,0:T(8,128)(2,1)S(1)} %slice.289), channel_id=1, source_target_pairs={{0,2},{1,3},{2,4},{3,5},{4,6},{5,7},{6,0},{7,1},{8,10},{9,11},{10,... | collective-permute-start | bytes 786440 | tf_op jit(solution)/shard_map/ppermute | solution.py:92
  353.5 10.2 %collective-permute-start.24 = (bf16[128,2048]{1,0:T(8,128)(2,1)S(1)}, bf16[128,2048]{1,0:T(8,128)(2,1)S(1)}, u32[]{:S(2)}, u32[]{:S(2)}) collective-permute-start(bf16[128,2048]{1,0:T(8,128)(2,1)S(1)} %collective-permute-done.19), channel_id=1, source_target_pairs={{0,1},{1,0},{2,3},{3,2},{4,5},{5,4},{6,7},{7,6},{8,9},{9,8},{10,11... | collective-permute-start | bytes 1572872 | tf_op jit(solution)/shard_map/ppermute | solution.py:92
  354.0 11.4 %collective-permute-start.26 = (bf16[128,2048]{1,0:T(8,128)(2,1)S(1)}, bf16[128,2048]{1,0:T(8,128)(2,1)S(1)}, u32[]{:S(2)}, u32[]{:S(2)}) collective-permute-start(bf16[128,2048]{1,0:T(8,128)(2,1)S(1)} %collective-permute-done.21), channel_id=1, source_target_pairs={{0,1},{1,0},{2,3},{3,2},{4,5},{5,4},{6,7},{7,6},{8,9},{9,8},{10,11... | collective-permute-start | bytes 1572872 | tf_op jit(solution)/shard_map/ppermute | solution.py:92
  380.4 5.1 collective-permute-start.29
  390.9 28.8 %all-to-all-start.7 = ((bf16[16,256,128]{2,1,0:T(8,128)(2,1)}), bf16[16,256,128]{2,1,0:T(8,128)(2,1)}, u32[]{:S(2)}, u32[]{:S(2)}) async-start(bf16[16,256,128]{2,1,0:T(8,128)(2,1)} %get-tuple-element.172), calls=%async_computation.10 | async-start | bytes 2097152 | tf_op jit(solution)/shard_map/all_to_all | solution.py:170
  398.0 72.7 %reduce-scatter.15.cloned.1.call-start = ((), (), s32[]{:S(2)}) async-start(), calls=%async_computation.25 | async-start | bytes 4587520 | tf_op jit(solution)/shard_map/reduce_scatter | solution.py:1553
  434.2 10.9 %all-to-all-start.8 = ((bf16[8,128,128]{2,1,0:T(8,128)(2,1)}), bf16[8,128,128]{2,1,0:T(8,128)(2,1)S(1)}, u32[]{:S(2)}, u32[]{:S(2)}) async-start(bf16[8,128,128]{2,1,0:T(8,128)(2,1)} %bitcast.43), calls=%async_computation.12 | async-start | bytes 524288 | tf_op jit(solution)/shard_map/all_to_all | solution.py:174
  437.6 61.8 %reduce-scatter.17.cloned.1.call-start = ((), (), s32[]{:S(2)}) async-start(), calls=%async_computation.26 | async-start | bytes 1146880 | tf_op jit(solution)/shard_map/reduce_scatter | solution.py:1553
  446.2 6.5 collective-permute-start.31
  446.9 5.9 collective-permute-start.35
  449.5 19.4 %collective-permute-start.33 = (bf16[32,2048]{1,0:T(8,128)(2,1)S(1)}, bf16[32,2048]{1,0:T(8,128)(2,1)S(1)}, u32[]{:S(2)}, u32[]{:S(2)}) collective-permute-start(bf16[32,2048]{1,0:T(8,128)(2,1)S(1)} %get-tuple-element.261), channel_id=1, source_target_pairs={{0,2},{1,3},{2,4},{3,5},{4,6},{5,7},{6,0},{7,1},{8,10},{9,11},{10,... | collective-permute-start | bytes 393224 | tf_op jit(solution)/shard_map/ppermute | solution.py:92
  449.5 19.4 %collective-permute-start.34 = (bf16[32,2048]{1,0:T(8,128)(2,1)S(1)}, bf16[32,2048]{1,0:T(8,128)(2,1)S(1)}, u32[]{:S(2)}, u32[]{:S(2)}) collective-permute-start(bf16[32,2048]{1,0:T(8,128)(2,1)S(1)} %get-tuple-element.259), channel_id=1, source_target_pairs={{0,6},{1,7},{2,0},{3,1},{4,2},{5,3},{6,4},{7,5},{8,14},{9,15},{10,... | collective-permute-start | bytes 393224 | tf_op jit(solution)/shard_map/ppermute | solution.py:92
  453.8 15.2 %collective-permute-start.32 = (bf16[32,2048]{1,0:T(8,128)(2,1)S(1)}, bf16[32,2048]{1,0:T(8,128)(2,1)S(1)}, u32[]{:S(2)}, u32[]{:S(2)}) collective-permute-start(bf16[32,2048]{1,0:T(8,128)(2,1)S(1)} %get-tuple-element.264), channel_id=1, source_target_pairs={{0,2},{1,3},{2,4},{3,5},{4,6},{5,7},{6,0},{7,1},{8,10},{9,11},{10,... | collective-permute-start | bytes 393224 | tf_op jit(solution)/shard_map/ppermute | solution.py:92
  454.2 14.7 %collective-permute-start.36 = (bf16[32,2048]{1,0:T(8,128)(2,1)S(1)}, bf16[32,2048]{1,0:T(8,128)(2,1)S(1)}, u32[]{:S(2)}, u32[]{:S(2)}) collective-permute-start(bf16[32,2048]{1,0:T(8,128)(2,1)S(1)} %get-tuple-element.263), channel_id=1, source_target_pairs={{0,6},{1,7},{2,0},{3,1},{4,2},{5,3},{6,4},{7,5},{8,14},{9,15},{10,... | collective-permute-start | bytes 393224 | tf_op jit(solution)/shard_map/ppermute | solution.py:92
  470.8 28.5 %all-to-all-start.9 = ((bf16[16,320,128]{2,1,0:T(8,128)(2,1)}), bf16[16,320,128]{2,1,0:T(8,128)(2,1)}, u32[]{:S(2)}, u32[]{:S(2)}) async-start(bf16[16,320,128]{2,1,0:T(8,128)(2,1)} %attn_bwd.1), calls=%async_computation.14 | async-start | bytes 2621440 | tf_op jit(solution)/shard_map/all_to_all | solution.py:170
  476.3 153.4 %all-gather.13.cloned.1.call-start = ((), (), s32[]{:S(2)}) async-start(), calls=%async_computation.27 | async-start | bytes 8912896 | tf_op jit(solution)/shard_map/all_gather | solution.py:1560
  501.1 28.8 %all-to-all-start.10 = ((bf16[16,272,128]{2,1,0:T(8,128)(2,1)}), bf16[16,272,128]{2,1,0:T(8,128)(2,1)}, u32[]{:S(2)}, u32[]{:S(2)}) async-start(bf16[16,272,128]{2,1,0:T(8,128)(2,1)} %get-tuple-element.196), calls=%async_computation.16 | async-start | bytes 2228224 | tf_op jit(solution)/shard_map/all_to_all | solution.py:170
  541.9 73.3 %all-to-all-start.11 = ((bf16[16,896,128]{2,1,0:T(8,128)(2,1)}), bf16[16,896,128]{2,1,0:T(8,128)(2,1)}, u32[]{:S(2)}, u32[]{:S(2)}) async-start(bf16[16,896,128]{2,1,0:T(8,128)(2,1)} %bitcast.164), calls=%async_computation.17 | async-start | bytes 7340032 | tf_op jit(solution)/shard_map/all_to_all | solution.py:170
  546.8 153.8 %all-gather.15.cloned.1.call-start = ((), (), s32[]{:S(2)}) async-start(), calls=%async_computation.28 | async-start | bytes 5570560 | tf_op jit(solution)/shard_map/all_gather | solution.py:1560
  558.6 4.6 collective-permute-start.38
  558.7 9.0 %collective-permute-start.37 = (bf16[512,2048]{1,0:T(8,128)(2,1)}, bf16[512,2048]{1,0:T(8,128)(2,1)}, u32[]{:S(2)}, u32[]{:S(2)}) collective-permute-start(bf16[512,2048]{1,0:T(8,128)(2,1)} %bitcast.212), channel_id=1, source_target_pairs={{0,1},{1,0},{2,3},{3,2},{4,5},{5,4},{6,7},{7,6},{8,9},{9,8},{10,11... | collective-permute-start | bytes 6291464 | tf_op jit(solution)/shard_map/ppermute | solution.py:92
  632.6 20.0 %collective-permute-start.42 = (bf16[64,4096]{1,0:T(8,128)(2,1)S(1)}, bf16[64,4096]{1,0:T(8,128)(2,1)S(1)}, u32[]{:S(2)}, u32[]{:S(2)}) collective-permute-start(bf16[64,4096]{1,0:T(8,128)(2,1)S(1)} %get-tuple-element.250), channel_id=1, source_target_pairs={{0,2},{1,3},{2,4},{3,5},{4,6},{5,7},{6,0},{7,1},{8,10},{9,11},{10,... | collective-permute-start | bytes 1572872 | tf_op jit(solution)/shard_map/ppermute | solution.py:92
  633.2 19.4 %collective-permute-start.43 = (bf16[64,4096]{1,0:T(8,128)(2,1)S(1)}, bf16[64,4096]{1,0:T(8,128)(2,1)S(1)}, u32[]{:S(2)}, u32[]{:S(2)}) collective-permute-start(bf16[64,4096]{1,0:T(8,128)(2,1)S(1)} %get-tuple-element.249), channel_id=1, source_target_pairs={{0,6},{1,7},{2,0},{3,1},{4,2},{5,3},{6,4},{7,5},{8,14},{9,15},{10,... | collective-permute-start | bytes 1572872 | tf_op jit(solution)/shard_map/ppermute | solution.py:92
  635.9 22.8 %collective-permute-start.44 = (bf16[64,4096]{1,0:T(8,128)(2,1)S(1)}, bf16[64,4096]{1,0:T(8,128)(2,1)S(1)}, u32[]{:S(2)}, u32[]{:S(2)}) collective-permute-start(bf16[64,4096]{1,0:T(8,128)(2,1)S(1)} %get-tuple-element.248), channel_id=1, source_target_pairs={{0,2},{1,3},{2,4},{3,5},{4,6},{5,7},{6,0},{7,1},{8,10},{9,11},{10,... | collective-permute-start | bytes 1572872 | tf_op jit(solution)/shard_map/ppermute | solution.py:92
  635.9 22.8 %collective-permute-start.45 = (bf16[64,4096]{1,0:T(8,128)(2,1)S(1)}, bf16[64,4096]{1,0:T(8,128)(2,1)S(1)}, u32[]{:S(2)}, u32[]{:S(2)}) collective-permute-start(bf16[64,4096]{1,0:T(8,128)(2,1)S(1)} %get-tuple-element.247), channel_id=1, source_target_pairs={{0,6},{1,7},{2,0},{3,1},{4,2},{5,3},{6,4},{7,5},{8,14},{9,15},{10,... | collective-permute-start | bytes 1572872 | tf_op jit(solution)/shard_map/ppermute | solution.py:92
  643.0 5.7 collective-permute-start.40
  659.7 24.8 %collective-permute-start.49 = (bf16[64,4096]{1,0:T(8,128)(2,1)}, bf16[64,4096]{1,0:T(8,128)(2,1)}, u32[]{:S(2)}, u32[]{:S(2)}) collective-permute-start(bf16[64,4096]{1,0:T(8,128)(2,1)} %add_convert_fusion), channel_id=1, source_target_pairs={{0,6},{1,7},{2,0},{3,1},{4,2},{5,3},{6,4},{7,5},{8,14},{9,15},{10,... | collective-permute-start | bytes 1572872 | tf_op jit(solution)/shard_map/ppermute | solution.py:92
  662.6 6.0 collective-permute-start.46
  664.8 19.7 %collective-permute-start.48 = (bf16[64,4096]{1,0:T(8,128)(2,1)}, bf16[64,4096]{1,0:T(8,128)(2,1)}, u32[]{:S(2)}, u32[]{:S(2)}) collective-permute-start(bf16[64,4096]{1,0:T(8,128)(2,1)} %add_convert_fusion.1), channel_id=1, source_target_pairs={{0,2},{1,3},{2,4},{3,5},{4,6},{5,7},{6,0},{7,1},{8,10},{9,11},{10,... | collective-permute-start | bytes 1572872 | tf_op jit(solution)/shard_map/ppermute | solution.py:92
  684.5 5.0 collective-permute-start.50
  689.5 6.2 collective-permute-start.51
  (43 other events, 311.1 us)
Sparse Core Ops, SparseCore 0:
  27.2 55.5 all-gather.16
  92.4 32.0 all-gather.8
  127.3 62.9 all-gather.18
  207.6 36.8 reduce-scatter.6
  248.1 31.0 all-gather.10
  293.3 38.7 reduce-scatter.8
  336.4 43.9 reduce-scatter.10
  391.1 28.5 reduce-scatter.12
  422.7 38.8 reduce-scatter.14
  470.9 28.3 reduce-scatter.16
  502.1 111.9 all-gather.12
  629.9 54.7 all-gather.14

commit v6 on v5

--- a/solution.py
+++ b/solution.py
@@ -1583,7 +1583,7 @@
     packed_two = side_by_side(
         column_grad(gated_heads, branch, by_y=True), column_grad(normed, dz, by_y=True)
     )
-    d_mixers, packed_two, sum_gu = together(d_mixers, packed_two, sum_gu)
+    d_mixers, packed_two = together(d_mixers, packed_two)
     sum_two = scatter_ctx(packed_two, along_y)
     dx, dbc_mine, dbc_other, drow, dskip = mamba_bwd(
         place, x_act, d_mixers, bc, row_terms, states, my_skip
@@ -1591,7 +1591,7 @@
     dbc_joined = ring_join(
         dbc_mine.reshape(NZ * BC_F, LENGTH), dbc_other.reshape(NZ * BC_F, LENGTH)
     )
-    dx, d_mixers = together(dx, d_mixers)
+    dx, d_mixers, sum_gu = together(dx, d_mixers, sum_gu)
     down_at = NF * gu_tiles
     out_at = down_at + row_tiles
     gu_part = swap_fsdp(sum_gu.reshape(NF, -1, LANES))
@@ -1668,7 +1668,7 @@
     placed = jnp.where(mine, own[None, :own_pad], 0.0).reshape(-1)
     total = jnp.concatenate([placed, own[own_pad:]]).reshape(-1, LANES)
     total, g_gate_up, g_down, g_mout, g_aout, *both = together(
-        butterfly(total, "fsdp", (1,)),
+        butterfly(total, "fsdp", (1, 2, 4)),
         unpack_gate_up(all_one),
         *unpack_rows(all_one, down_at),
         *ring_second(*both),
@@ -1682,7 +1682,7 @@
     d_hidden, _ = norm_back(hidden, scale_one, norm_gain, d_normed)
     d_tokens = even_first((d_hidden + d_mixed).astype(BF)).reshape(tokens.shape)
 
-    total = butterfly(total, "fsdp", (2, 4)).reshape(-1)
+    total = total.reshape(-1)
     each = total[: NF * own_pad].reshape(NF, own_pad)
     cut = [(CONV_K + 1) * INNER_F]
     cut.append(cut[0] + (CONV_K + 1) * BC_F)

time: 729 us -> 742 us (1.018)
  transfers between devices with their start and end apart: 75 -> 75, of which waited for: 35 -> 34; matrix products, arithmetic and copies ran while one was open for 10% -> 10% of each run, Pallas kernels for 23% -> 23%
where the time goes in v6:
time: 742 us; the launch traced here: 730 us
  waiting for transfers between devices  277 us (37%)
  Pallas kernels  206 us (28%)
  starting transfers between devices  111 us (15%)
  local copies, waits for them, and re-layouts  46.2 us (6%)
  other arithmetic  43.2 us (6%)
  blocking collectives  25.2 us (3%)
  between operations  21 us (3%)
    all_to_all x9, waiting for transfers between devices, swap_ctx(): return lax.all_to_all(value, 'ctx', 0, 0, tiled=True)  90.5 us
    all_to_all x9, starting transfers between devices, swap_ctx(): return lax.all_to_all(value, 'ctx', 0, 0, tiled=True)  55.4 us
    reduce_scatter x2, waiting for transfers between devices, scatter_fsdp(): lax.psum_scatter(parts, 'fsdp', scatter_dimension=0, tiled=True).astype(F32)  45.7 us
    ppermute x13, waiting for transfers between devices, exchange(): lax.ppermute(value, axis, [(i, i ^ bit) for i in range(size)])  45.4 us
    ppermute x39, waiting for transfers between devices, send(): return lax.ppermute(value, 'fsdp', route)  44.6 us
    ppermute x39, starting transfers between devices, send(): return lax.ppermute(value, 'fsdp', route)  41.6 us
    pallas_call x5, Pallas kernels, column_grad(): pl.pallas_call(functools.partial(column_grad_kernel, by_y), grid=(count /...  35.4 us
    all_to_all x2, blocking collectives, swap_fsdp(): return lax.all_to_all(value, 'fsdp', 0, 0, tiled=True)  25.2 us
  transfers between devices with their start and end apart: 75, of which 34 were waited for; matrix products, arithmetic and copies ran while one was open for 10% of the time, Pallas kernels for 23%

profile of v6, /device:TPU:16, one launch (start us, length us, event | category | flops | bytes accessed | tf_op | source)
XLA Modules:
  0.0 729.8 jit_solution(12559651372866798018)
XLA Ops:
  13.6 13.5 %all_to_all.65 = bf16[8,16,1280]{2,1,0:T(8,128)(2,1)} all-to-all(bf16[8,16,1280]{2,1,0:T(8,128)(2,1)S(1)} %copy.115), channel_id=1, replica_groups=mesh['ctx'=16,'fsdp'=8] {'fsdp'}, dimensions={0} | all-to-all | bytes 655360 | tf_op jit(solution)/shard_map/all_to_all | solution.py:174
  42.3 3.6 collective-permute-done
  57.6 8.5 %collective-permute-done.3 = bf16[64,2048]{1,0:T(8,128)(2,1)S(1)} collective-permute-done((bf16[64,2048]{1,0:T(8,128)(2,1)S(1)}, bf16[64,2048]{1,0:T(8,128)(2,1)S(1)}, u32[]{:S(2)}, u32[]{:S(2)}) %collective-permute-start.3) | collective-permute-done | bytes 262176 | tf_op jit(solution)/shard_map/ppermute | solution.py:92
  71.2 11.6 %all-gather.17.cloned.1.call-done = bf16[128,16,1280]{2,1,0:T(8,128)(2,1)} async-done(((bf16[8,16,1280]{2,1,0:T(8,128)(2,1)}), bf16[128,16,1280]{2,1,0:T(8,128)(2,1)}) %all-gather.17.cloned.1.call-update) | async-done | bytes 5242896 | tf_op jit(solution)/shard_map/all_gather | solution.py:1476
  82.8 9.4 %project.1 = (bf16[16,272,128]{2,1,0:T(8,128)(2,1)}, bf16[16,320,128]{2,1,0:T(8,128)(2,1)}) custom-call(bf16[1024,2048]{1,0:T(8,128)(2,1)} %constant_dynamic-update-slice_fusion.27.n_ref.left_ref, bf16[16,8,16,1280]{3,2,1,0:T(8,128)(2,1)} %bitcast.162, f32[128,64]{1,0:T(8,128)} %get-tuple-element.270.cos_ref, f32[128,64]{1,0:T(8,128)} %get-tuple-element.269.sin_ref), custom_call_target="tpu_custom_call" | custom-call | flops 3758096384 | bytes 10000000 | tf_op jit(solution)/shard_map/project/pallas_call | solution.py:238
  92.4 5.7 all-to-all-start.2
  99.6 7.8 %project_z.1.z_ref = f32[8,384,128]{2,1,0:T(8,128)} custom-call(bf16[1024,2048]{1,0:T(8,128)(2,1)} %constant_dynamic-update-slice_fusion.27.n_ref.left_ref, bf16[16,8,16,1280]{3,2,1,0:T(8,128)(2,1)} %bitcast.163), custom_call_target="tpu_custom_call" | custom-call | flops 1610612736 | bytes 8000000 | tf_op jit(solution)/shard_map/project_z/pallas_call | solution.py:269
  107.4 6.6 all-to-all-done.2.got_ref
  115.0 6.4 front.1
  126.2 6.2 all-to-all-start.3
  142.7 8.5 %mamba_fwd.1 = (bf16[16,192,128]{2,1,0:T(8,128)(2,1)}, f32[8,192,256]{2,1,0:T(8,128)}) custom-call(s32[8]{0:T(128)} %fusion.14.place_ref, bf16[192,2048]{1,0:T(8,128)(2,1)} %get-tuple-element.136.x_ref, bf16[8,64,2048]{2,1,0:T(8,128)(2,1)} %bitcast.208, f32[16,2048]{1,0:T(8,128)} %get-tuple-element.140.row_ref, f32[192,1]{1,0:T(8,128)} %broadcast_in_dim_reshape.4.skip_ref), custom_call_target="tpu_custom_call" | custom-call | flops 872415232 | bytes 7000000 | tf_op jit(solution)/shard_map/mamba_fwd/pallas_call | solution.py:958
  151.1 4.3 all-to-all-done.3.q_ref.k_ref.v_ref
  155.5 6.1 all-to-all-start.4
  161.6 9.2 %attn_fwd.1 = (bf16[16,64,128]{2,1,0:T(8,128)(2,1)}, f32[1024,1]{1,0:T(8,128)}) custom-call(s32[1]{0:T(128)} %bitcast.31.odd_ref, bf16[16,320,128]{2,1,0:T(8,128)(2,1)} %copy-done.10, bf16[16,320,128]{2,1,0:T(8,128)(2,1)} %copy-done.10, bf16[16,320,128]{2,1,0:T(8,128)(2,1)} %copy-done.10), custom_call_target="tpu_custom_call" | custom-call | flops 1073741824 | bytes 3000000 | tf_op jit(solution)/shard_map/attn_fwd/pallas_call | solution.py:1160
  170.7 8.8 %all-to-all-done.4.got_ref = bf16[16,192,128]{2,1,0:T(8,128)(2,1)S(1)} async-done(((bf16[16,192,128]{2,1,0:T(8,128)(2,1)}), bf16[16,192,128]{2,1,0:T(8,128)(2,1)S(1)}, u32[]{:S(2)}, u32[]{:S(2)}) %all-to-all-start.4) | async-done | bytes 786464 | tf_op jit(solution)/shard_map/all_to_all | solution.py:170
  183.2 6.3 all-to-all-start.5
  200.3 7.2 branch_out.1
  207.5 37.0 %reduce-scatter.7.cloned.1.call-done = bf16[128,2048]{1,0:T(8,128)(2,1)} async-done(((bf16[1024,2048]{1,0:T(8,128)(2,1)}), bf16[128,2048]{1,0:T(8,128)(2,1)}) %reduce-scatter.7.cloned.1.call-update) | async-done | bytes 524304 | tf_op jit(solution)/shard_map/reduce_scatter | solution.py:100
  248.0 6.5 act_back.1.d_act_ref
  254.5 24.7 %all-gather.11.cloned.1.call-done.n_ref.left_ref = bf16[1024,2048]{1,0:T(8,128)(2,1)} async-done(((bf16[128,2048]{1,0:T(8,128)(2,1)}), bf16[1024,2048]{1,0:T(8,128)(2,1)}) %all-gather.11.cloned.1.call-update) | async-done | bytes 4194320 | tf_op jit(solution)/shard_map/all_gather | solution.py:96
  279.2 13.9 %mlp.1 = (bf16[1024,512]{1,0:T(8,128)(2,1)}, bf16[1024,1024]{1,0:T(8,128)(2,1)}, bf16[1024,2048]{1,0:T(8,128)(2,1)}) custom-call(bf16[1024,2048]{1,0:T(8,128)(2,1)} %all-gather.11.cloned.1.call-done.n_ref.left_ref, f32[1024,512]{1,0:T(8,128)} %act_back.1.d_act_ref, bf16[16,8,16,1024]{3,2,1,0:T(8,128)(2,1)} %bitcast.214), custom_call_target="tpu_custom_call" | custom-call | flops 8589934592 | bytes 20000000 | tf_op jit(solution)/shard_map/mlp/pallas_call | solution.py:610
  293.2 6.2 column_grad.6
  299.4 7.4 %all-to-all-start.6 = ((bf16[16,512,128]{2,1,0:T(8,128)(2,1)}), bf16[16,512,128]{2,1,0:T(8,128)(2,1)}, u32[]{:S(2)}, u32[]{:S(2)}) async-start(bf16[16,512,128]{2,1,0:T(8,128)(2,1)} %bitcast.172), calls=%async_computation.8 | async-start | bytes 4194304 | tf_op jit(solution)/shard_map/all_to_all | solution.py:170
  307.9 6.9 down_out.1
  314.8 8.5 %column_grad.5 = bf16[16,8,8,16,128]{4,3,2,1,0:T(8,128)(2,1)} custom-call(bf16[1024,2048]{1,0:T(8,128)(2,1)} %all-gather.11.cloned.1.call-done.n_ref.left_ref, bf16[1024,1024]{1,0:T(8,128)(2,1)} %get-tuple-element.162.refs_0_), custom_call_target="tpu_custom_call" | custom-call | flops 4294967296 | bytes 10485760 | tf_op jit(solution)/shard_map/column_grad/pallas_call | solution.py:405
  323.4 8.7 %reduce-scatter.9.cloned.1.call-done = bf16[128,2048]{1,0:T(8,128)(2,1)} async-done(((bf16[1024,2048]{1,0:T(8,128)(2,1)}), bf16[128,2048]{1,0:T(8,128)(2,1)}) %reduce-scatter.9.cloned.1.call-update) | async-done | bytes 524304 | tf_op jit(solution)/shard_map/reduce_scatter | solution.py:100
  341.3 9.9 %collective-permute-done.19 = bf16[128,2048]{1,0:T(8,128)(2,1)S(1)} collective-permute-done((bf16[128,2048]{1,0:T(8,128)(2,1)S(1)}, bf16[128,2048]{1,0:T(8,128)(2,1)S(1)}, u32[]{:S(2)}, u32[]{:S(2)}) %collective-permute-start.19) | collective-permute-done | bytes 524320 | tf_op jit(solution)/shard_map/ppermute | solution.py:92
  354.0 3.6 collective-permute-done.20
  357.6 5.5 collective-permute-done.22
  367.3 7.1 branch_back.1
  376.6 3.6 collective-permute-done.28
  380.2 5.1 collective-permute-done.29
  385.9 4.8 gate_back.1
  390.7 7.2 all-to-all-start.7
  398.1 6.2 column_grad.7
  404.4 6.1 column_grad.8
  410.5 3.6 pad_maximum_fusion
  414.0 5.0 all-to-all-done.7.got_ref.do_ref
  419.1 14.3 %mamba_bwd.1 = (f32[192,2048]{1,0:T(8,128)}, bf16[4,64,2048]{2,1,0:T(8,128)(2,1)}, bf16[4,64,2048]{2,1,0:T(8,128)(2,1)}, f32[8,2048]{1,0:T(8,128)}, f32[192,1]{1,0:T(8,128)}) custom-call(s32[8]{0:T(128)} %fusion.14.place_ref, bf16[192,2048]{1,0:T(8,128)(2,1)} %get-tuple-element.136.x_ref, bf16[16,256,128]{2,1,0:T(8,128)(2,1)} %all-to-all-done.7.got_ref.do_ref, ...), custom_call_target="tpu_custom_call" | custom-call | flops 2214592512 | bytes 12000000 | tf_op jit(solution)/shard_map/mamba_bwd/pallas_call | solution.py:1089
  433.5 3.4 all-to-all-start.8
  439.9 4.5 all-to-all-done.8
  456.7 11.6 %attn_bwd.1 = bf16[16,320,128]{2,1,0:T(8,128)(2,1)} custom-call(s32[1]{0:T(128)} %bitcast.31.odd_ref, bf16[16,320,128]{2,1,0:T(8,128)(2,1)} %copy-done.10, bf16[16,320,128]{2,1,0:T(8,128)(2,1)} %copy-done.10, bf16[16,320,128]{2,1,0:T(8,128)(2,1)} %copy-done.10, bf16[16,256,128]{2,1,0:T(8,128)(2,1)} %all-to-all-done.7.got_ref.do_ref, ...), custom_call_target="tpu_custom_call" | custom-call | flops 2684354560 | bytes 4000000 | tf_op jit(solution)/shard_map/attn_bwd/pallas_call | solution.py:1212
  470.2 6.1 all-to-all-start.9
  478.2 11.0 %front_back.1 = (bf16[16,272,128]{2,1,0:T(8,128)(2,1)}, f32[256,8]{1,0:T(8,128)}, f32[8,1]{1,0:T(8,128)}) custom-call(bf16[16,272,128]{2,1,0:T(8,128)(2,1)} %copy-done.3, f32[256,8]{1,0:T(8,128)} %bitcast.176, f32[8,128]{1,0:T(8,128)} %broadcast_in_dim.71.heads_ref, f32[16,2048]{1,0:T(8,128)} %get-tuple-element.140.row_ref, ...), custom_call_target="tpu_custom_call" | custom-call | flops 31457280 | bytes 9000000 | tf_op jit(solution)/shard_map/front_back/pallas_call | solution.py:853
  489.2 10.1 %reduce-scatter.17.cloned.1.call-done = bf16[1,896,128]{2,1,0:T(8,128)(2,1)} async-done(((bf16[4,896,128]{2,1,0:T(8,128)(2,1)}), bf16[1,896,128]{2,1,0:T(8,128)(2,1)}) %reduce-scatter.17.cloned.1.call-update) | async-done | bytes 229392 | tf_op jit(solution)/shard_map/reduce_scatter | solution.py:1553
  501.1 5.7 all-to-all-start.10
  506.8 4.0 attn_grads.1.refs_1_.dqkv_ref
  510.8 18.9 %all-to-all-done.10.got_ref = bf16[16,272,128]{2,1,0:T(8,128)(2,1)} async-done(((bf16[16,272,128]{2,1,0:T(8,128)(2,1)}), bf16[16,272,128]{2,1,0:T(8,128)(2,1)}, u32[]{:S(2)}, u32[]{:S(2)}) %all-to-all-start.10) | async-done | bytes 1114144 | tf_op jit(solution)/shard_map/all_to_all | solution.py:170
  529.8 3.6 mix_grads.1.refs_0_.mix_ref
  533.4 8.3 %column_grad.9 = bf16[16,8,7,16,128]{4,3,2,1,0:T(8,128)(2,1)} custom-call(bf16[1024,2048]{1,0:T(8,128)(2,1)} %constant_dynamic-update-slice_fusion.27.n_ref.left_ref, bf16[1024,512]{1,0:T(8,128)(2,1)} %mix_grads.1.refs_0_.mix_ref, bf16[1024,384]{1,0:T(8,128)(2,1)} %attn_grads.1.refs_1_.dqkv_ref), custom_call_target="tpu_custom_call" | custom-call | flops 3758096384 | bytes 9699328 | tf_op jit(solution)/shard_map/column_grad/pallas_call | solution.py:405
  541.7 4.8 all-to-all-start.11
  546.6 11.8 %back_project.1 = (bf16[4,128,2048]{2,1,0:T(8,128)(2,1)}, bf16[4,128,2048]{2,1,0:T(8,128)(2,1)}, f32[1,2048]{1,0:T(1,128)}) custom-call(s32[5]{0:T(128)} %pad_add_fusion.1.spot_ref, bf16[1024,512]{1,0:T(8,128)(2,1)} %mix_grads.1.refs_0_.mix_ref, bf16[1024,384]{1,0:T(8,128)(2,1)} %attn_grads.1.refs_1_.dqkv_ref, ...), custom_call_target="tpu_custom_call" | custom-call | flops 5368709120 | bytes 18000000 | tf_op jit(solution)/shard_map/back_project/pallas_call | solution.py:360
  563.0 4.5 fusion
  567.5 3.8 fusion.1
  571.3 43.9 %all-to-all-done.11 = bf16[16,896,128]{2,1,0:T(8,128)(2,1)} async-done(((bf16[16,896,128]{2,1,0:T(8,128)(2,1)}), bf16[16,896,128]{2,1,0:T(8,128)(2,1)}, u32[]{:S(2)}, u32[]{:S(2)}) %all-to-all-start.11) | async-done | bytes 3670048 | tf_op jit(solution)/shard_map/all_to_all | solution.py:170
  617.8 11.8 %all_to_all.66 = bf16[8,160,128]{2,1,0:T(8,128)(2,1)} all-to-all(bf16[8,160,128]{2,1,0:T(8,128)(2,1)S(1)} %pad_maximum_fusion.2), channel_id=1, replica_groups=mesh['ctx'=16,'fsdp'=8] {'fsdp'}, dimensions={0} | all-to-all | bytes 655360 | tf_op jit(solution)/shard_map/all_to_all | solution.py:174
  643.5 5.4 collective-permute-done.40
  652.9 6.3 collective-permute-done.44
  660.7 4.4 collective-permute-done.46
  672.0 11.3 %collective-permute-done.48 = f32[200,128]{1,0:T(8,128)S(1)} collective-permute-done((f32[200,128]{1,0:T(8,128)S(1)}, f32[200,128]{1,0:T(8,128)S(1)}, u32[]{:S(2)}, u32[]{:S(2)}) %collective-permute-start.48) | collective-permute-done | bytes 102432 | tf_op jit(solution)/shard_map/ppermute | solution.py:179
  686.2 3.6 collective-permute-done.49
  689.8 8.3 %unpack_rows.1 = (f32[512,2048]{1,0:T(8,128)}, f32[384,2048]{1,0:T(8,128)}, f32[128,2048]{1,0:T(8,128)}) custom-call(bf16[16,128,16,128]{3,2,1,0:T(8,128)(2,1)} %all-gather.13.cloned.1.call-done.refs_0_.refs_1_.refs_2_.refs_3_.tiles_ref), custom_call_target="tpu_custom_call" | custom-call | flops 2097152 | bytes 12582912 | tf_op jit(solution)/shard_map/unpack_rows/pallas_call | solution.py:1271
  698.1 6.0 unpack_gate_up.1
  713.4 6.3 unpack_in.1
  (385 shorter events, 157.7 us)
Async XLA Ops:
  7.2 75.7 %all-gather.17.cloned.1.call-start = ((), (), s32[]{:S(2)}) async-start(), calls=%async_computation.29 | async-start | bytes 5570560 | tf_op jit(solution)/shard_map/all_gather | solution.py:1476
  32.3 13.6 %collective-permute-start = (bf16[128,2048]{1,0:T(8,128)(2,1)S(1)}, bf16[128,2048]{1,0:T(8,128)(2,1)S(1)}, u32[]{:S(2)}, u32[]{:S(2)}) collective-permute-start(bf16[128,2048]{1,0:T(8,128)(2,1)S(1)} %get-tuple-element.282), channel_id=1, source_target_pairs={{0,6},{1,7},{2,0},{3,1},{4,2},{5,3},{6,4},{7,5},{8,14},{9,15},{10,... | collective-permute-start | bytes 1572872 | tf_op jit(solution)/shard_map/ppermute | solution.py:92
  33.5 19.9 %collective-permute-start.2 = (bf16[128,2048]{1,0:T(8,128)(2,1)S(1)}, bf16[128,2048]{1,0:T(8,128)(2,1)S(1)}, u32[]{:S(2)}, u32[]{:S(2)}) collective-permute-start(bf16[128,2048]{1,0:T(8,128)(2,1)S(1)} %get-tuple-element.282), channel_id=1, source_target_pairs={{0,2},{1,3},{2,4},{3,5},{4,6},{5,7},{6,0},{7,1},{8,10},{9,11},{10,... | collective-permute-start | bytes 1572872 | tf_op jit(solution)/shard_map/ppermute | solution.py:92
  34.3 33.5 %collective-permute-start.4 = (bf16[128,2048]{1,0:T(8,128)(2,1)S(1)}, bf16[128,2048]{1,0:T(8,128)(2,1)S(1)}, u32[]{:S(2)}, u32[]{:S(2)}) collective-permute-start(bf16[128,2048]{1,0:T(8,128)(2,1)S(1)} %get-tuple-element.282), channel_id=1, source_target_pairs={{0,1},{1,0},{2,3},{3,2},{4,5},{5,4},{6,7},{7,6},{8,9},{9,8},{10,11... | collective-permute-start | bytes 1572872 | tf_op jit(solution)/shard_map/ppermute | solution.py:92
  46.6 10.0 %collective-permute-start.1 = (bf16[64,2048]{1,0:T(8,128)(2,1)}, bf16[64,2048]{1,0:T(8,128)(2,1)}, u32[]{:S(2)}, u32[]{:S(2)}) collective-permute-start(bf16[64,2048]{1,0:T(8,128)(2,1)} %slice.284), channel_id=1, source_target_pairs={{0,6},{1,7},{2,0},{3,1},{4,2},{5,3},{6,4},{7,5},{8,14},{9,15},{10,... | collective-permute-start | bytes 786440 | tf_op jit(solution)/shard_map/ppermute | solution.py:92
  49.9 21.3 %all-to-all-start.1 = ((bf16[8,16,1024]{2,1,0:T(8,128)(2,1)}), bf16[8,16,1024]{2,1,0:T(8,128)(2,1)S(1)}, u32[]{:S(2)}, u32[]{:S(2)}) async-start(bf16[8,16,1024]{2,1,0:T(8,128)(2,1)} %copy.116), calls=%async_computation.1 | async-start | bytes 524288 | tf_op jit(solution)/shard_map/all_to_all | solution.py:174
  53.3 102.2 %all-gather.9.cloned.1.call-start = ((), (), s32[]{:S(2)}) async-start(), calls=%async_computation.19 | async-start | bytes 4718592 | tf_op jit(solution)/shard_map/all_gather | solution.py:96
  53.4 12.7 %collective-permute-start.3 = (bf16[64,2048]{1,0:T(8,128)(2,1)S(1)}, bf16[64,2048]{1,0:T(8,128)(2,1)S(1)}, u32[]{:S(2)}, u32[]{:S(2)}) collective-permute-start(bf16[64,2048]{1,0:T(8,128)(2,1)S(1)} %slice.285), channel_id=1, source_target_pairs={{0,2},{1,3},{2,4},{3,5},{4,6},{5,7},{6,0},{7,1},{8,10},{9,11},{10,... | collective-permute-start | bytes 786440 | tf_op jit(solution)/shard_map/ppermute | solution.py:92
  55.3 13.4 %collective-permute-start.5 = (bf16[128,2048]{1,0:T(8,128)(2,1)S(1)}, bf16[128,2048]{1,0:T(8,128)(2,1)S(1)}, u32[]{:S(2)}, u32[]{:S(2)}) collective-permute-start(bf16[128,2048]{1,0:T(8,128)(2,1)S(1)} %collective-permute-done), channel_id=1, source_target_pairs={{0,1},{1,0},{2,3},{3,2},{4,5},{5,4},{6,7},{7,6},{8,9},{9,8},{10,11... | collective-permute-start | bytes 1572872 | tf_op jit(solution)/shard_map/ppermute | solution.py:92
  55.3 15.0 %collective-permute-start.7 = (bf16[128,2048]{1,0:T(8,128)(2,1)S(1)}, bf16[128,2048]{1,0:T(8,128)(2,1)S(1)}, u32[]{:S(2)}, u32[]{:S(2)}) collective-permute-start(bf16[128,2048]{1,0:T(8,128)(2,1)S(1)} %collective-permute-done.2), channel_id=1, source_target_pairs={{0,1},{1,0},{2,3},{3,2},{4,5},{5,4},{6,7},{7,6},{8,9},{9,8},{10,11... | collective-permute-start | bytes 1572872 | tf_op jit(solution)/shard_map/ppermute | solution.py:92
  92.4 21.5 %all-to-all-start.2 = ((bf16[16,272,128]{2,1,0:T(8,128)(2,1)}), bf16[16,272,128]{2,1,0:T(8,128)(2,1)S(1)}, u32[]{:S(2)}, u32[]{:S(2)}) async-start(bf16[16,272,128]{2,1,0:T(8,128)(2,1)} %get-tuple-element.132), calls=%async_computation.2 | async-start | bytes 2228224 | tf_op jit(solution)/shard_map/all_to_all | solution.py:170
  98.2 101.4 %all-gather.19.cloned.1.call-start = ((), (), s32[]{:S(2)}) async-start(), calls=%async_computation.30 | async-start | bytes 4456448 | tf_op jit(solution)/shard_map/all_gather | solution.py:1520
  121.5 11.0 %collective-permute-start.10 = (bf16[64,2048]{1,0:T(8,128)(2,1)}, bf16[64,2048]{1,0:T(8,128)(2,1)S(1)}, u32[]{:S(2)}, u32[]{:S(2)}) collective-permute-start(bf16[64,2048]{1,0:T(8,128)(2,1)} %get-tuple-element.139), channel_id=1, source_target_pairs={{0,2},{1,3},{2,4},{3,5},{4,6},{5,7},{6,0},{7,1},{8,10},{9,11},{10,... | collective-permute-start | bytes 786440 | tf_op jit(solution)/shard_map/ppermute | solution.py:92
  123.0 10.1 %collective-permute-start.8 = (bf16[64,2048]{1,0:T(8,128)(2,1)}, bf16[64,2048]{1,0:T(8,128)(2,1)S(1)}, u32[]{:S(2)}, u32[]{:S(2)}) collective-permute-start(bf16[64,2048]{1,0:T(8,128)(2,1)} %get-tuple-element.139), channel_id=1, source_target_pairs={{0,6},{1,7},{2,0},{3,1},{4,2},{5,3},{6,4},{7,5},{8,14},{9,15},{10,... | collective-permute-start | bytes 786440 | tf_op jit(solution)/shard_map/ppermute | solution.py:92
  126.2 13.6 %collective-permute-start.12 = (bf16[64,2048]{1,0:T(8,128)(2,1)}, bf16[64,2048]{1,0:T(8,128)(2,1)S(1)}, u32[]{:S(2)}, u32[]{:S(2)}) collective-permute-start(bf16[64,2048]{1,0:T(8,128)(2,1)} %get-tuple-element.139), channel_id=1, source_target_pairs={{0,1},{1,0},{2,3},{3,2},{4,5},{5,4},{6,7},{7,6},{8,9},{9,8},{10,11... | collective-permute-start | bytes 786440 | tf_op jit(solution)/shard_map/ppermute | solution.py:92
  126.2 29.3 %all-to-all-start.3 = ((bf16[16,320,128]{2,1,0:T(8,128)(2,1)}), bf16[16,320,128]{2,1,0:T(8,128)(2,1)S(1)}, u32[]{:S(2)}, u32[]{:S(2)}) async-start(bf16[16,320,128]{2,1,0:T(8,128)(2,1)} %get-tuple-element.142), calls=%async_computation.3 | async-start | bytes 2621440 | tf_op jit(solution)/shard_map/all_to_all | solution.py:170
  132.5 7.1 collective-permute-start.11
  133.2 6.5 collective-permute-start.9
  136.1 5.2 collective-permute-start.15
  155.5 24.1 %all-to-all-start.4 = ((bf16[16,192,128]{2,1,0:T(8,128)(2,1)}), bf16[16,192,128]{2,1,0:T(8,128)(2,1)S(1)}, u32[]{:S(2)}, u32[]{:S(2)}) async-start(bf16[16,192,128]{2,1,0:T(8,128)(2,1)} %get-tuple-element.144), calls=%async_computation.4 | async-start | bytes 1572864 | tf_op jit(solution)/shard_map/all_to_all | solution.py:170
  183.2 6.3 collective-permute-start.16
  183.2 16.3 %all-to-all-start.5 = ((bf16[16,64,128]{2,1,0:T(8,128)(2,1)}), bf16[16,64,128]{2,1,0:T(8,128)(2,1)S(1)}, u32[]{:S(2)}, u32[]{:S(2)}) async-start(bf16[16,64,128]{2,1,0:T(8,128)(2,1)} %get-tuple-element.147), calls=%async_computation.5 | async-start | bytes 524288 | tf_op jit(solution)/shard_map/all_to_all | solution.py:170
  189.5 55.0 %reduce-scatter.7.cloned.1.call-start = ((), (), s32[]{:S(2)}) async-start(), calls=%async_computation.20 | async-start | bytes 4718592 | tf_op jit(solution)/shard_map/reduce_scatter | solution.py:100
  193.8 5.1 collective-permute-start.18
  207.5 71.7 %all-gather.11.cloned.1.call-start = ((), (), s32[]{:S(2)}) async-start(), calls=%async_computation.21 | async-start | bytes 4718592 | tf_op jit(solution)/shard_map/all_gather | solution.py:96
  248.0 84.1 %reduce-scatter.9.cloned.1.call-start = ((), (), s32[]{:S(2)}) async-start(), calls=%async_computation.22 | async-start | bytes 4718592 | tf_op jit(solution)/shard_map/reduce_scatter | solution.py:100
  299.4 36.8 %all-to-all-start.6 = ((bf16[16,512,128]{2,1,0:T(8,128)(2,1)}), bf16[16,512,128]{2,1,0:T(8,128)(2,1)}, u32[]{:S(2)}, u32[]{:S(2)}) async-start(bf16[16,512,128]{2,1,0:T(8,128)(2,1)} %bitcast.172), calls=%async_computation.8 | async-start | bytes 4194304 | tf_op jit(solution)/shard_map/all_to_all | solution.py:170
  306.7 84.0 %reduce-scatter.11.cloned.1.call-start = ((), (), s32[]{:S(2)}) async-start(), calls=%async_computation.23 | async-start | bytes 5242880 | tf_op jit(solution)/shard_map/reduce_scatter | solution.py:1553
  336.2 97.3 %reduce-scatter.13.cloned.1.call-start = ((), (), s32[]{:S(2)}) async-start(), calls=%async_computation.24 | async-start | bytes 1310720 | tf_op jit(solution)/shard_map/reduce_scatter | solution.py:1553
  339.2 12.0 %collective-permute-start.19 = (bf16[128,2048]{1,0:T(8,128)(2,1)S(1)}, bf16[128,2048]{1,0:T(8,128)(2,1)S(1)}, u32[]{:S(2)}, u32[]{:S(2)}) collective-permute-start(bf16[128,2048]{1,0:T(8,128)(2,1)S(1)} %get-tuple-element.284), channel_id=1, source_target_pairs={{0,6},{1,7},{2,0},{3,1},{4,2},{5,3},{6,4},{7,5},{8,14},{9,15},{10,... | collective-permute-start | bytes 1572872 | tf_op jit(solution)/shard_map/ppermute | solution.py:92
  340.0 13.1 %collective-permute-start.21 = (bf16[128,2048]{1,0:T(8,128)(2,1)S(1)}, bf16[128,2048]{1,0:T(8,128)(2,1)S(1)}, u32[]{:S(2)}, u32[]{:S(2)}) collective-permute-start(bf16[128,2048]{1,0:T(8,128)(2,1)S(1)} %get-tuple-element.284), channel_id=1, source_target_pairs={{0,2},{1,3},{2,4},{3,5},{4,6},{5,7},{6,0},{7,1},{8,10},{9,11},{10,... | collective-permute-start | bytes 1572872 | tf_op jit(solution)/shard_map/ppermute | solution.py:92
  351.2 6.4 collective-permute-start.20
  353.1 10.3 %collective-permute-start.23 = (bf16[128,2048]{1,0:T(8,128)(2,1)S(1)}, bf16[128,2048]{1,0:T(8,128)(2,1)S(1)}, u32[]{:S(2)}, u32[]{:S(2)}) collective-permute-start(bf16[128,2048]{1,0:T(8,128)(2,1)S(1)} %get-tuple-element.284), channel_id=1, source_target_pairs={{0,1},{1,0},{2,3},{3,2},{4,5},{5,4},{6,7},{7,6},{8,9},{9,8},{10,11... | collective-permute-start | bytes 1572872 | tf_op jit(solution)/shard_map/ppermute | solution.py:92
  353.1 10.0 %collective-permute-start.22 = (bf16[64,2048]{1,0:T(8,128)(2,1)S(1)}, bf16[64,2048]{1,0:T(8,128)(2,1)S(1)}, u32[]{:S(2)}, u32[]{:S(2)}) collective-permute-start(bf16[64,2048]{1,0:T(8,128)(2,1)S(1)} %slice.289), channel_id=1, source_target_pairs={{0,2},{1,3},{2,4},{3,5},{4,6},{5,7},{6,0},{7,1},{8,10},{9,11},{10,... | collective-permute-start | bytes 786440 | tf_op jit(solution)/shard_map/ppermute | solution.py:92
  353.4 10.1 %collective-permute-start.24 = (bf16[128,2048]{1,0:T(8,128)(2,1)S(1)}, bf16[128,2048]{1,0:T(8,128)(2,1)S(1)}, u32[]{:S(2)}, u32[]{:S(2)}) collective-permute-start(bf16[128,2048]{1,0:T(8,128)(2,1)S(1)} %collective-permute-done.19), channel_id=1, source_target_pairs={{0,1},{1,0},{2,3},{3,2},{4,5},{5,4},{6,7},{7,6},{8,9},{9,8},{10,11... | collective-permute-start | bytes 1572872 | tf_op jit(solution)/shard_map/ppermute | solution.py:92
  353.8 11.4 %collective-permute-start.26 = (bf16[128,2048]{1,0:T(8,128)(2,1)S(1)}, bf16[128,2048]{1,0:T(8,128)(2,1)S(1)}, u32[]{:S(2)}, u32[]{:S(2)}) collective-permute-start(bf16[128,2048]{1,0:T(8,128)(2,1)S(1)} %collective-permute-done.21), channel_id=1, source_target_pairs={{0,1},{1,0},{2,3},{3,2},{4,5},{5,4},{6,7},{7,6},{8,9},{9,8},{10,11... | collective-permute-start | bytes 1572872 | tf_op jit(solution)/shard_map/ppermute | solution.py:92
  380.2 5.1 collective-permute-start.29
  390.7 28.3 %all-to-all-start.7 = ((bf16[16,256,128]{2,1,0:T(8,128)(2,1)}), bf16[16,256,128]{2,1,0:T(8,128)(2,1)}, u32[]{:S(2)}, u32[]{:S(2)}) async-start(bf16[16,256,128]{2,1,0:T(8,128)(2,1)} %get-tuple-element.172), calls=%async_computation.10 | async-start | bytes 2097152 | tf_op jit(solution)/shard_map/all_to_all | solution.py:170
  397.9 72.3 %reduce-scatter.15.cloned.1.call-start = ((), (), s32[]{:S(2)}) async-start(), calls=%async_computation.25 | async-start | bytes 4587520 | tf_op jit(solution)/shard_map/reduce_scatter | solution.py:1553
  433.5 10.9 %all-to-all-start.8 = ((bf16[8,128,128]{2,1,0:T(8,128)(2,1)}), bf16[8,128,128]{2,1,0:T(8,128)(2,1)S(1)}, u32[]{:S(2)}, u32[]{:S(2)}) async-start(bf16[8,128,128]{2,1,0:T(8,128)(2,1)} %bitcast.191), calls=%async_computation.12 | async-start | bytes 524288 | tf_op jit(solution)/shard_map/all_to_all | solution.py:174
  436.9 62.4 %reduce-scatter.17.cloned.1.call-start = ((), (), s32[]{:S(2)}) async-start(), calls=%async_computation.26 | async-start | bytes 1146880 | tf_op jit(solution)/shard_map/reduce_scatter | solution.py:1553
  445.6 6.5 collective-permute-start.31
  446.2 5.9 collective-permute-start.35
  448.9 19.4 %collective-permute-start.33 = (bf16[32,2048]{1,0:T(8,128)(2,1)S(1)}, bf16[32,2048]{1,0:T(8,128)(2,1)S(1)}, u32[]{:S(2)}, u32[]{:S(2)}) collective-permute-start(bf16[32,2048]{1,0:T(8,128)(2,1)S(1)} %get-tuple-element.261), channel_id=1, source_target_pairs={{0,2},{1,3},{2,4},{3,5},{4,6},{5,7},{6,0},{7,1},{8,10},{9,11},{10,... | collective-permute-start | bytes 393224 | tf_op jit(solution)/shard_map/ppermute | solution.py:92
  448.9 19.4 %collective-permute-start.34 = (bf16[32,2048]{1,0:T(8,128)(2,1)S(1)}, bf16[32,2048]{1,0:T(8,128)(2,1)S(1)}, u32[]{:S(2)}, u32[]{:S(2)}) collective-permute-start(bf16[32,2048]{1,0:T(8,128)(2,1)S(1)} %get-tuple-element.259), channel_id=1, source_target_pairs={{0,6},{1,7},{2,0},{3,1},{4,2},{5,3},{6,4},{7,5},{8,14},{9,15},{10,... | collective-permute-start | bytes 393224 | tf_op jit(solution)/shard_map/ppermute | solution.py:92
  453.1 15.2 %collective-permute-start.32 = (bf16[32,2048]{1,0:T(8,128)(2,1)S(1)}, bf16[32,2048]{1,0:T(8,128)(2,1)S(1)}, u32[]{:S(2)}, u32[]{:S(2)}) collective-permute-start(bf16[32,2048]{1,0:T(8,128)(2,1)S(1)} %get-tuple-element.264), channel_id=1, source_target_pairs={{0,2},{1,3},{2,4},{3,5},{4,6},{5,7},{6,0},{7,1},{8,10},{9,11},{10,... | collective-permute-start | bytes 393224 | tf_op jit(solution)/shard_map/ppermute | solution.py:92
  453.5 14.8 %collective-permute-start.36 = (bf16[32,2048]{1,0:T(8,128)(2,1)S(1)}, bf16[32,2048]{1,0:T(8,128)(2,1)S(1)}, u32[]{:S(2)}, u32[]{:S(2)}) collective-permute-start(bf16[32,2048]{1,0:T(8,128)(2,1)S(1)} %get-tuple-element.263), channel_id=1, source_target_pairs={{0,6},{1,7},{2,0},{3,1},{4,2},{5,3},{6,4},{7,5},{8,14},{9,15},{10,... | collective-permute-start | bytes 393224 | tf_op jit(solution)/shard_map/ppermute | solution.py:92
  470.2 29.1 %all-to-all-start.9 = ((bf16[16,320,128]{2,1,0:T(8,128)(2,1)}), bf16[16,320,128]{2,1,0:T(8,128)(2,1)}, u32[]{:S(2)}, u32[]{:S(2)}) async-start(bf16[16,320,128]{2,1,0:T(8,128)(2,1)} %attn_bwd.1), calls=%async_computation.14 | async-start | bytes 2621440 | tf_op jit(solution)/shard_map/all_to_all | solution.py:170
  476.3 153.3 %all-gather.13.cloned.1.call-start = ((), (), s32[]{:S(2)}) async-start(), calls=%async_computation.27 | async-start | bytes 8912896 | tf_op jit(solution)/shard_map/all_gather | solution.py:1560
  501.1 28.7 %all-to-all-start.10 = ((bf16[16,272,128]{2,1,0:T(8,128)(2,1)}), bf16[16,272,128]{2,1,0:T(8,128)(2,1)}, u32[]{:S(2)}, u32[]{:S(2)}) async-start(bf16[16,272,128]{2,1,0:T(8,128)(2,1)} %get-tuple-element.196), calls=%async_computation.16 | async-start | bytes 2228224 | tf_op jit(solution)/shard_map/all_to_all | solution.py:170
  541.7 73.4 %all-to-all-start.11 = ((bf16[16,896,128]{2,1,0:T(8,128)(2,1)}), bf16[16,896,128]{2,1,0:T(8,128)(2,1)}, u32[]{:S(2)}, u32[]{:S(2)}) async-start(bf16[16,896,128]{2,1,0:T(8,128)(2,1)} %bitcast.166), calls=%async_computation.17 | async-start | bytes 7340032 | tf_op jit(solution)/shard_map/all_to_all | solution.py:170
  546.6 166.8 %all-gather.15.cloned.1.call-start = ((), (), s32[]{:S(2)}) async-start(), calls=%async_computation.28 | async-start | bytes 5570560 | tf_op jit(solution)/shard_map/all_gather | solution.py:1560
  558.4 4.6 collective-permute-start.38
  558.5 8.9 %collective-permute-start.37 = (bf16[512,2048]{1,0:T(8,128)(2,1)}, bf16[512,2048]{1,0:T(8,128)(2,1)}, u32[]{:S(2)}, u32[]{:S(2)}) collective-permute-start(bf16[512,2048]{1,0:T(8,128)(2,1)} %bitcast.215), channel_id=1, source_target_pairs={{0,1},{1,0},{2,3},{3,2},{4,5},{5,4},{6,7},{7,6},{8,9},{9,8},{10,11... | collective-permute-start | bytes 6291464 | tf_op jit(solution)/shard_map/ppermute | solution.py:92
  633.2 19.7 %collective-permute-start.42 = (bf16[64,4096]{1,0:T(8,128)(2,1)S(1)}, bf16[64,4096]{1,0:T(8,128)(2,1)S(1)}, u32[]{:S(2)}, u32[]{:S(2)}) collective-permute-start(bf16[64,4096]{1,0:T(8,128)(2,1)S(1)} %get-tuple-element.250), channel_id=1, source_target_pairs={{0,2},{1,3},{2,4},{3,5},{4,6},{5,7},{6,0},{7,1},{8,10},{9,11},{10,... | collective-permute-start | bytes 1572872 | tf_op jit(solution)/shard_map/ppermute | solution.py:92
  633.7 19.1 %collective-permute-start.43 = (bf16[64,4096]{1,0:T(8,128)(2,1)S(1)}, bf16[64,4096]{1,0:T(8,128)(2,1)S(1)}, u32[]{:S(2)}, u32[]{:S(2)}) collective-permute-start(bf16[64,4096]{1,0:T(8,128)(2,1)S(1)} %get-tuple-element.249), channel_id=1, source_target_pairs={{0,6},{1,7},{2,0},{3,1},{4,2},{5,3},{6,4},{7,5},{8,14},{9,15},{10,... | collective-permute-start | bytes 1572872 | tf_op jit(solution)/shard_map/ppermute | solution.py:92
  636.4 22.8 %collective-permute-start.44 = (bf16[64,4096]{1,0:T(8,128)(2,1)S(1)}, bf16[64,4096]{1,0:T(8,128)(2,1)S(1)}, u32[]{:S(2)}, u32[]{:S(2)}) collective-permute-start(bf16[64,4096]{1,0:T(8,128)(2,1)S(1)} %get-tuple-element.248), channel_id=1, source_target_pairs={{0,2},{1,3},{2,4},{3,5},{4,6},{5,7},{6,0},{7,1},{8,10},{9,11},{10,... | collective-permute-start | bytes 1572872 | tf_op jit(solution)/shard_map/ppermute | solution.py:92
  636.4 22.8 %collective-permute-start.45 = (bf16[64,4096]{1,0:T(8,128)(2,1)S(1)}, bf16[64,4096]{1,0:T(8,128)(2,1)S(1)}, u32[]{:S(2)}, u32[]{:S(2)}) collective-permute-start(bf16[64,4096]{1,0:T(8,128)(2,1)S(1)} %get-tuple-element.247), channel_id=1, source_target_pairs={{0,6},{1,7},{2,0},{3,1},{4,2},{5,3},{6,4},{7,5},{8,14},{9,15},{10,... | collective-permute-start | bytes 1572872 | tf_op jit(solution)/shard_map/ppermute | solution.py:92
  643.5 5.5 collective-permute-start.40
  659.2 5.9 collective-permute-start.46
  666.8 37.3 %collective-permute-start.51 = (bf16[64,4096]{1,0:T(8,128)(2,1)S(1)}, bf16[64,4096]{1,0:T(8,128)(2,1)}, u32[]{:S(2)}, u32[]{:S(2)}) collective-permute-start(bf16[64,4096]{1,0:T(8,128)(2,1)S(1)} %add_convert_fusion), channel_id=1, source_target_pairs={{0,6},{1,7},{2,0},{3,1},{4,2},{5,3},{6,4},{7,5},{8,14},{9,15},{10,... | collective-permute-start | bytes 1572872 | tf_op jit(solution)/shard_map/ppermute | solution.py:92
  669.7 13.6 %collective-permute-start.48 = (f32[200,128]{1,0:T(8,128)S(1)}, f32[200,128]{1,0:T(8,128)S(1)}, u32[]{:S(2)}, u32[]{:S(2)}) collective-permute-start(f32[200,128]{1,0:T(8,128)S(1)} %fusion.27), channel_id=1, source_target_pairs={{0,2},{1,3},{2,0},{3,1},{4,6},{5,7},{6,4},{7,5},{8,10},{9,11},{10,... | collective-permute-start | bytes 307208 | tf_op jit(solution)/shard_map/ppermute | solution.py:179
  670.0 34.1 %collective-permute-start.50 = (bf16[64,4096]{1,0:T(8,128)(2,1)S(1)}, bf16[64,4096]{1,0:T(8,128)(2,1)}, u32[]{:S(2)}, u32[]{:S(2)}) collective-permute-start(bf16[64,4096]{1,0:T(8,128)(2,1)S(1)} %add_convert_fusion.1), channel_id=1, source_target_pairs={{0,2},{1,3},{2,4},{3,5},{4,6},{5,7},{6,0},{7,1},{8,10},{9,11},{10,... | collective-permute-start | bytes 1572872 | tf_op jit(solution)/shard_map/ppermute | solution.py:92
  683.3 6.5 collective-permute-start.49
  (46 other events, 342.9 us)
Sparse Core Ops, SparseCore 0:
  27.2 55.5 all-gather.16
  92.4 32.0 all-gather.8
  127.3 62.9 all-gather.18
  207.6 36.8 reduce-scatter.6
  248.1 31.0 all-gather.10
  293.3 38.7 reduce-scatter.8
  336.3 43.9 reduce-scatter.10
  390.9 28.7 reduce-scatter.12
  422.6 38.8 reduce-scatter.14
  470.3 28.9 reduce-scatter.16
  502.0 111.9 all-gather.12
  629.7 54.7 all-gather.14
